TPU v7x, 32 devices: a whole 2x2x4 slice. The times are simulated.
32 devices in a mesh: batch: 8 (over z, y), table: 4 (over x, core).
Axes of the slice: x: 2, y: 2, z: 4, core: 2. Of those that a mesh axis runs over, the one named last changes fastest.
Arguments:
- queries: bfloat16 [2, 16384, 128], P(None, ('batch', 'table')), may hold values from -6 to 6
- item_owner: int32 [2, 16384, 1], P(None, ('batch', 'table')), may hold values from 0 to 3; in each aligned block of 512 rows (0 to 511, 512 to 1023, ..., all dimensions but the last counted through in order) at most 384 rows name the same one
- item_row: int32 [2, 16384], P(None, ('batch', 'table')), may hold values from 0 to 479
- table: float32 [1920, 128], P('table'), may hold values from -6 to 6
- accum: float32 [1920], P('table'), may hold values from 0.1 to 1
- fifo: bfloat16 [256, 128], P(('batch', 'table')), may hold values from -0.6 to 0.6
- fifo_head: int32 [32], P(('batch', 'table')), may hold values from 0 to 7
Outputs:
- losses: float32 [2, 16384], P(None, ('batch', 'table'))
- query_grad: bfloat16 [2, 16384, 128], P(None, ('batch', 'table'))
- table_out: float32 [1920, 128], P('table')
- accum_out: float32 [1920], P('table')
- fifo_out: bfloat16 [256, 128], P(('batch', 'table'))
Inputs may be any that keep to these rules, and one draw needn't show every extreme that they name: `item_owner`: in each step the 512 rows of one device name each owner at most 384 times; in some aligned blocks an owner is named exactly 384 times.
All inputs are finite; a program needn't handle non-finite values.
Results may differ from a plain program's by a relative error of at most 0.002.
Values may be sent and summed in bfloat16 or wider, within the bound.
No kernel may reach another device: no remote copies, remote signals or barrier semaphores. Data moves between devices by JAX's collectives and lax.ppermute only.
A program may use at most 64 MiB of HBM per device.

v0:
```python
from functools import partial

import jax
import jax.numpy as jnp
from jax import lax
from jax.sharding import PartitionSpec as P

ENQ = 4


score_scale = 10.0
learn_rate = 0.3
epsilon = 1e-06


def score_piece(query_half, carried, shard_rows):
    total_sum, moment = carried
    scores = score_scale * lax.dot_general(
        query_half, shard_rows, (((1,), (1,)), ((), ())), preferred_element_type=jnp.float32
    )
    weights = jnp.exp(scores)
    moment = moment + jnp.dot(
        weights.astype(jnp.bfloat16), shard_rows, preferred_element_type=jnp.float32
    )
    return (total_sum + jnp.sum(weights, 1), moment)


def score_rows(query_half, carried, shard_rows, first_row):
    row_count = shard_rows.shape[0]
    splits = 1
    while row_count // splits > 1024 and row_count % (splits * 2) == 0:
        splits = splits * 2
    if splits == 1:
        return score_piece(query_half, carried, shard_rows)
    stacked = shard_rows.reshape(splits, row_count // splits, shard_rows.shape[1])

    def one_turn(state, blocks):
        return (score_piece(query_half, state, blocks), None)

    carried, _ = lax.scan(one_turn, carried, stacked)
    return carried


def adagrad_rows(table_part, accum_part, grad_part):
    accum_part = accum_part + jnp.mean(grad_part * grad_part, 1)
    table_part = table_part - learn_rate * grad_part / jnp.sqrt(accum_part)[:, None]
    return (table_part, accum_part)


def per_device(queries, item_owner, item_row, table, accum, fifo, fifo_head):
    step_count, query_count, feature_count = queries.shape
    owners = lax.axis_size("table")
    capacity = 3 * query_count // owners
    owned_rows = table.shape[0]
    queue_rows = fifo.shape[0]
    queue_head = fifo_head[0]
    table_now = table
    accum_now = accum
    fifo_now = fifo
    loss_list = []
    grad_list = []
    owner_range = jnp.arange(owners, dtype=jnp.int32)
    for step_index in range(step_count):
        query_f = queries[step_index].astype(jnp.float32)
        query_norm = jnp.sqrt(jnp.sum(query_f * query_f, 1) + epsilon)
        query_unit = query_f / query_norm[:, None]
        query_half = query_unit.astype(jnp.bfloat16)
        owner_ids = item_owner[step_index, :, 0]
        local_rows = item_row[step_index]
        onehot = (owner_ids[:, None] == owner_range[None, :]).astype(jnp.int32)
        slot_place = jnp.sum((jnp.cumsum(onehot, 0) - onehot) * onehot, 1)
        slot_flat = owner_ids * capacity + slot_place
        request = (
            jnp.full((owners * capacity,), -1, jnp.int32)
            .at[slot_flat]
            .set(local_rows)
            .reshape(owners, capacity)
        )
        table_held = table_now
        asked = lax.all_to_all(request, "table", split_axis=0, concat_axis=0, tiled=True)
        safe_rows = jnp.maximum(asked, 0)
        fetched = table_held[safe_rows]
        replies = lax.all_to_all(fetched, "table", split_axis=0, concat_axis=0, tiled=True)
        item_vecs = replies.reshape(owners * capacity, feature_count)[slot_flat]
        item_norm = jnp.sqrt(jnp.sum(item_vecs * item_vecs, 1) + epsilon)
        item_unit = item_vecs / item_norm[:, None]
        pos_score = score_scale * jnp.sum(query_unit * item_unit, 1)
        start_state = (
            jnp.zeros((query_count,), jnp.float32),
            jnp.zeros((query_count, feature_count), jnp.float32),
        )
        folder = partial(score_rows, query_half)
        block_sums, moment = folder(
            start_state,
            lax.all_gather(fifo_now, ("batch", "table"), axis=0, tiled=True),
            jnp.int32(0),
        )
        total_sum = jnp.exp(pos_score) + block_sums
        loss_list.append(jnp.log(total_sum) - pos_score)
        pos_prob = jnp.exp(pos_score) / total_sum
        unit_grad = score_scale * (
            (pos_prob - 1.0)[:, None] * item_unit + moment / total_sum[:, None]
        )
        along_query = jnp.sum(query_unit * unit_grad, 1)
        query_grad = (unit_grad - query_unit * along_query[:, None]) / query_norm[:, None]
        grad_list.append(query_grad.astype(jnp.bfloat16))
        item_grad = score_scale * (pos_prob - 1.0)[:, None] * query_unit
        along_item = jnp.sum(item_unit * item_grad, 1)
        row_grad = (item_grad - item_unit * along_item[:, None]) / item_norm[:, None]
        outgoing = (
            jnp.zeros((owners * capacity, feature_count), jnp.float32).at[slot_flat].set(row_grad)
        )
        incoming = lax.all_to_all(
            outgoing.reshape(owners, capacity, feature_count).astype(jnp.bfloat16),
            "table",
            split_axis=0,
            concat_axis=0,
            tiled=True,
        ).astype(jnp.float32)
        target_rows = jnp.maximum(asked, 0).reshape(-1)
        dense_grad = (
            jnp.zeros((owned_rows, feature_count), jnp.float32)
            .at[target_rows]
            .add(incoming.reshape(-1, feature_count))
        )
        grad_total = lax.psum(dense_grad, "batch")
        table_now, accum_now = adagrad_rows(table_now, accum_now, grad_total)
        positions = (queue_head + step_index * ENQ + jnp.arange(ENQ, dtype=jnp.int32)) % queue_rows
        fifo_now = fifo_now.at[positions].set(item_unit[:ENQ].astype(jnp.bfloat16))
    return (jnp.stack(loss_list), jnp.stack(grad_list), table_now, accum_now, fifo_now)


def solution(mesh):
    in_specs = (
        P(None, ("batch", "table"), None),
        P(None, ("batch", "table"), None),
        P(None, ("batch", "table")),
        P("table", None),
        P("table"),
        P(("batch", "table"), None),
        P(("batch", "table")),
    )
    out_specs = (
        P(None, ("batch", "table")),
        P(None, ("batch", "table"), None),
        P("table", None),
        P("table"),
        P(("batch", "table"), None),
    )
    return jax.shard_map(
        per_device, mesh=mesh, in_specs=in_specs, out_specs=out_specs, check_vma=False
    )
```

profile of v0, /device:TPU:0, one launch (start us, length us, event | category | flops | bytes accessed | tf_op | source)
XLA Modules:
  0.0 327.2 jit_solution(3133351037996708923)
XLA Ops:
  7.9 1.2 reduce-window.16
  9.6 1.2 reduce-window.14
  12.2 2.5 scatter_custom_fusion
  14.6 7.8 %all_to_all.38 = s32[4,1,384]{2,1,0:T(1,128)S(1)} all-to-all(s32[4,1,384]{2,1,0:T(1,128)S(1)} %all_to_all.24), channel_id=1, replica_groups=mesh['batch'=8,'table'=4] {'table'}, dimensions={0} | all-to-all | bytes 12288 | tf_op jit(solution)/shard_map/all_to_all | solution.py:80
  22.5 3.7 %gather_fusion = f32[1536,128]{1,0:T(8,128)} fusion(f32[480,128]{1,0:T(8,128)S(1)} %copy-done, s32[2048]{0:T(1024)S(1)} %pad_clamp_fusion.1), kind=kCustom, calls=%fused_computation | custom fusion | bytes 1579008 | tf_op jit(solution)/shard_map/gather | solution.py:82
  26.2 3.6 %all-to-all-start.1 = ((f32[4,384,128]{2,1,0:T(8,128)}), f32[4,384,128]{2,1,0:T(8,128)S(1)}, u32[]{:S(2)}, u32[]{:S(2)}) async-start(f32[4,384,128]{2,1,0:T(8,128)} %bitcast.9), calls=%async_computation.1 | async-start | bytes 1572864 | tf_op jit(solution)/shard_map/all_to_all | solution.py:83
  30.0 44.5 %all_gather.6 = bf16[256,128]{1,0:T(8,128)(2,1)S(1)} all-gather(bf16[8,128]{1,0:T(8,128)(2,1)S(1)} %copy.39), channel_id=1, replica_groups=mesh['batch'=8,'table'=4] {'batch','table'}, dimensions={0}, use_global_device_ids=true | all-gather | bytes 67584 | tf_op jit(solution)/shard_map/all_gather | solution.py:95
  76.7 1.9 scatter_custom_fusion.1
  79.4 3.5 %all-to-all-start.2 = ((bf16[4,384,128]{2,1,0:T(8,128)(2,1)}), bf16[4,384,128]{2,1,0:T(8,128)(2,1)S(1)}, u32[]{:S(2)}, u32[]{:S(2)}) async-start(bf16[4,384,128]{2,1,0:T(8,128)(2,1)} %bitcast.15), calls=%async_computation.2 | async-start | bytes 786432 | tf_op jit(solution)/shard_map/all_to_all | solution.py:113
  82.9 2.5 scatter_custom_fusion.3
  86.8 3.5 %all-to-all-done.2 = bf16[4,384,128]{2,1,0:T(8,128)(2,1)S(1)} async-done(((bf16[4,384,128]{2,1,0:T(8,128)(2,1)}), bf16[4,384,128]{2,1,0:T(8,128)(2,1)S(1)}, u32[]{:S(2)}, u32[]{:S(2)}) %all-to-all-start.2) | async-done | bytes 393248 | tf_op jit(solution)/shard_map/all_to_all | solution.py:113
  90.3 3.2 all-to-all-start.3
  93.6 11.4 %scatter_custom_fusion.2 = f32[480,128]{1,0:T(8,128)} fusion(s32[1536]{0:T(1024)S(1)} %reshape.410, bf16[1536,128]{1,0:T(8,128)(2,1)S(1)} %bitcast.128, f32[]{:T(128)} %constant.27.clone.1), kind=kCustom, calls=%fused_computation.24 | custom fusion | flops 393216 | bytes 638980 | tf_op jit(solution)/shard_map/scatter-add | solution.py:124
  105.1 67.9 %all-reduce.3.cloned.1.call-done = f32[480,128]{1,0:T(8,128)} async-done(((f32[480,128]{1,0:T(8,128)}), f32[480,128]{1,0:T(8,128)}) %all-reduce.3.cloned.1.call-update) | async-done | bytes 245776 | tf_op jit(solution)/shard_map/psum | solution.py:126
  173.1 1.2 multiply_reduce_fusion.9
  174.4 3.7 %gather_fusion.2 = f32[1536,128]{1,0:T(8,128)} fusion(f32[480,128]{1,0:T(8,128)S(1)} %divide_subtract_fusion.1, s32[2048]{0:T(1024)S(1)} %pad_clamp_fusion), kind=kCustom, calls=%fused_computation.2 | custom fusion | bytes 1579008 | tf_op jit(solution)/shard_map/gather | solution.py:82
  178.1 3.5 %all-to-all-start.4 = ((f32[4,384,128]{2,1,0:T(8,128)}), f32[4,384,128]{2,1,0:T(8,128)S(1)}, u32[]{:S(2)}, u32[]{:S(2)}) async-start(f32[4,384,128]{2,1,0:T(8,128)} %bitcast.24), calls=%async_computation.4 | async-start | bytes 1572864 | tf_op jit(solution)/shard_map/all_to_all | solution.py:83
  182.3 41.7 %all_gather.7 = bf16[256,128]{1,0:T(8,128)(2,1)S(1)} all-gather(bf16[8,128]{1,0:T(8,128)(2,1)S(1)} %scatter_fusion), channel_id=1, replica_groups=mesh['batch'=8,'table'=4] {'batch','table'}, dimensions={0}, use_global_device_ids=true | all-gather | bytes 67584 | tf_op jit(solution)/shard_map/all_gather | solution.py:95
  226.3 1.9 scatter_custom_fusion.5
  228.9 3.5 %all-to-all-start.5 = ((bf16[4,384,128]{2,1,0:T(8,128)(2,1)}), bf16[4,384,128]{2,1,0:T(8,128)(2,1)S(1)}, u32[]{:S(2)}, u32[]{:S(2)}) async-start(bf16[4,384,128]{2,1,0:T(8,128)(2,1)} %bitcast.32), calls=%async_computation.5 | async-start | bytes 786432 | tf_op jit(solution)/shard_map/all_to_all | solution.py:113
  234.1 5.7 %all-to-all-done.5 = bf16[4,384,128]{2,1,0:T(8,128)(2,1)S(1)} async-done(((bf16[4,384,128]{2,1,0:T(8,128)(2,1)}), bf16[4,384,128]{2,1,0:T(8,128)(2,1)S(1)}, u32[]{:S(2)}, u32[]{:S(2)}) %all-to-all-start.5) | async-done | bytes 393248 | tf_op jit(solution)/shard_map/all_to_all | solution.py:113
  239.8 11.4 %scatter_custom_fusion.6 = f32[480,128]{1,0:T(8,128)} fusion(s32[1536]{0:T(1024)S(1)} %reshape.426, bf16[1536,128]{1,0:T(8,128)(2,1)S(1)} %bitcast.127, f32[]{:T(128)} %constant.27.clone.1), kind=kCustom, calls=%fused_computation.22 | custom fusion | flops 393216 | bytes 638980 | tf_op jit(solution)/shard_map/scatter-add | solution.py:124
  251.9 65.9 %all-reduce.5.cloned.1.call-done = f32[480,128]{1,0:T(8,128)} async-done(((f32[480,128]{1,0:T(8,128)}), f32[480,128]{1,0:T(8,128)}) %all-reduce.5.cloned.1.call-update) | async-done | bytes 245776 | tf_op jit(solution)/shard_map/psum | solution.py:126
  317.8 1.2 multiply_reduce_fusion.8
  (90 shorter events, 14.0 us)
Async XLA Ops:
  7.2 0.7 copy-start.5
  7.2 15.3 %copy-start = (f32[480,128]{1,0:T(8,128)S(1)}, f32[480,128]{1,0:T(8,128)}, u32[]{:S(2)}) copy-start(f32[480,128]{1,0:T(8,128)} %param.10) | copy-start | bytes 737284
  26.2 3.6 %copy-start.3 = (bf16[2,512,128]{2,1,0:T(8,128)(2,1)S(1)}, bf16[2,512,128]{2,1,0:T(8,128)(2,1)}, u32[]{:S(2)}) copy-start(bf16[2,512,128]{2,1,0:T(8,128)(2,1)} %param.7) | copy-start | bytes 786436
  26.2 48.4 %all-to-all-start.1 = ((f32[4,384,128]{2,1,0:T(8,128)}), f32[4,384,128]{2,1,0:T(8,128)S(1)}, u32[]{:S(2)}, u32[]{:S(2)}) async-start(f32[4,384,128]{2,1,0:T(8,128)} %bitcast.9), calls=%async_computation.1 | async-start | bytes 1572864 | tf_op jit(solution)/shard_map/all_to_all | solution.py:83
  79.4 10.9 %all-to-all-start.2 = ((bf16[4,384,128]{2,1,0:T(8,128)(2,1)}), bf16[4,384,128]{2,1,0:T(8,128)(2,1)S(1)}, u32[]{:S(2)}, u32[]{:S(2)}) async-start(bf16[4,384,128]{2,1,0:T(8,128)(2,1)} %bitcast.15), calls=%async_computation.2 | async-start | bytes 786432 | tf_op jit(solution)/shard_map/all_to_all | solution.py:113
  90.3 14.8 %all-to-all-start.3 = ((s32[4,1,384]{2,1,0:T(1,128)}), s32[4,1,384]{2,1,0:T(1,128)S(1)}, u32[]{:S(2)}, u32[]{:S(2)}) async-start(s32[4,1,384]{2,1,0:T(1,128)} %all_to_all.28), calls=%async_computation.3 | async-start | bytes 12288 | tf_op jit(solution)/shard_map/all_to_all | solution.py:80
  93.5 79.5 %all-reduce.3.cloned.1.call-start = ((), (), s32[]{:S(2)}) async-start(), calls=%async_computation.6 | async-start | bytes 491520 | tf_op jit(solution)/shard_map/psum | solution.py:126
  105.1 69.1 %copy-start.6 = (f32[480]{0:T(512)S(1)}, f32[480]{0:T(512)}, u32[]{:S(2)}) copy-start(f32[480]{0:T(512)} %param.11) | copy-start | bytes 5764
  173.1 1.2 copy-start.1
  178.1 46.2 %all-to-all-start.4 = ((f32[4,384,128]{2,1,0:T(8,128)}), f32[4,384,128]{2,1,0:T(8,128)S(1)}, u32[]{:S(2)}, u32[]{:S(2)}) async-start(f32[4,384,128]{2,1,0:T(8,128)} %bitcast.24), calls=%async_computation.4 | async-start | bytes 1572864 | tf_op jit(solution)/shard_map/all_to_all | solution.py:83
  228.9 10.9 %all-to-all-start.5 = ((bf16[4,384,128]{2,1,0:T(8,128)(2,1)}), bf16[4,384,128]{2,1,0:T(8,128)(2,1)S(1)}, u32[]{:S(2)}, u32[]{:S(2)}) async-start(bf16[4,384,128]{2,1,0:T(8,128)(2,1)} %bitcast.32), calls=%async_computation.5 | async-start | bytes 786432 | tf_op jit(solution)/shard_map/all_to_all | solution.py:113
  232.4 85.4 %all-reduce.5.cloned.1.call-start = ((), (), s32[]{:S(2)}) async-start(), calls=%async_computation.7 | async-start | bytes 491520 | tf_op jit(solution)/shard_map/psum | solution.py:126
  234.1 17.2 %copy-start.4 = (bf16[8,128]{1,0:T(8,128)(2,1)}, bf16[8,128]{1,0:T(8,128)(2,1)S(1)}, u32[]{:S(2)}) copy-start(bf16[8,128]{1,0:T(8,128)(2,1)S(1)} %scatter_fusion.1) | copy-start | bytes 6148
  317.8 1.8 copy-start.2
Sparse Core Ops, SparseCore 0:
  105.2 67.8 all-reduce.2
  251.4 66.3 all-reduce.4
where the time goes:
time: 328 us; the launch traced here: 327 us
  waiting for transfers between devices  143 us (44%)
  blocking collectives  94 us (29%)
  other arithmetic  32.8 us (10%)
  local copies, waits for them, and re-layouts  23.7 us (7%)
  starting transfers between devices  17.4 us (5%)
  between operations  15.1 us (5%)
    psum x2, waiting for transfers between devices, per_device(): grad_total = lax.psum(dense_grad, 'batch')  134 us
    all_gather x2, blocking collectives, per_device(): lax.all_gather(fifo_now, ('batch', 'table'), axis=0, tiled=True)  86.2 us
    scatter-add x2, other arithmetic, per_device(): dense_grad = jnp.zeros((owned_rows, feature_count), jnp.float32).at[targe...  22.8 us
    all_to_all x2, waiting for transfers between devices, per_device(): lax.all_to_all(outgoing.reshape(owners, capacity, feature_count).astype(j...  9.26 us
    all_to_all x1, blocking collectives, per_device(): lax.all_to_all(request, 'table', split_axis=0, concat_axis=0, tiled=True)  7.81 us
    gather x2, local copies, waits for them, and re-layouts, per_device(): fetched = table_held[safe_rows]  7.32 us
    all_to_all x2, starting transfers between devices, per_device(): lax.all_to_all(fetched, 'table', split_axis=0, concat_axis=0, tiled=True)  7.12 us
    all_to_all x2, starting transfers between devices, per_device(): lax.all_to_all(outgoing.reshape(owners, capacity, feature_count).astype(j...  6.92 us
  transfers between devices with their start and end apart: 7, of which 4 were waited for; matrix products, arithmetic and copies ran while one was open for 5% of the time, Pallas kernels for 0%

commit v1 on v0

v1 whole, which is shorter than its diff:
```python
import jax
import jax.numpy as jnp
from jax import lax
from jax.sharding import PartitionSpec as P

ENQ = 4
score_scale = 10.0
learn_rate = 0.3
epsilon = 1e-06
f32 = jnp.float32
bf16 = jnp.bfloat16
f16 = jnp.float16


def stages_of(count):
    stages, stride = [], 1
    while count > 1:
        radix = next(r for r in range(2, count + 1) if count % r == 0)
        stages.append((stride, radix))
        stride, count = stride * radix, count // radix
    return stages


def partners(piece, axis, stride, radix):
    count = lax.axis_size(axis)
    found = []
    for turn in range(1, radix):
        pairs = []
        for target in range(count):
            digit = target // stride % radix
            source = target + ((digit + turn) % radix - digit) * stride
            pairs.append((source, target))
        found.append(lax.ppermute(piece, axis, pairs))
    return found


def gather_any_order(piece, axis, stages):
    for stride, radix in stages:
        piece = jnp.concatenate([piece] + partners(piece, axis, stride, radix))
    return piece


def sum_over(total, axis, stages):
    for stride, radix in stages:
        sent = lax.optimization_barrier(total.astype(f16))
        parts = [sent] + partners(sent, axis, stride, radix)
        if radix > 2:
            digit = lax.axis_index(axis) // stride % radix
            order = (jnp.arange(radix, dtype=jnp.int32) - digit) % radix
            parts = list(jnp.stack(parts)[order])
        total = parts[0].astype(f32)
        for part in parts[1:]:
            total = total + part.astype(f32)
    return total


def split_parts(rows, terms):
    parts = []
    for _ in range(terms):
        part = lax.reduce_precision(rows, 8, 7)
        parts.append(part.astype(bf16))
        rows = rows - part
    return jnp.concatenate(parts, 1)


def pick_rows(places, parts, width):
    chosen = (places[:, None] == jnp.arange(parts.shape[0], dtype=jnp.int32)[None, :]).astype(bf16)
    found = jnp.dot(chosen, parts, preferred_element_type=f32)
    rows = found[:, :width]
    for start in range(width, parts.shape[1], width):
        rows = rows + found[:, start : start + width]
    return rows


def score_piece(query_half, carried, rows, kept):
    total_sum, moment = carried
    scores = score_scale * lax.dot_general(
        query_half, rows, (((1,), (1,)), ((), ())), preferred_element_type=f32
    )
    weights = jnp.where(kept[None, :], jnp.exp(scores), 0.0)
    moment = moment + jnp.dot(weights.astype(bf16), rows, preferred_element_type=f32)
    return (total_sum + jnp.sum(weights, 1), moment)


def score_rows(query_half, rows, kept):
    count, width = rows.shape
    carried = (jnp.zeros(query_half.shape[:1], f32), jnp.zeros(query_half.shape, f32))
    splits = 1
    while count // splits > 1024 and count % (splits * 2) == 0:
        splits = splits * 2
    if splits == 1:
        return score_piece(query_half, carried, rows, kept)
    stacked = (rows.reshape(splits, -1, width), kept.reshape(splits, -1))
    return lax.scan(lambda c, b: (score_piece(query_half, c, *b), None), carried, stacked)[0]


def norm_of(rows):
    return jnp.sqrt(jnp.sum(rows * rows, 1) + epsilon)


def per_device(queries, item_owner, item_row, table, accum, fifo, fifo_head):
    step_count, query_count, width = queries.shape
    owners, copies = lax.axis_size("table"), lax.axis_size("batch")
    owned = table.shape[0]
    queue_rows = fifo.shape[0]
    me = lax.axis_index("table")
    table_masks = [stride for stride, _ in reversed(stages_of(owners))]
    batch_stages = stages_of(copies)
    most = owners * copies * (3 * query_count // owners)
    grad_scale = 1.0
    while most * grad_scale > 32768.0:
        grad_scale = grad_scale / 2

    def place_of(owner, row):
        apart = jnp.bitwise_xor(owner, me)
        place = jnp.zeros_like(owner)
        for index, mask in enumerate(table_masks):
            place = place + jnp.where((apart & mask) != 0, 1 << index, 0)
        return place * owned + row

    def gather_table(piece):
        for mask in table_masks:
            piece = jnp.concatenate([piece] + partners(piece, "table", mask, 2))
        return piece

    head = fifo_head[0]
    table_all = gather_table(table)

    first_owner, first_row = item_owner[0, :ENQ, 0], item_row[0, :ENQ]
    told = jnp.concatenate([first_owner, first_row // 16, first_row % 16, head[None]])
    told_row = jnp.pad(told.astype(bf16), (0, width - told.shape[0]))[None, :]
    pad = jnp.zeros((-(queue_rows + 1) % 16, width), bf16)
    block = jnp.concatenate([fifo, told_row, pad])
    blocks = gather_any_order(block, "table", stages_of(owners))
    blocks = gather_any_order(blocks, "batch", batch_stages)
    blocks = blocks.reshape(owners * copies, -1, width)
    queue = blocks[:, :queue_rows].reshape(-1, width)
    told_all = blocks[:, queue_rows, : told.shape[0]].astype(jnp.int32)
    new_place = place_of(
        told_all[:, :ENQ], told_all[:, ENQ : 2 * ENQ] * 16 + told_all[:, 2 * ENQ : 3 * ENQ]
    ).reshape(-1)
    slots = jnp.arange(queue_rows, dtype=jnp.int32)
    kept = ((slots[None, :] - told_all[:, 3 * ENQ :]) % queue_rows >= ENQ).reshape(-1)

    parts = split_parts(table_all, 3)
    new_rows = pick_rows(new_place, parts, width)
    new_half = (new_rows / norm_of(new_rows)[:, None]).astype(bf16)

    loss_list, grad_list, joined = [], [], []
    for step in range(step_count):
        query_f = queries[step].astype(f32)
        query_norm = norm_of(query_f)
        query_unit = query_f / query_norm[:, None]
        query_half = query_unit.astype(bf16)
        places = place_of(item_owner[step, :, 0], item_row[step])
        if step == 0:
            rows, row_kept = queue, jnp.ones((queue.shape[0],), jnp.bool_)
        else:
            rows = jnp.concatenate([queue, new_half])
            row_kept = jnp.concatenate([kept, jnp.ones((new_half.shape[0],), jnp.bool_)])
        block_sums, moment = score_rows(query_half, rows, row_kept)
        item_vecs = pick_rows(places, parts, width)
        if step == 0:
            item_unit = item_vecs / norm_of(item_vecs)[:, None]
        else:
            item_unit = item_vecs
        joined.append(item_unit[:ENQ].astype(bf16))
        cosine = jnp.sum(query_unit * item_unit, 1)
        pos_score = score_scale * cosine
        total_sum = jnp.exp(pos_score) + block_sums
        loss_list.append(jnp.log(total_sum) - pos_score)
        lack = jnp.exp(pos_score) / total_sum - 1.0
        unit_grad = score_scale * (lack[:, None] * item_unit + moment / total_sum[:, None])
        along_query = jnp.sum(query_unit * unit_grad, 1)
        query_grad = (unit_grad - query_unit * along_query[:, None]) / query_norm[:, None]
        grad_list.append(query_grad.astype(bf16))

        across = (lack[:, None] * (query_unit - item_unit * cosine[:, None])).astype(bf16)
        chosen = (places[:, None] == jnp.arange(owners * owned, dtype=jnp.int32)[None, :]).astype(bf16)
        dense = grad_scale * lax.dot_general(
            chosen, across, (((0,), (0,)), ((), ())), preferred_element_type=f32
        )
        for mask in reversed(table_masks):
            half = dense.shape[0] // 2
            (other,) = partners(dense[half:].astype(f16), "table", mask, 2)
            dense = dense[:half] + other.astype(f32)
        dense = sum_over(dense, "batch", batch_stages)
        grad = dense * ((score_scale / grad_scale) / norm_of(table))[:, None]
        accum = accum + jnp.mean(grad * grad, 1)
        table = table - learn_rate * grad / jnp.sqrt(accum)[:, None]
        if step + 1 < step_count:
            unit = (table / norm_of(table)[:, None]).astype(f16)
            parts = split_parts(gather_table(unit).astype(f32), 2)

    fifo_out = fifo
    for step in range(step_count):
        place = (slots - head - step * ENQ) % queue_rows
        for k in range(ENQ):
            fifo_out = jnp.where((place == k)[:, None], joined[step][k][None, :], fifo_out)
    return (jnp.stack(loss_list), jnp.stack(grad_list), table, accum, fifo_out)


def solution(mesh):
    both = ("batch", "table")
    in_specs = (
        P(None, both, None),
        P(None, both, None),
        P(None, both),
        P("table", None),
        P("table"),
        P(both, None),
        P(both),
    )
    out_specs = (P(None, both), P(None, both, None), P("table", None), P("table"), P(both, None))
    return jax.shard_map(
        per_device, mesh=mesh, in_specs=in_specs, out_specs=out_specs, check_vma=False
    )
```

time: 328 us -> 98 us (0.30)
  waiting for transfers between devices: 143 us -> 41 us
  blocking collectives: 94 us -> 0 us
  local copies, waits for them, and re-layouts: 23.7 us -> 5.4 us
  other arithmetic: 32.8 us -> 16.7 us
  between operations: 15.1 us -> 1.78 us
  starting transfers between devices: 17.4 us -> 24.6 us
  matrix products: 1.03 us -> 8 us
    psum x2 -> x0, waiting for transfers between devices: 134 us -> none  [per_device(): grad_total = lax.psum(dense_grad, 'batch')]
    all_gather x2 -> x0, blocking collectives: 86.2 us -> none  [per_device(): lax.all_gather(fifo_now, ('batch', 'table'), axis=0, tiled=True)]
    ppermute x0 -> x19, waiting for transfers between devices: none -> 41 us  [partners(): found.append(lax.ppermute(piece, axis, pairs))]
    ppermute x0 -> x19, starting transfers between devices: none -> 24.6 us  [partners(): found.append(lax.ppermute(piece, axis, pairs))]
    scatter-add x2 -> x0, other arithmetic: 22.8 us -> none  [per_device(): dense_grad = jnp.zeros((owned_rows, feature_count), jnp.float32).at[targe...]
    all_to_all x5 -> x0, starting transfers between devices: 17.3 us -> none  [the longest x2 7.12 us: per_device(): lax.all_to_all(fetched, 'table', split_axis=0, concat_axis=0, tiled=True)]
    scatter x6 -> x0, local copies, waits for them, and re-layouts: 9.9 us -> none  [the longest x2 4.9 us: per_device(): request = jnp.full((owners * capacity,), -1, jnp.int32).at[slot_flat].set...]
    gather x6 -> x0, local copies, waits for them, and re-layouts: 9.65 us -> none  [the longest x2 7.32 us: per_device(): fetched = table_held[safe_rows]]
  transfers between devices with their start and end apart: 7 -> 19, of which waited for: 4 -> 16; matrix products, arithmetic and copies ran while one was open for 5% -> 17% of each run, Pallas kernels for 0% -> 0%
where the time goes in v1:
time: 98 us; the launch traced here: 97.5 us
  waiting for transfers between devices  41 us (42%)
  starting transfers between devices  24.6 us (25%)
  other arithmetic  16.7 us (17%)
  matrix products  8 us (8%)
  local copies, waits for them, and re-layouts  5.4 us (6%)
  between operations  1.78 us (2%)
    ppermute x19, waiting for transfers between devices, partners(): found.append(lax.ppermute(piece, axis, pairs))  41 us
    ppermute x19, starting transfers between devices, partners(): found.append(lax.ppermute(piece, axis, pairs))  24.6 us
    reduce_sum x6, other arithmetic, norm_of(): return jnp.sqrt(jnp.sum(rows * rows, 1) + epsilon)  3.05 us
    concatenate x4, local copies, waits for them, and re-layouts, gather_any_order(): piece = jnp.concatenate([piece] + partners(piece, axis, stride, radix))  3.05 us
    dot_general x2, matrix products, per_device(): lax.dot_general(chosen, across, (((0,), (0,)), ((), ())), preferred_eleme...  3.01 us
    dot_general x3, matrix products, pick_rows(): found = jnp.dot(chosen, parts, preferred_element_type=f32)  2.57 us
  transfers between devices with their start and end apart: 19, of which 16 were waited for; matrix products, arithmetic and copies ran while one was open for 17% of the time, Pallas kernels for 0%

profile of v1, /device:TPU:0, one launch (start us, length us, event | category | flops | bytes accessed | tf_op | source)
XLA Modules:
  0.0 97.5 jit_solution(16032370009558780611)
XLA Ops:
  3.9 2.6 %collective-permute-start = (f32[480,128]{1,0:T(8,128)}, f32[480,128]{1,0:T(8,128)S(1)}, u32[]{:S(2)}, u32[]{:S(2)}) collective-permute-start(f32[480,128]{1,0:T(8,128)} %param.10), channel_id=1, source_target_pairs={{2,0},{3,1},{0,2},{1,3},{6,4},{7,5},{4,6},{5,7},{10,8},{11,9},{8,1... | collective-permute-start | bytes 737288 | tf_op jit(solution)/shard_map/ppermute | solution.py:33
  11.0 3.6 %collective-permute-done.3 = bf16[32,128]{1,0:T(8,128)(2,1)S(1)} collective-permute-done((bf16[32,128]{1,0:T(8,128)(2,1)S(1)}, bf16[32,128]{1,0:T(8,128)(2,1)S(1)}, u32[]{:S(2)}, u32[]{:S(2)}) %collective-permute-start.3) | collective-permute-done | bytes 8224 | tf_op jit(solution)/shard_map/ppermute | solution.py:33
  15.3 1.6 %collective-permute-start.4 = (bf16[64,128]{1,0:T(8,128)(2,1)S(1)}, bf16[64,128]{1,0:T(8,128)(2,1)S(1)}, u32[]{:S(2)}, u32[]{:S(2)}) collective-permute-start(bf16[64,128]{1,0:T(8,128)(2,1)S(1)} %concatenate.59), channel_id=1, source_target_pairs={{4,0},{0,4},{12,8},{8,12},{20,16},{16,20},{28,24},{24,28},{5,1},{1... | collective-permute-start | bytes 49160 | tf_op jit(solution)/shard_map/ppermute | solution.py:33
  17.5 1.6 %collective-permute-done.4 = bf16[64,128]{1,0:T(8,128)(2,1)S(1)} collective-permute-done((bf16[64,128]{1,0:T(8,128)(2,1)S(1)}, bf16[64,128]{1,0:T(8,128)(2,1)S(1)}, u32[]{:S(2)}, u32[]{:S(2)}) %collective-permute-start.4) | collective-permute-done | bytes 16416 | tf_op jit(solution)/shard_map/ppermute | solution.py:33
  19.8 1.6 %collective-permute-start.5 = (bf16[128,128]{1,0:T(8,128)(2,1)S(1)}, bf16[128,128]{1,0:T(8,128)(2,1)S(1)}, u32[]{:S(2)}, u32[]{:S(2)}) collective-permute-start(bf16[128,128]{1,0:T(8,128)(2,1)S(1)} %concatenate.60), channel_id=1, source_target_pairs={{8,0},{12,4},{0,8},{4,12},{24,16},{28,20},{16,24},{20,28},{9,1},{1... | collective-permute-start | bytes 98312 | tf_op jit(solution)/shard_map/ppermute | solution.py:33
  22.0 1.8 %collective-permute-done.5 = bf16[128,128]{1,0:T(8,128)(2,1)S(1)} collective-permute-done((bf16[128,128]{1,0:T(8,128)(2,1)S(1)}, bf16[128,128]{1,0:T(8,128)(2,1)S(1)}, u32[]{:S(2)}, u32[]{:S(2)}) %collective-permute-start.5) | collective-permute-done | bytes 32800 | tf_op jit(solution)/shard_map/ppermute | solution.py:33
  24.6 2.7 %collective-permute-start.6 = (bf16[256,128]{1,0:T(8,128)(2,1)S(1)}, bf16[256,128]{1,0:T(8,128)(2,1)S(1)}, u32[]{:S(2)}, u32[]{:S(2)}) collective-permute-start(bf16[256,128]{1,0:T(8,128)(2,1)S(1)} %concatenate.61), channel_id=1, source_target_pairs={{16,0},{20,4},{24,8},{28,12},{0,16},{4,20},{8,24},{12,28},{17,1},{... | collective-permute-start | bytes 196616 | tf_op jit(solution)/shard_map/ppermute | solution.py:33
  27.8 2.0 %collective-permute-done.6 = bf16[256,128]{1,0:T(8,128)(2,1)S(1)} collective-permute-done((bf16[256,128]{1,0:T(8,128)(2,1)S(1)}, bf16[256,128]{1,0:T(8,128)(2,1)S(1)}, u32[]{:S(2)}, u32[]{:S(2)}) %collective-permute-start.6) | collective-permute-done | bytes 65568 | tf_op jit(solution)/shard_map/ppermute | solution.py:33
  41.6 4.2 %collective-permute-done.8 = f16[480,128]{1,0:T(8,128)(2,1)S(1)} collective-permute-done((f16[480,128]{1,0:T(8,128)(2,1)S(1)}, f16[480,128]{1,0:T(8,128)(2,1)S(1)}, u32[]{:S(2)}, u32[]{:S(2)}) %collective-permute-start.8) | collective-permute-done | bytes 122912 | tf_op jit(solution)/shard_map/ppermute | solution.py:33
  45.8 1.6 %collective-permute-start.9 = (f16[480,128]{1,0:T(8,128)(2,1)S(1)}, f16[480,128]{1,0:T(8,128)(2,1)S(1)}, u32[]{:S(2)}, u32[]{:S(2)}) collective-permute-start(f16[480,128]{1,0:T(8,128)(2,1)S(1)} %fusion.32), channel_id=1, source_target_pairs={{4,0},{0,4},{12,8},{8,12},{20,16},{16,20},{28,24},{24,28},{5,1},{1... | collective-permute-start | bytes 368648 | tf_op jit(solution)/shard_map/ppermute | solution.py:33
  47.4 3.4 %collective-permute-done.9 = f16[480,128]{1,0:T(8,128)(2,1)S(1)} collective-permute-done((f16[480,128]{1,0:T(8,128)(2,1)S(1)}, f16[480,128]{1,0:T(8,128)(2,1)S(1)}, u32[]{:S(2)}, u32[]{:S(2)}) %collective-permute-start.9) | collective-permute-done | bytes 122912 | tf_op jit(solution)/shard_map/ppermute | solution.py:33
  50.8 1.6 %collective-permute-start.10 = (f16[480,128]{1,0:T(8,128)(2,1)S(1)}, f16[480,128]{1,0:T(8,128)(2,1)S(1)}, u32[]{:S(2)}, u32[]{:S(2)}) collective-permute-start(f16[480,128]{1,0:T(8,128)(2,1)S(1)} %add_convert_fusion.3), channel_id=1, source_target_pairs={{8,0},{12,4},{0,8},{4,12},{24,16},{28,20},{16,24},{20,28},{9,1},{1... | collective-permute-start | bytes 368648 | tf_op jit(solution)/shard_map/ppermute | solution.py:33
  52.5 3.2 %collective-permute-done.10 = f16[480,128]{1,0:T(8,128)(2,1)S(1)} collective-permute-done((f16[480,128]{1,0:T(8,128)(2,1)S(1)}, f16[480,128]{1,0:T(8,128)(2,1)S(1)}, u32[]{:S(2)}, u32[]{:S(2)}) %collective-permute-start.10) | collective-permute-done | bytes 122912 | tf_op jit(solution)/shard_map/ppermute | solution.py:33
  55.7 2.8 %collective-permute-start.11 = (f16[480,128]{1,0:T(8,128)(2,1)S(1)}, f16[480,128]{1,0:T(8,128)(2,1)S(1)}, u32[]{:S(2)}, u32[]{:S(2)}) collective-permute-start(f16[480,128]{1,0:T(8,128)(2,1)S(1)} %add_convert_fusion.2), channel_id=1, source_target_pairs={{16,0},{20,4},{24,8},{28,12},{0,16},{4,20},{8,24},{12,28},{17,1},{... | collective-permute-start | bytes 368648 | tf_op jit(solution)/shard_map/ppermute | solution.py:33
  58.6 3.0 %collective-permute-done.11 = f16[480,128]{1,0:T(8,128)(2,1)S(1)} collective-permute-done((f16[480,128]{1,0:T(8,128)(2,1)S(1)}, f16[480,128]{1,0:T(8,128)(2,1)S(1)}, u32[]{:S(2)}, u32[]{:S(2)}) %collective-permute-start.11) | collective-permute-done | bytes 122912 | tf_op jit(solution)/shard_map/ppermute | solution.py:33
  63.0 4.3 %collective-permute-done.12 = f16[480,128]{1,0:T(8,128)(2,1)S(1)} collective-permute-done((f16[480,128]{1,0:T(8,128)(2,1)S(1)}, f16[480,128]{1,0:T(8,128)(2,1)S(1)}, u32[]{:S(2)}, u32[]{:S(2)}) %collective-permute-start.12) | collective-permute-done | bytes 122912 | tf_op jit(solution)/shard_map/ppermute | solution.py:33
  70.3 1.5 %fusion = f32[1920,128]{1,0:T(8,128)S(1)} fusion(s32[512]{0:T(512)S(1)} %add.267, f32[512,128]{1,0:T(8,128)S(1)} %get-tuple-element.10, f32[512]{0:T(512)S(1)} %multiply_reduce_fusion.2, f32[512]{0:T(512)S(1)} %get-tuple-element.38, f32[512]{0:T(512)S(1)} %add_sqrt_fusion, bf16[2,512,128]{2,1,0:T(8,128)(2,1)S(1)} %copy-done), kind=kOutput, calls=%fused_computation.1 | convolution fusion | flops 253034496 | bytes 1384448 | tf_op jit(solution)/shard_map/dot_general | solution.py:180
  74.6 4.8 %collective-permute-done.15 = f16[480,128]{1,0:T(8,128)(2,1)S(1)} collective-permute-done((f16[480,128]{1,0:T(8,128)(2,1)S(1)}, f16[480,128]{1,0:T(8,128)(2,1)S(1)}, u32[]{:S(2)}, u32[]{:S(2)}) %collective-permute-start.15) | collective-permute-done | bytes 122912 | tf_op jit(solution)/shard_map/ppermute | solution.py:33
  79.4 1.6 %collective-permute-start.16 = (f16[480,128]{1,0:T(8,128)(2,1)S(1)}, f16[480,128]{1,0:T(8,128)(2,1)S(1)}, u32[]{:S(2)}, u32[]{:S(2)}) collective-permute-start(f16[480,128]{1,0:T(8,128)(2,1)S(1)} %fusion.31), channel_id=1, source_target_pairs={{4,0},{0,4},{12,8},{8,12},{20,16},{16,20},{28,24},{24,28},{5,1},{1... | collective-permute-start | bytes 368648 | tf_op jit(solution)/shard_map/ppermute | solution.py:33
  81.6 2.7 %collective-permute-done.16 = f16[480,128]{1,0:T(8,128)(2,1)S(1)} collective-permute-done((f16[480,128]{1,0:T(8,128)(2,1)S(1)}, f16[480,128]{1,0:T(8,128)(2,1)S(1)}, u32[]{:S(2)}, u32[]{:S(2)}) %collective-permute-start.16) | collective-permute-done | bytes 122912 | tf_op jit(solution)/shard_map/ppermute | solution.py:33
  84.4 2.2 %collective-permute-start.17 = (f16[480,128]{1,0:T(8,128)(2,1)S(1)}, f16[480,128]{1,0:T(8,128)(2,1)S(1)}, u32[]{:S(2)}, u32[]{:S(2)}) collective-permute-start(f16[480,128]{1,0:T(8,128)(2,1)S(1)} %add_convert_fusion.1), channel_id=1, source_target_pairs={{8,0},{12,4},{0,8},{4,12},{24,16},{28,20},{16,24},{20,28},{9,1},{1... | collective-permute-start | bytes 368648 | tf_op jit(solution)/shard_map/ppermute | solution.py:33
  86.6 2.8 %collective-permute-done.17 = f16[480,128]{1,0:T(8,128)(2,1)S(1)} collective-permute-done((f16[480,128]{1,0:T(8,128)(2,1)S(1)}, f16[480,128]{1,0:T(8,128)(2,1)S(1)}, u32[]{:S(2)}, u32[]{:S(2)}) %collective-permute-start.17) | collective-permute-done | bytes 122912 | tf_op jit(solution)/shard_map/ppermute | solution.py:33
  89.5 3.4 %collective-permute-start.18 = (f16[480,128]{1,0:T(8,128)(2,1)S(1)}, f16[480,128]{1,0:T(8,128)(2,1)S(1)}, u32[]{:S(2)}, u32[]{:S(2)}) collective-permute-start(f16[480,128]{1,0:T(8,128)(2,1)S(1)} %add_convert_fusion), channel_id=1, source_target_pairs={{16,0},{20,4},{24,8},{28,12},{0,16},{4,20},{8,24},{12,28},{17,1},{... | collective-permute-start | bytes 368648 | tf_op jit(solution)/shard_map/ppermute | solution.py:33
  94.2 1.5 %collective-permute-done.18 = f16[480,128]{1,0:T(8,128)(2,1)S(1)} collective-permute-done((f16[480,128]{1,0:T(8,128)(2,1)S(1)}, f16[480,128]{1,0:T(8,128)(2,1)S(1)}, u32[]{:S(2)}, u32[]{:S(2)}) %collective-permute-start.18) | collective-permute-done | bytes 122912 | tf_op jit(solution)/shard_map/ppermute | solution.py:33
  (124 shorter events, 33.7 us)
Async XLA Ops:
  0.6 30.4 %copy-start.1 = (f32[480,128]{1,0:T(8,128)S(1)}, f32[480,128]{1,0:T(8,128)}, u32[]{:S(2)}) copy-start(f32[480,128]{1,0:T(8,128)} %param.10) | copy-start | bytes 737284
  3.5 6.7 %collective-permute-start.2 = (bf16[16,128]{1,0:T(8,128)(2,1)S(1)}, bf16[16,128]{1,0:T(8,128)(2,1)S(1)}, u32[]{:S(2)}, u32[]{:S(2)}) collective-permute-start(bf16[16,128]{1,0:T(8,128)(2,1)S(1)} %pad_maximum_fusion.11), channel_id=1, source_target_pairs={{1,0},{0,1},{3,2},{2,3},{5,4},{4,5},{7,6},{6,7},{9,8},{8,9},{11,10... | collective-permute-start | bytes 12296 | tf_op jit(solution)/shard_map/ppermute | solution.py:33
  3.9 27.0 %collective-permute-start = (f32[480,128]{1,0:T(8,128)}, f32[480,128]{1,0:T(8,128)S(1)}, u32[]{:S(2)}, u32[]{:S(2)}) collective-permute-start(f32[480,128]{1,0:T(8,128)} %param.10), channel_id=1, source_target_pairs={{2,0},{3,1},{0,2},{1,3},{6,4},{7,5},{4,6},{5,7},{10,8},{11,9},{8,1... | collective-permute-start | bytes 737288 | tf_op jit(solution)/shard_map/ppermute | solution.py:33
  8.3 22.9 %copy-start = (bf16[2,512,128]{2,1,0:T(8,128)(2,1)S(1)}, bf16[2,512,128]{2,1,0:T(8,128)(2,1)}, u32[]{:S(2)}) copy-start(bf16[2,512,128]{2,1,0:T(8,128)(2,1)} %param.7) | copy-start | bytes 786436
  10.9 3.7 %collective-permute-start.3 = (bf16[32,128]{1,0:T(8,128)(2,1)S(1)}, bf16[32,128]{1,0:T(8,128)(2,1)S(1)}, u32[]{:S(2)}, u32[]{:S(2)}) collective-permute-start(bf16[32,128]{1,0:T(8,128)(2,1)S(1)} %pad_maximum_fusion.10), channel_id=1, source_target_pairs={{2,0},{3,1},{0,2},{1,3},{6,4},{7,5},{4,6},{5,7},{10,8},{11,9},{8,1... | collective-permute-start | bytes 24584 | tf_op jit(solution)/shard_map/ppermute | solution.py:33
  15.3 3.8 %collective-permute-start.4 = (bf16[64,128]{1,0:T(8,128)(2,1)S(1)}, bf16[64,128]{1,0:T(8,128)(2,1)S(1)}, u32[]{:S(2)}, u32[]{:S(2)}) collective-permute-start(bf16[64,128]{1,0:T(8,128)(2,1)S(1)} %concatenate.59), channel_id=1, source_target_pairs={{4,0},{0,4},{12,8},{8,12},{20,16},{16,20},{28,24},{24,28},{5,1},{1... | collective-permute-start | bytes 49160 | tf_op jit(solution)/shard_map/ppermute | solution.py:33
  19.8 4.0 %collective-permute-start.5 = (bf16[128,128]{1,0:T(8,128)(2,1)S(1)}, bf16[128,128]{1,0:T(8,128)(2,1)S(1)}, u32[]{:S(2)}, u32[]{:S(2)}) collective-permute-start(bf16[128,128]{1,0:T(8,128)(2,1)S(1)} %concatenate.60), channel_id=1, source_target_pairs={{8,0},{12,4},{0,8},{4,12},{24,16},{28,20},{16,24},{20,28},{9,1},{1... | collective-permute-start | bytes 98312 | tf_op jit(solution)/shard_map/ppermute | solution.py:33
  24.6 5.2 %collective-permute-start.6 = (bf16[256,128]{1,0:T(8,128)(2,1)S(1)}, bf16[256,128]{1,0:T(8,128)(2,1)S(1)}, u32[]{:S(2)}, u32[]{:S(2)}) collective-permute-start(bf16[256,128]{1,0:T(8,128)(2,1)S(1)} %concatenate.61), channel_id=1, source_target_pairs={{16,0},{20,4},{24,8},{28,12},{0,16},{4,20},{8,24},{12,28},{17,1},{... | collective-permute-start | bytes 196616 | tf_op jit(solution)/shard_map/ppermute | solution.py:33
  31.0 1.9 %collective-permute-start.1 = (f32[960,128]{1,0:T(8,128)S(1)}, f32[960,128]{1,0:T(8,128)S(1)}, u32[]{:S(2)}, u32[]{:S(2)}) collective-permute-start(f32[960,128]{1,0:T(8,128)S(1)} %pad_maximum_fusion.3), channel_id=1, source_target_pairs={{1,0},{0,1},{3,2},{2,3},{5,4},{4,5},{7,6},{6,7},{9,8},{8,9},{11,10... | collective-permute-start | bytes 1474568 | tf_op jit(solution)/shard_map/ppermute | solution.py:33
  37.4 1.9 %collective-permute-start.7 = (f16[960,128]{1,0:T(8,128)(2,1)}, f16[960,128]{1,0:T(8,128)(2,1)}, u32[]{:S(2)}, u32[]{:S(2)}) collective-permute-start(f16[960,128]{1,0:T(8,128)(2,1)} %slice_convert_fusion.1), channel_id=1, source_target_pairs={{1,0},{0,1},{3,2},{2,3},{5,4},{4,5},{7,6},{6,7},{9,8},{8,9},{11,10... | collective-permute-start | bytes 737288 | tf_op jit(solution)/shard_map/ppermute | solution.py:33
  40.3 5.4 %collective-permute-start.8 = (f16[480,128]{1,0:T(8,128)(2,1)S(1)}, f16[480,128]{1,0:T(8,128)(2,1)S(1)}, u32[]{:S(2)}, u32[]{:S(2)}) collective-permute-start(f16[480,128]{1,0:T(8,128)(2,1)S(1)} %slice_convert_fusion.3), channel_id=1, source_target_pairs={{2,0},{3,1},{0,2},{1,3},{6,4},{7,5},{4,6},{5,7},{10,8},{11,9},{8,1... | collective-permute-start | bytes 368648 | tf_op jit(solution)/shard_map/ppermute | solution.py:33
  41.4 20.4 %copy-start.3 = (f32[480]{0:T(512)S(1)}, f32[480]{0:T(512)}, u32[]{:S(2)}) copy-start(f32[480]{0:T(512)} %param.11) | copy-start | bytes 5764
  45.8 4.9 %collective-permute-start.9 = (f16[480,128]{1,0:T(8,128)(2,1)S(1)}, f16[480,128]{1,0:T(8,128)(2,1)S(1)}, u32[]{:S(2)}, u32[]{:S(2)}) collective-permute-start(f16[480,128]{1,0:T(8,128)(2,1)S(1)} %fusion.32), channel_id=1, source_target_pairs={{4,0},{0,4},{12,8},{8,12},{20,16},{16,20},{28,24},{24,28},{5,1},{1... | collective-permute-start | bytes 368648 | tf_op jit(solution)/shard_map/ppermute | solution.py:33
  50.8 4.9 %collective-permute-start.10 = (f16[480,128]{1,0:T(8,128)(2,1)S(1)}, f16[480,128]{1,0:T(8,128)(2,1)S(1)}, u32[]{:S(2)}, u32[]{:S(2)}) collective-permute-start(f16[480,128]{1,0:T(8,128)(2,1)S(1)} %add_convert_fusion.3), channel_id=1, source_target_pairs={{8,0},{12,4},{0,8},{4,12},{24,16},{28,20},{16,24},{20,28},{9,1},{1... | collective-permute-start | bytes 368648 | tf_op jit(solution)/shard_map/ppermute | solution.py:33
  55.7 5.9 %collective-permute-start.11 = (f16[480,128]{1,0:T(8,128)(2,1)S(1)}, f16[480,128]{1,0:T(8,128)(2,1)S(1)}, u32[]{:S(2)}, u32[]{:S(2)}) collective-permute-start(f16[480,128]{1,0:T(8,128)(2,1)S(1)} %add_convert_fusion.2), channel_id=1, source_target_pairs={{16,0},{20,4},{24,8},{28,12},{0,16},{4,20},{8,24},{12,28},{17,1},{... | collective-permute-start | bytes 368648 | tf_op jit(solution)/shard_map/ppermute | solution.py:33
  62.3 4.9 %collective-permute-start.12 = (f16[480,128]{1,0:T(8,128)(2,1)S(1)}, f16[480,128]{1,0:T(8,128)(2,1)S(1)}, u32[]{:S(2)}, u32[]{:S(2)}) collective-permute-start(f16[480,128]{1,0:T(8,128)(2,1)S(1)} %divide_convert_fusion.2), channel_id=1, source_target_pairs={{2,0},{3,1},{0,2},{1,3},{6,4},{7,5},{4,6},{5,7},{10,8},{11,9},{8,1... | collective-permute-start | bytes 368648 | tf_op jit(solution)/shard_map/ppermute | solution.py:33
  67.3 1.6 %collective-permute-start.13 = (f16[960,128]{1,0:T(8,128)(2,1)S(1)}, f16[960,128]{1,0:T(8,128)(2,1)S(1)}, u32[]{:S(2)}, u32[]{:S(2)}) collective-permute-start(f16[960,128]{1,0:T(8,128)(2,1)S(1)} %pad_maximum_fusion.6), channel_id=1, source_target_pairs={{1,0},{0,1},{3,2},{2,3},{5,4},{4,5},{7,6},{6,7},{9,8},{8,9},{11,10... | collective-permute-start | bytes 737288 | tf_op jit(solution)/shard_map/ppermute | solution.py:33
  71.8 2.0 %collective-permute-start.14 = (f16[960,128]{1,0:T(8,128)(2,1)S(1)}, f16[960,128]{1,0:T(8,128)(2,1)S(1)}, u32[]{:S(2)}, u32[]{:S(2)}) collective-permute-start(f16[960,128]{1,0:T(8,128)(2,1)S(1)} %slice_convert_fusion), channel_id=1, source_target_pairs={{1,0},{0,1},{3,2},{2,3},{5,4},{4,5},{7,6},{6,7},{9,8},{8,9},{11,10... | collective-permute-start | bytes 737288 | tf_op jit(solution)/shard_map/ppermute | solution.py:33
  73.7 7.2 %copy-start.2 = (bf16[8,128]{1,0:T(8,128)(2,1)S(1)}, bf16[8,128]{1,0:T(8,128)(2,1)}, u32[]{:S(2)}) copy-start(bf16[8,128]{1,0:T(8,128)(2,1)} %param.12) | copy-start | bytes 6148
  73.7 7.2 %copy-start.4 = (pred[8]{0:T(512)(128)(4,1)S(1)}, pred[8]{0:T(512)(128)(4,1)}, u32[]{:S(2)}) copy-start(pred[8]{0:T(512)(128)(4,1)} %get-tuple-element.57) | copy-start | bytes 28
  73.9 5.4 %collective-permute-start.15 = (f16[480,128]{1,0:T(8,128)(2,1)S(1)}, f16[480,128]{1,0:T(8,128)(2,1)S(1)}, u32[]{:S(2)}, u32[]{:S(2)}) collective-permute-start(f16[480,128]{1,0:T(8,128)(2,1)S(1)} %slice_convert_fusion.2), channel_id=1, source_target_pairs={{2,0},{3,1},{0,2},{1,3},{6,4},{7,5},{4,6},{5,7},{10,8},{11,9},{8,1... | collective-permute-start | bytes 368648 | tf_op jit(solution)/shard_map/ppermute | solution.py:33
  79.4 4.9 %collective-permute-start.16 = (f16[480,128]{1,0:T(8,128)(2,1)S(1)}, f16[480,128]{1,0:T(8,128)(2,1)S(1)}, u32[]{:S(2)}, u32[]{:S(2)}) collective-permute-start(f16[480,128]{1,0:T(8,128)(2,1)S(1)} %fusion.31), channel_id=1, source_target_pairs={{4,0},{0,4},{12,8},{8,12},{20,16},{16,20},{28,24},{24,28},{5,1},{1... | collective-permute-start | bytes 368648 | tf_op jit(solution)/shard_map/ppermute | solution.py:33
  84.4 5.0 %collective-permute-start.17 = (f16[480,128]{1,0:T(8,128)(2,1)S(1)}, f16[480,128]{1,0:T(8,128)(2,1)S(1)}, u32[]{:S(2)}, u32[]{:S(2)}) collective-permute-start(f16[480,128]{1,0:T(8,128)(2,1)S(1)} %add_convert_fusion.1), channel_id=1, source_target_pairs={{8,0},{12,4},{0,8},{4,12},{24,16},{28,20},{16,24},{20,28},{9,1},{1... | collective-permute-start | bytes 368648 | tf_op jit(solution)/shard_map/ppermute | solution.py:33
  89.5 6.3 %collective-permute-start.18 = (f16[480,128]{1,0:T(8,128)(2,1)S(1)}, f16[480,128]{1,0:T(8,128)(2,1)S(1)}, u32[]{:S(2)}, u32[]{:S(2)}) collective-permute-start(f16[480,128]{1,0:T(8,128)(2,1)S(1)} %add_convert_fusion), channel_id=1, source_target_pairs={{16,0},{20,4},{24,8},{28,12},{0,16},{4,20},{8,24},{12,28},{17,1},{... | collective-permute-start | bytes 368648 | tf_op jit(solution)/shard_map/ppermute | solution.py:33
  (6 other events, 37.0 us)

commit v2 on v1

--- a/solution.py
+++ b/solution.py
@@ -12,46 +12,77 @@
 f16 = jnp.float16
 
 
-def stages_of(count):
-    stages, stride = [], 1
+def masks_of(count):
+    masks = []
     while count > 1:
-        radix = next(r for r in range(2, count + 1) if count % r == 0)
+        assert count % 2 == 0
+        count //= 2
+        masks.append(count)
+    return masks
+
+
+def stages_of(count, stride):
+    stages, count = [], count // stride
+    while count > 1:
+        radix = next(r for r in (4, 2, 3, *range(5, count + 1)) if count % r == 0)
         stages.append((stride, radix))
         stride, count = stride * radix, count // radix
     return stages
 
 
-def partners(piece, axis, stride, radix):
-    count = lax.axis_size(axis)
+def flip(piece, table_mask, batch_mask=0):
+    owners = lax.axis_size("table")
+    mask = batch_mask * owners + table_mask
+    count = lax.axis_size("batch") * owners
+    return lax.ppermute(piece, ("batch", "table"), [(i ^ mask, i) for i in range(count)])
+
+
+def turned(piece, stride, radix):
+    count = lax.axis_size("batch")
     found = []
     for turn in range(1, radix):
         pairs = []
         for target in range(count):
             digit = target // stride % radix
-            source = target + ((digit + turn) % radix - digit) * stride
-            pairs.append((source, target))
-        found.append(lax.ppermute(piece, axis, pairs))
+            pairs.append((target + ((digit + turn) % radix - digit) * stride, target))
+        found.append(lax.ppermute(piece, "batch", pairs))
     return found
 
 
-def gather_any_order(piece, axis, stages):
-    for stride, radix in stages:
-        piece = jnp.concatenate([piece] + partners(piece, axis, stride, radix))
-    return piece
-
-
-def sum_over(total, axis, stages):
-    for stride, radix in stages:
-        sent = lax.optimization_barrier(total.astype(f16))
-        parts = [sent] + partners(sent, axis, stride, radix)
-        if radix > 2:
-            digit = lax.axis_index(axis) // stride % radix
-            order = (jnp.arange(radix, dtype=jnp.int32) - digit) % radix
-            parts = list(jnp.stack(parts)[order])
-        total = parts[0].astype(f32)
-        for part in parts[1:]:
-            total = total + part.astype(f32)
-    return total
+def sum_stage(total, stride, radix):
+    sent = lax.optimization_barrier(total.astype(f16))
+    if radix in (2, 4) and stride & (stride - 1) == 0:
+        parts = [sent] + [flip(sent, 0, stride * turn) for turn in range(1, radix)]
+    else:
+        parts = jnp.stack([sent] + turned(sent, stride, radix))
+        digit = lax.axis_index("batch") // stride % radix
+        parts = list(parts[(jnp.arange(radix, dtype=jnp.int32) - digit) % radix])
+    parts = [part.astype(f32) for part in parts]
+    while len(parts) > 1:
+        parts = [sum(parts[i + 1 : i + 2], parts[i]) for i in range(0, len(parts), 2)]
+    return parts[0]
+
+
+def reduce_rows(kept, sent, masks, copies):
+    masks = masks[::-1]
+    for index, mask in enumerate(masks):
+        if index + 1 == len(masks) and copies % 2 == 0:
+            break
+        kept = kept + flip(sent.astype(f16), mask).astype(f32)
+        half = kept.shape[0] // 2
+        if index + 1 < len(masks):
+            kept, sent = kept[:half], kept[half:]
+    stride = 1
+    if copies % 2 == 0:
+        own, away = lax.optimization_barrier((kept.astype(f16), sent.astype(f16)))
+        beside = flip(away, masks[-1])
+        copy = flip(own, 0, 1)
+        across = flip(away, masks[-1], 1)
+        kept = (own.astype(f32) + beside.astype(f32)) + (copy.astype(f32) + across.astype(f32))
+        stride = 2
+    for stage in stages_of(copies, stride):
+        kept = sum_stage(kept, *stage)
+    return kept
 
 
 def split_parts(rows, terms):
@@ -63,13 +94,18 @@
     return jnp.concatenate(parts, 1)
 
 
-def pick_rows(places, parts, width):
-    chosen = (places[:, None] == jnp.arange(parts.shape[0], dtype=jnp.int32)[None, :]).astype(bf16)
-    found = jnp.dot(chosen, parts, preferred_element_type=f32)
-    rows = found[:, :width]
-    for start in range(width, parts.shape[1], width):
-        rows = rows + found[:, start : start + width]
-    return rows
+def pick_rows(places, blocks, width):
+    total, first = None, 0
+    for block in blocks:
+        count = block.shape[0]
+        chosen = (places[:, None] - first == jnp.arange(count, dtype=jnp.int32)[None, :]).astype(bf16)
+        found = jnp.dot(chosen, block, preferred_element_type=f32)
+        rows = found[:, :width]
+        for start in range(width, block.shape[1], width):
+            rows = rows + found[:, start : start + width]
+        total = rows if total is None else total + rows
+        first += count
+    return total
 
 
 def score_piece(query_half, carried, rows, kept):
@@ -104,8 +140,7 @@
     owned = table.shape[0]
     queue_rows = fifo.shape[0]
     me = lax.axis_index("table")
-    table_masks = [stride for stride, _ in reversed(stages_of(owners))]
-    batch_stages = stages_of(copies)
+    masks = masks_of(owners)
     most = owners * copies * (3 * query_count // owners)
     grad_scale = 1.0
     while most * grad_scale > 32768.0:
@@ -114,35 +149,33 @@
     def place_of(owner, row):
         apart = jnp.bitwise_xor(owner, me)
         place = jnp.zeros_like(owner)
-        for index, mask in enumerate(table_masks):
+        for index, mask in enumerate(masks):
             place = place + jnp.where((apart & mask) != 0, 1 << index, 0)
         return place * owned + row
 
-    def gather_table(piece):
-        for mask in table_masks:
-            piece = jnp.concatenate([piece] + partners(piece, "table", mask, 2))
-        return piece
+    def gather_table(piece, terms):
+        blocks = [split_parts(piece.astype(f32), terms)]
+        for mask in masks:
+            other = flip(piece, mask)
+            blocks.append(split_parts(other.astype(f32), terms))
+            piece = jnp.concatenate([piece, other])
+        return blocks
+
+    parts = gather_table(table, 3)
 
     head = fifo_head[0]
-    table_all = gather_table(table)
-
-    first_owner, first_row = item_owner[0, :ENQ, 0], item_row[0, :ENQ]
-    told = jnp.concatenate([first_owner, first_row // 16, first_row % 16, head[None]])
-    told_row = jnp.pad(told.astype(bf16), (0, width - told.shape[0]))[None, :]
-    pad = jnp.zeros((-(queue_rows + 1) % 16, width), bf16)
-    block = jnp.concatenate([fifo, told_row, pad])
-    blocks = gather_any_order(block, "table", stages_of(owners))
-    blocks = gather_any_order(blocks, "batch", batch_stages)
-    blocks = blocks.reshape(owners * copies, -1, width)
+    first_owner, first_row = item_owner[0, :width, 0], item_row[0, :width]
+    told = jnp.stack([first_owner, first_row // 16, first_row % 16, jnp.full((width,), head)])
+    pad = jnp.zeros((-(queue_rows + 4) % 16, width), bf16)
+    block = jnp.concatenate([fifo, told.astype(bf16), pad])
+    blocks = jnp.broadcast_to(block[None], (owners * copies, *block.shape))
+    blocks = lax.all_to_all(blocks, ("batch", "table"), 0, 0, tiled=True)
     queue = blocks[:, :queue_rows].reshape(-1, width)
-    told_all = blocks[:, queue_rows, : told.shape[0]].astype(jnp.int32)
-    new_place = place_of(
-        told_all[:, :ENQ], told_all[:, ENQ : 2 * ENQ] * 16 + told_all[:, 2 * ENQ : 3 * ENQ]
-    ).reshape(-1)
+    told_all = blocks[:, queue_rows : queue_rows + 4, :ENQ].astype(jnp.int32)
+    new_place = place_of(told_all[:, 0], told_all[:, 1] * 16 + told_all[:, 2]).reshape(-1)
     slots = jnp.arange(queue_rows, dtype=jnp.int32)
-    kept = ((slots[None, :] - told_all[:, 3 * ENQ :]) % queue_rows >= ENQ).reshape(-1)
-
-    parts = split_parts(table_all, 3)
+    kept = ((slots[None, :] - told_all[:, 3, :1]) % queue_rows >= ENQ).reshape(-1)
+
     new_rows = pick_rows(new_place, parts, width)
     new_half = (new_rows / norm_of(new_rows)[:, None]).astype(bf16)
 
@@ -176,21 +209,22 @@
         grad_list.append(query_grad.astype(bf16))
 
         across = (lack[:, None] * (query_unit - item_unit * cosine[:, None])).astype(bf16)
-        chosen = (places[:, None] == jnp.arange(owners * owned, dtype=jnp.int32)[None, :]).astype(bf16)
-        dense = grad_scale * lax.dot_general(
-            chosen, across, (((0,), (0,)), ((), ())), preferred_element_type=f32
-        )
-        for mask in reversed(table_masks):
-            half = dense.shape[0] // 2
-            (other,) = partners(dense[half:].astype(f16), "table", mask, 2)
-            dense = dense[:half] + other.astype(f32)
-        dense = sum_over(dense, "batch", batch_stages)
+        halves = []
+        for half in range(2):
+            count = owners * owned // 2
+            rows_of = jnp.arange(count, dtype=jnp.int32) + half * count
+            chosen = (places[:, None] == rows_of[None, :]).astype(bf16)
+            dense = lax.dot_general(
+                chosen, across, (((0,), (0,)), ((), ())), preferred_element_type=f32
+            )
+            halves.append(grad_scale * dense)
+        dense = reduce_rows(halves[0], halves[1], masks, copies)
         grad = dense * ((score_scale / grad_scale) / norm_of(table))[:, None]
         accum = accum + jnp.mean(grad * grad, 1)
         table = table - learn_rate * grad / jnp.sqrt(accum)[:, None]
         if step + 1 < step_count:
             unit = (table / norm_of(table)[:, None]).astype(f16)
-            parts = split_parts(gather_table(unit).astype(f32), 2)
+            parts = gather_table(unit, 2)
 
     fifo_out = fifo
     for step in range(step_count):

time: 98 us -> 91.3 us (0.932)
  other arithmetic: 16.7 us -> 10.5 us
  waiting for transfers between devices: 41 us -> 37.6 us
  starting transfers between devices: 24.6 us -> 27 us
  matrix products: 8 us -> 10 us
  local copies, waits for them, and re-layouts: 5.4 us -> 3.91 us
    all_to_all x0 -> x1, starting transfers between devices: none -> 7.3 us  [per_device(): blocks = lax.all_to_all(blocks, ('batch', 'table'), 0, 0, tiled=True)]
    ppermute x19 -> x18, starting transfers between devices: 24.6 us -> 19.7 us  [flip(): lax.ppermute(piece, ('batch', 'table'), [(i ^ mask, i) for i in range(cou...]
    ppermute x19 -> x18, waiting for transfers between devices: 41 us -> 37.6 us  [flip(): lax.ppermute(piece, ('batch', 'table'), [(i ^ mask, i) for i in range(cou...]
    concatenate x5 -> x1, local copies, waits for them, and re-layouts: 3.08 us -> 0.72 us  [per_device(): block = jnp.concatenate([fifo, told.astype(bf16), pad])]
    dot_general x3 -> x9, matrix products: 2.57 us -> 4.86 us  [pick_rows(): found = jnp.dot(chosen, block, preferred_element_type=f32)]
    reduce_sum x6 -> x5, other arithmetic: 3.05 us -> 1.11 us  [norm_of(): return jnp.sqrt(jnp.sum(rows * rows, 1) + epsilon)]
    eq x4, other arithmetic: 1.74 us -> 0.06 us  [per_device(): place == k]
    concatenate x4 -> x2, other arithmetic: 1.49 us -> 0.1 us  [gather_table(): piece = jnp.concatenate([piece, other])]
  transfers between devices with their start and end apart: 19 -> 19, of which waited for: 16 -> 13; matrix products, arithmetic and copies ran while one was open for 17% -> 10% of each run, Pallas kernels for 0% -> 0%
where the time goes in v2:
time: 91.3 us; the launch traced here: 91 us
  waiting for transfers between devices  37.6 us (41%)
  starting transfers between devices  27 us (30%)
  other arithmetic  10.5 us (12%)
  matrix products  10 us (11%)
  local copies, waits for them, and re-layouts  3.91 us (4%)
  between operations  1.93 us (2%)
    ppermute x18, waiting for transfers between devices, flip(): lax.ppermute(piece, ('batch', 'table'), [(i ^ mask, i) for i in range(cou...  37.6 us
    ppermute x18, starting transfers between devices, flip(): lax.ppermute(piece, ('batch', 'table'), [(i ^ mask, i) for i in range(cou...  19.7 us
    all_to_all x1, starting transfers between devices, per_device(): blocks = lax.all_to_all(blocks, ('batch', 'table'), 0, 0, tiled=True)  7.3 us
    dot_general x9, matrix products, pick_rows(): found = jnp.dot(chosen, block, preferred_element_type=f32)  4.86 us
    dot_general x4, matrix products, per_device(): lax.dot_general(chosen, across, (((0,), (0,)), ((), ())), preferred_eleme...  3.23 us
  transfers between devices with their start and end apart: 19, of which 13 were waited for; matrix products, arithmetic and copies ran while one was open for 10% of the time, Pallas kernels for 0%

profile of v2, /device:TPU:0, one launch (start us, length us, event | category | flops | bytes accessed | tf_op | source)
XLA Modules:
  0.0 91.0 jit_solution(13635729516762526692)
XLA Ops:
  4.8 7.3 %all-to-all-start = ((bf16[32,16,128]{2,1,0:T(8,128)(2,1)}), bf16[32,16,128]{2,1,0:T(8,128)(2,1)S(1)}, u32[]{:S(2)}, u32[]{:S(2)}) async-start(bf16[32,16,128]{2,1,0:T(8,128)(2,1)} %broadcast_in_dim.208), calls=%async_computation | async-start | bytes 262144 | tf_op jit(solution)/shard_map/all_to_all | solution.py:172
  12.1 1.8 %collective-permute-start = (f32[480,128]{1,0:T(8,128)}, f32[480,128]{1,0:T(8,128)S(1)}, u32[]{:S(2)}, u32[]{:S(2)}) collective-permute-start(f32[480,128]{1,0:T(8,128)} %param.10), channel_id=1, source_target_pairs={{2,0},{3,1},{0,2},{1,3},{6,4},{7,5},{4,6},{5,7},{10,8},{11,9},{8,1... | collective-permute-start | bytes 737288 | tf_op jit(solution)/shard_map/ppermute | solution.py:37
  14.7 1.1 %reduce-precision_convert_fusion.8 = (bf16[480,128]{1,0:T(8,128)(2,1)S(1)}, bf16[480,128]{1,0:T(8,128)(2,1)S(1)}, bf16[480,128]{1,0:T(8,128)(2,1)S(1)}, f32[480]{0:T(512)S(1)}) fusion(f32[480,128]{1,0:T(8,128)} %param.10), kind=kLoop, calls=%fused_computation.78 | loop fusion | flops 613920 | bytes 616320 | tf_op jit(solution)/shard_map/convert_element_type | solution.py:92
  16.7 5.0 %collective-permute-done = f32[480,128]{1,0:T(8,128)S(1)} collective-permute-done((f32[480,128]{1,0:T(8,128)}, f32[480,128]{1,0:T(8,128)S(1)}, u32[]{:S(2)}, u32[]{:S(2)}) %collective-permute-start) | collective-permute-done | bytes 245792 | tf_op jit(solution)/shard_map/ppermute | solution.py:37
  24.3 1.3 %fusion.57 = f32[128,384]{1,0:T(8,128)S(1)} fusion(bf16[480,128]{1,0:T(8,128)(2,1)} %copy-done.4, bf16[480,128]{1,0:T(8,128)(2,1)} %copy-done.5, bf16[480,128]{1,0:T(8,128)(2,1)S(1)} %copy-done.3, s32[128]{0:T(128)S(1)} %reshape.381), kind=kOutput, calls=%fused_computation.115 | convolution fusion | flops 48353280 | bytes 565760 | tf_op jit(solution)/shard_map/dot_general | solution.py:102
  28.6 0.8 fusion.11
  32.0 2.3 %collective-permute-start.5 = (f16[480,128]{1,0:T(8,128)(2,1)S(1)}, f16[480,128]{1,0:T(8,128)(2,1)S(1)}, u32[]{:S(2)}, u32[]{:S(2)}) collective-permute-start(f16[480,128]{1,0:T(8,128)(2,1)S(1)} %get-tuple-element.10), channel_id=1, source_target_pairs={{6,0},{7,1},{4,2},{5,3},{2,4},{3,5},{0,6},{1,7},{14,8},{15,9},{12,... | collective-permute-start | bytes 368648 | tf_op jit(solution)/shard_map/ppermute | solution.py:37
  34.3 0.9 collective-permute-start.3
  35.6 5.6 %collective-permute-done.4 = f16[480,128]{1,0:T(8,128)(2,1)S(1)} collective-permute-done((f16[480,128]{1,0:T(8,128)(2,1)S(1)}, f16[480,128]{1,0:T(8,128)(2,1)S(1)}, u32[]{:S(2)}, u32[]{:S(2)}) %collective-permute-start.4) | collective-permute-done | bytes 122912 | tf_op jit(solution)/shard_map/ppermute | solution.py:37
  41.5 3.1 %collective-permute-start.8 = (f16[480,128]{1,0:T(8,128)(2,1)S(1)}, f16[480,128]{1,0:T(8,128)(2,1)S(1)}, u32[]{:S(2)}, u32[]{:S(2)}) collective-permute-start(f16[480,128]{1,0:T(8,128)(2,1)S(1)} %add_convert_fusion.3), channel_id=1, source_target_pairs={{24,0},{25,1},{26,2},{27,3},{28,4},{29,5},{30,6},{31,7},{16,8},{17... | collective-permute-start | bytes 368648 | tf_op jit(solution)/shard_map/ppermute | solution.py:37
  44.7 1.3 %collective-permute-start.6 = (f16[480,128]{1,0:T(8,128)(2,1)S(1)}, f16[480,128]{1,0:T(8,128)(2,1)S(1)}, u32[]{:S(2)}, u32[]{:S(2)}) collective-permute-start(f16[480,128]{1,0:T(8,128)(2,1)S(1)} %add_convert_fusion.3), channel_id=1, source_target_pairs={{8,0},{9,1},{10,2},{11,3},{12,4},{13,5},{14,6},{15,7},{0,8},{1,9},... | collective-permute-start | bytes 368648 | tf_op jit(solution)/shard_map/ppermute | solution.py:37
  46.0 3.7 %collective-permute-done.8 = f16[480,128]{1,0:T(8,128)(2,1)S(1)} collective-permute-done((f16[480,128]{1,0:T(8,128)(2,1)S(1)}, f16[480,128]{1,0:T(8,128)(2,1)S(1)}, u32[]{:S(2)}, u32[]{:S(2)}) %collective-permute-start.8) | collective-permute-done | bytes 122912 | tf_op jit(solution)/shard_map/ppermute | solution.py:37
  49.6 5.7 %collective-permute-done.7 = f16[480,128]{1,0:T(8,128)(2,1)S(1)} collective-permute-done((f16[480,128]{1,0:T(8,128)(2,1)S(1)}, f16[480,128]{1,0:T(8,128)(2,1)S(1)}, u32[]{:S(2)}, u32[]{:S(2)}) %collective-permute-start.7) | collective-permute-done | bytes 122912 | tf_op jit(solution)/shard_map/ppermute | solution.py:37
  56.1 1.0 %collective-permute-start.9 = (f16[480,128]{1,0:T(8,128)(2,1)S(1)}, f16[480,128]{1,0:T(8,128)(2,1)S(1)}, u32[]{:S(2)}, u32[]{:S(2)}) collective-permute-start(f16[480,128]{1,0:T(8,128)(2,1)S(1)} %get-tuple-element.24), channel_id=1, source_target_pairs={{2,0},{3,1},{0,2},{1,3},{6,4},{7,5},{4,6},{5,7},{10,8},{11,9},{8,1... | collective-permute-start | bytes 368648 | tf_op jit(solution)/shard_map/ppermute | solution.py:37
  57.4 3.6 %collective-permute-done.9 = f16[480,128]{1,0:T(8,128)(2,1)S(1)} collective-permute-done((f16[480,128]{1,0:T(8,128)(2,1)S(1)}, f16[480,128]{1,0:T(8,128)(2,1)S(1)}, u32[]{:S(2)}, u32[]{:S(2)}) %collective-permute-start.9) | collective-permute-done | bytes 122912 | tf_op jit(solution)/shard_map/ppermute | solution.py:37
  61.6 1.1 %collective-permute-done.10 = f16[960,128]{1,0:T(8,128)(2,1)S(1)} collective-permute-done((f16[960,128]{1,0:T(8,128)(2,1)S(1)}, f16[960,128]{1,0:T(8,128)(2,1)S(1)}, u32[]{:S(2)}, u32[]{:S(2)}) %collective-permute-start.10) | collective-permute-done | bytes 245792 | tf_op jit(solution)/shard_map/ppermute | solution.py:37
  68.1 2.2 %collective-permute-start.14 = (f16[480,128]{1,0:T(8,128)(2,1)S(1)}, f16[480,128]{1,0:T(8,128)(2,1)S(1)}, u32[]{:S(2)}, u32[]{:S(2)}) collective-permute-start(f16[480,128]{1,0:T(8,128)(2,1)S(1)} %get-tuple-element.12), channel_id=1, source_target_pairs={{6,0},{7,1},{4,2},{5,3},{2,4},{3,5},{0,6},{1,7},{14,8},{15,9},{12,... | collective-permute-start | bytes 368648 | tf_op jit(solution)/shard_map/ppermute | solution.py:37
  70.3 1.0 %collective-permute-start.12 = (f16[480,128]{1,0:T(8,128)(2,1)S(1)}, f16[480,128]{1,0:T(8,128)(2,1)S(1)}, u32[]{:S(2)}, u32[]{:S(2)}) collective-permute-start(f16[480,128]{1,0:T(8,128)(2,1)S(1)} %get-tuple-element.12), channel_id=1, source_target_pairs={{2,0},{3,1},{0,2},{1,3},{6,4},{7,5},{4,6},{5,7},{10,8},{11,9},{8,1... | collective-permute-start | bytes 368648 | tf_op jit(solution)/shard_map/ppermute | solution.py:37
  71.7 5.4 %collective-permute-done.13 = f16[480,128]{1,0:T(8,128)(2,1)S(1)} collective-permute-done((f16[480,128]{1,0:T(8,128)(2,1)S(1)}, f16[480,128]{1,0:T(8,128)(2,1)S(1)}, u32[]{:S(2)}, u32[]{:S(2)}) %collective-permute-start.13) | collective-permute-done | bytes 122912 | tf_op jit(solution)/shard_map/ppermute | solution.py:37
  77.3 2.4 %collective-permute-start.17 = (f16[480,128]{1,0:T(8,128)(2,1)S(1)}, f16[480,128]{1,0:T(8,128)(2,1)S(1)}, u32[]{:S(2)}, u32[]{:S(2)}) collective-permute-start(f16[480,128]{1,0:T(8,128)(2,1)S(1)} %add_convert_fusion.2), channel_id=1, source_target_pairs={{24,0},{25,1},{26,2},{27,3},{28,4},{29,5},{30,6},{31,7},{16,8},{17... | collective-permute-start | bytes 368648 | tf_op jit(solution)/shard_map/ppermute | solution.py:37
  79.7 2.1 %collective-permute-start.15 = (f16[480,128]{1,0:T(8,128)(2,1)S(1)}, f16[480,128]{1,0:T(8,128)(2,1)S(1)}, u32[]{:S(2)}, u32[]{:S(2)}) collective-permute-start(f16[480,128]{1,0:T(8,128)(2,1)S(1)} %add_convert_fusion.2), channel_id=1, source_target_pairs={{8,0},{9,1},{10,2},{11,3},{12,4},{13,5},{14,6},{15,7},{0,8},{1,9},... | collective-permute-start | bytes 368648 | tf_op jit(solution)/shard_map/ppermute | solution.py:37
  83.1 2.3 %collective-permute-done.17 = f16[480,128]{1,0:T(8,128)(2,1)S(1)} collective-permute-done((f16[480,128]{1,0:T(8,128)(2,1)S(1)}, f16[480,128]{1,0:T(8,128)(2,1)S(1)}, u32[]{:S(2)}, u32[]{:S(2)}) %collective-permute-start.17) | collective-permute-done | bytes 122912 | tf_op jit(solution)/shard_map/ppermute | solution.py:37
  85.4 3.8 %collective-permute-done.16 = f16[480,128]{1,0:T(8,128)(2,1)S(1)} collective-permute-done((f16[480,128]{1,0:T(8,128)(2,1)S(1)}, f16[480,128]{1,0:T(8,128)(2,1)S(1)}, u32[]{:S(2)}, u32[]{:S(2)}) %collective-permute-start.16) | collective-permute-done | bytes 122912 | tf_op jit(solution)/shard_map/ppermute | solution.py:37
  90.1 0.9 divide_subtract_fusion
  (131 shorter events, 23.3 us)
Async XLA Ops:
  0.6 15.4 %copy-start.14 = (s32[2,512,1]{1,2,0:T(1,128)S(1)}, s32[2,512,1]{1,2,0:T(1,128)}, u32[]{:S(2)}) copy-start(s32[2,512,1]{1,2,0:T(1,128)} %param.8) | copy-start | bytes 12292
  0.6 15.3 %copy-start = (bf16[2,512,128]{2,1,0:T(8,128)(2,1)S(1)}, bf16[2,512,128]{2,1,0:T(8,128)(2,1)}, u32[]{:S(2)}) copy-start(bf16[2,512,128]{2,1,0:T(8,128)(2,1)} %param.7) | copy-start | bytes 786436
  4.8 18.3 %all-to-all-start = ((bf16[32,16,128]{2,1,0:T(8,128)(2,1)}), bf16[32,16,128]{2,1,0:T(8,128)(2,1)S(1)}, u32[]{:S(2)}, u32[]{:S(2)}) async-start(bf16[32,16,128]{2,1,0:T(8,128)(2,1)} %broadcast_in_dim.208), calls=%async_computation | async-start | bytes 262144 | tf_op jit(solution)/shard_map/all_to_all | solution.py:172
  12.1 9.6 %collective-permute-start = (f32[480,128]{1,0:T(8,128)}, f32[480,128]{1,0:T(8,128)S(1)}, u32[]{:S(2)}, u32[]{:S(2)}) collective-permute-start(f32[480,128]{1,0:T(8,128)} %param.10), channel_id=1, source_target_pairs={{2,0},{3,1},{0,2},{1,3},{6,4},{7,5},{4,6},{5,7},{10,8},{11,9},{8,1... | collective-permute-start | bytes 737288 | tf_op jit(solution)/shard_map/ppermute | solution.py:37
  16.2 5.6 %copy-start.1 = (f32[480,128]{1,0:T(8,128)S(1)}, f32[480,128]{1,0:T(8,128)}, u32[]{:S(2)}) copy-start(f32[480,128]{1,0:T(8,128)} %param.10) | copy-start | bytes 737284
  21.8 4.2 %collective-permute-start.1 = (f32[960,128]{1,0:T(8,128)S(1)}, f32[960,128]{1,0:T(8,128)S(1)}, u32[]{:S(2)}, u32[]{:S(2)}) collective-permute-start(f32[960,128]{1,0:T(8,128)S(1)} %pad_maximum_fusion.1), channel_id=1, source_target_pairs={{1,0},{0,1},{3,2},{2,3},{5,4},{4,5},{7,6},{6,7},{9,8},{8,9},{11,10... | collective-permute-start | bytes 1474568 | tf_op jit(solution)/shard_map/ppermute | solution.py:37
  22.6 1.7 %copy-start.3 = (bf16[480,128]{1,0:T(8,128)(2,1)S(1)}, bf16[480,128]{1,0:T(8,128)(2,1)}, u32[]{:S(2)}) copy-start(bf16[480,128]{1,0:T(8,128)(2,1)} %copy-done.2) | copy-start | bytes 368644
  29.5 1.7 %collective-permute-start.2 = (f16[960,128]{1,0:T(8,128)(2,1)S(1)}, f16[960,128]{1,0:T(8,128)(2,1)S(1)}, u32[]{:S(2)}, u32[]{:S(2)}) collective-permute-start(f16[960,128]{1,0:T(8,128)(2,1)S(1)} %fusion.11), channel_id=1, source_target_pairs={{1,0},{0,1},{3,2},{2,3},{5,4},{4,5},{7,6},{6,7},{9,8},{8,9},{11,10... | collective-permute-start | bytes 737288 | tf_op jit(solution)/shard_map/ppermute | solution.py:37
  31.9 23.6 %copy-start.12 = (f32[480]{0:T(512)S(1)}, f32[480]{0:T(512)}, u32[]{:S(2)}) copy-start(f32[480]{0:T(512)} %param.11) | copy-start | bytes 5764
  32.0 9.2 %collective-permute-start.5 = (f16[480,128]{1,0:T(8,128)(2,1)S(1)}, f16[480,128]{1,0:T(8,128)(2,1)S(1)}, u32[]{:S(2)}, u32[]{:S(2)}) collective-permute-start(f16[480,128]{1,0:T(8,128)(2,1)S(1)} %get-tuple-element.10), channel_id=1, source_target_pairs={{6,0},{7,1},{4,2},{5,3},{2,4},{3,5},{0,6},{1,7},{14,8},{15,9},{12,... | collective-permute-start | bytes 368648 | tf_op jit(solution)/shard_map/ppermute | solution.py:37
  34.3 7.1 %collective-permute-start.3 = (f16[480,128]{1,0:T(8,128)(2,1)S(1)}, f16[480,128]{1,0:T(8,128)(2,1)S(1)}, u32[]{:S(2)}, u32[]{:S(2)}) collective-permute-start(f16[480,128]{1,0:T(8,128)(2,1)S(1)} %get-tuple-element.10), channel_id=1, source_target_pairs={{2,0},{3,1},{0,2},{1,3},{6,4},{7,5},{4,6},{5,7},{10,8},{11,9},{8,1... | collective-permute-start | bytes 368648 | tf_op jit(solution)/shard_map/ppermute | solution.py:37
  35.2 6.0 %collective-permute-start.4 = (f16[480,128]{1,0:T(8,128)(2,1)S(1)}, f16[480,128]{1,0:T(8,128)(2,1)S(1)}, u32[]{:S(2)}, u32[]{:S(2)}) collective-permute-start(f16[480,128]{1,0:T(8,128)(2,1)S(1)} %get-tuple-element.9), channel_id=1, source_target_pairs={{4,0},{5,1},{6,2},{7,3},{0,4},{1,5},{2,6},{3,7},{12,8},{13,9},{14,... | collective-permute-start | bytes 368648 | tf_op jit(solution)/shard_map/ppermute | solution.py:37
  41.5 8.1 %collective-permute-start.8 = (f16[480,128]{1,0:T(8,128)(2,1)S(1)}, f16[480,128]{1,0:T(8,128)(2,1)S(1)}, u32[]{:S(2)}, u32[]{:S(2)}) collective-permute-start(f16[480,128]{1,0:T(8,128)(2,1)S(1)} %add_convert_fusion.3), channel_id=1, source_target_pairs={{24,0},{25,1},{26,2},{27,3},{28,4},{29,5},{30,6},{31,7},{16,8},{17... | collective-permute-start | bytes 368648 | tf_op jit(solution)/shard_map/ppermute | solution.py:37
  44.6 10.7 %collective-permute-start.7 = (f16[480,128]{1,0:T(8,128)(2,1)S(1)}, f16[480,128]{1,0:T(8,128)(2,1)S(1)}, u32[]{:S(2)}, u32[]{:S(2)}) collective-permute-start(f16[480,128]{1,0:T(8,128)(2,1)S(1)} %add_convert_fusion.3), channel_id=1, source_target_pairs={{16,0},{17,1},{18,2},{19,3},{20,4},{21,5},{22,6},{23,7},{24,8},{25... | collective-permute-start | bytes 368648 | tf_op jit(solution)/shard_map/ppermute | solution.py:37
  44.7 10.7 %collective-permute-start.6 = (f16[480,128]{1,0:T(8,128)(2,1)S(1)}, f16[480,128]{1,0:T(8,128)(2,1)S(1)}, u32[]{:S(2)}, u32[]{:S(2)}) collective-permute-start(f16[480,128]{1,0:T(8,128)(2,1)S(1)} %add_convert_fusion.3), channel_id=1, source_target_pairs={{8,0},{9,1},{10,2},{11,3},{12,4},{13,5},{14,6},{15,7},{0,8},{1,9},... | collective-permute-start | bytes 368648 | tf_op jit(solution)/shard_map/ppermute | solution.py:37
  56.1 4.9 %collective-permute-start.9 = (f16[480,128]{1,0:T(8,128)(2,1)S(1)}, f16[480,128]{1,0:T(8,128)(2,1)S(1)}, u32[]{:S(2)}, u32[]{:S(2)}) collective-permute-start(f16[480,128]{1,0:T(8,128)(2,1)S(1)} %get-tuple-element.24), channel_id=1, source_target_pairs={{2,0},{3,1},{0,2},{1,3},{6,4},{7,5},{4,6},{5,7},{10,8},{11,9},{8,1... | collective-permute-start | bytes 368648 | tf_op jit(solution)/shard_map/ppermute | solution.py:37
  61.1 1.6 %collective-permute-start.10 = (f16[960,128]{1,0:T(8,128)(2,1)S(1)}, f16[960,128]{1,0:T(8,128)(2,1)S(1)}, u32[]{:S(2)}, u32[]{:S(2)}) collective-permute-start(f16[960,128]{1,0:T(8,128)(2,1)S(1)} %pad_maximum_fusion.7), channel_id=1, source_target_pairs={{1,0},{0,1},{3,2},{2,3},{5,4},{4,5},{7,6},{6,7},{9,8},{8,9},{11,10... | collective-permute-start | bytes 737288 | tf_op jit(solution)/shard_map/ppermute | solution.py:37
  65.7 1.6 %collective-permute-start.11 = (f16[960,128]{1,0:T(8,128)(2,1)S(1)}, f16[960,128]{1,0:T(8,128)(2,1)S(1)}, u32[]{:S(2)}, u32[]{:S(2)}) collective-permute-start(f16[960,128]{1,0:T(8,128)(2,1)S(1)} %fusion.14), channel_id=1, source_target_pairs={{1,0},{0,1},{3,2},{2,3},{5,4},{4,5},{7,6},{6,7},{9,8},{8,9},{11,10... | collective-permute-start | bytes 737288 | tf_op jit(solution)/shard_map/ppermute | solution.py:37
  68.1 9.0 %collective-permute-start.14 = (f16[480,128]{1,0:T(8,128)(2,1)S(1)}, f16[480,128]{1,0:T(8,128)(2,1)S(1)}, u32[]{:S(2)}, u32[]{:S(2)}) collective-permute-start(f16[480,128]{1,0:T(8,128)(2,1)S(1)} %get-tuple-element.12), channel_id=1, source_target_pairs={{6,0},{7,1},{4,2},{5,3},{2,4},{3,5},{0,6},{1,7},{14,8},{15,9},{12,... | collective-permute-start | bytes 368648 | tf_op jit(solution)/shard_map/ppermute | solution.py:37
  70.3 7.0 %collective-permute-start.12 = (f16[480,128]{1,0:T(8,128)(2,1)S(1)}, f16[480,128]{1,0:T(8,128)(2,1)S(1)}, u32[]{:S(2)}, u32[]{:S(2)}) collective-permute-start(f16[480,128]{1,0:T(8,128)(2,1)S(1)} %get-tuple-element.12), channel_id=1, source_target_pairs={{2,0},{3,1},{0,2},{1,3},{6,4},{7,5},{4,6},{5,7},{10,8},{11,9},{8,1... | collective-permute-start | bytes 368648 | tf_op jit(solution)/shard_map/ppermute | solution.py:37
  71.3 5.8 %collective-permute-start.13 = (f16[480,128]{1,0:T(8,128)(2,1)S(1)}, f16[480,128]{1,0:T(8,128)(2,1)S(1)}, u32[]{:S(2)}, u32[]{:S(2)}) collective-permute-start(f16[480,128]{1,0:T(8,128)(2,1)S(1)} %get-tuple-element.11), channel_id=1, source_target_pairs={{4,0},{5,1},{6,2},{7,3},{0,4},{1,5},{2,6},{3,7},{12,8},{13,9},{14,... | collective-permute-start | bytes 368648 | tf_op jit(solution)/shard_map/ppermute | solution.py:37
  77.3 8.1 %collective-permute-start.17 = (f16[480,128]{1,0:T(8,128)(2,1)S(1)}, f16[480,128]{1,0:T(8,128)(2,1)S(1)}, u32[]{:S(2)}, u32[]{:S(2)}) collective-permute-start(f16[480,128]{1,0:T(8,128)(2,1)S(1)} %add_convert_fusion.2), channel_id=1, source_target_pairs={{24,0},{25,1},{26,2},{27,3},{28,4},{29,5},{30,6},{31,7},{16,8},{17... | collective-permute-start | bytes 368648 | tf_op jit(solution)/shard_map/ppermute | solution.py:37
  79.7 9.6 %collective-permute-start.16 = (f16[480,128]{1,0:T(8,128)(2,1)S(1)}, f16[480,128]{1,0:T(8,128)(2,1)S(1)}, u32[]{:S(2)}, u32[]{:S(2)}) collective-permute-start(f16[480,128]{1,0:T(8,128)(2,1)S(1)} %add_convert_fusion.2), channel_id=1, source_target_pairs={{16,0},{17,1},{18,2},{19,3},{20,4},{21,5},{22,6},{23,7},{24,8},{25... | collective-permute-start | bytes 368648 | tf_op jit(solution)/shard_map/ppermute | solution.py:37
  79.7 9.6 %collective-permute-start.15 = (f16[480,128]{1,0:T(8,128)(2,1)S(1)}, f16[480,128]{1,0:T(8,128)(2,1)S(1)}, u32[]{:S(2)}, u32[]{:S(2)}) collective-permute-start(f16[480,128]{1,0:T(8,128)(2,1)S(1)} %add_convert_fusion.2), channel_id=1, source_target_pairs={{8,0},{9,1},{10,2},{11,3},{12,4},{13,5},{14,6},{15,7},{0,8},{1,9},... | collective-permute-start | bytes 368648 | tf_op jit(solution)/shard_map/ppermute | solution.py:37
  (10 other events, 10.1 us)

commit v3 on v2

v3 whole, which is shorter than its diff:
```python
import jax
import jax.numpy as jnp
from jax import lax
from jax.experimental import pallas as pl
from jax.experimental.pallas import tpu as pltpu
from jax.sharding import PartitionSpec as P

ENQ = 4
score_scale = 10.0
learn_rate = 0.3
epsilon = 1e-06
f32 = jnp.float32
bf16 = jnp.bfloat16
f16 = jnp.float16


def masks_of(count):
    masks = []
    while count > 1:
        assert count % 2 == 0
        count //= 2
        masks.append(count)
    return masks


def stages_of(count, stride):
    stages, count = [], count // stride
    while count > 1:
        radix = next(r for r in range(2, count + 1) if count % r == 0)
        stages.append((stride, radix))
        stride, count = stride * radix, count // radix
    return stages


def flip(piece, mask):
    count = lax.axis_size("batch") * lax.axis_size("table")
    return lax.ppermute(piece, ("batch", "table"), [(i ^ mask, i) for i in range(count)])


def turned(piece, stride, radix):
    count = lax.axis_size("batch")
    found = []
    for turn in range(1, radix):
        pairs = []
        for target in range(count):
            digit = target // stride % radix
            pairs.append((target + ((digit + turn) % radix - digit) * stride, target))
        found.append(lax.ppermute(piece, "batch", pairs))
    return found


def sum_stage(total, stride, radix):
    sent = lax.optimization_barrier(total.astype(f16))
    parts = jnp.stack([sent] + turned(sent, stride, radix)) if radix > 2 else None
    if radix > 2:
        digit = lax.axis_index("batch") // stride % radix
        parts = list(parts[(jnp.arange(radix, dtype=jnp.int32) - digit) % radix])
    else:
        parts = [sent] + turned(sent, stride, radix)
    total = parts[0].astype(f32)
    for part in parts[1:]:
        total = total + part.astype(f32)
    return total


def split_parts(rows, terms):
    parts = []
    for _ in range(terms):
        part = lax.reduce_precision(rows, 8, 7)
        parts.append(part.astype(bf16))
        rows = rows - part
    return jnp.concatenate(parts, 1)


def pick_rows(places, blocks, width):
    total, first = None, 0
    for block in blocks:
        count = block.shape[0]
        chosen = (places[:, None] - first == jnp.arange(count, dtype=jnp.int32)[None, :]).astype(bf16)
        found = jnp.dot(chosen, block, preferred_element_type=f32)
        rows = found[:, :width]
        for start in range(width, block.shape[1], width):
            rows = rows + found[:, start : start + width]
        total = rows if total is None else total + rows
        first += count
    return total


def score_piece(query_half, carried, rows, kept):
    total_sum, moment = carried
    scores = score_scale * lax.dot_general(
        query_half, rows, (((1,), (1,)), ((), ())), preferred_element_type=f32
    )
    weights = jnp.where(kept[None, :], jnp.exp(scores), 0.0)
    moment = moment + jnp.dot(weights.astype(bf16), rows, preferred_element_type=f32)
    return (total_sum + jnp.sum(weights, 1), moment)


def score_rows(query_half, rows, kept):
    count, width = rows.shape
    carried = (jnp.zeros(query_half.shape[:1], f32), jnp.zeros(query_half.shape, f32))
    splits = 1
    while count // splits > 1024 and count % (splits * 2) == 0:
        splits = splits * 2
    if splits == 1:
        return score_piece(query_half, carried, rows, kept)
    stacked = (rows.reshape(splits, -1, width), kept.reshape(splits, -1))
    return lax.scan(lambda c, b: (score_piece(query_half, c, *b), None), carried, stacked)[0]


def norm_of(rows):
    return jnp.sqrt(jnp.sum(rows * rows, 1) + epsilon)


def prologue_kernel(fifo, owner, row, head, out):
    queue_rows, width = fifo.shape
    line = lax.broadcasted_iota(jnp.int32, (out.shape[1] - queue_rows, width), 0)
    owner, row = owner[0:1, :width], row[0:1, :width]
    told = jnp.where(line == 0, owner, jnp.where(line == 1, row // 16, row % 16))
    told = jnp.where(line == 3, head[0], told).astype(f32)
    block = jnp.concatenate([fifo[...].astype(f32), told]).astype(bf16)
    out[...] = jnp.broadcast_to(block[None], out.shape)


def per_device(queries, item_owner, item_row, table, accum, fifo, fifo_head):
    step_count, query_count, width = queries.shape
    owners, copies = lax.axis_size("table"), lax.axis_size("batch")
    owned = table.shape[0]
    part_rows = owned // 2
    queue_rows = fifo.shape[0]
    me = lax.axis_index("table")
    side = lax.axis_index("batch") % 2
    masks = masks_of(owners)
    most = owners * copies * (3 * query_count // owners)
    grad_scale = 1.0
    while most * grad_scale > 32768.0:
        grad_scale = grad_scale / 2

    def owner_place(owner):
        apart = jnp.bitwise_xor(owner, me)
        place = jnp.zeros_like(owner)
        for index, mask in enumerate(masks):
            place = place + jnp.where((apart & mask) != 0, 1 << index, 0)
        return place

    def place_whole(owner, row):
        return owner_place(owner) * owned + row

    def place_part(owner, row):
        return owner_place(owner) * owned + jnp.where(side == 0, row, (row + part_rows) % owned)

    def gather_whole(piece, terms):
        blocks = [split_parts(piece, terms)]
        for mask in masks:
            other = flip(piece, mask)
            blocks.append(split_parts(other, terms))
            piece = jnp.concatenate([piece, other])
        return blocks

    def gather_parts(piece, terms):
        wide = [piece] + [flip(piece, mask) for mask in (owners, masks[0], owners + masks[0])]
        piece = lax.optimization_barrier(jnp.concatenate(wide))
        blocks = [split_parts(piece.astype(f32), terms)]
        for mask in masks[1:]:
            other = flip(piece, mask)
            blocks.append(split_parts(other.astype(f32), terms))
            piece = jnp.concatenate([piece, other])
        return blocks

    def reduce_parts(kept, sent):
        for mask in masks[:0:-1]:
            kept = kept + flip(sent.astype(f16), mask).astype(f32)
            half = kept.shape[0] // 2
            if mask != masks[1]:
                kept, sent = kept[:half], kept[half:]
        pieces = [kept[i * part_rows : (i + 1) * part_rows] for i in range(4)]
        beside = [
            flip(piece.astype(f16), mask).astype(f32)
            for piece, mask in zip(pieces[1:], (owners, masks[0], owners + masks[0]))
        ]
        total = (pieces[0] + beside[0]) + (beside[1] + beside[2])
        for stage in stages_of(copies, 2):
            total = sum_stage(total, *stage)
        return total

    head = fifo_head[0]
    parts = gather_whole(table, 3)

    block_rows = queue_rows + 4 + -(queue_rows + 4) % 16
    vmem, smem = pl.BlockSpec(memory_space=pltpu.VMEM), pl.BlockSpec(memory_space=pltpu.SMEM)
    blocks = pl.pallas_call(
        prologue_kernel,
        out_shape=jax.ShapeDtypeStruct((owners * copies, block_rows, width), bf16),
        in_specs=[vmem, vmem, vmem, smem],
        out_specs=vmem,
    )(fifo, item_owner[:, :, 0], item_row, fifo_head)
    blocks = lax.all_to_all(blocks, ("batch", "table"), 0, 0, tiled=True)
    queue = blocks[:, :queue_rows].reshape(-1, width)
    told_all = blocks[:, queue_rows : queue_rows + 4, :ENQ].astype(jnp.int32)
    slots = jnp.arange(queue_rows, dtype=jnp.int32)

    part_table = lax.dynamic_slice_in_dim(table, side * part_rows, part_rows, 0)
    part_accum = lax.dynamic_slice_in_dim(accum, side * part_rows, part_rows, 0)
    loss_list, grad_list, joined = [], [], []
    new_half = kept = None
    for step in range(step_count):
        query_f = queries[step].astype(f32)
        query_norm = norm_of(query_f)
        query_unit = query_f / query_norm[:, None]
        query_half = query_unit.astype(bf16)
        owner, row = item_owner[step, :, 0], item_row[step]
        places = place_part(owner, row)
        if step == 0:
            rows, row_kept = queue, jnp.ones((queue.shape[0],), jnp.bool_)
        else:
            rows = jnp.concatenate([queue, new_half])
            row_kept = jnp.concatenate([kept, jnp.ones((new_half.shape[0],), jnp.bool_)])
        block_sums, moment = score_rows(query_half, rows, row_kept)
        if step == 0:
            item_vecs = pick_rows(place_whole(owner, row), parts, width)
            item_unit = item_vecs / norm_of(item_vecs)[:, None]
        else:
            item_unit = pick_rows(places, parts, width)
        joined.append(item_unit[:ENQ].astype(bf16))
        cosine = jnp.sum(query_unit * item_unit, 1)
        pos_score = score_scale * cosine
        total_sum = jnp.exp(pos_score) + block_sums
        lack = jnp.exp(pos_score) / total_sum - 1.0
        across = (lack[:, None] * (query_unit - item_unit * cosine[:, None])).astype(bf16)
        halves = []
        for half in range(2):
            count = owners * owned // 2
            rows_of = jnp.arange(count, dtype=jnp.int32) + half * count
            chosen = (places[:, None] == rows_of[None, :]).astype(bf16)
            dense = lax.dot_general(
                chosen, across, (((0,), (0,)), ((), ())), preferred_element_type=f32
            )
            halves.append(grad_scale * dense)
        halves[0] = lax.optimization_barrier(halves[0])
        total = reduce_parts(*halves)

        moment, total_sum, pos_score, lack, told_late, _ = lax.optimization_barrier(
            (moment, total_sum, pos_score, lack, told_all, halves[0])
        )
        loss_list.append(jnp.log(total_sum) - pos_score)
        unit_grad = score_scale * (lack[:, None] * item_unit + moment / total_sum[:, None])
        along_query = jnp.sum(query_unit * unit_grad, 1)
        query_grad = (unit_grad - query_unit * along_query[:, None]) / query_norm[:, None]
        grad_list.append(query_grad.astype(bf16))
        if step == 0:
            new_place = place_whole(told_late[:, 0], told_late[:, 1] * 16 + told_late[:, 2])
            new_rows = pick_rows(new_place.reshape(-1), parts, width)
            new_half = (new_rows / norm_of(new_rows)[:, None]).astype(bf16)
            kept = ((slots[None, :] - told_late[:, 3, :1]) % queue_rows >= ENQ).reshape(-1)

        grad = total * ((score_scale / grad_scale) / norm_of(part_table))[:, None]
        part_accum = part_accum + jnp.mean(grad * grad, 1)
        part_table = part_table - learn_rate * grad / jnp.sqrt(part_accum)[:, None]
        if step + 1 < step_count:
            unit = (part_table / norm_of(part_table)[:, None]).astype(f16)
            parts = gather_parts(unit, 2)

    lines = -(-part_rows // width)
    lines += -lines % 8
    packed = jnp.pad(part_accum, (0, lines * width - part_rows)).reshape(lines, width)
    mine = jnp.concatenate([part_table, packed])
    other = flip(mine, owners)
    both = [jnp.where(side == 0, mine, other), jnp.where(side == 0, other, mine)]
    table_out = jnp.concatenate([half[:part_rows] for half in both])
    accum_out = jnp.concatenate([half[part_rows:].reshape(-1)[:part_rows] for half in both])
    fifo_out = fifo
    for step in range(step_count):
        place = (slots - head - step * ENQ) % queue_rows
        for k in range(ENQ):
            fifo_out = jnp.where((place == k)[:, None], joined[step][k][None, :], fifo_out)
    return (jnp.stack(loss_list), jnp.stack(grad_list), table_out, accum_out, fifo_out)


def solution(mesh):
    both = ("batch", "table")
    in_specs = (
        P(None, both, None),
        P(None, both, None),
        P(None, both),
        P("table", None),
        P("table"),
        P(both, None),
        P(both),
    )
    out_specs = (P(None, both), P(None, both, None), P("table", None), P("table"), P(both, None))
    return jax.shard_map(
        per_device, mesh=mesh, in_specs=in_specs, out_specs=out_specs, check_vma=False
    )
```

time: 91.3 us -> 83.9 us (0.919)
  waiting for transfers between devices: 37.6 us -> 32.3 us
  starting transfers between devices: 27 us -> 22.8 us
  Pallas kernels: 0 us -> 1.39 us
  local copies, waits for them, and re-layouts: 3.91 us -> 5.12 us
  matrix products: 10 us -> 8.97 us
    ppermute x18 -> x15, waiting for transfers between devices: 37.6 us -> 13.4 us  [flip(): lax.ppermute(piece, ('batch', 'table'), [(i ^ mask, i) for i in range(cou...]
    ppermute x0 -> x4, waiting for transfers between devices: none -> 16 us  [turned(): found.append(lax.ppermute(piece, 'batch', pairs))]
    ppermute x18 -> x15, starting transfers between devices: 19.7 us -> 15.6 us  [flip(): lax.ppermute(piece, ('batch', 'table'), [(i ^ mask, i) for i in range(cou...]
    all_to_all x1, waiting for transfers between devices: 0.01 us -> 2.93 us  [per_device(): blocks = lax.all_to_all(blocks, ('batch', 'table'), 0, 0, tiled=True)]
    unnamed x30 -> x43, local copies, waits for them, and re-layouts: 0.76 us -> 3.35 us
    all_to_all x1, starting transfers between devices: 7.3 us -> 4.92 us  [per_device(): blocks = lax.all_to_all(blocks, ('batch', 'table'), 0, 0, tiled=True)]
    ppermute x0 -> x4, starting transfers between devices: none -> 2.24 us  [turned(): found.append(lax.ppermute(piece, 'batch', pairs))]
    concatenate x2 -> x5, other arithmetic: 0.1 us -> 2.28 us  [the longest x1 0.82 us: gather_whole(): piece = jnp.concatenate([piece, other])]
  transfers between devices with their start and end apart: 19 -> 20, of which waited for: 13 -> 17; matrix products, arithmetic and copies ran while one was open for 10% -> 14% of each run, Pallas kernels for 0% -> 2%
where the time goes in v3:
time: 83.9 us; the launch traced here: 83.5 us
  waiting for transfers between devices  32.3 us (38%)
  starting transfers between devices  22.8 us (27%)
  other arithmetic  10.9 us (13%)
  matrix products  8.97 us (11%)
  local copies, waits for them, and re-layouts  5.12 us (6%)
  between operations  2.05 us (2%)
  Pallas kernels  1.39 us (2%)
    ppermute x4, waiting for transfers between devices, turned(): found.append(lax.ppermute(piece, 'batch', pairs))  16 us
    ppermute x15, starting transfers between devices, flip(): lax.ppermute(piece, ('batch', 'table'), [(i ^ mask, i) for i in range(cou...  15.6 us
    ppermute x15, waiting for transfers between devices, flip(): lax.ppermute(piece, ('batch', 'table'), [(i ^ mask, i) for i in range(cou...  13.4 us
    all_to_all x1, starting transfers between devices, per_device(): blocks = lax.all_to_all(blocks, ('batch', 'table'), 0, 0, tiled=True)  4.92 us
    dot_general x4, matrix products, per_device(): lax.dot_general(chosen, across, (((0,), (0,)), ((), ())), preferred_eleme...  3.93 us
    dot_general x8, matrix products, pick_rows(): found = jnp.dot(chosen, block, preferred_element_type=f32)  3.66 us
    unnamed x43, local copies, waits for them, and re-layouts  3.35 us
    all_to_all x1, waiting for transfers between devices, per_device(): blocks = lax.all_to_all(blocks, ('batch', 'table'), 0, 0, tiled=True)  2.93 us
  transfers between devices with their start and end apart: 20, of which 17 were waited for; matrix products, arithmetic and copies ran while one was open for 14% of the time, Pallas kernels for 2%

profile of v3, /device:TPU:0, one launch (start us, length us, event | category | flops | bytes accessed | tf_op | source)
XLA Modules:
  0.0 83.5 jit_solution(10635651034995665636)
XLA Ops:
  0.7 3.0 %collective-permute-start = (f32[480,128]{1,0:T(8,128)}, f32[480,128]{1,0:T(8,128)S(1)}, u32[]{:S(2)}, u32[]{:S(2)}) collective-permute-start(f32[480,128]{1,0:T(8,128)} %param.10), channel_id=1, source_target_pairs={{2,0},{3,1},{0,2},{1,3},{6,4},{7,5},{4,6},{5,7},{10,8},{11,9},{8,1... | collective-permute-start | bytes 737288 | tf_op jit(solution)/shard_map/ppermute | solution.py:37
  4.3 1.3 %copy.14 = s32[2,512,1]{1,0,2:T(2,128)} copy(s32[2,512,1]{1,2,0:T(1,128)} %param.8) | data formatting | bytes 8192
  5.6 1.4 %shard_map.110 = bf16[32,16,128]{2,1,0:T(8,128)(2,1)} custom-call(bf16[8,128]{1,0:T(8,128)(2,1)} %fifo.1, s32[2,512]{1,0:T(2,128)} %bitcast.90, s32[2,512]{1,0:T(2,128)} %row.1, s32[1]{0:T(128)} %copy.15.head), custom_call_target="tpu_custom_call" | custom-call | tf_op jit(solution)/shard_map/pallas_call | solution.py:191
  7.0 4.9 %all-to-all-start = ((bf16[32,16,128]{2,1,0:T(8,128)(2,1)}), bf16[32,16,128]{2,1,0:T(8,128)(2,1)S(1)}, u32[]{:S(2)}, u32[]{:S(2)}) async-start(bf16[32,16,128]{2,1,0:T(8,128)(2,1)} %shard_map.110), calls=%async_computation | async-start | bytes 262144 | tf_op jit(solution)/shard_map/all_to_all | solution.py:197
  12.7 1.0 %reduce-precision_convert_fusion.7 = (bf16[480,128]{1,0:T(8,128)(2,1)S(1)}, bf16[480,128]{1,0:T(8,128)(2,1)S(1)}, bf16[480,128]{1,0:T(8,128)(2,1)S(1)}) fusion(f32[480,128]{1,0:T(8,128)} %param.10), kind=kLoop, calls=%fused_computation.72 | loop fusion | flops 491520 | bytes 614400 | tf_op jit(solution)/shard_map/convert_element_type | solution.py:70
  17.2 2.9 %all-to-all-done = bf16[32,16,128]{2,1,0:T(8,128)(2,1)S(1)} async-done(((bf16[32,16,128]{2,1,0:T(8,128)(2,1)}), bf16[32,16,128]{2,1,0:T(8,128)(2,1)S(1)}, u32[]{:S(2)}, u32[]{:S(2)}) %all-to-all-start) | async-done | bytes 131104 | tf_op jit(solution)/shard_map/all_to_all | solution.py:197
  25.5 1.5 %fusion.12 = f16[960,128]{1,0:T(8,128)(2,1)} fusion(bf16[512,128]{1,0:T(8,128)(2,1)S(1)} %multiply_convert_fusion.1, s32[960]{0:T(1024)S(1)} %iota_add_fusion, s32[512]{0:T(512)S(1)} %get-tuple-element.83), kind=kOutput, calls=%fused_computation.18 | convolution fusion | flops 126443520 | bytes 382720 | tf_op jit(solution)/shard_map/dot_general | solution.py:235
  30.4 2.1 %collective-permute-start.5 = (f16[240,128]{1,0:T(8,128)(2,1)S(1)}, f16[240,128]{1,0:T(8,128)(2,1)S(1)}, u32[]{:S(2)}, u32[]{:S(2)}) collective-permute-start(f16[240,128]{1,0:T(8,128)(2,1)S(1)} %get-tuple-element.61), channel_id=1, source_target_pairs={{6,0},{7,1},{4,2},{5,3},{2,4},{3,5},{0,6},{1,7},{14,8},{15,9},{12,... | collective-permute-start | bytes 184328 | tf_op jit(solution)/shard_map/ppermute | solution.py:37
  33.2 1.1 %collective-permute-done.4 = f16[240,128]{1,0:T(8,128)(2,1)S(1)} collective-permute-done((f16[240,128]{1,0:T(8,128)(2,1)S(1)}, f16[240,128]{1,0:T(8,128)(2,1)S(1)}, u32[]{:S(2)}, u32[]{:S(2)}) %collective-permute-start.4) | collective-permute-done | bytes 61472 | tf_op jit(solution)/shard_map/ppermute | solution.py:37
  34.4 1.3 %collective-permute-done.5 = f16[240,128]{1,0:T(8,128)(2,1)S(1)} collective-permute-done((f16[240,128]{1,0:T(8,128)(2,1)S(1)}, f16[240,128]{1,0:T(8,128)(2,1)S(1)}, u32[]{:S(2)}, u32[]{:S(2)}) %collective-permute-start.5) | collective-permute-done | bytes 61472 | tf_op jit(solution)/shard_map/ppermute | solution.py:37
  36.8 3.1 %collective-permute-done.6 = f16[240,128]{1,0:T(8,128)(2,1)S(1)} collective-permute-done((f16[240,128]{1,0:T(8,128)(2,1)S(1)}, f16[240,128]{1,0:T(8,128)(2,1)S(1)}, u32[]{:S(2)}, u32[]{:S(2)}) %collective-permute-start.6) | collective-permute-done | bytes 61472 | tf_op jit(solution)/shard_map/ppermute | solution.py:48
  40.0 1.2 %collective-permute-start.7 = (f16[240,128]{1,0:T(8,128)(2,1)S(1)}, f16[240,128]{1,0:T(8,128)(2,1)S(1)}, u32[]{:S(2)}, u32[]{:S(2)}) collective-permute-start(f16[240,128]{1,0:T(8,128)(2,1)S(1)} %add_convert_fusion.1), channel_id=1, source_target_pairs={{16,0},{20,4},{24,8},{28,12},{0,16},{4,20},{8,24},{12,28},{17,1},{... | collective-permute-start | bytes 184328 | tf_op jit(solution)/shard_map/ppermute | solution.py:48
  41.5 4.3 %collective-permute-done.7 = f16[240,128]{1,0:T(8,128)(2,1)S(1)} collective-permute-done((f16[240,128]{1,0:T(8,128)(2,1)S(1)}, f16[240,128]{1,0:T(8,128)(2,1)S(1)}, u32[]{:S(2)}, u32[]{:S(2)}) %collective-permute-start.7) | collective-permute-done | bytes 61472 | tf_op jit(solution)/shard_map/ppermute | solution.py:48
  46.5 2.1 %collective-permute-start.10 = (f16[240,128]{1,0:T(8,128)(2,1)S(1)}, f16[240,128]{1,0:T(8,128)(2,1)S(1)}, u32[]{:S(2)}, u32[]{:S(2)}) collective-permute-start(f16[240,128]{1,0:T(8,128)(2,1)S(1)} %divide_convert_fusion.2), channel_id=1, source_target_pairs={{6,0},{7,1},{4,2},{5,3},{2,4},{3,5},{0,6},{1,7},{14,8},{15,9},{12,... | collective-permute-start | bytes 184328 | tf_op jit(solution)/shard_map/ppermute | solution.py:37
  50.0 1.6 %collective-permute-done.10 = f16[240,128]{1,0:T(8,128)(2,1)S(1)} collective-permute-done((f16[240,128]{1,0:T(8,128)(2,1)S(1)}, f16[240,128]{1,0:T(8,128)(2,1)S(1)}, u32[]{:S(2)}, u32[]{:S(2)}) %collective-permute-start.10) | collective-permute-done | bytes 61472 | tf_op jit(solution)/shard_map/ppermute | solution.py:37
  51.6 1.1 %collective-permute-done.8 = f16[240,128]{1,0:T(8,128)(2,1)S(1)} collective-permute-done((f16[240,128]{1,0:T(8,128)(2,1)S(1)}, f16[240,128]{1,0:T(8,128)(2,1)S(1)}, u32[]{:S(2)}, u32[]{:S(2)}) %collective-permute-start.8) | collective-permute-done | bytes 61472 | tf_op jit(solution)/shard_map/ppermute | solution.py:37
  60.0 1.4 %collective-permute-start.13 = (f16[240,128]{1,0:T(8,128)(2,1)S(1)}, f16[240,128]{1,0:T(8,128)(2,1)S(1)}, u32[]{:S(2)}, u32[]{:S(2)}) collective-permute-start(f16[240,128]{1,0:T(8,128)(2,1)S(1)} %get-tuple-element.53), channel_id=1, source_target_pairs={{4,0},{5,1},{6,2},{7,3},{0,4},{1,5},{2,6},{3,7},{12,8},{13,9},{14,... | collective-permute-start | bytes 184328 | tf_op jit(solution)/shard_map/ppermute | solution.py:37
  61.8 1.7 %collective-permute-start.15 = (f16[240,128]{1,0:T(8,128)(2,1)S(1)}, f16[240,128]{1,0:T(8,128)(2,1)S(1)}, u32[]{:S(2)}, u32[]{:S(2)}) collective-permute-start(f16[240,128]{1,0:T(8,128)(2,1)S(1)} %get-tuple-element.54), channel_id=1, source_target_pairs={{6,0},{7,1},{4,2},{5,3},{2,4},{3,5},{0,6},{1,7},{14,8},{15,9},{12,... | collective-permute-start | bytes 184328 | tf_op jit(solution)/shard_map/ppermute | solution.py:37
  64.2 1.7 %collective-permute-done.14 = f16[240,128]{1,0:T(8,128)(2,1)S(1)} collective-permute-done((f16[240,128]{1,0:T(8,128)(2,1)S(1)}, f16[240,128]{1,0:T(8,128)(2,1)S(1)}, u32[]{:S(2)}, u32[]{:S(2)}) %collective-permute-start.14) | collective-permute-done | bytes 61472 | tf_op jit(solution)/shard_map/ppermute | solution.py:37
  66.0 1.0 %collective-permute-done.15 = f16[240,128]{1,0:T(8,128)(2,1)S(1)} collective-permute-done((f16[240,128]{1,0:T(8,128)(2,1)S(1)}, f16[240,128]{1,0:T(8,128)(2,1)S(1)}, u32[]{:S(2)}, u32[]{:S(2)}) %collective-permute-start.15) | collective-permute-done | bytes 61472 | tf_op jit(solution)/shard_map/ppermute | solution.py:37
  67.8 3.5 %collective-permute-done.16 = f16[240,128]{1,0:T(8,128)(2,1)S(1)} collective-permute-done((f16[240,128]{1,0:T(8,128)(2,1)S(1)}, f16[240,128]{1,0:T(8,128)(2,1)S(1)}, u32[]{:S(2)}, u32[]{:S(2)}) %collective-permute-start.16) | collective-permute-done | bytes 61472 | tf_op jit(solution)/shard_map/ppermute | solution.py:48
  71.6 5.0 %collective-permute-done.17 = f16[240,128]{1,0:T(8,128)(2,1)S(1)} collective-permute-done((f16[240,128]{1,0:T(8,128)(2,1)S(1)}, f16[240,128]{1,0:T(8,128)(2,1)S(1)}, u32[]{:S(2)}, u32[]{:S(2)}) %collective-permute-start.17) | collective-permute-done | bytes 61472 | tf_op jit(solution)/shard_map/ppermute | solution.py:48
  77.1 1.2 %collective-permute-start.18 = (f32[248,128]{1,0:T(8,128)S(1)}, f32[248,128]{1,0:T(8,128)S(1)}, u32[]{:S(2)}, u32[]{:S(2)}) collective-permute-start(f32[248,128]{1,0:T(8,128)S(1)} %pad_maximum_fusion.13), channel_id=1, source_target_pairs={{4,0},{5,1},{6,2},{7,3},{0,4},{1,5},{2,6},{3,7},{12,8},{13,9},{14,... | collective-permute-start | bytes 380936 | tf_op jit(solution)/shard_map/ppermute | solution.py:37
  79.6 2.4 %collective-permute-done.18 = f32[248,128]{1,0:T(8,128)S(1)} collective-permute-done((f32[248,128]{1,0:T(8,128)S(1)}, f32[248,128]{1,0:T(8,128)S(1)}, u32[]{:S(2)}, u32[]{:S(2)}) %collective-permute-start.18) | collective-permute-done | bytes 127008 | tf_op jit(solution)/shard_map/ppermute | solution.py:37
  (155 shorter events, 29.4 us)
Async XLA Ops:
  0.6 13.4 %copy-start.1 = (f32[480,128]{1,0:T(8,128)S(1)}, f32[480,128]{1,0:T(8,128)}, u32[]{:S(2)}) copy-start(f32[480,128]{1,0:T(8,128)} %param.10) | copy-start | bytes 737284
  0.6 13.1 %copy-start.18 = (s32[2,512,1]{1,2,0:T(1,128)S(1)}, s32[2,512,1]{1,2,0:T(1,128)}, u32[]{:S(2)}) copy-start(s32[2,512,1]{1,2,0:T(1,128)} %param.8) | copy-start | bytes 12292
  0.7 13.2 %copy-start = (bf16[2,512,128]{2,1,0:T(8,128)(2,1)S(1)}, bf16[2,512,128]{2,1,0:T(8,128)(2,1)}, u32[]{:S(2)}) copy-start(bf16[2,512,128]{2,1,0:T(8,128)(2,1)} %param.7) | copy-start | bytes 786436
  0.7 14.2 %collective-permute-start = (f32[480,128]{1,0:T(8,128)}, f32[480,128]{1,0:T(8,128)S(1)}, u32[]{:S(2)}, u32[]{:S(2)}) collective-permute-start(f32[480,128]{1,0:T(8,128)} %param.10), channel_id=1, source_target_pairs={{2,0},{3,1},{0,2},{1,3},{6,4},{7,5},{4,6},{5,7},{10,8},{11,9},{8,1... | collective-permute-start | bytes 737288 | tf_op jit(solution)/shard_map/ppermute | solution.py:37
  7.0 13.2 %all-to-all-start = ((bf16[32,16,128]{2,1,0:T(8,128)(2,1)}), bf16[32,16,128]{2,1,0:T(8,128)(2,1)S(1)}, u32[]{:S(2)}, u32[]{:S(2)}) async-start(bf16[32,16,128]{2,1,0:T(8,128)(2,1)} %shard_map.110), calls=%async_computation | async-start | bytes 262144 | tf_op jit(solution)/shard_map/all_to_all | solution.py:197
  15.7 5.1 %collective-permute-start.1 = (f32[960,128]{1,0:T(8,128)}, f32[960,128]{1,0:T(8,128)S(1)}, u32[]{:S(2)}, u32[]{:S(2)}) collective-permute-start(f32[960,128]{1,0:T(8,128)} %pad_maximum_fusion.1), channel_id=1, source_target_pairs={{1,0},{0,1},{3,2},{2,3},{5,4},{4,5},{7,6},{6,7},{9,8},{8,9},{11,10... | collective-permute-start | bytes 1474568 | tf_op jit(solution)/shard_map/ppermute | solution.py:37
  27.0 1.8 %collective-permute-start.2 = (f16[960,128]{1,0:T(8,128)(2,1)}, f16[960,128]{1,0:T(8,128)(2,1)S(1)}, u32[]{:S(2)}, u32[]{:S(2)}) collective-permute-start(f16[960,128]{1,0:T(8,128)(2,1)} %fusion.12), channel_id=1, source_target_pairs={{1,0},{0,1},{3,2},{2,3},{5,4},{4,5},{7,6},{6,7},{9,8},{8,9},{11,10... | collective-permute-start | bytes 737288 | tf_op jit(solution)/shard_map/ppermute | solution.py:37
  28.9 4.3 %collective-permute-start.3 = (f16[240,128]{1,0:T(8,128)(2,1)S(1)}, f16[240,128]{1,0:T(8,128)(2,1)S(1)}, u32[]{:S(2)}, u32[]{:S(2)}) collective-permute-start(f16[240,128]{1,0:T(8,128)(2,1)S(1)} %get-tuple-element.60), channel_id=1, source_target_pairs={{4,0},{5,1},{6,2},{7,3},{0,4},{1,5},{2,6},{3,7},{12,8},{13,9},{14,... | collective-permute-start | bytes 184328 | tf_op jit(solution)/shard_map/ppermute | solution.py:37
  29.6 4.7 %collective-permute-start.4 = (f16[240,128]{1,0:T(8,128)(2,1)S(1)}, f16[240,128]{1,0:T(8,128)(2,1)S(1)}, u32[]{:S(2)}, u32[]{:S(2)}) collective-permute-start(f16[240,128]{1,0:T(8,128)(2,1)S(1)} %get-tuple-element.62), channel_id=1, source_target_pairs={{2,0},{3,1},{0,2},{1,3},{6,4},{7,5},{4,6},{5,7},{10,8},{11,9},{8,1... | collective-permute-start | bytes 184328 | tf_op jit(solution)/shard_map/ppermute | solution.py:37
  30.4 5.2 %collective-permute-start.5 = (f16[240,128]{1,0:T(8,128)(2,1)S(1)}, f16[240,128]{1,0:T(8,128)(2,1)S(1)}, u32[]{:S(2)}, u32[]{:S(2)}) collective-permute-start(f16[240,128]{1,0:T(8,128)(2,1)S(1)} %get-tuple-element.61), channel_id=1, source_target_pairs={{6,0},{7,1},{4,2},{5,3},{2,4},{3,5},{0,6},{1,7},{14,8},{15,9},{12,... | collective-permute-start | bytes 184328 | tf_op jit(solution)/shard_map/ppermute | solution.py:37
  35.7 4.3 %collective-permute-start.6 = (f16[240,128]{1,0:T(8,128)(2,1)S(1)}, f16[240,128]{1,0:T(8,128)(2,1)S(1)}, u32[]{:S(2)}, u32[]{:S(2)}) collective-permute-start(f16[240,128]{1,0:T(8,128)(2,1)S(1)} %fusion.74), channel_id=1, source_target_pairs={{8,0},{12,4},{0,8},{4,12},{24,16},{28,20},{16,24},{20,28},{9,1},{1... | collective-permute-start | bytes 184328 | tf_op jit(solution)/shard_map/ppermute | solution.py:48
  36.8 9.2 %copy-start.20 = (f32[480]{0:T(512)S(1)}, f32[480]{0:T(512)}, u32[]{:S(2)}) copy-start(f32[480]{0:T(512)} %param.11) | copy-start | bytes 5764
  40.0 5.8 %collective-permute-start.7 = (f16[240,128]{1,0:T(8,128)(2,1)S(1)}, f16[240,128]{1,0:T(8,128)(2,1)S(1)}, u32[]{:S(2)}, u32[]{:S(2)}) collective-permute-start(f16[240,128]{1,0:T(8,128)(2,1)S(1)} %add_convert_fusion.1), channel_id=1, source_target_pairs={{16,0},{20,4},{24,8},{28,12},{0,16},{4,20},{8,24},{12,28},{17,1},{... | collective-permute-start | bytes 184328 | tf_op jit(solution)/shard_map/ppermute | solution.py:48
  46.5 5.2 %collective-permute-start.10 = (f16[240,128]{1,0:T(8,128)(2,1)S(1)}, f16[240,128]{1,0:T(8,128)(2,1)S(1)}, u32[]{:S(2)}, u32[]{:S(2)}) collective-permute-start(f16[240,128]{1,0:T(8,128)(2,1)S(1)} %divide_convert_fusion.2), channel_id=1, source_target_pairs={{6,0},{7,1},{4,2},{5,3},{2,4},{3,5},{0,6},{1,7},{14,8},{15,9},{12,... | collective-permute-start | bytes 184328 | tf_op jit(solution)/shard_map/ppermute | solution.py:37
  48.5 4.2 %collective-permute-start.8 = (f16[240,128]{1,0:T(8,128)(2,1)S(1)}, f16[240,128]{1,0:T(8,128)(2,1)S(1)}, u32[]{:S(2)}, u32[]{:S(2)}) collective-permute-start(f16[240,128]{1,0:T(8,128)(2,1)S(1)} %divide_convert_fusion.2), channel_id=1, source_target_pairs={{4,0},{5,1},{6,2},{7,3},{0,4},{1,5},{2,6},{3,7},{12,8},{13,9},{14,... | collective-permute-start | bytes 184328 | tf_op jit(solution)/shard_map/ppermute | solution.py:37
  49.2 4.2 %collective-permute-start.9 = (f16[240,128]{1,0:T(8,128)(2,1)S(1)}, f16[240,128]{1,0:T(8,128)(2,1)S(1)}, u32[]{:S(2)}, u32[]{:S(2)}) collective-permute-start(f16[240,128]{1,0:T(8,128)(2,1)S(1)} %divide_convert_fusion.2), channel_id=1, source_target_pairs={{2,0},{3,1},{0,2},{1,3},{6,4},{7,5},{4,6},{5,7},{10,8},{11,9},{8,1... | collective-permute-start | bytes 184328 | tf_op jit(solution)/shard_map/ppermute | solution.py:37
  53.5 1.6 %collective-permute-start.11 = (f16[960,128]{1,0:T(8,128)(2,1)S(1)}, f16[960,128]{1,0:T(8,128)(2,1)S(1)}, u32[]{:S(2)}, u32[]{:S(2)}) collective-permute-start(f16[960,128]{1,0:T(8,128)(2,1)S(1)} %pad_maximum_fusion.7), channel_id=1, source_target_pairs={{1,0},{0,1},{3,2},{2,3},{5,4},{4,5},{7,6},{6,7},{9,8},{8,9},{11,10... | collective-permute-start | bytes 737288 | tf_op jit(solution)/shard_map/ppermute | solution.py:37
  58.3 1.6 %collective-permute-start.12 = (f16[960,128]{1,0:T(8,128)(2,1)S(1)}, f16[960,128]{1,0:T(8,128)(2,1)S(1)}, u32[]{:S(2)}, u32[]{:S(2)}) collective-permute-start(f16[960,128]{1,0:T(8,128)(2,1)S(1)} %fusion.15), channel_id=1, source_target_pairs={{1,0},{0,1},{3,2},{2,3},{5,4},{4,5},{7,6},{6,7},{9,8},{8,9},{11,10... | collective-permute-start | bytes 737288 | tf_op jit(solution)/shard_map/ppermute | solution.py:37
  60.0 4.3 %collective-permute-start.13 = (f16[240,128]{1,0:T(8,128)(2,1)S(1)}, f16[240,128]{1,0:T(8,128)(2,1)S(1)}, u32[]{:S(2)}, u32[]{:S(2)}) collective-permute-start(f16[240,128]{1,0:T(8,128)(2,1)S(1)} %get-tuple-element.53), channel_id=1, source_target_pairs={{4,0},{5,1},{6,2},{7,3},{0,4},{1,5},{2,6},{3,7},{12,8},{13,9},{14,... | collective-permute-start | bytes 184328 | tf_op jit(solution)/shard_map/ppermute | solution.py:37
  61.4 4.6 %collective-permute-start.14 = (f16[240,128]{1,0:T(8,128)(2,1)S(1)}, f16[240,128]{1,0:T(8,128)(2,1)S(1)}, u32[]{:S(2)}, u32[]{:S(2)}) collective-permute-start(f16[240,128]{1,0:T(8,128)(2,1)S(1)} %get-tuple-element.55), channel_id=1, source_target_pairs={{2,0},{3,1},{0,2},{1,3},{6,4},{7,5},{4,6},{5,7},{10,8},{11,9},{8,1... | collective-permute-start | bytes 184328 | tf_op jit(solution)/shard_map/ppermute | solution.py:37
  61.8 5.2 %collective-permute-start.15 = (f16[240,128]{1,0:T(8,128)(2,1)S(1)}, f16[240,128]{1,0:T(8,128)(2,1)S(1)}, u32[]{:S(2)}, u32[]{:S(2)}) collective-permute-start(f16[240,128]{1,0:T(8,128)(2,1)S(1)} %get-tuple-element.54), channel_id=1, source_target_pairs={{6,0},{7,1},{4,2},{5,3},{2,4},{3,5},{0,6},{1,7},{14,8},{15,9},{12,... | collective-permute-start | bytes 184328 | tf_op jit(solution)/shard_map/ppermute | solution.py:37
  67.0 4.3 %collective-permute-start.16 = (f16[240,128]{1,0:T(8,128)(2,1)S(1)}, f16[240,128]{1,0:T(8,128)(2,1)S(1)}, u32[]{:S(2)}, u32[]{:S(2)}) collective-permute-start(f16[240,128]{1,0:T(8,128)(2,1)S(1)} %fusion.72), channel_id=1, source_target_pairs={{8,0},{12,4},{0,8},{4,12},{24,16},{28,20},{16,24},{20,28},{9,1},{1... | collective-permute-start | bytes 184328 | tf_op jit(solution)/shard_map/ppermute | solution.py:48
  71.4 5.3 %collective-permute-start.17 = (f16[240,128]{1,0:T(8,128)(2,1)S(1)}, f16[240,128]{1,0:T(8,128)(2,1)S(1)}, u32[]{:S(2)}, u32[]{:S(2)}) collective-permute-start(f16[240,128]{1,0:T(8,128)(2,1)S(1)} %add_convert_fusion), channel_id=1, source_target_pairs={{16,0},{20,4},{24,8},{28,12},{0,16},{4,20},{8,24},{12,28},{17,1},{... | collective-permute-start | bytes 184328 | tf_op jit(solution)/shard_map/ppermute | solution.py:48
  77.1 5.0 %collective-permute-start.18 = (f32[248,128]{1,0:T(8,128)S(1)}, f32[248,128]{1,0:T(8,128)S(1)}, u32[]{:S(2)}, u32[]{:S(2)}) collective-permute-start(f32[248,128]{1,0:T(8,128)S(1)} %pad_maximum_fusion.13), channel_id=1, source_target_pairs={{4,0},{5,1},{6,2},{7,3},{0,4},{1,5},{2,6},{3,7},{12,8},{13,9},{14,... | collective-permute-start | bytes 380936 | tf_op jit(solution)/shard_map/ppermute | solution.py:37
  (17 other events, 29.1 us)

commit v4 on v3

v4 whole, which is shorter than its diff:
```python
import functools

import jax
import jax.numpy as jnp
from jax import lax
from jax.experimental import pallas as pl
from jax.experimental.pallas import tpu as pltpu
from jax.sharding import PartitionSpec as P

ENQ = 4
score_scale = 10.0
learn_rate = 0.3
epsilon = 1e-06
f32 = jnp.float32
bf16 = jnp.bfloat16
f16 = jnp.float16


def masks_of(count):
    masks = []
    while count > 1:
        assert count % 2 == 0
        count //= 2
        masks.append(count)
    return masks


def stages_of(count, stride):
    stages, count = [], count // stride
    while count > 1:
        radix = next(r for r in range(2, count + 1) if count % r == 0)
        stages.append((stride, radix))
        stride, count = stride * radix, count // radix
    return stages


def flip(piece, mask):
    count = lax.axis_size("batch") * lax.axis_size("table")
    return lax.ppermute(piece, ("batch", "table"), [(i ^ mask, i) for i in range(count)])


def turned(piece, stride, radix):
    count = lax.axis_size("batch")
    found = []
    for turn in range(1, radix):
        pairs = []
        for target in range(count):
            digit = target // stride % radix
            pairs.append((target + ((digit + turn) % radix - digit) * stride, target))
        found.append(lax.ppermute(piece, "batch", pairs))
    return found


def sum_stage(total, stride, radix):
    sent = lax.optimization_barrier(total.astype(f16))
    parts = jnp.stack([sent] + turned(sent, stride, radix)) if radix > 2 else None
    if radix > 2:
        digit = lax.axis_index("batch") // stride % radix
        parts = list(parts[(jnp.arange(radix, dtype=jnp.int32) - digit) % radix])
    else:
        parts = [sent] + turned(sent, stride, radix)
    total = parts[0].astype(f32)
    for part in parts[1:]:
        total = total + part.astype(f32)
    return total


def split_parts(rows, terms):
    parts = []
    for _ in range(terms):
        part = lax.reduce_precision(rows, 8, 7)
        parts.append(part.astype(bf16))
        rows = rows - part
    return jnp.concatenate(parts, 1)


def pick_rows(places, blocks, width):
    total, first = None, 0
    for block in blocks:
        count = block.shape[0]
        chosen = (places[:, None] - first == jnp.arange(count, dtype=jnp.int32)[None, :]).astype(bf16)
        found = jnp.dot(chosen, block, preferred_element_type=f32)
        rows = found[:, :width]
        for start in range(width, block.shape[1], width):
            rows = rows + found[:, start : start + width]
        total = rows if total is None else total + rows
        first += count
    return total


def score_piece(query_half, carried, rows, kept):
    total_sum, moment = carried
    scores = score_scale * lax.dot_general(
        query_half, rows, (((1,), (1,)), ((), ())), preferred_element_type=f32
    )
    weights = jnp.where(kept[None, :], jnp.exp(scores), 0.0)
    moment = moment + jnp.dot(weights.astype(bf16), rows, preferred_element_type=f32)
    return (total_sum + jnp.sum(weights, 1), moment)


def score_rows(query_half, rows, kept):
    count, width = rows.shape
    carried = (jnp.zeros(query_half.shape[:1], f32), jnp.zeros(query_half.shape, f32))
    splits = 1
    while count // splits > 1024 and count % (splits * 2) == 0:
        splits = splits * 2
    if splits == 1:
        return score_piece(query_half, carried, rows, kept)
    stacked = (rows.reshape(splits, -1, width), kept.reshape(splits, -1))
    return lax.scan(lambda c, b: (score_piece(query_half, c, *b), None), carried, stacked)[0]


def norm_of(rows):
    return jnp.sqrt(jnp.sum(rows * rows, 1) + epsilon)


def prologue_kernel(fifo, owner, row, head, out):
    queue_rows, width = fifo.shape
    line = lax.broadcasted_iota(jnp.int32, (queue_rows, width), 0)
    lane = lax.broadcasted_iota(jnp.int32, (queue_rows, width), 1)
    told = jnp.full((queue_rows, width), -1, jnp.int32)
    for k in range(ENQ):
        slot = lax.rem(head[0] + k, queue_rows)
        item = jnp.where(lane == 0, owner[0, 0, k], jnp.where(lane == 1, row[0, k] // 16, row[0, k] % 16))
        told = jnp.where(line == slot, item, told)
    block = jnp.concatenate([fifo[...].astype(f32), told.astype(f32)]).astype(bf16)
    out[...] = jnp.broadcast_to(block[None], out.shape)


def one_hot(places, first, count, columns):
    shape = (places.shape[0], count) if columns else (count, places.shape[1])
    numbers = lax.broadcasted_iota(jnp.int32, shape, 1 if columns else 0)
    return (numbers == places - first).astype(f32).astype(bf16)


def split_dot(places, blocks, terms, first=0):
    found = 0.0
    for block in blocks:
        chosen = one_hot(places, first, block.shape[0], True)
        first += block.shape[0]
        rest = block[...]
        for _ in range(terms):
            part = rest.astype(bf16)
            rest = rest - part.astype(f32)
            found = found + jnp.dot(chosen, part, preferred_element_type=f32)
    return found


def unit_of(rows):
    norm = jnp.sqrt(jnp.sum(rows * rows, 1, keepdims=True) + epsilon)
    return rows / norm, norm


def weights_of(unit, negatives):
    scores = lax.dot_general(
        unit.astype(bf16), negatives, (((1,), (1,)), ((), ())), preferred_element_type=f32
    )
    return jnp.exp(score_scale * scores)


def first_kernel(terms, count, queries, places, negatives, *refs):
    blocks, (unit, found, sums) = refs[:count], refs[count:]
    unit[...], _ = unit_of(queries[...].astype(f32))
    found[...] = split_dot(places[...], blocks, terms)
    if negatives.shape[1] > 1:
        sums[...] = jnp.sum(weights_of(unit[...], negatives[...]), 1, keepdims=True)
    else:
        sums[...] = negatives[...]


def main_kernel(step, terms, first, found, block, places, line, queries, negatives, sent, kept, unit):
    item = found[...] + split_dot(places[...], [block], terms, first)
    if step == 0:
        item, _ = unit_of(item)
    unit[...] = item
    query = queries[...]
    if negatives.shape[1] > 1:
        sums = jnp.sum(weights_of(query, negatives[...]), 1, keepdims=True)
    else:
        sums = negatives[...]
    cosine = jnp.sum(query * item, 1, keepdims=True)
    weight = jnp.exp(score_scale * cosine)
    lack = weight / (weight + sums) - 1.0
    rows = (lack * (query - item * cosine)).astype(bf16)
    half = kept.shape[0]
    for out, start in ((sent, half), (kept, 0)):
        chosen = one_hot(line[...], start, half, False)
        out[...] = jnp.dot(chosen, rows, preferred_element_type=f32).astype(out.dtype)


def late_kernel(given, queries, item, negatives, _, *refs):
    query, query_norm = unit_of(queries[...].astype(f32))
    if given:
        (moment_in, loss, grad), sums = refs, negatives[...]
        moment = moment_in[...]
    else:
        loss, grad = refs
        weights = weights_of(query, negatives[...])
        sums = jnp.sum(weights, 1, keepdims=True)
        moment = jnp.dot(weights.astype(bf16), negatives[...], preferred_element_type=f32)
    item = item[...]
    score = score_scale * jnp.sum(query * item, 1, keepdims=True)
    weight = jnp.exp(score)
    total = weight + sums
    loss[...] = jnp.log(total) - score
    unit_grad = score_scale * ((weight / total - 1.0) * item + moment / total)
    along = jnp.sum(query * unit_grad, 1, keepdims=True)
    grad[...] = ((unit_grad - query * along) / query_norm).astype(bf16)


def queue_kernel(terms, count, told, negatives, _, *refs):
    blocks, (out,) = refs[:count], refs[count:]
    item, _ = unit_of(split_dot(told[...], blocks, terms))
    out[...] = jnp.where(told[...] >= 0, item, negatives[...].astype(f32)).astype(bf16)


def update_kernel(scale, side, mine, other, table, accum, _, table_out, accum_out, *unit):
    count = mine.shape[0]
    first = side[...] == 0
    for half, grad in enumerate(((mine, other), (other, mine))):
        place = pl.ds(half * count, count)
        rows = table[place, :]
        _, norm = unit_of(rows)
        grad = jnp.where(first, grad[0][...], grad[1][...]) * (scale / norm)
        moved = accum[place, :] + jnp.mean(grad * grad, 1, keepdims=True)
        accum_out[place, :] = moved
        rows = rows - learn_rate * grad / jnp.sqrt(moved)
        table_out[place, :] = rows
        if unit:
            unit[0][place, :], _ = unit_of(rows)


def call(kernel, outs, *args):
    vmem = pl.BlockSpec(memory_space=pltpu.VMEM)
    return pl.pallas_call(
        kernel,
        out_shape=[jax.ShapeDtypeStruct(shape, dtype) for shape, dtype in outs],
        in_specs=[vmem] * len(args),
        out_specs=[vmem] * len(outs),
        compiler_params=pltpu.CompilerParams(vmem_limit_bytes=20 * 2**20),
    )(*args)


def per_device(queries, item_owner, item_row, table, accum, fifo, fifo_head):
    step_count, query_count, width = queries.shape
    owners, copies = lax.axis_size("table"), lax.axis_size("batch")
    owned = table.shape[0]
    part_rows = owned // 2
    half_rows = owners * owned // 2
    queue_rows = fifo.shape[0]
    me = lax.axis_index("table")
    side = lax.axis_index("batch") % 2
    masks = masks_of(owners)
    small = owners * copies * queue_rows <= 1024
    most = owners * copies * (3 * query_count // owners)
    grad_scale = 1.0
    while most * grad_scale > 32768.0:
        grad_scale = grad_scale / 2

    def owner_place(owner):
        apart = jnp.bitwise_xor(owner, me)
        place = jnp.zeros_like(owner)
        for index, mask in enumerate(masks):
            place = place + jnp.where((apart & mask) != 0, 1 << index, 0)
        return place

    def place_whole(owner, row):
        return owner_place(owner) * owned + row

    def place_part(owner, row):
        return owner_place(owner) * owned + jnp.where(side == 0, row, (row + part_rows) % owned)

    def gather_whole(piece):
        pieces = [piece]
        for mask in masks:
            pieces = pieces + [flip(piece, mask) for piece in pieces]
        return pieces

    def reduce_near(kept):
        pieces = [kept[i * part_rows : (i + 1) * part_rows] for i in range(4)]
        near = [
            flip(piece.astype(f16), mask)
            for piece, mask in zip(pieces[1:], (owners, masks[0], owners + masks[0]))
        ]
        beside = [piece.astype(f32) for piece in near]
        return (pieces[0] + beside[0]) + (beside[1] + beside[2]), near[0][:8].astype(f32)

    def reduce_far(total):
        stages = stages_of(copies, 2)
        for stage in stages[1:]:
            total = sum_stage(total, *stage)
        sent = lax.optimization_barrier(total.astype(f16))
        if stages and stages[0][1] == 2:
            pairs = [[sent, flip(sent, 2 * owners)], [flip(sent, owners), flip(sent, 3 * owners)]]
        else:
            pairs = [[sent], [flip(sent, owners)]]
        return [sum(part.astype(f32) for part in pair) for pair in pairs]

    def next_queue(queue, early):
        if small:
            args = (told, queue, early, *parts)
            return call(functools.partial(queue_kernel, 3, len(parts)), [(queue.shape, bf16)], *args)[0]
        blocks = [split_parts(part, 3) for part in parts]
        new = lax.map(lambda at: pick_rows(at, blocks, width), told.reshape(-1, copies * queue_rows))
        return jnp.where(told >= 0, unit_of(new.reshape(queue.shape))[0].astype(bf16), queue)

    parts, terms = gather_whole(table), 3

    vmem, smem = pl.BlockSpec(memory_space=pltpu.VMEM), pl.BlockSpec(memory_space=pltpu.SMEM)
    blocks = pl.pallas_call(
        prologue_kernel,
        out_shape=jax.ShapeDtypeStruct((owners * copies, 2 * queue_rows, width), bf16),
        in_specs=[vmem, smem, smem, smem],
        out_specs=vmem,
    )(fifo, jnp.transpose(item_owner, (0, 2, 1)), item_row, fifo_head)
    blocks = lax.all_to_all(blocks, ("batch", "table"), 0, 0, tiled=True)
    queue = blocks[:, :queue_rows].reshape(-1, width)
    told = blocks[:, queue_rows:, :3].reshape(-1, 3).astype(jnp.int32)
    replaced = told[:, 0] >= 0
    told = jnp.where(replaced, place_whole(told[:, 0], told[:, 1] * 16 + told[:, 2]), -1)[:, None]

    accum = accum[:, None]
    loss_list, grad_list, joined = [], [], []
    for step in range(step_count):
        places = place_part(item_owner[step, :, 0], item_row[step])
        found_at = place_whole(item_owner[step, :, 0], item_row[step])
        last_place = owners * owned - parts[-1].shape[0]
        parts = [part.astype(f32) for part in parts]
        scalars, matrix = (query_count, 1), (query_count, width)
        if small:
            negatives = queue if step else jnp.zeros(scalars, f32)
        else:
            query_half = unit_of(queries[step].astype(f32))[0].astype(bf16)
            negatives, moment = score_rows(query_half, queue, jnp.ones(queue.shape[:1], jnp.bool_))
            negatives = negatives[:, None]
        query_unit, found, sums = call(
            functools.partial(first_kernel, terms, len(parts) - 1),
            [(matrix, f32), (matrix, f32), (scalars, f32)],
            queries[step],
            found_at[:, None],
            negatives,
            *parts[:-1],
        )
        sent, kept, unit = call(
            functools.partial(main_kernel, step, terms, last_place),
            [((half_rows, width), bf16), ((half_rows, width), f32), (matrix, f32)],
            found,
            parts[-1],
            found_at[:, None],
            places[None, :],
            query_unit,
            queue if small and step == 0 else sums,
        )
        joined.append(unit[:ENQ].astype(bf16))
        sent = (grad_scale * sent).astype(bf16)
        kept = grad_scale * kept
        for mask in masks[:0:-1]:
            kept = kept + flip(sent, mask).astype(f32)
            if mask != masks[1]:
                middle = kept.shape[0] // 2
                kept, sent = kept[:middle], kept[middle:].astype(f16)
        total, early = reduce_near(kept)

        loss, query_grad = call(
            functools.partial(late_kernel, not small),
            [(scalars, f32), (matrix, bf16)],
            queries[step],
            unit,
            queue if small else negatives,
            early,
            *([] if small else [moment]),
        )
        loss_list.append(loss[:, 0])
        grad_list.append(query_grad)
        if step == 0:
            queue = next_queue(queue, early)
        mine, other = reduce_far(total)
        more = step + 1 < step_count
        table, accum, *unit = call(
            functools.partial(update_kernel, score_scale / grad_scale),
            [(table.shape, f32), (accum.shape, f32)] + [(table.shape, f32)] * more,
            jnp.full((1, 1), side),
            mine,
            other,
            table,
            accum,
            queue[:16] if small and more else early,
        )
        if more:
            parts, terms = gather_whole(unit[0].astype(f16)), 2

    slots = jnp.arange(queue_rows, dtype=jnp.int32)
    fifo_out = fifo
    for step in range(step_count):
        place = (slots - fifo_head[0] - step * ENQ) % queue_rows
        for k in range(ENQ):
            fifo_out = jnp.where((place == k)[:, None], joined[step][k][None, :], fifo_out)
    return (jnp.stack(loss_list), jnp.stack(grad_list), table, accum[:, 0], fifo_out)


def solution(mesh):
    both = ("batch", "table")
    in_specs = (
        P(None, both, None),
        P(None, both, None),
        P(None, both),
        P("table", None),
        P("table"),
        P(both, None),
        P(both),
    )
    out_specs = (P(None, both), P(None, both, None), P("table", None), P("table"), P(both, None))
    return jax.shard_map(
        per_device, mesh=mesh, in_specs=in_specs, out_specs=out_specs, check_vma=False
    )
```

time: 83.9 us -> 76.3 us (0.909)
  Pallas kernels: 1.39 us -> 11.9 us
  matrix products: 8.97 us -> 0 us
  other arithmetic: 10.9 us -> 3.72 us
  starting transfers between devices: 22.8 us -> 26.9 us
  waiting for transfers between devices: 32.3 us -> 28.7 us
  local copies, waits for them, and re-layouts: 5.12 us -> 3.07 us
    pallas_call x0 -> x9, Pallas kernels: none -> 10.3 us  [call(): pl.pallas_call(kernel, out_shape=[jax.ShapeDtypeStruct(shape, dtype) for...]
    dot_general x16 -> x0, matrix products: 8.97 us -> none  [the longest x4 3.93 us: per_device(): lax.dot_general(chosen, across, (((0,), (0,)), ((), ())), preferred_eleme...]
    ppermute x4 -> x2, waiting for transfers between devices: 16 us -> 8.4 us  [turned(): found.append(lax.ppermute(piece, 'batch', pairs))]
    ppermute x15 -> x20, starting transfers between devices: 15.6 us -> 20.2 us  [flip(): lax.ppermute(piece, ('batch', 'table'), [(i ^ mask, i) for i in range(cou...]
    ppermute x15 -> x20, waiting for transfers between devices: 13.4 us -> 16.3 us  [flip(): lax.ppermute(piece, ('batch', 'table'), [(i ^ mask, i) for i in range(cou...]
    concatenate x5 -> x0, other arithmetic: 2.28 us -> none  [the longest x1 0.82 us: gather_whole(): piece = jnp.concatenate([piece, other])]
    reduce_sum x9 -> x0, other arithmetic: 2.09 us -> none  [the longest x5 0.86 us: norm_of(): return jnp.sqrt(jnp.sum(rows * rows, 1) + epsilon)]
    convert_element_type x10 -> x9, other arithmetic: 2.23 us -> 0.16 us  [the longest x4 0.09 us: per_device(): parts = [part.astype(f32) for part in parts]]
  transfers between devices with their start and end apart: 20 -> 23, of which waited for: 17 -> 16; matrix products, arithmetic and copies ran while one was open for 14% -> 4% of each run, Pallas kernels for 2% -> 10%
where the time goes in v4:
time: 76.3 us; the launch traced here: 75.9 us
  waiting for transfers between devices  28.7 us (38%)
  starting transfers between devices  26.9 us (35%)
  Pallas kernels  11.9 us (16%)
  other arithmetic  3.72 us (5%)
  local copies, waits for them, and re-layouts  3.07 us (4%)
  between operations  1.63 us (2%)
    ppermute x20, starting transfers between devices, flip(): lax.ppermute(piece, ('batch', 'table'), [(i ^ mask, i) for i in range(cou...  20.2 us
    ppermute x20, waiting for transfers between devices, flip(): lax.ppermute(piece, ('batch', 'table'), [(i ^ mask, i) for i in range(cou...  16.3 us
    pallas_call x9, Pallas kernels, call(): pl.pallas_call(kernel, out_shape=[jax.ShapeDtypeStruct(shape, dtype) for...  10.3 us
    ppermute x2, waiting for transfers between devices, turned(): found.append(lax.ppermute(piece, 'batch', pairs))  8.4 us
    all_to_all x1, starting transfers between devices, per_device(): blocks = lax.all_to_all(blocks, ('batch', 'table'), 0, 0, tiled=True)  5.03 us
    all_to_all x1, waiting for transfers between devices, per_device(): blocks = lax.all_to_all(blocks, ('batch', 'table'), 0, 0, tiled=True)  4.04 us
    unnamed x12, local copies, waits for them, and re-layouts  2.51 us
    ppermute x2, starting transfers between devices, turned(): found.append(lax.ppermute(piece, 'batch', pairs))  1.67 us
  transfers between devices with their start and end apart: 23, of which 16 were waited for; matrix products, arithmetic and copies ran while one was open for 4% of the time, Pallas kernels for 10%

profile of v4, /device:TPU:0, one launch (start us, length us, event | category | flops | bytes accessed | tf_op | source)
XLA Modules:
  0.0 75.9 jit_solution(16453697625559579662)
XLA Ops:
  0.6 3.0 %collective-permute-start = (f32[480,128]{1,0:T(8,128)}, f32[480,128]{1,0:T(8,128)S(1)}, u32[]{:S(2)}, u32[]{:S(2)}) collective-permute-start(f32[480,128]{1,0:T(8,128)} %table.1), channel_id=1, source_target_pairs={{2,0},{3,1},{0,2},{1,3},{6,4},{7,5},{4,6},{5,7},{10,8},{11,9},{8,1... | collective-permute-start | bytes 737288 | tf_op jit(solution)/shard_map/ppermute | solution.py:39
  4.3 1.6 %shard_map.111 = bf16[32,16,128]{2,1,0:T(8,128)(2,1)} custom-call(bf16[8,128]{1,0:T(8,128)(2,1)} %fifo.1, s32[2,1,512]{2,1,0:T(1,128)} %bitcast.53, s32[2,512]{1,0:T(2,128)} %row.1, s32[1]{0:T(128)} %copy.22.head), custom_call_target="tpu_custom_call" | custom-call | tf_op jit(solution)/shard_map/pallas_call | solution.py:310
  5.9 5.0 %all-to-all-start = ((bf16[32,16,128]{2,1,0:T(8,128)(2,1)}), bf16[32,16,128]{2,1,0:T(8,128)(2,1)S(1)}, u32[]{:S(2)}, u32[]{:S(2)}) async-start(bf16[32,16,128]{2,1,0:T(8,128)(2,1)} %shard_map.111), calls=%async_computation | async-start | bytes 262144 | tf_op jit(solution)/shard_map/all_to_all | solution.py:316
  13.0 2.1 %shard_map.110 = (f32[512,128]{1,0:T(8,128)S(1)}, f32[512,128]{1,0:T(8,128)S(1)}, f32[512,1]{1,0:T(8,128)}) custom-call(bf16[512,128]{1,0:T(8,128)(2,1)S(1)} %get-tuple-element.55.queries, s32[512,1]{1,0:T(8,128)S(1)} %copy.17.places, f32[512,1]{1,0:T(8,128)S(1)} %broadcast_in_dim.160.negatives, f32[480,128]{1,0:T(8,128)S(1)} %copy-done, ...), custom_call_target="tpu_custom_call" | custom-call | tf_op jit(solution)/shard_map/pallas_call | solution.py:235
  15.2 4.0 %all-to-all-done = bf16[32,16,128]{2,1,0:T(8,128)(2,1)S(1)} async-done(((bf16[32,16,128]{2,1,0:T(8,128)(2,1)}), bf16[32,16,128]{2,1,0:T(8,128)(2,1)S(1)}, u32[]{:S(2)}, u32[]{:S(2)}) %all-to-all-start) | async-done | bytes 131104 | tf_op jit(solution)/shard_map/all_to_all | solution.py:316
  19.2 1.6 %shard_map.112 = (bf16[960,128]{1,0:T(8,128)(2,1)S(1)}, f32[960,128]{1,0:T(8,128)S(1)}, f32[512,128]{1,0:T(8,128)S(1)}) custom-call(f32[512,128]{1,0:T(8,128)S(1)} %get-tuple-element.25.found, f32[480,128]{1,0:T(8,128)S(1)} %collective-permute-done.2.block.refs_3_, s32[512,1]{1,0:T(8,128)S(1)} %copy.17.places, s32[1,512]{1,0:T(1,128)S(1)} %get-tuple-element.53.line, ...), custom_call_target="tpu_custom_call" | custom-call | tf_op jit(solution)/shard_map/pallas_call | solution.py:235
  24.0 2.0 %collective-permute-start.6 = (f16[240,128]{1,0:T(8,128)(2,1)S(1)}, f16[240,128]{1,0:T(8,128)(2,1)S(1)}, u32[]{:S(2)}, u32[]{:S(2)}) collective-permute-start(f16[240,128]{1,0:T(8,128)(2,1)S(1)} %get-tuple-element.61), channel_id=1, source_target_pairs={{6,0},{7,1},{4,2},{5,3},{2,4},{3,5},{0,6},{1,7},{14,8},{15,9},{12,... | collective-permute-start | bytes 184328 | tf_op jit(solution)/shard_map/ppermute | solution.py:39
  28.0 1.2 %collective-permute-done.6 = f16[240,128]{1,0:T(8,128)(2,1)S(1)} collective-permute-done((f16[240,128]{1,0:T(8,128)(2,1)S(1)}, f16[240,128]{1,0:T(8,128)(2,1)S(1)}, u32[]{:S(2)}, u32[]{:S(2)}) %collective-permute-start.6) | collective-permute-done | bytes 61472 | tf_op jit(solution)/shard_map/ppermute | solution.py:39
  30.1 4.9 %collective-permute-done.7 = f16[240,128]{1,0:T(8,128)(2,1)S(1)} collective-permute-done((f16[240,128]{1,0:T(8,128)(2,1)S(1)}, f16[240,128]{1,0:T(8,128)(2,1)S(1)}, u32[]{:S(2)}, u32[]{:S(2)}) %collective-permute-start.7) | collective-permute-done | bytes 61472 | tf_op jit(solution)/shard_map/ppermute | solution.py:50
  36.4 2.4 %collective-permute-start.10 = (f16[240,128]{1,0:T(8,128)(2,1)S(1)}, f16[240,128]{1,0:T(8,128)(2,1)S(1)}, u32[]{:S(2)}, u32[]{:S(2)}) collective-permute-start(f16[240,128]{1,0:T(8,128)(2,1)S(1)} %add_convert_fusion.1), channel_id=1, source_target_pairs={{12,0},{13,1},{14,2},{15,3},{8,4},{9,5},{10,6},{11,7},{4,8},{5,9},... | collective-permute-start | bytes 184328 | tf_op jit(solution)/shard_map/ppermute | solution.py:39
  39.9 1.7 %collective-permute-done.10 = f16[240,128]{1,0:T(8,128)(2,1)S(1)} collective-permute-done((f16[240,128]{1,0:T(8,128)(2,1)S(1)}, f16[240,128]{1,0:T(8,128)(2,1)S(1)}, u32[]{:S(2)}, u32[]{:S(2)}) %collective-permute-start.10) | collective-permute-done | bytes 61472 | tf_op jit(solution)/shard_map/ppermute | solution.py:39
  41.6 1.5 %collective-permute-done.9 = f16[240,128]{1,0:T(8,128)(2,1)S(1)} collective-permute-done((f16[240,128]{1,0:T(8,128)(2,1)S(1)}, f16[240,128]{1,0:T(8,128)(2,1)S(1)}, u32[]{:S(2)}, u32[]{:S(2)}) %collective-permute-start.9) | collective-permute-done | bytes 61472 | tf_op jit(solution)/shard_map/ppermute | solution.py:39
  43.8 1.7 %collective-permute-start.11 = (f16[480,128]{1,0:T(8,128)(2,1)S(1)}, f16[480,128]{1,0:T(8,128)(2,1)S(1)}, u32[]{:S(2)}, u32[]{:S(2)}) collective-permute-start(f16[480,128]{1,0:T(8,128)(2,1)S(1)} %get-tuple-element.50), channel_id=1, source_target_pairs={{2,0},{3,1},{0,2},{1,3},{6,4},{7,5},{4,6},{5,7},{10,8},{11,9},{8,1... | collective-permute-start | bytes 368648 | tf_op jit(solution)/shard_map/ppermute | solution.py:39
  45.5 3.2 %collective-permute-done.11 = f16[480,128]{1,0:T(8,128)(2,1)S(1)} collective-permute-done((f16[480,128]{1,0:T(8,128)(2,1)S(1)}, f16[480,128]{1,0:T(8,128)(2,1)S(1)}, u32[]{:S(2)}, u32[]{:S(2)}) %collective-permute-start.11) | collective-permute-done | bytes 122912 | tf_op jit(solution)/shard_map/ppermute | solution.py:39
  49.0 1.2 %shard_map.116 = (f32[512,128]{1,0:T(8,128)S(1)}, f32[512,128]{1,0:T(8,128)S(1)}, f32[512,1]{1,0:T(8,128)S(1)}) custom-call(bf16[512,128]{1,0:T(8,128)(2,1)S(1)} %get-tuple-element.56.queries, s32[512,1]{1,0:T(8,128)S(1)} %copy.20.places, bf16[256,128]{1,0:T(8,128)(2,1)S(1)} %shard_map.114.negatives, f32[480,128]{1,0:T(8,128)S(1)} %get-tuple-element.49.refs_0_, ...), custom_call_target="tpu_custom_call" | custom-call | tf_op jit(solution)/shard_map/pallas_call | solution.py:235
  50.2 1.2 %shard_map.117 = (bf16[960,128]{1,0:T(8,128)(2,1)S(1)}, f32[960,128]{1,0:T(8,128)S(1)}, f32[512,128]{1,0:T(8,128)S(1)}) custom-call(f32[512,128]{1,0:T(8,128)S(1)} %get-tuple-element.32.found, f32[480,128]{1,0:T(8,128)S(1)} %convert_element_type.126.block, s32[512,1]{1,0:T(8,128)S(1)} %copy.20.places, s32[1,512]{1,0:T(1,128)S(1)} %get-tuple-element.71.line, ...), custom_call_target="tpu_custom_call" | custom-call | tf_op jit(solution)/shard_map/pallas_call | solution.py:235
  54.4 1.2 %collective-permute-start.16 = (f16[240,128]{1,0:T(8,128)(2,1)S(1)}, f16[240,128]{1,0:T(8,128)(2,1)S(1)}, u32[]{:S(2)}, u32[]{:S(2)}) collective-permute-start(f16[240,128]{1,0:T(8,128)(2,1)S(1)} %get-tuple-element.57), channel_id=1, source_target_pairs={{2,0},{3,1},{0,2},{1,3},{6,4},{7,5},{4,6},{5,7},{10,8},{11,9},{8,1... | collective-permute-start | bytes 184328 | tf_op jit(solution)/shard_map/ppermute | solution.py:39
  55.6 1.2 %collective-permute-start.17 = (f16[240,128]{1,0:T(8,128)(2,1)S(1)}, f16[240,128]{1,0:T(8,128)(2,1)S(1)}, u32[]{:S(2)}, u32[]{:S(2)}) collective-permute-start(f16[240,128]{1,0:T(8,128)(2,1)S(1)} %get-tuple-element.58), channel_id=1, source_target_pairs={{6,0},{7,1},{4,2},{5,3},{2,4},{3,5},{0,6},{1,7},{14,8},{15,9},{12,... | collective-permute-start | bytes 184328 | tf_op jit(solution)/shard_map/ppermute | solution.py:39
  58.6 2.1 %collective-permute-done.17 = f16[240,128]{1,0:T(8,128)(2,1)S(1)} collective-permute-done((f16[240,128]{1,0:T(8,128)(2,1)S(1)}, f16[240,128]{1,0:T(8,128)(2,1)S(1)}, u32[]{:S(2)}, u32[]{:S(2)}) %collective-permute-start.17) | collective-permute-done | bytes 61472 | tf_op jit(solution)/shard_map/ppermute | solution.py:39
  63.1 3.5 %collective-permute-done.18 = f16[240,128]{1,0:T(8,128)(2,1)S(1)} collective-permute-done((f16[240,128]{1,0:T(8,128)(2,1)S(1)}, f16[240,128]{1,0:T(8,128)(2,1)S(1)}, u32[]{:S(2)}, u32[]{:S(2)}) %collective-permute-start.18) | collective-permute-done | bytes 61472 | tf_op jit(solution)/shard_map/ppermute | solution.py:50
  67.5 1.3 %collective-permute-start.20 = (f16[240,128]{1,0:T(8,128)(2,1)S(1)}, f16[240,128]{1,0:T(8,128)(2,1)S(1)}, u32[]{:S(2)}, u32[]{:S(2)}) collective-permute-start(f16[240,128]{1,0:T(8,128)(2,1)S(1)} %add_convert_fusion), channel_id=1, source_target_pairs={{4,0},{5,1},{6,2},{7,3},{0,4},{1,5},{2,6},{3,7},{12,8},{13,9},{14,... | collective-permute-start | bytes 184328 | tf_op jit(solution)/shard_map/ppermute | solution.py:39
  68.9 1.9 %collective-permute-start.21 = (f16[240,128]{1,0:T(8,128)(2,1)S(1)}, f16[240,128]{1,0:T(8,128)(2,1)S(1)}, u32[]{:S(2)}, u32[]{:S(2)}) collective-permute-start(f16[240,128]{1,0:T(8,128)(2,1)S(1)} %add_convert_fusion), channel_id=1, source_target_pairs={{12,0},{13,1},{14,2},{15,3},{8,4},{9,5},{10,6},{11,7},{4,8},{5,9},... | collective-permute-start | bytes 184328 | tf_op jit(solution)/shard_map/ppermute | solution.py:39
  71.8 2.2 %collective-permute-done.21 = f16[240,128]{1,0:T(8,128)(2,1)S(1)} collective-permute-done((f16[240,128]{1,0:T(8,128)(2,1)S(1)}, f16[240,128]{1,0:T(8,128)(2,1)S(1)}, u32[]{:S(2)}, u32[]{:S(2)}) %collective-permute-start.21) | collective-permute-done | bytes 61472 | tf_op jit(solution)/shard_map/ppermute | solution.py:39
  74.0 1.2 %shard_map.119 = (f32[480,128]{1,0:T(8,128)}, f32[480,1]{1,0:T(8,128)S(1)}) custom-call(s32[1,1]{1,0:T(1,128)} %bitcast.11.side, f32[240,128]{1,0:T(8,128)S(1)} %convert_add_fusion.3.mine, f32[240,128]{1,0:T(8,128)S(1)} %convert_add_fusion.2.other, f32[480,128]{1,0:T(8,128)S(1)} %get-tuple-element.41.table, f32[480,1]{1,0:T(8,128)S(1)} %get-tuple-element.42.accum, ...), custom_call_target="tpu_custom_call" | custom-call | tf_op jit(solution)/shard_map/pallas_call | solution.py:235
  (86 shorter events, 21.2 us)
Async XLA Ops:
  0.6 10.3 %copy-start.1 = (bf16[2,512,128]{2,1,0:T(8,128)(2,1)S(1)}, bf16[2,512,128]{2,1,0:T(8,128)(2,1)}, u32[]{:S(2)}) copy-start(bf16[2,512,128]{2,1,0:T(8,128)(2,1)} %param.7) | copy-start | bytes 786436
  0.6 11.1 %collective-permute-start = (f32[480,128]{1,0:T(8,128)}, f32[480,128]{1,0:T(8,128)S(1)}, u32[]{:S(2)}, u32[]{:S(2)}) collective-permute-start(f32[480,128]{1,0:T(8,128)} %table.1), channel_id=1, source_target_pairs={{2,0},{3,1},{0,2},{1,3},{6,4},{7,5},{4,6},{5,7},{10,8},{11,9},{8,1... | collective-permute-start | bytes 737288 | tf_op jit(solution)/shard_map/ppermute | solution.py:39
  3.6 8.6 %collective-permute-start.1 = (f32[480,128]{1,0:T(8,128)}, f32[480,128]{1,0:T(8,128)S(1)}, u32[]{:S(2)}, u32[]{:S(2)}) collective-permute-start(f32[480,128]{1,0:T(8,128)} %table.1), channel_id=1, source_target_pairs={{1,0},{0,1},{3,2},{2,3},{5,4},{4,5},{7,6},{6,7},{9,8},{8,9},{11,10... | collective-permute-start | bytes 737288 | tf_op jit(solution)/shard_map/ppermute | solution.py:39
  5.9 13.3 %all-to-all-start = ((bf16[32,16,128]{2,1,0:T(8,128)(2,1)}), bf16[32,16,128]{2,1,0:T(8,128)(2,1)S(1)}, u32[]{:S(2)}, u32[]{:S(2)}) async-start(bf16[32,16,128]{2,1,0:T(8,128)(2,1)} %shard_map.111), calls=%async_computation | async-start | bytes 262144 | tf_op jit(solution)/shard_map/all_to_all | solution.py:316
  11.8 7.4 %collective-permute-start.2 = (f32[480,128]{1,0:T(8,128)S(1)}, f32[480,128]{1,0:T(8,128)S(1)}, u32[]{:S(2)}, u32[]{:S(2)}) collective-permute-start(f32[480,128]{1,0:T(8,128)S(1)} %collective-permute-done.refs_1_), channel_id=1, source_target_pairs={{1,0},{0,1},{3,2},{2,3},{5,4},{4,5},{7,6},{6,7},{9,8},{8,9},{11,10... | collective-permute-start | bytes 737288 | tf_op jit(solution)/shard_map/ppermute | solution.py:39
  20.8 1.6 %collective-permute-start.3 = (bf16[960,128]{1,0:T(8,128)(2,1)S(1)}, bf16[960,128]{1,0:T(8,128)(2,1)S(1)}, u32[]{:S(2)}, u32[]{:S(2)}) collective-permute-start(bf16[960,128]{1,0:T(8,128)(2,1)S(1)} %get-tuple-element.29), channel_id=1, source_target_pairs={{1,0},{0,1},{3,2},{2,3},{5,4},{4,5},{7,6},{6,7},{9,8},{8,9},{11,10... | collective-permute-start | bytes 737288 | tf_op jit(solution)/shard_map/ppermute | solution.py:39
  22.5 4.3 %collective-permute-start.4 = (f16[240,128]{1,0:T(8,128)(2,1)S(1)}, f16[240,128]{1,0:T(8,128)(2,1)S(1)}, u32[]{:S(2)}, u32[]{:S(2)}) collective-permute-start(f16[240,128]{1,0:T(8,128)(2,1)S(1)} %get-tuple-element.62), channel_id=1, source_target_pairs={{4,0},{5,1},{6,2},{7,3},{0,4},{1,5},{2,6},{3,7},{12,8},{13,9},{14,... | collective-permute-start | bytes 184328 | tf_op jit(solution)/shard_map/ppermute | solution.py:39
  23.2 4.7 %collective-permute-start.5 = (f16[240,128]{1,0:T(8,128)(2,1)S(1)}, f16[240,128]{1,0:T(8,128)(2,1)S(1)}, u32[]{:S(2)}, u32[]{:S(2)}) collective-permute-start(f16[240,128]{1,0:T(8,128)(2,1)S(1)} %get-tuple-element.60), channel_id=1, source_target_pairs={{2,0},{3,1},{0,2},{1,3},{6,4},{7,5},{4,6},{5,7},{10,8},{11,9},{8,1... | collective-permute-start | bytes 184328 | tf_op jit(solution)/shard_map/ppermute | solution.py:39
  24.0 5.2 %collective-permute-start.6 = (f16[240,128]{1,0:T(8,128)(2,1)S(1)}, f16[240,128]{1,0:T(8,128)(2,1)S(1)}, u32[]{:S(2)}, u32[]{:S(2)}) collective-permute-start(f16[240,128]{1,0:T(8,128)(2,1)S(1)} %get-tuple-element.61), channel_id=1, source_target_pairs={{6,0},{7,1},{4,2},{5,3},{2,4},{3,5},{0,6},{1,7},{14,8},{15,9},{12,... | collective-permute-start | bytes 184328 | tf_op jit(solution)/shard_map/ppermute | solution.py:39
  29.2 5.8 %collective-permute-start.7 = (f16[240,128]{1,0:T(8,128)(2,1)S(1)}, f16[240,128]{1,0:T(8,128)(2,1)S(1)}, u32[]{:S(2)}, u32[]{:S(2)}) collective-permute-start(f16[240,128]{1,0:T(8,128)(2,1)S(1)} %fusion.5), channel_id=1, source_target_pairs={{16,0},{20,4},{24,8},{28,12},{0,16},{4,20},{8,24},{12,28},{17,1},{... | collective-permute-start | bytes 184328 | tf_op jit(solution)/shard_map/ppermute | solution.py:50
  35.1 4.8 %collective-permute-start.8 = (f16[240,128]{1,0:T(8,128)(2,1)S(1)}, f16[240,128]{1,0:T(8,128)(2,1)S(1)}, u32[]{:S(2)}, u32[]{:S(2)}) collective-permute-start(f16[240,128]{1,0:T(8,128)(2,1)S(1)} %add_convert_fusion.1), channel_id=1, source_target_pairs={{8,0},{9,1},{10,2},{11,3},{12,4},{13,5},{14,6},{15,7},{0,8},{1,9},... | collective-permute-start | bytes 184328 | tf_op jit(solution)/shard_map/ppermute | solution.py:39
  36.4 5.2 %collective-permute-start.10 = (f16[240,128]{1,0:T(8,128)(2,1)S(1)}, f16[240,128]{1,0:T(8,128)(2,1)S(1)}, u32[]{:S(2)}, u32[]{:S(2)}) collective-permute-start(f16[240,128]{1,0:T(8,128)(2,1)S(1)} %add_convert_fusion.1), channel_id=1, source_target_pairs={{12,0},{13,1},{14,2},{15,3},{8,4},{9,5},{10,6},{11,7},{4,8},{5,9},... | collective-permute-start | bytes 184328 | tf_op jit(solution)/shard_map/ppermute | solution.py:39
  38.8 4.2 %collective-permute-start.9 = (f16[240,128]{1,0:T(8,128)(2,1)S(1)}, f16[240,128]{1,0:T(8,128)(2,1)S(1)}, u32[]{:S(2)}, u32[]{:S(2)}) collective-permute-start(f16[240,128]{1,0:T(8,128)(2,1)S(1)} %add_convert_fusion.1), channel_id=1, source_target_pairs={{4,0},{5,1},{6,2},{7,3},{0,4},{1,5},{2,6},{3,7},{12,8},{13,9},{14,... | collective-permute-start | bytes 184328 | tf_op jit(solution)/shard_map/ppermute | solution.py:39
  43.8 4.9 %collective-permute-start.11 = (f16[480,128]{1,0:T(8,128)(2,1)S(1)}, f16[480,128]{1,0:T(8,128)(2,1)S(1)}, u32[]{:S(2)}, u32[]{:S(2)}) collective-permute-start(f16[480,128]{1,0:T(8,128)(2,1)S(1)} %get-tuple-element.50), channel_id=1, source_target_pairs={{2,0},{3,1},{0,2},{1,3},{6,4},{7,5},{4,6},{5,7},{10,8},{11,9},{8,1... | collective-permute-start | bytes 368648 | tf_op jit(solution)/shard_map/ppermute | solution.py:39
  45.4 3.5 %collective-permute-start.12 = (f16[480,128]{1,0:T(8,128)(2,1)S(1)}, f16[480,128]{1,0:T(8,128)(2,1)S(1)}, u32[]{:S(2)}, u32[]{:S(2)}) collective-permute-start(f16[480,128]{1,0:T(8,128)(2,1)S(1)} %get-tuple-element.50), channel_id=1, source_target_pairs={{1,0},{0,1},{3,2},{2,3},{5,4},{4,5},{7,6},{6,7},{9,8},{8,9},{11,10... | collective-permute-start | bytes 368648 | tf_op jit(solution)/shard_map/ppermute | solution.py:39
  48.7 1.4 %collective-permute-start.13 = (f16[480,128]{1,0:T(8,128)(2,1)S(1)}, f16[480,128]{1,0:T(8,128)(2,1)S(1)}, u32[]{:S(2)}, u32[]{:S(2)}) collective-permute-start(f16[480,128]{1,0:T(8,128)(2,1)S(1)} %collective-permute-done.11), channel_id=1, source_target_pairs={{1,0},{0,1},{3,2},{2,3},{5,4},{4,5},{7,6},{6,7},{9,8},{8,9},{11,10... | collective-permute-start | bytes 368648 | tf_op jit(solution)/shard_map/ppermute | solution.py:39
  51.4 1.7 %collective-permute-start.14 = (bf16[960,128]{1,0:T(8,128)(2,1)S(1)}, bf16[960,128]{1,0:T(8,128)(2,1)S(1)}, u32[]{:S(2)}, u32[]{:S(2)}) collective-permute-start(bf16[960,128]{1,0:T(8,128)(2,1)S(1)} %get-tuple-element.37), channel_id=1, source_target_pairs={{1,0},{0,1},{3,2},{2,3},{5,4},{4,5},{7,6},{6,7},{9,8},{8,9},{11,10... | collective-permute-start | bytes 737288 | tf_op jit(solution)/shard_map/ppermute | solution.py:39
  53.3 4.9 %collective-permute-start.15 = (f16[240,128]{1,0:T(8,128)(2,1)S(1)}, f16[240,128]{1,0:T(8,128)(2,1)S(1)}, u32[]{:S(2)}, u32[]{:S(2)}) collective-permute-start(f16[240,128]{1,0:T(8,128)(2,1)S(1)} %get-tuple-element.59), channel_id=1, source_target_pairs={{4,0},{5,1},{6,2},{7,3},{0,4},{1,5},{2,6},{3,7},{12,8},{13,9},{14,... | collective-permute-start | bytes 184328 | tf_op jit(solution)/shard_map/ppermute | solution.py:39
  54.4 4.2 %collective-permute-start.16 = (f16[240,128]{1,0:T(8,128)(2,1)S(1)}, f16[240,128]{1,0:T(8,128)(2,1)S(1)}, u32[]{:S(2)}, u32[]{:S(2)}) collective-permute-start(f16[240,128]{1,0:T(8,128)(2,1)S(1)} %get-tuple-element.57), channel_id=1, source_target_pairs={{2,0},{3,1},{0,2},{1,3},{6,4},{7,5},{4,6},{5,7},{10,8},{11,9},{8,1... | collective-permute-start | bytes 184328 | tf_op jit(solution)/shard_map/ppermute | solution.py:39
  55.6 5.1 %collective-permute-start.17 = (f16[240,128]{1,0:T(8,128)(2,1)S(1)}, f16[240,128]{1,0:T(8,128)(2,1)S(1)}, u32[]{:S(2)}, u32[]{:S(2)}) collective-permute-start(f16[240,128]{1,0:T(8,128)(2,1)S(1)} %get-tuple-element.58), channel_id=1, source_target_pairs={{6,0},{7,1},{4,2},{5,3},{2,4},{3,5},{0,6},{1,7},{14,8},{15,9},{12,... | collective-permute-start | bytes 184328 | tf_op jit(solution)/shard_map/ppermute | solution.py:39
  60.8 5.8 %collective-permute-start.18 = (f16[240,128]{1,0:T(8,128)(2,1)S(1)}, f16[240,128]{1,0:T(8,128)(2,1)S(1)}, u32[]{:S(2)}, u32[]{:S(2)}) collective-permute-start(f16[240,128]{1,0:T(8,128)(2,1)S(1)} %fusion.3), channel_id=1, source_target_pairs={{16,0},{20,4},{24,8},{28,12},{0,16},{4,20},{8,24},{12,28},{17,1},{... | collective-permute-start | bytes 184328 | tf_op jit(solution)/shard_map/ppermute | solution.py:50
  66.6 4.3 %collective-permute-start.19 = (f16[240,128]{1,0:T(8,128)(2,1)S(1)}, f16[240,128]{1,0:T(8,128)(2,1)S(1)}, u32[]{:S(2)}, u32[]{:S(2)}) collective-permute-start(f16[240,128]{1,0:T(8,128)(2,1)S(1)} %add_convert_fusion), channel_id=1, source_target_pairs={{8,0},{9,1},{10,2},{11,3},{12,4},{13,5},{14,6},{15,7},{0,8},{1,9},... | collective-permute-start | bytes 184328 | tf_op jit(solution)/shard_map/ppermute | solution.py:39
  67.5 4.2 %collective-permute-start.20 = (f16[240,128]{1,0:T(8,128)(2,1)S(1)}, f16[240,128]{1,0:T(8,128)(2,1)S(1)}, u32[]{:S(2)}, u32[]{:S(2)}) collective-permute-start(f16[240,128]{1,0:T(8,128)(2,1)S(1)} %add_convert_fusion), channel_id=1, source_target_pairs={{4,0},{5,1},{6,2},{7,3},{0,4},{1,5},{2,6},{3,7},{12,8},{13,9},{14,... | collective-permute-start | bytes 184328 | tf_op jit(solution)/shard_map/ppermute | solution.py:39
  68.9 5.1 %collective-permute-start.21 = (f16[240,128]{1,0:T(8,128)(2,1)S(1)}, f16[240,128]{1,0:T(8,128)(2,1)S(1)}, u32[]{:S(2)}, u32[]{:S(2)}) collective-permute-start(f16[240,128]{1,0:T(8,128)(2,1)S(1)} %add_convert_fusion), channel_id=1, source_target_pairs={{12,0},{13,1},{14,2},{15,3},{8,4},{9,5},{10,6},{11,7},{4,8},{5,9},... | collective-permute-start | bytes 184328 | tf_op jit(solution)/shard_map/ppermute | solution.py:39
  (5 other events, 3.7 us)

commit v5 on v4

v5 whole, which is shorter than its diff:
```python
import functools

import jax
import jax.numpy as jnp
from jax import lax
from jax.experimental import pallas as pl
from jax.experimental.pallas import tpu as pltpu
from jax.sharding import PartitionSpec as P

ENQ = 4
score_scale = 10.0
learn_rate = 0.3
epsilon = 1e-06
f32 = jnp.float32
bf16 = jnp.bfloat16
f16 = jnp.float16
VMEM = 10 * 2**20


def masks_of(count):
    masks = []
    while count > 1:
        assert count % 2 == 0
        count //= 2
        masks.append(count)
    return masks


def stages_of(count, stride):
    stages, count = [], count // stride
    while count > 1:
        radix = next(r for r in range(2, count + 1) if count % r == 0)
        stages.append((stride, radix))
        stride, count = stride * radix, count // radix
    return stages


def flip(piece, mask):
    count = lax.axis_size("batch") * lax.axis_size("table")
    return lax.ppermute(piece, ("batch", "table"), [(i ^ mask, i) for i in range(count)])


def turned(piece, stride, radix):
    count = lax.axis_size("batch")
    found = []
    for turn in range(1, radix):
        pairs = []
        for target in range(count):
            digit = target // stride % radix
            pairs.append((target + ((digit + turn) % radix - digit) * stride, target))
        found.append(lax.ppermute(piece, "batch", pairs))
    return found


def sum_stage(total, stride, radix, zero=0.0):
    sent = lax.optimization_barrier(total.astype(f16))
    parts = jnp.stack([sent] + turned(sent, stride, radix)) if radix > 2 else None
    if radix > 2:
        digit = lax.axis_index("batch") // stride % radix
        parts = list(parts[(jnp.arange(radix, dtype=jnp.int32) - digit) % radix])
    else:
        parts = [sent] + turned(sent, stride, radix)
    total = parts[0].astype(f32) + zero
    for part in parts[1:]:
        total = total + part.astype(f32)
    return total


def split_parts(rows, terms):
    parts = []
    for _ in range(terms):
        part = lax.reduce_precision(rows, 8, 7)
        parts.append(part.astype(bf16))
        rows = rows - part
    return jnp.concatenate(parts, 1)


def pick_rows(places, blocks, width):
    total, first = None, 0
    for block in blocks:
        count = block.shape[0]
        chosen = (places[:, None] - first == jnp.arange(count, dtype=jnp.int32)[None, :]).astype(bf16)
        found = jnp.dot(chosen, block, preferred_element_type=f32)
        rows = found[:, :width]
        for start in range(width, block.shape[1], width):
            rows = rows + found[:, start : start + width]
        total = rows if total is None else total + rows
        first += count
    return total


def score_piece(query_half, carried, rows, kept):
    total_sum, moment = carried
    scores = score_scale * lax.dot_general(
        query_half, rows, (((1,), (1,)), ((), ())), preferred_element_type=f32
    )
    weights = jnp.where(kept[None, :], jnp.exp(scores), 0.0)
    moment = moment + jnp.dot(weights.astype(bf16), rows, preferred_element_type=f32)
    return (total_sum + jnp.sum(weights, 1), moment)


def score_rows(query_half, rows, kept):
    count, width = rows.shape
    carried = (jnp.zeros(query_half.shape[:1], f32), jnp.zeros(query_half.shape, f32))
    splits = 1
    while count // splits > 1024 and count % (splits * 2) == 0:
        splits = splits * 2
    if splits == 1:
        return score_piece(query_half, carried, rows, kept)
    stacked = (rows.reshape(splits, -1, width), kept.reshape(splits, -1))
    return lax.scan(lambda c, b: (score_piece(query_half, c, *b), None), carried, stacked)[0]


def norm_of(rows):
    return jnp.sqrt(jnp.sum(rows * rows, 1) + epsilon)


def one_hot(places, first, count, columns):
    shape = (places.shape[0], count) if columns else (count, places.shape[1])
    numbers = lax.broadcasted_iota(jnp.int32, shape, 1 if columns else 0)
    return (numbers == places - first).astype(f32).astype(bf16)


def column(line):
    count = line.shape[1]
    tall = jnp.broadcast_to(line, (128, count))
    return jnp.transpose(jnp.pad(tall, ((0, 0), (0, -count % 128))))[:count, :1]


def split_dot(places, blocks, first=0):
    found = 0.0
    for block in blocks:
        count, width = block.shape
        chosen = one_hot(places, first, count, True)
        first += count
        rows = block[...]
        high = rows.astype(bf16)
        low = (rows - high.astype(f32)).astype(bf16)
        both = jnp.concatenate([high, low], 1)
        found = found + jnp.dot(chosen, both, preferred_element_type=f32)
    return found[:, :width] + found[:, width:]


def unit_of(rows):
    norm = jnp.sqrt(jnp.sum(rows * rows, 1, keepdims=True) + epsilon)
    return rows / norm, norm


def weights_of(unit, negatives):
    scores = lax.dot_general(
        unit.astype(bf16), negatives, (((1,), (1,)), ((), ())), preferred_element_type=f32
    )
    return jnp.exp(score_scale * scores)


def told_block(device, owner, row, head, queue_rows, width):
    line = lax.broadcasted_iota(jnp.int32, (queue_rows, width), 0)
    lane = lax.broadcasted_iota(jnp.int32, (queue_rows, width), 1)
    part = jnp.where(lane // 4 == device[...], lane % 4, -1)
    told = jnp.zeros((queue_rows, width), jnp.int32)
    for k in range(ENQ):
        item, number = owner[0, :, k : k + 1], row[0:1, k : k + 1]
        values = jnp.where(part == 0, item + 1, jnp.where(part == 1, number // 16, number % 16))
        values = jnp.where((part >= 0) & (part < 3), values, 0)
        told = jnp.where(line == lax.rem(head[...] + k, queue_rows), values, told)
    return told.astype(f32)


def first_kernel(step, count, scalars, queries, line, negatives, *refs):
    ids, blocks, (unit, found, sums, *told) = refs[:scalars], refs[scalars : scalars + count], refs[scalars + count :]
    unit[...], _ = unit_of(queries[step].astype(f32))
    item = split_dot(column(line[...]), blocks)
    found[...] = unit_of(item)[0] if step == 0 else item
    if negatives.shape[1] > 1:
        sums[...] = jnp.sum(weights_of(unit[...], negatives[...]), 1, keepdims=True)
    else:
        sums[...] = negatives[...]
    if told:
        told[0][...] = told_block(*ids, *told[0].shape)


def main_kernel(first, count, found, found_line, line, queries, negatives, *refs):
    blocks, (told, sent, rows, unit, top) = refs[:count], refs[count:]
    item = found[...]
    if blocks:
        item = item + split_dot(column(found_line[...]), blocks, first)
    unit[...] = item
    top[...] = item[: top.shape[0]]
    query = queries[...]
    if negatives.shape[1] > 1:
        sums = jnp.sum(weights_of(query, negatives[...]), 1, keepdims=True)
    else:
        sums = negatives[...]
    cosine = jnp.sum(query * item, 1, keepdims=True)
    weight = jnp.exp(score_scale * cosine)
    lack = weight / (weight + sums) - 1.0
    rows[...] = (lack * (query - item * cosine)).astype(bf16)
    dense(sent.shape[0], line, rows, told, sent)


def dense(first, line, rows, told, out):
    half, count = out.shape[0], told.shape[0]
    chosen = one_hot(line[...], first, half, False)
    out[...] = jnp.dot(chosen, rows[...], preferred_element_type=f32).astype(out.dtype)
    for end in range(half // 4, half + 1, half // 4):
        out[pl.ds(end - count, count), :] = told[...].astype(out.dtype)


def kept_kernel(line, rows, told, out):
    dense(0, line, rows, told, out)


def late_kernel(step, given, queries, item, negatives, _, *refs):
    query, query_norm = unit_of(queries[step].astype(f32))
    if given:
        moment, sums, refs = refs[0][...], negatives[...], refs[1:]
    else:
        weights = weights_of(query, negatives[...])
        sums = jnp.sum(weights, 1, keepdims=True)
        moment = jnp.dot(weights.astype(bf16), negatives[...], preferred_element_type=f32)
    item = item[...]
    score = score_scale * jnp.sum(query * item, 1, keepdims=True)
    weight = jnp.exp(score)
    total = weight + sums
    loss = jnp.transpose(jnp.broadcast_to(jnp.log(total) - score, item.shape))[:1]
    unit_grad = score_scale * ((weight / total - 1.0) * item + moment / total)
    along = jnp.sum(query * unit_grad, 1, keepdims=True)
    grad = ((unit_grad - query * along) / query_norm).astype(bf16)
    zero, refs = refs[-1], refs[:-1]
    zero[...] = jnp.zeros_like(zero)
    if step == 0:
        fifo, accum, loss_out, grad_out, fifo_out, accum_out = refs
        loss_out[...], grad_out[...] = loss, grad
        fifo_out[...], accum_out[...] = fifo[...], accum[...]
        return
    loss_before, grad_before, fifo, head, *tops, losses, grads, fifo_out = refs
    losses[0:1, :], losses[1:2, :] = loss_before[...], loss
    grads[0], grads[1] = grad_before[...], grad
    queue_rows = fifo.shape[0]
    line = lax.broadcasted_iota(jnp.int32, fifo.shape, 0)
    queue = fifo[...].astype(f32)
    for number, top in enumerate(tops):
        for k in range(ENQ):
            slot = lax.rem(head[...] + (number * ENQ + k), queue_rows)
            queue = jnp.where(line == slot, top[k : k + 1, :], queue)
    fifo_out[...] = queue.astype(bf16)


def queue_kernel(count, told, negatives, *refs):
    blocks, (out, zero) = refs[:count], refs[count:]
    item, _ = unit_of(split_dot(told[...], blocks))
    zero[...] = jnp.zeros_like(zero)
    out[...] = jnp.where(told[...] >= 0, item, negatives[...].astype(f32)).astype(bf16)


def update_kernel(scale, side, mine, other, table, line, table_out, line_out, *unit):
    count = table.shape[0] // 2
    mine, other, first = mine[:count, :], other[:count, :], side[...] == 0
    grad = jnp.concatenate([jnp.where(first, mine, other), jnp.where(first, other, mine)])
    rows = table[...]
    _, norm = unit_of(rows)
    grad = grad * (scale / norm)
    square = grad * grad
    moved = column(line[...]) + jnp.mean(square, 1, keepdims=True)
    ones = jnp.full((8, square.shape[1]), 1.0, f32)
    sums = lax.dot_general(
        ones, square, (((1,), (1,)), ((), ())), precision=lax.Precision.HIGHEST,
        preferred_element_type=f32,
    )
    line_out[...] = line[...] + sums[:1] / square.shape[1]
    rows = rows - learn_rate * grad / jnp.sqrt(moved)
    table_out[...] = rows
    if unit:
        unit[0][...], _ = unit_of(rows)


def call(kernel, outs, *args):
    vmem = pl.BlockSpec(memory_space=pltpu.VMEM)
    return pl.pallas_call(
        kernel,
        out_shape=[jax.ShapeDtypeStruct(shape, dtype) for shape, dtype in outs],
        in_specs=[vmem] * len(args),
        out_specs=[vmem] * len(outs),
        compiler_params=pltpu.CompilerParams(vmem_limit_bytes=VMEM),
    )(*args)


def per_device(queries, item_owner, item_row, table, accum, fifo, fifo_head):
    step_count, query_count, width = queries.shape
    owners, copies = lax.axis_size("table"), lax.axis_size("batch")
    owned = table.shape[0]
    part_rows = owned // 2
    queue_rows = fifo.shape[0]
    devices = owners * copies
    lanes = width // 4
    tiles = -(-devices // lanes)
    stride = part_rows + tiles * queue_rows
    half_rows = owners * stride
    me = lax.axis_index("table")
    side = lax.axis_index("batch") % 2
    masks = masks_of(owners)
    small = devices * queue_rows <= 1024
    most = owners * copies * (3 * query_count // owners)
    grad_scale = 1.0
    while most * grad_scale > 32768.0:
        grad_scale = grad_scale / 2

    def owner_place(owner):
        apart = jnp.bitwise_xor(owner, me)
        place = jnp.zeros_like(owner)
        for index, mask in enumerate(masks):
            place = place + jnp.where((apart & mask) != 0, 1 << index, 0)
        return place

    def place_whole(owner, row):
        return owner_place(owner) * owned + row

    def place_part(owner, row):
        half = row // part_rows
        return (2 * owner_place(owner) + jnp.bitwise_xor(half, side)) * stride + row % part_rows

    def gather_whole(piece):
        pieces = [piece]
        for mask in masks:
            pieces = pieces + [flip(piece, mask) for piece in pieces]
        return pieces

    def reduce_near(kept, came):
        spans = [slice(i * stride, (i + 1) * stride) for i in range(4)]
        pieces = [kept[span] + came[span].astype(f32) for span in spans]
        near = [
            flip(piece.astype(f16), mask)
            for piece, mask in zip(pieces[1:], (owners, masks[0], owners + masks[0]))
        ]
        beside = [piece.astype(f32) for piece in near]
        return (pieces[0] + beside[0]) + (beside[1] + beside[2]), near[0][:8].astype(f32)

    def reduce_far(total, zero):
        stages = stages_of(copies, 2)
        for stage in stages[1:]:
            total = sum_stage(total, *stage, zero)
        sent = lax.optimization_barrier(total.astype(f16))
        if stages and stages[0][1] == 2:
            pairs = [[sent, flip(sent, 2 * owners)], [flip(sent, owners), flip(sent, 3 * owners)]]
        else:
            pairs = [[sent], [flip(sent, owners)]]
        return [sum(part.astype(f32) for part in pair) for pair in pairs]

    def own_told():
        slot = jnp.arange(queue_rows, dtype=jnp.int32)[:, None]
        taken = (slot - fifo_head) % queue_rows == jnp.arange(ENQ, dtype=jnp.int32)
        owner, row = item_owner[0, :ENQ, 0], item_row[0, :ENQ]
        told = [jnp.sum(jnp.where(taken, part, 0), 1) for part in (owner + 1, row // 16, row % 16)]
        told = jnp.stack(told + [jnp.zeros((queue_rows,), jnp.int32)], 1).astype(f32)
        mine = jnp.arange(tiles * lanes, dtype=jnp.int32) == lax.axis_index(("batch", "table"))
        told = jnp.where(mine[:, None, None], told, 0.0).reshape(tiles, lanes, queue_rows, 4)
        return told.transpose(0, 2, 1, 3).reshape(tiles * queue_rows, width)

    def next_queue(queue, told):
        told = (told / grad_scale).reshape(tiles, queue_rows, lanes, 4).transpose(0, 2, 1, 3)
        told = told.reshape(-1, 4)[: devices * queue_rows].astype(jnp.int32)
        place = place_whole(told[:, 0] - 1, told[:, 1] * 16 + told[:, 2])
        place = jnp.where(told[:, 0] > 0, place, -1)[:, None]
        if small:
            kernel = functools.partial(queue_kernel, len(parts))
            queue, zero = call(kernel, [(queue.shape, bf16), (table.shape, f32)], place, queue, *parts)
            return queue, zero
        blocks = [split_parts(part, 2) for part in parts]
        new = lax.map(lambda at: pick_rows(at, blocks, width), place.reshape(-1, copies * queue_rows))
        return jnp.where(place >= 0, unit_of(new.reshape(queue.shape))[0].astype(bf16), queue), 0.0

    parts = gather_whole(table)

    queue = jnp.broadcast_to(jnp.maximum(fifo, bf16(-3e38))[None], (devices, *fifo.shape))
    queue = lax.all_to_all(queue, ("batch", "table"), 0, 0, tiled=True).reshape(-1, width)
    device = jnp.full((1, 1), lax.axis_index(("batch", "table")))

    line = accum[None, :]
    tops = []
    for step in range(step_count):
        places = place_part(item_owner[step, :, 0], item_row[step])
        found_at = place_whole(item_owner[step, :, 0], item_row[step])
        last_place = owners * owned - parts[-1].shape[0]
        parts = [part.astype(f32) for part in parts]
        if step:
            parts[1] = parts[1] + zero
        scalars, matrix = (query_count, 1), (query_count, width)
        if small:
            negatives = queue if step else jnp.zeros(scalars, f32)
        else:
            query_half = unit_of(queries[step].astype(f32))[0].astype(bf16)
            negatives, moment = score_rows(query_half, queue, jnp.ones(queue.shape[:1], jnp.bool_))
            negatives = negatives[:, None]
        split = len(parts) if step == 0 else -1
        ids = [device, jnp.transpose(item_owner, (0, 2, 1)), item_row, fifo_head[None]]
        ids = ids if small and step == 0 else []
        query_unit, found, sums, *own = call(
            functools.partial(first_kernel, step, len(parts[:split]), len(ids)),
            [(matrix, f32), (matrix, f32), (scalars, f32)] + [((queue_rows, width), f32)] * bool(ids),
            queries,
            found_at[None, :],
            negatives,
            *ids,
            *parts[:split],
        )
        if step == 0:
            told = own[0] if own else own_told()
        sent, rows, unit, top = call(
            functools.partial(main_kernel, last_place, len(parts[split:])),
            [((half_rows, width), bf16), (matrix, bf16), (matrix, f32), ((8, width), f32)],
            found,
            found_at[None, :],
            places[None, :],
            query_unit,
            queue if small and step == 0 else sums,
            *parts[split:],
            told,
        )
        tops.append(top)
        (kept,) = call(kept_kernel, [((half_rows, width), f32)], places[None, :], rows, told)
        sent = (grad_scale * sent).astype(bf16)
        kept = grad_scale * kept
        for mask in masks[:1:-1]:
            kept = kept + flip(sent, mask).astype(f32)
            middle = kept.shape[0] // 2
            kept, sent = kept[:middle], kept[middle:].astype(f16)
        total, early = reduce_near(kept, flip(sent, masks[1]))

        more = step + 1 < step_count
        args = [queries, unit, queue if small else negatives, early, *([] if small else [moment])]
        if more:
            outs = [((1, query_count), f32), (matrix, bf16), (fifo.shape, bf16), (line.shape, f32)]
            args += [fifo, line]
        else:
            outs = [((step_count, query_count), f32), (queries.shape, bf16), (fifo.shape, bf16)]
            args += [loss, query_grad, fifo, fifo_head[None], *tops]
        kernel = functools.partial(late_kernel, step, not small)
        loss, query_grad, fifo, *rest, zero = call(kernel, outs + [(total.shape, f32)], *args)
        line = rest[0] if more else line
        mine, other = reduce_far(total, zero)
        table, line, *rest = call(
            functools.partial(update_kernel, score_scale / grad_scale),
            [(table.shape, f32), (line.shape, f32)] + [(table.shape, f32)] * more,
            jnp.full((1, 1), side),
            mine,
            other,
            table,
            line,
        )
        if more:
            queue, zero = next_queue(queue, mine[part_rows:])
            parts = gather_whole(rest[0].astype(f16))

    return (loss, query_grad, table, line[0], fifo)


def solution(mesh):
    both = ("batch", "table")
    in_specs = (
        P(None, both, None),
        P(None, both, None),
        P(None, both),
        P("table", None),
        P("table"),
        P(both, None),
        P(both),
    )
    out_specs = (P(None, both), P(None, both, None), P("table", None), P("table"), P(both, None))
    return jax.shard_map(
        per_device, mesh=mesh, in_specs=in_specs, out_specs=out_specs, check_vma=False
    )
```

time: 76.3 us -> 70.3 us (0.921)
  other arithmetic: 3.72 us -> 1.4 us
  starting transfers between devices: 26.9 us -> 24.6 us
  waiting for transfers between devices: 28.7 us -> 30.3 us
  local copies, waits for them, and re-layouts: 3.07 us -> 1.72 us
  Pallas kernels: 11.9 us -> 10.6 us
    ppermute x20, waiting for transfers between devices: 16.3 us -> 18.6 us  [flip(): lax.ppermute(piece, ('batch', 'table'), [(i ^ mask, i) for i in range(cou...]
    unnamed x12, local copies, waits for them, and re-layouts: 2.51 us -> 0.71 us
    ppermute x20, starting transfers between devices: 20.2 us -> 18.6 us  [flip(): lax.ppermute(piece, ('batch', 'table'), [(i ^ mask, i) for i in range(cou...]
    pallas_call x1 -> x0, Pallas kernels: 1.62 us -> none  [per_device(): pl.pallas_call(prologue_kernel, out_shape=jax.ShapeDtypeStruct((owners *...]
    another operation x6 -> x0, other arithmetic: 1.5 us -> none  [the longest x1 0.74 us: per_device(): jnp.stack(grad_list)]
    pallas_call x3 -> x0, other arithmetic: 1.01 us -> none  [call(): pl.pallas_call(kernel, out_shape=[jax.ShapeDtypeStruct(shape, dtype) for...]
    pallas_call x9 -> x11, Pallas kernels: 10.3 us -> 10.6 us  [call(): pl.pallas_call(kernel, out_shape=[jax.ShapeDtypeStruct(shape, dtype) for...]
  transfers between devices with their start and end apart: 23 -> 23, of which waited for: 16 -> 20; matrix products, arithmetic and copies ran while one was open for 4% -> 3% of each run, Pallas kernels for 10% -> 9%
where the time goes in v5:
time: 70.3 us; the launch traced here: 70.1 us
  waiting for transfers between devices  30.3 us (43%)
  starting transfers between devices  24.6 us (35%)
  Pallas kernels  10.6 us (15%)
  local copies, waits for them, and re-layouts  1.72 us (2%)
  between operations  1.47 us (2%)
  other arithmetic  1.4 us (2%)
    ppermute x20, starting transfers between devices, flip(): lax.ppermute(piece, ('batch', 'table'), [(i ^ mask, i) for i in range(cou...  18.6 us
    ppermute x20, waiting for transfers between devices, flip(): lax.ppermute(piece, ('batch', 'table'), [(i ^ mask, i) for i in range(cou...  18.6 us
    pallas_call x11, Pallas kernels, call(): pl.pallas_call(kernel, out_shape=[jax.ShapeDtypeStruct(shape, dtype) for...  10.6 us
    ppermute x2, waiting for transfers between devices, turned(): found.append(lax.ppermute(piece, 'batch', pairs))  7.93 us
    all_to_all x1, starting transfers between devices, per_device(): lax.all_to_all(queue, ('batch', 'table'), 0, 0, tiled=True)  5.03 us
    all_to_all x1, waiting for transfers between devices, per_device(): lax.all_to_all(queue, ('batch', 'table'), 0, 0, tiled=True)  3.86 us
  transfers between devices with their start and end apart: 23, of which 20 were waited for; matrix products, arithmetic and copies ran while one was open for 3% of the time, Pallas kernels for 9%

profile of v5, /device:TPU:0, one launch (start us, length us, event | category | flops | bytes accessed | tf_op | source)
XLA Modules:
  0.0 70.1 jit_solution(10680670303640445642)
XLA Ops:
  0.6 3.0 %collective-permute-start = (f32[480,128]{1,0:T(8,128)}, f32[480,128]{1,0:T(8,128)S(1)}, u32[]{:S(2)}, u32[]{:S(2)}) collective-permute-start(f32[480,128]{1,0:T(8,128)} %table.1), channel_id=1, source_target_pairs={{2,0},{3,1},{0,2},{1,3},{6,4},{7,5},{4,6},{5,7},{10,8},{11,9},{8,1... | collective-permute-start | bytes 737288 | tf_op jit(solution)/shard_map/ppermute | solution.py:40
  5.0 5.0 %all-to-all-start = ((bf16[32,8,128]{2,1,0:T(8,128)(2,1)}), bf16[32,8,128]{2,1,0:T(8,128)(2,1)S(1)}, u32[]{:S(2)}, u32[]{:S(2)}) async-start(bf16[32,8,128]{2,1,0:T(8,128)(2,1)} %broadcast_in_dim.67), calls=%async_computation | async-start | bytes 131072 | tf_op jit(solution)/shard_map/all_to_all | solution.py:375
  11.7 1.9 %shard_map.110 = (f32[512,128]{1,0:T(8,128)S(1)}, f32[512,128]{1,0:T(8,128)S(1)}, f32[512,1]{1,0:T(8,128)}, f32[8,128]{1,0:T(8,128)S(1)}) custom-call(bf16[2,512,128]{2,1,0:T(8,128)(2,1)S(1)} %copy-done, s32[1,512]{1,0:T(1,128)S(1)} %get-tuple-element.69.line.found_line, f32[512,1]{1,0:T(8,128)S(1)} %broadcast_in_dim.64.negatives, s32[1,1]{1,0:T(1,128)} %bitcast.3.refs_0_, ...), custom_call_target="tpu_custom_call" | custom-call | tf_op jit(solution)/shard_map/pallas_call | solution.py:279
  13.6 3.9 %all-to-all-done = bf16[32,8,128]{2,1,0:T(8,128)(2,1)S(1)} async-done(((bf16[32,8,128]{2,1,0:T(8,128)(2,1)}), bf16[32,8,128]{2,1,0:T(8,128)(2,1)S(1)}, u32[]{:S(2)}, u32[]{:S(2)}) %all-to-all-start) | async-done | bytes 65568 | tf_op jit(solution)/shard_map/all_to_all | solution.py:375
  20.7 1.3 %collective-permute-start.5 = (f16[248,128]{1,0:T(8,128)(2,1)S(1)}, f16[248,128]{1,0:T(8,128)(2,1)S(1)}, u32[]{:S(2)}, u32[]{:S(2)}) collective-permute-start(f16[248,128]{1,0:T(8,128)(2,1)S(1)} %get-tuple-element.76), channel_id=1, source_target_pairs={{2,0},{3,1},{0,2},{1,3},{6,4},{7,5},{4,6},{5,7},{10,8},{11,9},{8,1... | collective-permute-start | bytes 190472 | tf_op jit(solution)/shard_map/ppermute | solution.py:40
  22.1 1.4 %collective-permute-start.4 = (f16[248,128]{1,0:T(8,128)(2,1)S(1)}, f16[248,128]{1,0:T(8,128)(2,1)S(1)}, u32[]{:S(2)}, u32[]{:S(2)}) collective-permute-start(f16[248,128]{1,0:T(8,128)(2,1)S(1)} %get-tuple-element.74), channel_id=1, source_target_pairs={{4,0},{5,1},{6,2},{7,3},{0,4},{1,5},{2,6},{3,7},{12,8},{13,9},{14,... | collective-permute-start | bytes 190472 | tf_op jit(solution)/shard_map/ppermute | solution.py:40
  23.5 2.2 %collective-permute-done.6 = f16[248,128]{1,0:T(8,128)(2,1)S(1)} collective-permute-done((f16[248,128]{1,0:T(8,128)(2,1)S(1)}, f16[248,128]{1,0:T(8,128)(2,1)S(1)}, u32[]{:S(2)}, u32[]{:S(2)}) %collective-permute-start.6) | collective-permute-done | bytes 63520 | tf_op jit(solution)/shard_map/ppermute | solution.py:40
  28.5 3.8 %collective-permute-done.7 = f16[248,128]{1,0:T(8,128)(2,1)S(1)} collective-permute-done((f16[248,128]{1,0:T(8,128)(2,1)S(1)}, f16[248,128]{1,0:T(8,128)(2,1)S(1)}, u32[]{:S(2)}, u32[]{:S(2)}) %collective-permute-start.7) | collective-permute-done | bytes 63520 | tf_op jit(solution)/shard_map/ppermute | solution.py:51
  32.4 2.8 %collective-permute-start.10 = (f16[248,128]{1,0:T(8,128)(2,1)S(1)}, f16[248,128]{1,0:T(8,128)(2,1)S(1)}, u32[]{:S(2)}, u32[]{:S(2)}) collective-permute-start(f16[248,128]{1,0:T(8,128)(2,1)S(1)} %add_convert_fusion.1), channel_id=1, source_target_pairs={{12,0},{13,1},{14,2},{15,3},{8,4},{9,5},{10,6},{11,7},{4,8},{5,9},... | collective-permute-start | bytes 190472 | tf_op jit(solution)/shard_map/ppermute | solution.py:40
  36.7 1.5 %collective-permute-done.10 = f16[248,128]{1,0:T(8,128)(2,1)S(1)} collective-permute-done((f16[248,128]{1,0:T(8,128)(2,1)S(1)}, f16[248,128]{1,0:T(8,128)(2,1)S(1)}, u32[]{:S(2)}, u32[]{:S(2)}) %collective-permute-start.10) | collective-permute-done | bytes 63520 | tf_op jit(solution)/shard_map/ppermute | solution.py:40
  38.2 1.3 %collective-permute-done.9 = f16[248,128]{1,0:T(8,128)(2,1)S(1)} collective-permute-done((f16[248,128]{1,0:T(8,128)(2,1)S(1)}, f16[248,128]{1,0:T(8,128)(2,1)S(1)}, u32[]{:S(2)}, u32[]{:S(2)}) %collective-permute-start.9) | collective-permute-done | bytes 63520 | tf_op jit(solution)/shard_map/ppermute | solution.py:40
  42.1 3.1 %collective-permute-done.11 = f16[480,128]{1,0:T(8,128)(2,1)S(1)} collective-permute-done((f16[480,128]{1,0:T(8,128)(2,1)S(1)}, f16[480,128]{1,0:T(8,128)(2,1)S(1)}, u32[]{:S(2)}, u32[]{:S(2)}) %collective-permute-start.11) | collective-permute-done | bytes 122912 | tf_op jit(solution)/shard_map/ppermute | solution.py:40
  46.5 1.3 %shard_map.117 = (bf16[992,128]{1,0:T(8,128)(2,1)S(1)}, bf16[512,128]{1,0:T(8,128)(2,1)S(1)}, f32[512,128]{1,0:T(8,128)S(1)}, f32[8,128]{1,0:T(8,128)S(1)}) custom-call(f32[512,128]{1,0:T(8,128)S(1)} %get-tuple-element.46.found, s32[1,512]{1,0:T(1,128)S(1)} %get-tuple-element.80.line.found_line, s32[1,512]{1,0:T(1,128)S(1)} %get-tuple-element.77.line, ...), custom_call_target="tpu_custom_call" | custom-call | tf_op jit(solution)/shard_map/pallas_call | solution.py:279
  50.2 1.3 %collective-permute-start.17 = (f16[248,128]{1,0:T(8,128)(2,1)S(1)}, f16[248,128]{1,0:T(8,128)(2,1)S(1)}, u32[]{:S(2)}, u32[]{:S(2)}) collective-permute-start(f16[248,128]{1,0:T(8,128)(2,1)S(1)} %get-tuple-element.72), channel_id=1, source_target_pairs={{6,0},{7,1},{4,2},{5,3},{2,4},{3,5},{0,6},{1,7},{14,8},{15,9},{12,... | collective-permute-start | bytes 190472 | tf_op jit(solution)/shard_map/ppermute | solution.py:40
  51.4 1.6 %collective-permute-start.16 = (f16[248,128]{1,0:T(8,128)(2,1)S(1)}, f16[248,128]{1,0:T(8,128)(2,1)S(1)}, u32[]{:S(2)}, u32[]{:S(2)}) collective-permute-start(f16[248,128]{1,0:T(8,128)(2,1)S(1)} %get-tuple-element.71), channel_id=1, source_target_pairs={{2,0},{3,1},{0,2},{1,3},{6,4},{7,5},{4,6},{5,7},{10,8},{11,9},{8,1... | collective-permute-start | bytes 190472 | tf_op jit(solution)/shard_map/ppermute | solution.py:40
  53.0 1.4 %collective-permute-done.15 = f16[248,128]{1,0:T(8,128)(2,1)S(1)} collective-permute-done((f16[248,128]{1,0:T(8,128)(2,1)S(1)}, f16[248,128]{1,0:T(8,128)(2,1)S(1)}, u32[]{:S(2)}, u32[]{:S(2)}) %collective-permute-start.15) | collective-permute-done | bytes 63520 | tf_op jit(solution)/shard_map/ppermute | solution.py:40
  54.5 1.2 %collective-permute-done.17 = f16[248,128]{1,0:T(8,128)(2,1)S(1)} collective-permute-done((f16[248,128]{1,0:T(8,128)(2,1)S(1)}, f16[248,128]{1,0:T(8,128)(2,1)S(1)}, u32[]{:S(2)}, u32[]{:S(2)}) %collective-permute-start.17) | collective-permute-done | bytes 63520 | tf_op jit(solution)/shard_map/ppermute | solution.py:40
  56.6 1.5 %shard_map.119 = (f32[2,512]{1,0:T(2,128)}, bf16[2,512,128]{2,1,0:T(8,128)(2,1)}, bf16[8,128]{1,0:T(8,128)(2,1)}, f32[248,128]{1,0:T(8,128)S(1)}) custom-call(bf16[2,512,128]{2,1,0:T(8,128)(2,1)S(1)} %copy-done, f32[512,128]{1,0:T(8,128)S(1)} %get-tuple-element.49.item, bf16[256,128]{1,0:T(8,128)(2,1)S(1)} %get-tuple-element.42.negatives, ...), custom_call_target="tpu_custom_call" | custom-call | tf_op jit(solution)/shard_map/pallas_call | solution.py:279
  58.1 4.2 %collective-permute-done.18 = f16[248,128]{1,0:T(8,128)(2,1)S(1)} collective-permute-done((f16[248,128]{1,0:T(8,128)(2,1)S(1)}, f16[248,128]{1,0:T(8,128)(2,1)S(1)}, u32[]{:S(2)}, u32[]{:S(2)}) %collective-permute-start.18) | collective-permute-done | bytes 63520 | tf_op jit(solution)/shard_map/ppermute | solution.py:51
  62.5 2.1 %collective-permute-start.21 = (f16[248,128]{1,0:T(8,128)(2,1)S(1)}, f16[248,128]{1,0:T(8,128)(2,1)S(1)}, u32[]{:S(2)}, u32[]{:S(2)}) collective-permute-start(f16[248,128]{1,0:T(8,128)(2,1)S(1)} %add_convert_fusion), channel_id=1, source_target_pairs={{12,0},{13,1},{14,2},{15,3},{8,4},{9,5},{10,6},{11,7},{4,8},{5,9},... | collective-permute-start | bytes 190472 | tf_op jit(solution)/shard_map/ppermute | solution.py:40
  64.6 1.2 %collective-permute-start.20 = (f16[248,128]{1,0:T(8,128)(2,1)S(1)}, f16[248,128]{1,0:T(8,128)(2,1)S(1)}, u32[]{:S(2)}, u32[]{:S(2)}) collective-permute-start(f16[248,128]{1,0:T(8,128)(2,1)S(1)} %add_convert_fusion), channel_id=1, source_target_pairs={{4,0},{5,1},{6,2},{7,3},{0,4},{1,5},{2,6},{3,7},{12,8},{13,9},{14,... | collective-permute-start | bytes 190472 | tf_op jit(solution)/shard_map/ppermute | solution.py:40
  66.6 1.0 %collective-permute-done.21 = f16[248,128]{1,0:T(8,128)(2,1)S(1)} collective-permute-done((f16[248,128]{1,0:T(8,128)(2,1)S(1)}, f16[248,128]{1,0:T(8,128)(2,1)S(1)}, u32[]{:S(2)}, u32[]{:S(2)}) %collective-permute-start.21) | collective-permute-done | bytes 63520 | tf_op jit(solution)/shard_map/ppermute | solution.py:40
  67.7 1.2 %collective-permute-done.20 = f16[248,128]{1,0:T(8,128)(2,1)S(1)} collective-permute-done((f16[248,128]{1,0:T(8,128)(2,1)S(1)}, f16[248,128]{1,0:T(8,128)(2,1)S(1)}, u32[]{:S(2)}, u32[]{:S(2)}) %collective-permute-start.20) | collective-permute-done | bytes 63520 | tf_op jit(solution)/shard_map/ppermute | solution.py:40
  68.9 1.2 %shard_map.120 = (f32[480,128]{1,0:T(8,128)}, f32[1,480]{1,0:T(1,128)}) custom-call(s32[1,1]{1,0:T(1,128)} %bitcast.11.side, f32[248,128]{1,0:T(8,128)S(1)} %convert_add_fusion.2.mine, f32[248,128]{1,0:T(8,128)S(1)} %convert_add_fusion.1.other, f32[480,128]{1,0:T(8,128)S(1)} %get-tuple-element.60.table, f32[1,480]{1,0:T(1,128)S(1)} %get-tuple-element.61.line), custom_call_target="tpu_custom_call" | custom-call | tf_op jit(solution)/shard_map/pallas_call | solution.py:279
  (70 shorter events, 18.1 us)
Async XLA Ops:
  0.6 9.4 %collective-permute-start = (f32[480,128]{1,0:T(8,128)}, f32[480,128]{1,0:T(8,128)S(1)}, u32[]{:S(2)}, u32[]{:S(2)}) collective-permute-start(f32[480,128]{1,0:T(8,128)} %table.1), channel_id=1, source_target_pairs={{2,0},{3,1},{0,2},{1,3},{6,4},{7,5},{4,6},{5,7},{10,8},{11,9},{8,1... | collective-permute-start | bytes 737288 | tf_op jit(solution)/shard_map/ppermute | solution.py:40
  3.6 7.5 %collective-permute-start.1 = (f32[480,128]{1,0:T(8,128)}, f32[480,128]{1,0:T(8,128)S(1)}, u32[]{:S(2)}, u32[]{:S(2)}) collective-permute-start(f32[480,128]{1,0:T(8,128)} %table.1), channel_id=1, source_target_pairs={{1,0},{0,1},{3,2},{2,3},{5,4},{4,5},{7,6},{6,7},{9,8},{8,9},{11,10... | collective-permute-start | bytes 737288 | tf_op jit(solution)/shard_map/ppermute | solution.py:40
  4.4 7.3 %copy-start = (bf16[2,512,128]{2,1,0:T(8,128)(2,1)S(1)}, bf16[2,512,128]{2,1,0:T(8,128)(2,1)}, u32[]{:S(2)}) copy-start(bf16[2,512,128]{2,1,0:T(8,128)(2,1)} %queries.7) | copy-start | bytes 786436
  5.0 12.5 %all-to-all-start = ((bf16[32,8,128]{2,1,0:T(8,128)(2,1)}), bf16[32,8,128]{2,1,0:T(8,128)(2,1)S(1)}, u32[]{:S(2)}, u32[]{:S(2)}) async-start(bf16[32,8,128]{2,1,0:T(8,128)(2,1)} %broadcast_in_dim.67), calls=%async_computation | async-start | bytes 131072 | tf_op jit(solution)/shard_map/all_to_all | solution.py:375
  10.1 1.6 %collective-permute-start.2 = (f32[480,128]{1,0:T(8,128)S(1)}, f32[480,128]{1,0:T(8,128)S(1)}, u32[]{:S(2)}, u32[]{:S(2)}) collective-permute-start(f32[480,128]{1,0:T(8,128)S(1)} %collective-permute-done.refs_5_.refs_1_), channel_id=1, source_target_pairs={{1,0},{0,1},{3,2},{2,3},{5,4},{4,5},{7,6},{6,7},{9,8},{8,9},{11,10... | collective-permute-start | bytes 737288 | tf_op jit(solution)/shard_map/ppermute | solution.py:40
  18.3 1.6 %collective-permute-start.3 = (bf16[992,128]{1,0:T(8,128)(2,1)S(1)}, bf16[992,128]{1,0:T(8,128)(2,1)S(1)}, u32[]{:S(2)}, u32[]{:S(2)}) collective-permute-start(bf16[992,128]{1,0:T(8,128)(2,1)S(1)} %get-tuple-element.39), channel_id=1, source_target_pairs={{1,0},{0,1},{3,2},{2,3},{5,4},{4,5},{7,6},{6,7},{9,8},{8,9},{11,10... | collective-permute-start | bytes 761864 | tf_op jit(solution)/shard_map/ppermute | solution.py:40
  19.9 5.7 %collective-permute-start.6 = (f16[248,128]{1,0:T(8,128)(2,1)S(1)}, f16[248,128]{1,0:T(8,128)(2,1)S(1)}, u32[]{:S(2)}, u32[]{:S(2)}) collective-permute-start(f16[248,128]{1,0:T(8,128)(2,1)S(1)} %get-tuple-element.75), channel_id=1, source_target_pairs={{6,0},{7,1},{4,2},{5,3},{2,4},{3,5},{0,6},{1,7},{14,8},{15,9},{12,... | collective-permute-start | bytes 190472 | tf_op jit(solution)/shard_map/ppermute | solution.py:40
  20.7 5.0 %collective-permute-start.5 = (f16[248,128]{1,0:T(8,128)(2,1)S(1)}, f16[248,128]{1,0:T(8,128)(2,1)S(1)}, u32[]{:S(2)}, u32[]{:S(2)}) collective-permute-start(f16[248,128]{1,0:T(8,128)(2,1)S(1)} %get-tuple-element.76), channel_id=1, source_target_pairs={{2,0},{3,1},{0,2},{1,3},{6,4},{7,5},{4,6},{5,7},{10,8},{11,9},{8,1... | collective-permute-start | bytes 190472 | tf_op jit(solution)/shard_map/ppermute | solution.py:40
  22.1 4.3 %collective-permute-start.4 = (f16[248,128]{1,0:T(8,128)(2,1)S(1)}, f16[248,128]{1,0:T(8,128)(2,1)S(1)}, u32[]{:S(2)}, u32[]{:S(2)}) collective-permute-start(f16[248,128]{1,0:T(8,128)(2,1)S(1)} %get-tuple-element.74), channel_id=1, source_target_pairs={{4,0},{5,1},{6,2},{7,3},{0,4},{1,5},{2,6},{3,7},{12,8},{13,9},{14,... | collective-permute-start | bytes 190472 | tf_op jit(solution)/shard_map/ppermute | solution.py:40
  26.4 5.9 %collective-permute-start.7 = (f16[248,128]{1,0:T(8,128)(2,1)S(1)}, f16[248,128]{1,0:T(8,128)(2,1)S(1)}, u32[]{:S(2)}, u32[]{:S(2)}) collective-permute-start(f16[248,128]{1,0:T(8,128)(2,1)S(1)} %fusion.13), channel_id=1, source_target_pairs={{16,0},{20,4},{24,8},{28,12},{0,16},{4,20},{8,24},{12,28},{17,1},{... | collective-permute-start | bytes 190472 | tf_op jit(solution)/shard_map/ppermute | solution.py:51
  32.3 4.3 %collective-permute-start.8 = (f16[248,128]{1,0:T(8,128)(2,1)S(1)}, f16[248,128]{1,0:T(8,128)(2,1)S(1)}, u32[]{:S(2)}, u32[]{:S(2)}) collective-permute-start(f16[248,128]{1,0:T(8,128)(2,1)S(1)} %add_convert_fusion.1), channel_id=1, source_target_pairs={{8,0},{9,1},{10,2},{11,3},{12,4},{13,5},{14,6},{15,7},{0,8},{1,9},... | collective-permute-start | bytes 190472 | tf_op jit(solution)/shard_map/ppermute | solution.py:40
  32.4 5.7 %collective-permute-start.10 = (f16[248,128]{1,0:T(8,128)(2,1)S(1)}, f16[248,128]{1,0:T(8,128)(2,1)S(1)}, u32[]{:S(2)}, u32[]{:S(2)}) collective-permute-start(f16[248,128]{1,0:T(8,128)(2,1)S(1)} %add_convert_fusion.1), channel_id=1, source_target_pairs={{12,0},{13,1},{14,2},{15,3},{8,4},{9,5},{10,6},{11,7},{4,8},{5,9},... | collective-permute-start | bytes 190472 | tf_op jit(solution)/shard_map/ppermute | solution.py:40
  35.3 4.2 %collective-permute-start.9 = (f16[248,128]{1,0:T(8,128)(2,1)S(1)}, f16[248,128]{1,0:T(8,128)(2,1)S(1)}, u32[]{:S(2)}, u32[]{:S(2)}) collective-permute-start(f16[248,128]{1,0:T(8,128)(2,1)S(1)} %add_convert_fusion.1), channel_id=1, source_target_pairs={{4,0},{5,1},{6,2},{7,3},{0,4},{1,5},{2,6},{3,7},{12,8},{13,9},{14,... | collective-permute-start | bytes 190472 | tf_op jit(solution)/shard_map/ppermute | solution.py:40
  40.2 4.9 %collective-permute-start.11 = (f16[480,128]{1,0:T(8,128)(2,1)S(1)}, f16[480,128]{1,0:T(8,128)(2,1)S(1)}, u32[]{:S(2)}, u32[]{:S(2)}) collective-permute-start(f16[480,128]{1,0:T(8,128)(2,1)S(1)} %get-tuple-element.68), channel_id=1, source_target_pairs={{2,0},{3,1},{0,2},{1,3},{6,4},{7,5},{4,6},{5,7},{10,8},{11,9},{8,1... | collective-permute-start | bytes 368648 | tf_op jit(solution)/shard_map/ppermute | solution.py:40
  40.7 1.3 %collective-permute-start.12 = (f16[480,128]{1,0:T(8,128)(2,1)S(1)}, f16[480,128]{1,0:T(8,128)(2,1)S(1)}, u32[]{:S(2)}, u32[]{:S(2)}) collective-permute-start(f16[480,128]{1,0:T(8,128)(2,1)S(1)} %get-tuple-element.68), channel_id=1, source_target_pairs={{1,0},{0,1},{3,2},{2,3},{5,4},{4,5},{7,6},{6,7},{9,8},{8,9},{11,10... | collective-permute-start | bytes 368648 | tf_op jit(solution)/shard_map/ppermute | solution.py:40
  45.1 1.3 %collective-permute-start.13 = (f16[480,128]{1,0:T(8,128)(2,1)S(1)}, f16[480,128]{1,0:T(8,128)(2,1)S(1)}, u32[]{:S(2)}, u32[]{:S(2)}) collective-permute-start(f16[480,128]{1,0:T(8,128)(2,1)S(1)} %collective-permute-done.11), channel_id=1, source_target_pairs={{1,0},{0,1},{3,2},{2,3},{5,4},{4,5},{7,6},{6,7},{9,8},{8,9},{11,10... | collective-permute-start | bytes 368648 | tf_op jit(solution)/shard_map/ppermute | solution.py:40
  47.8 1.6 %collective-permute-start.14 = (bf16[992,128]{1,0:T(8,128)(2,1)S(1)}, bf16[992,128]{1,0:T(8,128)(2,1)S(1)}, u32[]{:S(2)}, u32[]{:S(2)}) collective-permute-start(bf16[992,128]{1,0:T(8,128)(2,1)S(1)} %get-tuple-element.51), channel_id=1, source_target_pairs={{1,0},{0,1},{3,2},{2,3},{5,4},{4,5},{7,6},{6,7},{9,8},{8,9},{11,10... | collective-permute-start | bytes 761864 | tf_op jit(solution)/shard_map/ppermute | solution.py:40
  49.5 5.0 %collective-permute-start.15 = (f16[248,128]{1,0:T(8,128)(2,1)S(1)}, f16[248,128]{1,0:T(8,128)(2,1)S(1)}, u32[]{:S(2)}, u32[]{:S(2)}) collective-permute-start(f16[248,128]{1,0:T(8,128)(2,1)S(1)} %get-tuple-element.73), channel_id=1, source_target_pairs={{4,0},{5,1},{6,2},{7,3},{0,4},{1,5},{2,6},{3,7},{12,8},{13,9},{14,... | collective-permute-start | bytes 190472 | tf_op jit(solution)/shard_map/ppermute | solution.py:40
  50.2 5.5 %collective-permute-start.17 = (f16[248,128]{1,0:T(8,128)(2,1)S(1)}, f16[248,128]{1,0:T(8,128)(2,1)S(1)}, u32[]{:S(2)}, u32[]{:S(2)}) collective-permute-start(f16[248,128]{1,0:T(8,128)(2,1)S(1)} %get-tuple-element.72), channel_id=1, source_target_pairs={{6,0},{7,1},{4,2},{5,3},{2,4},{3,5},{0,6},{1,7},{14,8},{15,9},{12,... | collective-permute-start | bytes 190472 | tf_op jit(solution)/shard_map/ppermute | solution.py:40
  51.4 4.9 %collective-permute-start.16 = (f16[248,128]{1,0:T(8,128)(2,1)S(1)}, f16[248,128]{1,0:T(8,128)(2,1)S(1)}, u32[]{:S(2)}, u32[]{:S(2)}) collective-permute-start(f16[248,128]{1,0:T(8,128)(2,1)S(1)} %get-tuple-element.71), channel_id=1, source_target_pairs={{2,0},{3,1},{0,2},{1,3},{6,4},{7,5},{4,6},{5,7},{10,8},{11,9},{8,1... | collective-permute-start | bytes 190472 | tf_op jit(solution)/shard_map/ppermute | solution.py:40
  56.4 5.9 %collective-permute-start.18 = (f16[248,128]{1,0:T(8,128)(2,1)S(1)}, f16[248,128]{1,0:T(8,128)(2,1)S(1)}, u32[]{:S(2)}, u32[]{:S(2)}) collective-permute-start(f16[248,128]{1,0:T(8,128)(2,1)S(1)} %fusion.6), channel_id=1, source_target_pairs={{16,0},{20,4},{24,8},{28,12},{0,16},{4,20},{8,24},{12,28},{17,1},{... | collective-permute-start | bytes 190472 | tf_op jit(solution)/shard_map/ppermute | solution.py:51
  62.3 4.3 %collective-permute-start.19 = (f16[248,128]{1,0:T(8,128)(2,1)S(1)}, f16[248,128]{1,0:T(8,128)(2,1)S(1)}, u32[]{:S(2)}, u32[]{:S(2)}) collective-permute-start(f16[248,128]{1,0:T(8,128)(2,1)S(1)} %add_convert_fusion), channel_id=1, source_target_pairs={{8,0},{9,1},{10,2},{11,3},{12,4},{13,5},{14,6},{15,7},{0,8},{1,9},... | collective-permute-start | bytes 190472 | tf_op jit(solution)/shard_map/ppermute | solution.py:40
  62.5 5.1 %collective-permute-start.21 = (f16[248,128]{1,0:T(8,128)(2,1)S(1)}, f16[248,128]{1,0:T(8,128)(2,1)S(1)}, u32[]{:S(2)}, u32[]{:S(2)}) collective-permute-start(f16[248,128]{1,0:T(8,128)(2,1)S(1)} %add_convert_fusion), channel_id=1, source_target_pairs={{12,0},{13,1},{14,2},{15,3},{8,4},{9,5},{10,6},{11,7},{4,8},{5,9},... | collective-permute-start | bytes 190472 | tf_op jit(solution)/shard_map/ppermute | solution.py:40
  64.6 4.2 %collective-permute-start.20 = (f16[248,128]{1,0:T(8,128)(2,1)S(1)}, f16[248,128]{1,0:T(8,128)(2,1)S(1)}, u32[]{:S(2)}, u32[]{:S(2)}) collective-permute-start(f16[248,128]{1,0:T(8,128)(2,1)S(1)} %add_convert_fusion), channel_id=1, source_target_pairs={{4,0},{5,1},{6,2},{7,3},{0,4},{1,5},{2,6},{3,7},{12,8},{13,9},{14,... | collective-permute-start | bytes 190472 | tf_op jit(solution)/shard_map/ppermute | solution.py:40
  (5 other events, 21.5 us)

commit v6 on v5

--- a/solution.py
+++ b/solution.py
@@ -201,13 +201,23 @@
 def dense(first, line, rows, told, out):
     half, count = out.shape[0], told.shape[0]
     chosen = one_hot(line[...], first, half, False)
-    out[...] = jnp.dot(chosen, rows[...], preferred_element_type=f32).astype(out.dtype)
-    for end in range(half // 4, half + 1, half // 4):
-        out[pl.ds(end - count, count), :] = told[...].astype(out.dtype)
+    found = jnp.dot(chosen, rows[...], preferred_element_type=f32)
+    pieces = []
+    for start in range(0, half, half // 4):
+        pieces += [found[start : start + half // 4 - count], told[...]]
+    out[...] = jnp.concatenate(pieces).astype(out.dtype)
 
 
 def kept_kernel(line, rows, told, out):
     dense(0, line, rows, told, out)
+
+
+def widen(line):
+    return jnp.pad(line, ((0, 0), (0, -line.shape[1] % 128)))
+
+
+def shift(line, count):
+    return pltpu.roll(line, count % line.shape[1], 1)
 
 
 def late_kernel(step, given, queries, item, negatives, _, *refs):
@@ -229,9 +239,14 @@
     zero, refs = refs[-1], refs[:-1]
     zero[...] = jnp.zeros_like(zero)
     if step == 0:
-        fifo, accum, loss_out, grad_out, fifo_out, accum_out = refs
-        loss_out[...], grad_out[...] = loss, grad
-        fifo_out[...], accum_out[...] = fifo[...], accum[...]
+        fifo, side, table, accum, loss_out, grad_out, fifo_out, *halves = refs
+        loss_out[...], grad_out[...], fifo_out[...] = loss, grad, fifo[...]
+        first, count = side[...] == 0, halves[0].shape[0]
+        low, high = table[:count, :], table[count:, :]
+        halves[0][...], halves[2][...] = jnp.where(first, low, high), jnp.where(first, high, low)
+        accum = widen(accum[...])
+        low, high = accum[:, :count], shift(accum, -count)[:, :count]
+        halves[1][...], halves[3][...] = jnp.where(first, low, high), jnp.where(first, high, low)
         return
     loss_before, grad_before, fifo, head, *tops, losses, grads, fifo_out = refs
     losses[0:1, :], losses[1:2, :] = loss_before[...], loss
@@ -253,25 +268,38 @@
     out[...] = jnp.where(told[...] >= 0, item, negatives[...].astype(f32)).astype(bf16)
 
 
-def update_kernel(scale, side, mine, other, table, line, table_out, line_out, *unit):
-    count = table.shape[0] // 2
-    mine, other, first = mine[:count, :], other[:count, :], side[...] == 0
-    grad = jnp.concatenate([jnp.where(first, mine, other), jnp.where(first, other, mine)])
-    rows = table[...]
-    _, norm = unit_of(rows)
+def adagrad(scale, grad, table, line):
+    _, norm = unit_of(table)
     grad = grad * (scale / norm)
     square = grad * grad
-    moved = column(line[...]) + jnp.mean(square, 1, keepdims=True)
+    moved = column(line) + jnp.mean(square, 1, keepdims=True)
     ones = jnp.full((8, square.shape[1]), 1.0, f32)
     sums = lax.dot_general(
         ones, square, (((1,), (1,)), ((), ())), precision=lax.Precision.HIGHEST,
         preferred_element_type=f32,
     )
-    line_out[...] = line[...] + sums[:1] / square.shape[1]
-    rows = rows - learn_rate * grad / jnp.sqrt(moved)
+    return table - learn_rate * grad / jnp.sqrt(moved), line + sums[:1] / square.shape[1]
+
+
+def update_kernel(scale, total, table, line, table_out, line_out, unit):
+    rows, line_out[...] = adagrad(scale, total[: table.shape[0], :], table[...], line[...])
     table_out[...] = rows
-    if unit:
-        unit[0][...], _ = unit_of(rows)
+    unit[...], _ = unit_of(rows)
+
+
+def finish_kernel(scale, side, mine, other, table, line, far_table, far_line, table_out, line_out):
+    count, first = table.shape[0], side[...] == 0
+
+    def in_order(near, far):
+        return jnp.concatenate([jnp.where(first, near, far), jnp.where(first, far, near)])
+
+    near, far = widen(line[...]), widen(far_line[...])
+    gap = jnp.zeros((1, -(-2 * count // 128) * 128 - near.shape[1]), f32)
+    near, far = jnp.concatenate([near, gap], 1), jnp.concatenate([far, gap], 1)
+    line = jnp.where(first, near, far) + shift(jnp.where(first, far, near), count)
+    grad = in_order(mine[:count, :], other[:count, :])
+    rows = in_order(table[...], far_table[...])
+    table_out[...], line_out[...] = adagrad(scale, grad, rows, line[:, : 2 * count])
 
 
 def call(kernel, outs, *args):
@@ -299,7 +327,7 @@
     me = lax.axis_index("table")
     side = lax.axis_index("batch") % 2
     masks = masks_of(owners)
-    small = devices * queue_rows <= 1024
+    small = devices * queue_rows <= 1024 and tiles == 1
     most = owners * copies * (3 * query_count // owners)
     grad_scale = 1.0
     while most * grad_scale > 32768.0:
@@ -315,12 +343,12 @@
     def place_whole(owner, row):
         return owner_place(owner) * owned + row
 
-    def place_part(owner, row):
+    def place_part(owner, row, stride):
         half = row // part_rows
         return (2 * owner_place(owner) + jnp.bitwise_xor(half, side)) * stride + row % part_rows
 
-    def gather_whole(piece):
-        pieces = [piece]
+    def gather_whole(*pieces):
+        pieces = list(pieces)
         for mask in masks:
             pieces = pieces + [flip(piece, mask) for piece in pieces]
         return pieces
@@ -337,10 +365,11 @@
 
     def reduce_far(total, zero):
         stages = stages_of(copies, 2)
-        for stage in stages[1:]:
+        paired = stages[:1] == [(2, 2)]
+        for stage in stages[paired:]:
             total = sum_stage(total, *stage, zero)
         sent = lax.optimization_barrier(total.astype(f16))
-        if stages and stages[0][1] == 2:
+        if paired:
             pairs = [[sent, flip(sent, 2 * owners)], [flip(sent, owners), flip(sent, 3 * owners)]]
         else:
             pairs = [[sent], [flip(sent, owners)]]
@@ -363,7 +392,7 @@
         place = jnp.where(told[:, 0] > 0, place, -1)[:, None]
         if small:
             kernel = functools.partial(queue_kernel, len(parts))
-            queue, zero = call(kernel, [(queue.shape, bf16), (table.shape, f32)], place, queue, *parts)
+            queue, zero = call(kernel, [(queue.shape, bf16), ((part_rows, width), f32)], place, queue, *parts)
             return queue, zero
         blocks = [split_parts(part, 2) for part in parts]
         new = lax.map(lambda at: pick_rows(at, blocks, width), place.reshape(-1, copies * queue_rows))
@@ -378,12 +407,13 @@
     line = accum[None, :]
     tops = []
     for step in range(step_count):
-        places = place_part(item_owner[step, :, 0], item_row[step])
-        found_at = place_whole(item_owner[step, :, 0], item_row[step])
+        owner, row = item_owner[step, :, 0], item_row[step]
+        places = place_part(owner, row, stride)
+        found_at = place_part(owner, row, part_rows) if step else place_whole(owner, row)
         last_place = owners * owned - parts[-1].shape[0]
         parts = [part.astype(f32) for part in parts]
         if step:
-            parts[1] = parts[1] + zero
+            parts[3] = parts[3] + zero
         scalars, matrix = (query_count, 1), (query_count, width)
         if small:
             negatives = queue if step else jnp.zeros(scalars, f32)
@@ -428,28 +458,28 @@
 
         more = step + 1 < step_count
         args = [queries, unit, queue if small else negatives, early, *([] if small else [moment])]
+        half_shard = [((part_rows, width), f32), ((1, part_rows), f32)]
         if more:
-            outs = [((1, query_count), f32), (matrix, bf16), (fifo.shape, bf16), (line.shape, f32)]
-            args += [fifo, line]
+            outs = [((1, query_count), f32), (matrix, bf16), (fifo.shape, bf16)]
+            outs += half_shard + half_shard
+            args += [fifo, jnp.full((1, 1), side), table, line]
         else:
             outs = [((step_count, query_count), f32), (queries.shape, bf16), (fifo.shape, bf16)]
             args += [loss, query_grad, fifo, fifo_head[None], *tops]
         kernel = functools.partial(late_kernel, step, not small)
         loss, query_grad, fifo, *rest, zero = call(kernel, outs + [(total.shape, f32)], *args)
-        line = rest[0] if more else line
         mine, other = reduce_far(total, zero)
-        table, line, *rest = call(
-            functools.partial(update_kernel, score_scale / grad_scale),
-            [(table.shape, f32), (line.shape, f32)] + [(table.shape, f32)] * more,
-            jnp.full((1, 1), side),
-            mine,
-            other,
-            table,
-            line,
-        )
+        scale = score_scale / grad_scale
         if more:
+            kernel, outs = functools.partial(update_kernel, scale), half_shard + half_shard[:1]
+            *near, unit = call(kernel, outs, mine, *rest[:2])
+            *far, far_unit = call(kernel, outs, other, *rest[2:])
             queue, zero = next_queue(queue, mine[part_rows:])
-            parts = gather_whole(rest[0].astype(f16))
+            parts = gather_whole(unit.astype(f16), far_unit.astype(f16))
+        else:
+            outs = [(table.shape, f32), (line.shape, f32)]
+            args = [jnp.full((1, 1), side), mine, other, *near, *far]
+            table, line = call(functools.partial(finish_kernel, scale), outs, *args)
 
     return (loss, query_grad, table, line[0], fifo)
 

time: 70.3 us -> 69.6 us (0.990)
  waiting for transfers between devices: 30.3 us -> 27.6 us
  starting transfers between devices: 24.6 us -> 26.1 us
    ppermute x20 -> x23, waiting for transfers between devices: 18.6 us -> 15.9 us  [flip(): lax.ppermute(piece, ('batch', 'table'), [(i ^ mask, i) for i in range(cou...]
    ppermute x20 -> x23, starting transfers between devices: 18.6 us -> 20.1 us  [flip(): lax.ppermute(piece, ('batch', 'table'), [(i ^ mask, i) for i in range(cou...]
    pallas_call x11 -> x12, Pallas kernels: 10.6 us -> 11 us  [call(): pl.pallas_call(kernel, out_shape=[jax.ShapeDtypeStruct(shape, dtype) for...]
  transfers between devices with their start and end apart: 23 -> 26, of which waited for: 20 -> 18; matrix products, arithmetic and copies ran while one was open for 3% -> 3% of each run, Pallas kernels for 9% -> 11%
where the time goes in v6:
time: 69.6 us; the launch traced here: 69.4 us
  waiting for transfers between devices  27.6 us (40%)
  starting transfers between devices  26.1 us (38%)
  Pallas kernels  11 us (16%)
  local copies, waits for them, and re-layouts  1.73 us (2%)
  between operations  1.57 us (2%)
  other arithmetic  1.41 us (2%)
    ppermute x23, starting transfers between devices, flip(): lax.ppermute(piece, ('batch', 'table'), [(i ^ mask, i) for i in range(cou...  20.1 us
    ppermute x23, waiting for transfers between devices, flip(): lax.ppermute(piece, ('batch', 'table'), [(i ^ mask, i) for i in range(cou...  15.9 us
    pallas_call x12, Pallas kernels, call(): pl.pallas_call(kernel, out_shape=[jax.ShapeDtypeStruct(shape, dtype) for...  11 us
    ppermute x2, waiting for transfers between devices, turned(): found.append(lax.ppermute(piece, 'batch', pairs))  7.85 us
    all_to_all x1, starting transfers between devices, per_device(): lax.all_to_all(queue, ('batch', 'table'), 0, 0, tiled=True)  5.03 us
    all_to_all x1, waiting for transfers between devices, per_device(): lax.all_to_all(queue, ('batch', 'table'), 0, 0, tiled=True)  3.86 us
  transfers between devices with their start and end apart: 26, of which 18 were waited for; matrix products, arithmetic and copies ran while one was open for 3% of the time, Pallas kernels for 11%

profile of v6, /device:TPU:0, one launch (start us, length us, event | category | flops | bytes accessed | tf_op | source)
XLA Modules:
  0.0 69.4 jit_solution(13785211487953925379)
XLA Ops:
  0.6 3.0 %collective-permute-start = (f32[480,128]{1,0:T(8,128)}, f32[480,128]{1,0:T(8,128)S(1)}, u32[]{:S(2)}, u32[]{:S(2)}) collective-permute-start(f32[480,128]{1,0:T(8,128)} %refs_0_.3), channel_id=1, source_target_pairs={{2,0},{3,1},{0,2},{1,3},{6,4},{7,5},{4,6},{5,7},{10,8},{11,9},{8,1... | collective-permute-start | bytes 737288 | tf_op jit(solution)/shard_map/ppermute | solution.py:40
  5.0 5.0 %all-to-all-start = ((bf16[32,8,128]{2,1,0:T(8,128)(2,1)}), bf16[32,8,128]{2,1,0:T(8,128)(2,1)S(1)}, u32[]{:S(2)}, u32[]{:S(2)}) async-start(bf16[32,8,128]{2,1,0:T(8,128)(2,1)} %broadcast_in_dim.67), calls=%async_computation | async-start | bytes 131072 | tf_op jit(solution)/shard_map/all_to_all | solution.py:404
  11.7 1.9 %shard_map.110 = (f32[512,128]{1,0:T(8,128)S(1)}, f32[512,128]{1,0:T(8,128)S(1)}, f32[512,1]{1,0:T(8,128)}, f32[8,128]{1,0:T(8,128)S(1)}) custom-call(bf16[2,512,128]{2,1,0:T(8,128)(2,1)S(1)} %copy-done, s32[1,512]{1,0:T(1,128)S(1)} %get-tuple-element.84.line.found_line, f32[512,1]{1,0:T(8,128)S(1)} %broadcast_in_dim.64.negatives, s32[1,1]{1,0:T(1,128)} %bitcast.3.refs_0_, ...), custom_call_target="tpu_custom_call" | custom-call | tf_op jit(solution)/shard_map/pallas_call | solution.py:307
  13.6 3.9 %all-to-all-done = bf16[32,8,128]{2,1,0:T(8,128)(2,1)S(1)} async-done(((bf16[32,8,128]{2,1,0:T(8,128)(2,1)}), bf16[32,8,128]{2,1,0:T(8,128)(2,1)S(1)}, u32[]{:S(2)}, u32[]{:S(2)}) %all-to-all-start) | async-done | bytes 65568 | tf_op jit(solution)/shard_map/all_to_all | solution.py:404
  18.9 1.0 %collective-permute-done.3 = bf16[992,128]{1,0:T(8,128)(2,1)S(1)} collective-permute-done((bf16[992,128]{1,0:T(8,128)(2,1)S(1)}, bf16[992,128]{1,0:T(8,128)(2,1)S(1)}, u32[]{:S(2)}, u32[]{:S(2)}) %collective-permute-start.3) | collective-permute-done | bytes 253984 | tf_op jit(solution)/shard_map/ppermute | solution.py:40
  20.7 1.3 %collective-permute-start.5 = (f16[248,128]{1,0:T(8,128)(2,1)S(1)}, f16[248,128]{1,0:T(8,128)(2,1)S(1)}, u32[]{:S(2)}, u32[]{:S(2)}) collective-permute-start(f16[248,128]{1,0:T(8,128)(2,1)S(1)} %get-tuple-element.91), channel_id=1, source_target_pairs={{2,0},{3,1},{0,2},{1,3},{6,4},{7,5},{4,6},{5,7},{10,8},{11,9},{8,1... | collective-permute-start | bytes 190472 | tf_op jit(solution)/shard_map/ppermute | solution.py:40
  22.1 1.4 %collective-permute-start.4 = (f16[248,128]{1,0:T(8,128)(2,1)S(1)}, f16[248,128]{1,0:T(8,128)(2,1)S(1)}, u32[]{:S(2)}, u32[]{:S(2)}) collective-permute-start(f16[248,128]{1,0:T(8,128)(2,1)S(1)} %get-tuple-element.89), channel_id=1, source_target_pairs={{4,0},{5,1},{6,2},{7,3},{0,4},{1,5},{2,6},{3,7},{12,8},{13,9},{14,... | collective-permute-start | bytes 190472 | tf_op jit(solution)/shard_map/ppermute | solution.py:40
  23.5 2.2 %collective-permute-done.6 = f16[248,128]{1,0:T(8,128)(2,1)S(1)} collective-permute-done((f16[248,128]{1,0:T(8,128)(2,1)S(1)}, f16[248,128]{1,0:T(8,128)(2,1)S(1)}, u32[]{:S(2)}, u32[]{:S(2)}) %collective-permute-start.6) | collective-permute-done | bytes 63520 | tf_op jit(solution)/shard_map/ppermute | solution.py:40
  28.6 3.7 %collective-permute-done.7 = f16[248,128]{1,0:T(8,128)(2,1)S(1)} collective-permute-done((f16[248,128]{1,0:T(8,128)(2,1)S(1)}, f16[248,128]{1,0:T(8,128)(2,1)S(1)}, u32[]{:S(2)}, u32[]{:S(2)}) %collective-permute-start.7) | collective-permute-done | bytes 63520 | tf_op jit(solution)/shard_map/ppermute | solution.py:51
  32.4 2.8 %collective-permute-start.10 = (f16[248,128]{1,0:T(8,128)(2,1)S(1)}, f16[248,128]{1,0:T(8,128)(2,1)S(1)}, u32[]{:S(2)}, u32[]{:S(2)}) collective-permute-start(f16[248,128]{1,0:T(8,128)(2,1)S(1)} %add_convert_fusion.1), channel_id=1, source_target_pairs={{12,0},{13,1},{14,2},{15,3},{8,4},{9,5},{10,6},{11,7},{4,8},{5,9},... | collective-permute-start | bytes 190472 | tf_op jit(solution)/shard_map/ppermute | solution.py:40
  38.1 1.4 %collective-permute-done.9 = f16[248,128]{1,0:T(8,128)(2,1)S(1)} collective-permute-done((f16[248,128]{1,0:T(8,128)(2,1)S(1)}, f16[248,128]{1,0:T(8,128)(2,1)S(1)}, u32[]{:S(2)}, u32[]{:S(2)}) %collective-permute-start.9) | collective-permute-done | bytes 63520 | tf_op jit(solution)/shard_map/ppermute | solution.py:40
  42.2 2.1 %collective-permute-done.12 = f16[240,128]{1,0:T(8,128)(2,1)S(1)} collective-permute-done((f16[240,128]{1,0:T(8,128)(2,1)S(1)}, f16[240,128]{1,0:T(8,128)(2,1)S(1)}, u32[]{:S(2)}, u32[]{:S(2)}) %collective-permute-start.12) | collective-permute-done | bytes 61472 | tf_op jit(solution)/shard_map/ppermute | solution.py:40
  44.4 1.1 %shard_map.117 = (f32[512,128]{1,0:T(8,128)S(1)}, f32[512,128]{1,0:T(8,128)S(1)}, f32[512,1]{1,0:T(8,128)S(1)}) custom-call(bf16[2,512,128]{2,1,0:T(8,128)(2,1)S(1)} %copy-done, s32[1,512]{1,0:T(1,128)S(1)} %multiply_add_fusion.1.line.found_line, bf16[256,128]{1,0:T(8,128)(2,1)S(1)} %get-tuple-element.48.negatives, ...), custom_call_target="tpu_custom_call" | custom-call | tf_op jit(solution)/shard_map/pallas_call | solution.py:307
  45.6 1.2 %shard_map.118 = (bf16[992,128]{1,0:T(8,128)(2,1)S(1)}, bf16[512,128]{1,0:T(8,128)(2,1)S(1)}, f32[512,128]{1,0:T(8,128)S(1)}, f32[8,128]{1,0:T(8,128)S(1)}) custom-call(f32[512,128]{1,0:T(8,128)S(1)} %get-tuple-element.56.found, s32[1,512]{1,0:T(1,128)S(1)} %multiply_add_fusion.1.line.found_line, s32[1,512]{1,0:T(1,128)S(1)} %get-tuple-element.92.line, ...), custom_call_target="tpu_custom_call" | custom-call | tf_op jit(solution)/shard_map/pallas_call | solution.py:307
  49.2 1.3 %collective-permute-start.20 = (f16[248,128]{1,0:T(8,128)(2,1)S(1)}, f16[248,128]{1,0:T(8,128)(2,1)S(1)}, u32[]{:S(2)}, u32[]{:S(2)}) collective-permute-start(f16[248,128]{1,0:T(8,128)(2,1)S(1)} %get-tuple-element.87), channel_id=1, source_target_pairs={{6,0},{7,1},{4,2},{5,3},{2,4},{3,5},{0,6},{1,7},{14,8},{15,9},{12,... | collective-permute-start | bytes 190472 | tf_op jit(solution)/shard_map/ppermute | solution.py:40
  50.5 1.6 %collective-permute-start.19 = (f16[248,128]{1,0:T(8,128)(2,1)S(1)}, f16[248,128]{1,0:T(8,128)(2,1)S(1)}, u32[]{:S(2)}, u32[]{:S(2)}) collective-permute-start(f16[248,128]{1,0:T(8,128)(2,1)S(1)} %get-tuple-element.86), channel_id=1, source_target_pairs={{2,0},{3,1},{0,2},{1,3},{6,4},{7,5},{4,6},{5,7},{10,8},{11,9},{8,1... | collective-permute-start | bytes 190472 | tf_op jit(solution)/shard_map/ppermute | solution.py:40
  52.9 1.9 %collective-permute-done.20 = f16[248,128]{1,0:T(8,128)(2,1)S(1)} collective-permute-done((f16[248,128]{1,0:T(8,128)(2,1)S(1)}, f16[248,128]{1,0:T(8,128)(2,1)S(1)}, u32[]{:S(2)}, u32[]{:S(2)}) %collective-permute-start.20) | collective-permute-done | bytes 63520 | tf_op jit(solution)/shard_map/ppermute | solution.py:40
  55.8 1.5 %shard_map.120 = (f32[2,512]{1,0:T(2,128)}, bf16[2,512,128]{2,1,0:T(8,128)(2,1)}, bf16[8,128]{1,0:T(8,128)(2,1)}, f32[248,128]{1,0:T(8,128)S(1)}) custom-call(bf16[2,512,128]{2,1,0:T(8,128)(2,1)S(1)} %copy-done, f32[512,128]{1,0:T(8,128)S(1)} %get-tuple-element.59.item, bf16[256,128]{1,0:T(8,128)(2,1)S(1)} %get-tuple-element.48.negatives, ...), custom_call_target="tpu_custom_call" | custom-call | tf_op jit(solution)/shard_map/pallas_call | solution.py:307
  57.2 4.2 %collective-permute-done.21 = f16[248,128]{1,0:T(8,128)(2,1)S(1)} collective-permute-done((f16[248,128]{1,0:T(8,128)(2,1)S(1)}, f16[248,128]{1,0:T(8,128)(2,1)S(1)}, u32[]{:S(2)}, u32[]{:S(2)}) %collective-permute-start.21) | collective-permute-done | bytes 63520 | tf_op jit(solution)/shard_map/ppermute | solution.py:51
  61.7 2.1 %collective-permute-start.24 = (f16[248,128]{1,0:T(8,128)(2,1)S(1)}, f16[248,128]{1,0:T(8,128)(2,1)S(1)}, u32[]{:S(2)}, u32[]{:S(2)}) collective-permute-start(f16[248,128]{1,0:T(8,128)(2,1)S(1)} %add_convert_fusion), channel_id=1, source_target_pairs={{12,0},{13,1},{14,2},{15,3},{8,4},{9,5},{10,6},{11,7},{4,8},{5,9},... | collective-permute-start | bytes 190472 | tf_op jit(solution)/shard_map/ppermute | solution.py:40
  63.7 1.2 %collective-permute-start.23 = (f16[248,128]{1,0:T(8,128)(2,1)S(1)}, f16[248,128]{1,0:T(8,128)(2,1)S(1)}, u32[]{:S(2)}, u32[]{:S(2)}) collective-permute-start(f16[248,128]{1,0:T(8,128)(2,1)S(1)} %add_convert_fusion), channel_id=1, source_target_pairs={{4,0},{5,1},{6,2},{7,3},{0,4},{1,5},{2,6},{3,7},{12,8},{13,9},{14,... | collective-permute-start | bytes 190472 | tf_op jit(solution)/shard_map/ppermute | solution.py:40
  65.8 1.1 %collective-permute-done.24 = f16[248,128]{1,0:T(8,128)(2,1)S(1)} collective-permute-done((f16[248,128]{1,0:T(8,128)(2,1)S(1)}, f16[248,128]{1,0:T(8,128)(2,1)S(1)}, u32[]{:S(2)}, u32[]{:S(2)}) %collective-permute-start.24) | collective-permute-done | bytes 63520 | tf_op jit(solution)/shard_map/ppermute | solution.py:40
  66.8 1.2 %collective-permute-done.23 = f16[248,128]{1,0:T(8,128)(2,1)S(1)} collective-permute-done((f16[248,128]{1,0:T(8,128)(2,1)S(1)}, f16[248,128]{1,0:T(8,128)(2,1)S(1)}, u32[]{:S(2)}, u32[]{:S(2)}) %collective-permute-start.23) | collective-permute-done | bytes 63520 | tf_op jit(solution)/shard_map/ppermute | solution.py:40
  68.0 1.4 %shard_map.121 = (f32[480,128]{1,0:T(8,128)}, f32[1,480]{1,0:T(1,128)}) custom-call(s32[1,1]{1,0:T(1,128)} %bitcast.7.refs_1_.side, f32[248,128]{1,0:T(8,128)S(1)} %convert_add_fusion.1.mine, f32[248,128]{1,0:T(8,128)S(1)} %convert_add_fusion.other, f32[240,128]{1,0:T(8,128)S(1)} %get-tuple-element.70.table, f32[1,240]{1,0:T(1,128)S(1)} %get-tuple-element.71.line, ...), custom_call_target="tpu_custom_call" | custom-call | tf_op jit(solution)/shard_map/pallas_call | solution.py:307
  (82 shorter events, 18.6 us)
Async XLA Ops:
  0.6 9.4 %collective-permute-start = (f32[480,128]{1,0:T(8,128)}, f32[480,128]{1,0:T(8,128)S(1)}, u32[]{:S(2)}, u32[]{:S(2)}) collective-permute-start(f32[480,128]{1,0:T(8,128)} %refs_0_.3), channel_id=1, source_target_pairs={{2,0},{3,1},{0,2},{1,3},{6,4},{7,5},{4,6},{5,7},{10,8},{11,9},{8,1... | collective-permute-start | bytes 737288 | tf_op jit(solution)/shard_map/ppermute | solution.py:40
  3.6 7.5 %collective-permute-start.1 = (f32[480,128]{1,0:T(8,128)}, f32[480,128]{1,0:T(8,128)S(1)}, u32[]{:S(2)}, u32[]{:S(2)}) collective-permute-start(f32[480,128]{1,0:T(8,128)} %refs_0_.3), channel_id=1, source_target_pairs={{1,0},{0,1},{3,2},{2,3},{5,4},{4,5},{7,6},{6,7},{9,8},{8,9},{11,10... | collective-permute-start | bytes 737288 | tf_op jit(solution)/shard_map/ppermute | solution.py:40
  5.0 12.5 %all-to-all-start = ((bf16[32,8,128]{2,1,0:T(8,128)(2,1)}), bf16[32,8,128]{2,1,0:T(8,128)(2,1)S(1)}, u32[]{:S(2)}, u32[]{:S(2)}) async-start(bf16[32,8,128]{2,1,0:T(8,128)(2,1)} %broadcast_in_dim.67), calls=%async_computation | async-start | bytes 131072 | tf_op jit(solution)/shard_map/all_to_all | solution.py:404
  18.3 1.6 %collective-permute-start.3 = (bf16[992,128]{1,0:T(8,128)(2,1)S(1)}, bf16[992,128]{1,0:T(8,128)(2,1)S(1)}, u32[]{:S(2)}, u32[]{:S(2)}) collective-permute-start(bf16[992,128]{1,0:T(8,128)(2,1)S(1)} %get-tuple-element.45), channel_id=1, source_target_pairs={{1,0},{0,1},{3,2},{2,3},{5,4},{4,5},{7,6},{6,7},{9,8},{8,9},{11,10... | collective-permute-start | bytes 761864 | tf_op jit(solution)/shard_map/ppermute | solution.py:40
  19.9 5.7 %collective-permute-start.6 = (f16[248,128]{1,0:T(8,128)(2,1)S(1)}, f16[248,128]{1,0:T(8,128)(2,1)S(1)}, u32[]{:S(2)}, u32[]{:S(2)}) collective-permute-start(f16[248,128]{1,0:T(8,128)(2,1)S(1)} %get-tuple-element.90), channel_id=1, source_target_pairs={{6,0},{7,1},{4,2},{5,3},{2,4},{3,5},{0,6},{1,7},{14,8},{15,9},{12,... | collective-permute-start | bytes 190472 | tf_op jit(solution)/shard_map/ppermute | solution.py:40
  20.7 5.0 %collective-permute-start.5 = (f16[248,128]{1,0:T(8,128)(2,1)S(1)}, f16[248,128]{1,0:T(8,128)(2,1)S(1)}, u32[]{:S(2)}, u32[]{:S(2)}) collective-permute-start(f16[248,128]{1,0:T(8,128)(2,1)S(1)} %get-tuple-element.91), channel_id=1, source_target_pairs={{2,0},{3,1},{0,2},{1,3},{6,4},{7,5},{4,6},{5,7},{10,8},{11,9},{8,1... | collective-permute-start | bytes 190472 | tf_op jit(solution)/shard_map/ppermute | solution.py:40
  22.1 4.3 %collective-permute-start.4 = (f16[248,128]{1,0:T(8,128)(2,1)S(1)}, f16[248,128]{1,0:T(8,128)(2,1)S(1)}, u32[]{:S(2)}, u32[]{:S(2)}) collective-permute-start(f16[248,128]{1,0:T(8,128)(2,1)S(1)} %get-tuple-element.89), channel_id=1, source_target_pairs={{4,0},{5,1},{6,2},{7,3},{0,4},{1,5},{2,6},{3,7},{12,8},{13,9},{14,... | collective-permute-start | bytes 190472 | tf_op jit(solution)/shard_map/ppermute | solution.py:40
  26.4 5.9 %collective-permute-start.7 = (f16[248,128]{1,0:T(8,128)(2,1)S(1)}, f16[248,128]{1,0:T(8,128)(2,1)S(1)}, u32[]{:S(2)}, u32[]{:S(2)}) collective-permute-start(f16[248,128]{1,0:T(8,128)(2,1)S(1)} %fusion.13), channel_id=1, source_target_pairs={{16,0},{20,4},{24,8},{28,12},{0,16},{4,20},{8,24},{12,28},{17,1},{... | collective-permute-start | bytes 190472 | tf_op jit(solution)/shard_map/ppermute | solution.py:51
  32.3 4.3 %collective-permute-start.8 = (f16[248,128]{1,0:T(8,128)(2,1)S(1)}, f16[248,128]{1,0:T(8,128)(2,1)S(1)}, u32[]{:S(2)}, u32[]{:S(2)}) collective-permute-start(f16[248,128]{1,0:T(8,128)(2,1)S(1)} %add_convert_fusion.1), channel_id=1, source_target_pairs={{8,0},{9,1},{10,2},{11,3},{12,4},{13,5},{14,6},{15,7},{0,8},{1,9},... | collective-permute-start | bytes 190472 | tf_op jit(solution)/shard_map/ppermute | solution.py:40
  32.4 5.7 %collective-permute-start.10 = (f16[248,128]{1,0:T(8,128)(2,1)S(1)}, f16[248,128]{1,0:T(8,128)(2,1)S(1)}, u32[]{:S(2)}, u32[]{:S(2)}) collective-permute-start(f16[248,128]{1,0:T(8,128)(2,1)S(1)} %add_convert_fusion.1), channel_id=1, source_target_pairs={{12,0},{13,1},{14,2},{15,3},{8,4},{9,5},{10,6},{11,7},{4,8},{5,9},... | collective-permute-start | bytes 190472 | tf_op jit(solution)/shard_map/ppermute | solution.py:40
  35.3 4.2 %collective-permute-start.9 = (f16[248,128]{1,0:T(8,128)(2,1)S(1)}, f16[248,128]{1,0:T(8,128)(2,1)S(1)}, u32[]{:S(2)}, u32[]{:S(2)}) collective-permute-start(f16[248,128]{1,0:T(8,128)(2,1)S(1)} %add_convert_fusion.1), channel_id=1, source_target_pairs={{4,0},{5,1},{6,2},{7,3},{0,4},{1,5},{2,6},{3,7},{12,8},{13,9},{14,... | collective-permute-start | bytes 190472 | tf_op jit(solution)/shard_map/ppermute | solution.py:40
  37.1 4.5 %collective-permute-start.11 = (f16[240,128]{1,0:T(8,128)(2,1)S(1)}, f16[240,128]{1,0:T(8,128)(2,1)S(1)}, u32[]{:S(2)}, u32[]{:S(2)}) collective-permute-start(f16[240,128]{1,0:T(8,128)(2,1)S(1)} %get-tuple-element.83), channel_id=1, source_target_pairs={{2,0},{3,1},{0,2},{1,3},{6,4},{7,5},{4,6},{5,7},{10,8},{11,9},{8,1... | collective-permute-start | bytes 184328 | tf_op jit(solution)/shard_map/ppermute | solution.py:40
  37.8 6.5 %collective-permute-start.13 = (f16[240,128]{1,0:T(8,128)(2,1)S(1)}, f16[240,128]{1,0:T(8,128)(2,1)S(1)}, u32[]{:S(2)}, u32[]{:S(2)}) collective-permute-start(f16[240,128]{1,0:T(8,128)(2,1)S(1)} %get-tuple-element.83), channel_id=1, source_target_pairs={{1,0},{0,1},{3,2},{2,3},{5,4},{4,5},{7,6},{6,7},{9,8},{8,9},{11,10... | collective-permute-start | bytes 184328 | tf_op jit(solution)/shard_map/ppermute | solution.py:40
  40.0 4.3 %collective-permute-start.12 = (f16[240,128]{1,0:T(8,128)(2,1)S(1)}, f16[240,128]{1,0:T(8,128)(2,1)S(1)}, u32[]{:S(2)}, u32[]{:S(2)}) collective-permute-start(f16[240,128]{1,0:T(8,128)(2,1)S(1)} %get-tuple-element.81), channel_id=1, source_target_pairs={{2,0},{3,1},{0,2},{1,3},{6,4},{7,5},{4,6},{5,7},{10,8},{11,9},{8,1... | collective-permute-start | bytes 184328 | tf_op jit(solution)/shard_map/ppermute | solution.py:40
  40.5 3.9 %collective-permute-start.14 = (f16[240,128]{1,0:T(8,128)(2,1)S(1)}, f16[240,128]{1,0:T(8,128)(2,1)S(1)}, u32[]{:S(2)}, u32[]{:S(2)}) collective-permute-start(f16[240,128]{1,0:T(8,128)(2,1)S(1)} %get-tuple-element.81), channel_id=1, source_target_pairs={{1,0},{0,1},{3,2},{2,3},{5,4},{4,5},{7,6},{6,7},{9,8},{8,9},{11,10... | collective-permute-start | bytes 184328 | tf_op jit(solution)/shard_map/ppermute | solution.py:40
  41.6 2.7 %collective-permute-start.15 = (f16[240,128]{1,0:T(8,128)(2,1)S(1)}, f16[240,128]{1,0:T(8,128)(2,1)S(1)}, u32[]{:S(2)}, u32[]{:S(2)}) collective-permute-start(f16[240,128]{1,0:T(8,128)(2,1)S(1)} %collective-permute-done.11), channel_id=1, source_target_pairs={{1,0},{0,1},{3,2},{2,3},{5,4},{4,5},{7,6},{6,7},{9,8},{8,9},{11,10... | collective-permute-start | bytes 184328 | tf_op jit(solution)/shard_map/ppermute | solution.py:40
  46.7 1.7 %collective-permute-start.17 = (bf16[992,128]{1,0:T(8,128)(2,1)S(1)}, bf16[992,128]{1,0:T(8,128)(2,1)S(1)}, u32[]{:S(2)}, u32[]{:S(2)}) collective-permute-start(bf16[992,128]{1,0:T(8,128)(2,1)S(1)} %get-tuple-element.61), channel_id=1, source_target_pairs={{1,0},{0,1},{3,2},{2,3},{5,4},{4,5},{7,6},{6,7},{9,8},{8,9},{11,10... | collective-permute-start | bytes 761864 | tf_op jit(solution)/shard_map/ppermute | solution.py:40
  48.5 4.4 %collective-permute-start.18 = (f16[248,128]{1,0:T(8,128)(2,1)S(1)}, f16[248,128]{1,0:T(8,128)(2,1)S(1)}, u32[]{:S(2)}, u32[]{:S(2)}) collective-permute-start(f16[248,128]{1,0:T(8,128)(2,1)S(1)} %get-tuple-element.88), channel_id=1, source_target_pairs={{4,0},{5,1},{6,2},{7,3},{0,4},{1,5},{2,6},{3,7},{12,8},{13,9},{14,... | collective-permute-start | bytes 190472 | tf_op jit(solution)/shard_map/ppermute | solution.py:40
  49.2 5.6 %collective-permute-start.20 = (f16[248,128]{1,0:T(8,128)(2,1)S(1)}, f16[248,128]{1,0:T(8,128)(2,1)S(1)}, u32[]{:S(2)}, u32[]{:S(2)}) collective-permute-start(f16[248,128]{1,0:T(8,128)(2,1)S(1)} %get-tuple-element.87), channel_id=1, source_target_pairs={{6,0},{7,1},{4,2},{5,3},{2,4},{3,5},{0,6},{1,7},{14,8},{15,9},{12,... | collective-permute-start | bytes 190472 | tf_op jit(solution)/shard_map/ppermute | solution.py:40
  50.5 5.0 %collective-permute-start.19 = (f16[248,128]{1,0:T(8,128)(2,1)S(1)}, f16[248,128]{1,0:T(8,128)(2,1)S(1)}, u32[]{:S(2)}, u32[]{:S(2)}) collective-permute-start(f16[248,128]{1,0:T(8,128)(2,1)S(1)} %get-tuple-element.86), channel_id=1, source_target_pairs={{2,0},{3,1},{0,2},{1,3},{6,4},{7,5},{4,6},{5,7},{10,8},{11,9},{8,1... | collective-permute-start | bytes 190472 | tf_op jit(solution)/shard_map/ppermute | solution.py:40
  55.5 5.9 %collective-permute-start.21 = (f16[248,128]{1,0:T(8,128)(2,1)S(1)}, f16[248,128]{1,0:T(8,128)(2,1)S(1)}, u32[]{:S(2)}, u32[]{:S(2)}) collective-permute-start(f16[248,128]{1,0:T(8,128)(2,1)S(1)} %fusion.6), channel_id=1, source_target_pairs={{16,0},{20,4},{24,8},{28,12},{0,16},{4,20},{8,24},{12,28},{17,1},{... | collective-permute-start | bytes 190472 | tf_op jit(solution)/shard_map/ppermute | solution.py:51
  61.4 4.3 %collective-permute-start.22 = (f16[248,128]{1,0:T(8,128)(2,1)S(1)}, f16[248,128]{1,0:T(8,128)(2,1)S(1)}, u32[]{:S(2)}, u32[]{:S(2)}) collective-permute-start(f16[248,128]{1,0:T(8,128)(2,1)S(1)} %add_convert_fusion), channel_id=1, source_target_pairs={{8,0},{9,1},{10,2},{11,3},{12,4},{13,5},{14,6},{15,7},{0,8},{1,9},... | collective-permute-start | bytes 190472 | tf_op jit(solution)/shard_map/ppermute | solution.py:40
  61.7 5.1 %collective-permute-start.24 = (f16[248,128]{1,0:T(8,128)(2,1)S(1)}, f16[248,128]{1,0:T(8,128)(2,1)S(1)}, u32[]{:S(2)}, u32[]{:S(2)}) collective-permute-start(f16[248,128]{1,0:T(8,128)(2,1)S(1)} %add_convert_fusion), channel_id=1, source_target_pairs={{12,0},{13,1},{14,2},{15,3},{8,4},{9,5},{10,6},{11,7},{4,8},{5,9},... | collective-permute-start | bytes 190472 | tf_op jit(solution)/shard_map/ppermute | solution.py:40
  63.7 4.2 %collective-permute-start.23 = (f16[248,128]{1,0:T(8,128)(2,1)S(1)}, f16[248,128]{1,0:T(8,128)(2,1)S(1)}, u32[]{:S(2)}, u32[]{:S(2)}) collective-permute-start(f16[248,128]{1,0:T(8,128)(2,1)S(1)} %add_convert_fusion), channel_id=1, source_target_pairs={{4,0},{5,1},{6,2},{7,3},{0,4},{1,5},{2,6},{3,7},{12,8},{13,9},{14,... | collective-permute-start | bytes 190472 | tf_op jit(solution)/shard_map/ppermute | solution.py:40
  (8 other events, 31.7 us)

commit v7 on v6

--- a/solution.py
+++ b/solution.py
@@ -179,7 +179,7 @@
         told[0][...] = told_block(*ids, *told[0].shape)
 
 
-def main_kernel(first, count, found, found_line, line, queries, negatives, *refs):
+def main_kernel(first, count, stride, found, found_line, line, queries, negatives, *refs):
     blocks, (told, sent, rows, unit, top) = refs[:count], refs[count:]
     item = found[...]
     if blocks:
@@ -195,21 +195,21 @@
     weight = jnp.exp(score_scale * cosine)
     lack = weight / (weight + sums) - 1.0
     rows[...] = (lack * (query - item * cosine)).astype(bf16)
-    dense(sent.shape[0], line, rows, told, sent)
-
-
-def dense(first, line, rows, told, out):
+    dense(sent.shape[0], stride, line, rows, told, sent)
+
+
+def dense(first, stride, line, rows, told, out):
     half, count = out.shape[0], told.shape[0]
     chosen = one_hot(line[...], first, half, False)
     found = jnp.dot(chosen, rows[...], preferred_element_type=f32)
     pieces = []
-    for start in range(0, half, half // 4):
-        pieces += [found[start : start + half // 4 - count], told[...]]
+    for start in range(0, half, stride):
+        pieces += [found[start : start + stride - count], told[...]]
     out[...] = jnp.concatenate(pieces).astype(out.dtype)
 
 
-def kept_kernel(line, rows, told, out):
-    dense(0, line, rows, told, out)
+def kept_kernel(stride, line, rows, told, out):
+    dense(0, stride, line, rows, told, out)
 
 
 def widen(line):
@@ -436,7 +436,7 @@
         if step == 0:
             told = own[0] if own else own_told()
         sent, rows, unit, top = call(
-            functools.partial(main_kernel, last_place, len(parts[split:])),
+            functools.partial(main_kernel, last_place, len(parts[split:]), stride),
             [((half_rows, width), bf16), (matrix, bf16), (matrix, f32), ((8, width), f32)],
             found,
             found_at[None, :],
@@ -447,7 +447,8 @@
             told,
         )
         tops.append(top)
-        (kept,) = call(kept_kernel, [((half_rows, width), f32)], places[None, :], rows, told)
+        kernel = functools.partial(kept_kernel, stride)
+        (kept,) = call(kernel, [((half_rows, width), f32)], places[None, :], rows, told)
         sent = (grad_scale * sent).astype(bf16)
         kept = grad_scale * kept
         for mask in masks[:1:-1]:

time: 69.6 us -> 69.6 us (level)
  no operation moved by 1% of the time
where the time goes in v7:
time: 69.6 us; the launch traced here: 69.4 us
  waiting for transfers between devices  27.6 us (40%)
  starting transfers between devices  26.1 us (38%)
  Pallas kernels  11 us (16%)
  local copies, waits for them, and re-layouts  1.73 us (2%)
  between operations  1.57 us (2%)
  other arithmetic  1.41 us (2%)
    ppermute x23, starting transfers between devices, flip(): lax.ppermute(piece, ('batch', 'table'), [(i ^ mask, i) for i in range(cou...  20.1 us
    ppermute x23, waiting for transfers between devices, flip(): lax.ppermute(piece, ('batch', 'table'), [(i ^ mask, i) for i in range(cou...  15.9 us
    pallas_call x12, Pallas kernels, call(): pl.pallas_call(kernel, out_shape=[jax.ShapeDtypeStruct(shape, dtype) for...  11 us
    ppermute x2, waiting for transfers between devices, turned(): found.append(lax.ppermute(piece, 'batch', pairs))  7.85 us
    all_to_all x1, starting transfers between devices, per_device(): lax.all_to_all(queue, ('batch', 'table'), 0, 0, tiled=True)  5.03 us
    all_to_all x1, waiting for transfers between devices, per_device(): lax.all_to_all(queue, ('batch', 'table'), 0, 0, tiled=True)  3.86 us
  transfers between devices with their start and end apart: 26, of which 18 were waited for; matrix products, arithmetic and copies ran while one was open for 3% of the time, Pallas kernels for 11%

profile of v7, /device:TPU:0, one launch (start us, length us, event | category | flops | bytes accessed | tf_op | source)
XLA Modules:
  0.0 69.4 jit_solution(13785211487953925379)
XLA Ops:
  0.6 3.0 %collective-permute-start = (f32[480,128]{1,0:T(8,128)}, f32[480,128]{1,0:T(8,128)S(1)}, u32[]{:S(2)}, u32[]{:S(2)}) collective-permute-start(f32[480,128]{1,0:T(8,128)} %refs_0_.3), channel_id=1, source_target_pairs={{2,0},{3,1},{0,2},{1,3},{6,4},{7,5},{4,6},{5,7},{10,8},{11,9},{8,1... | collective-permute-start | bytes 737288 | tf_op jit(solution)/shard_map/ppermute | solution.py:40
  5.0 5.0 %all-to-all-start = ((bf16[32,8,128]{2,1,0:T(8,128)(2,1)}), bf16[32,8,128]{2,1,0:T(8,128)(2,1)S(1)}, u32[]{:S(2)}, u32[]{:S(2)}) async-start(bf16[32,8,128]{2,1,0:T(8,128)(2,1)} %broadcast_in_dim.67), calls=%async_computation | async-start | bytes 131072 | tf_op jit(solution)/shard_map/all_to_all | solution.py:404
  11.7 1.9 %shard_map.110 = (f32[512,128]{1,0:T(8,128)S(1)}, f32[512,128]{1,0:T(8,128)S(1)}, f32[512,1]{1,0:T(8,128)}, f32[8,128]{1,0:T(8,128)S(1)}) custom-call(bf16[2,512,128]{2,1,0:T(8,128)(2,1)S(1)} %copy-done, s32[1,512]{1,0:T(1,128)S(1)} %get-tuple-element.84.line.found_line, f32[512,1]{1,0:T(8,128)S(1)} %broadcast_in_dim.64.negatives, s32[1,1]{1,0:T(1,128)} %bitcast.3.refs_0_, ...), custom_call_target="tpu_custom_call" | custom-call | tf_op jit(solution)/shard_map/pallas_call | solution.py:307
  13.6 3.9 %all-to-all-done = bf16[32,8,128]{2,1,0:T(8,128)(2,1)S(1)} async-done(((bf16[32,8,128]{2,1,0:T(8,128)(2,1)}), bf16[32,8,128]{2,1,0:T(8,128)(2,1)S(1)}, u32[]{:S(2)}, u32[]{:S(2)}) %all-to-all-start) | async-done | bytes 65568 | tf_op jit(solution)/shard_map/all_to_all | solution.py:404
  18.9 1.0 %collective-permute-done.3 = bf16[992,128]{1,0:T(8,128)(2,1)S(1)} collective-permute-done((bf16[992,128]{1,0:T(8,128)(2,1)S(1)}, bf16[992,128]{1,0:T(8,128)(2,1)S(1)}, u32[]{:S(2)}, u32[]{:S(2)}) %collective-permute-start.3) | collective-permute-done | bytes 253984 | tf_op jit(solution)/shard_map/ppermute | solution.py:40
  20.7 1.3 %collective-permute-start.5 = (f16[248,128]{1,0:T(8,128)(2,1)S(1)}, f16[248,128]{1,0:T(8,128)(2,1)S(1)}, u32[]{:S(2)}, u32[]{:S(2)}) collective-permute-start(f16[248,128]{1,0:T(8,128)(2,1)S(1)} %get-tuple-element.91), channel_id=1, source_target_pairs={{2,0},{3,1},{0,2},{1,3},{6,4},{7,5},{4,6},{5,7},{10,8},{11,9},{8,1... | collective-permute-start | bytes 190472 | tf_op jit(solution)/shard_map/ppermute | solution.py:40
  22.1 1.4 %collective-permute-start.4 = (f16[248,128]{1,0:T(8,128)(2,1)S(1)}, f16[248,128]{1,0:T(8,128)(2,1)S(1)}, u32[]{:S(2)}, u32[]{:S(2)}) collective-permute-start(f16[248,128]{1,0:T(8,128)(2,1)S(1)} %get-tuple-element.89), channel_id=1, source_target_pairs={{4,0},{5,1},{6,2},{7,3},{0,4},{1,5},{2,6},{3,7},{12,8},{13,9},{14,... | collective-permute-start | bytes 190472 | tf_op jit(solution)/shard_map/ppermute | solution.py:40
  23.5 2.2 %collective-permute-done.6 = f16[248,128]{1,0:T(8,128)(2,1)S(1)} collective-permute-done((f16[248,128]{1,0:T(8,128)(2,1)S(1)}, f16[248,128]{1,0:T(8,128)(2,1)S(1)}, u32[]{:S(2)}, u32[]{:S(2)}) %collective-permute-start.6) | collective-permute-done | bytes 63520 | tf_op jit(solution)/shard_map/ppermute | solution.py:40
  28.6 3.7 %collective-permute-done.7 = f16[248,128]{1,0:T(8,128)(2,1)S(1)} collective-permute-done((f16[248,128]{1,0:T(8,128)(2,1)S(1)}, f16[248,128]{1,0:T(8,128)(2,1)S(1)}, u32[]{:S(2)}, u32[]{:S(2)}) %collective-permute-start.7) | collective-permute-done | bytes 63520 | tf_op jit(solution)/shard_map/ppermute | solution.py:51
  32.4 2.8 %collective-permute-start.10 = (f16[248,128]{1,0:T(8,128)(2,1)S(1)}, f16[248,128]{1,0:T(8,128)(2,1)S(1)}, u32[]{:S(2)}, u32[]{:S(2)}) collective-permute-start(f16[248,128]{1,0:T(8,128)(2,1)S(1)} %add_convert_fusion.1), channel_id=1, source_target_pairs={{12,0},{13,1},{14,2},{15,3},{8,4},{9,5},{10,6},{11,7},{4,8},{5,9},... | collective-permute-start | bytes 190472 | tf_op jit(solution)/shard_map/ppermute | solution.py:40
  38.1 1.4 %collective-permute-done.9 = f16[248,128]{1,0:T(8,128)(2,1)S(1)} collective-permute-done((f16[248,128]{1,0:T(8,128)(2,1)S(1)}, f16[248,128]{1,0:T(8,128)(2,1)S(1)}, u32[]{:S(2)}, u32[]{:S(2)}) %collective-permute-start.9) | collective-permute-done | bytes 63520 | tf_op jit(solution)/shard_map/ppermute | solution.py:40
  42.2 2.1 %collective-permute-done.12 = f16[240,128]{1,0:T(8,128)(2,1)S(1)} collective-permute-done((f16[240,128]{1,0:T(8,128)(2,1)S(1)}, f16[240,128]{1,0:T(8,128)(2,1)S(1)}, u32[]{:S(2)}, u32[]{:S(2)}) %collective-permute-start.12) | collective-permute-done | bytes 61472 | tf_op jit(solution)/shard_map/ppermute | solution.py:40
  44.4 1.1 %shard_map.117 = (f32[512,128]{1,0:T(8,128)S(1)}, f32[512,128]{1,0:T(8,128)S(1)}, f32[512,1]{1,0:T(8,128)S(1)}) custom-call(bf16[2,512,128]{2,1,0:T(8,128)(2,1)S(1)} %copy-done, s32[1,512]{1,0:T(1,128)S(1)} %multiply_add_fusion.1.line.found_line, bf16[256,128]{1,0:T(8,128)(2,1)S(1)} %get-tuple-element.48.negatives, ...), custom_call_target="tpu_custom_call" | custom-call | tf_op jit(solution)/shard_map/pallas_call | solution.py:307
  45.6 1.2 %shard_map.118 = (bf16[992,128]{1,0:T(8,128)(2,1)S(1)}, bf16[512,128]{1,0:T(8,128)(2,1)S(1)}, f32[512,128]{1,0:T(8,128)S(1)}, f32[8,128]{1,0:T(8,128)S(1)}) custom-call(f32[512,128]{1,0:T(8,128)S(1)} %get-tuple-element.56.found, s32[1,512]{1,0:T(1,128)S(1)} %multiply_add_fusion.1.line.found_line, s32[1,512]{1,0:T(1,128)S(1)} %get-tuple-element.92.line, ...), custom_call_target="tpu_custom_call" | custom-call | tf_op jit(solution)/shard_map/pallas_call | solution.py:307
  49.2 1.3 %collective-permute-start.20 = (f16[248,128]{1,0:T(8,128)(2,1)S(1)}, f16[248,128]{1,0:T(8,128)(2,1)S(1)}, u32[]{:S(2)}, u32[]{:S(2)}) collective-permute-start(f16[248,128]{1,0:T(8,128)(2,1)S(1)} %get-tuple-element.87), channel_id=1, source_target_pairs={{6,0},{7,1},{4,2},{5,3},{2,4},{3,5},{0,6},{1,7},{14,8},{15,9},{12,... | collective-permute-start | bytes 190472 | tf_op jit(solution)/shard_map/ppermute | solution.py:40
  50.5 1.6 %collective-permute-start.19 = (f16[248,128]{1,0:T(8,128)(2,1)S(1)}, f16[248,128]{1,0:T(8,128)(2,1)S(1)}, u32[]{:S(2)}, u32[]{:S(2)}) collective-permute-start(f16[248,128]{1,0:T(8,128)(2,1)S(1)} %get-tuple-element.86), channel_id=1, source_target_pairs={{2,0},{3,1},{0,2},{1,3},{6,4},{7,5},{4,6},{5,7},{10,8},{11,9},{8,1... | collective-permute-start | bytes 190472 | tf_op jit(solution)/shard_map/ppermute | solution.py:40
  52.9 1.9 %collective-permute-done.20 = f16[248,128]{1,0:T(8,128)(2,1)S(1)} collective-permute-done((f16[248,128]{1,0:T(8,128)(2,1)S(1)}, f16[248,128]{1,0:T(8,128)(2,1)S(1)}, u32[]{:S(2)}, u32[]{:S(2)}) %collective-permute-start.20) | collective-permute-done | bytes 63520 | tf_op jit(solution)/shard_map/ppermute | solution.py:40
  55.8 1.5 %shard_map.120 = (f32[2,512]{1,0:T(2,128)}, bf16[2,512,128]{2,1,0:T(8,128)(2,1)}, bf16[8,128]{1,0:T(8,128)(2,1)}, f32[248,128]{1,0:T(8,128)S(1)}) custom-call(bf16[2,512,128]{2,1,0:T(8,128)(2,1)S(1)} %copy-done, f32[512,128]{1,0:T(8,128)S(1)} %get-tuple-element.59.item, bf16[256,128]{1,0:T(8,128)(2,1)S(1)} %get-tuple-element.48.negatives, ...), custom_call_target="tpu_custom_call" | custom-call | tf_op jit(solution)/shard_map/pallas_call | solution.py:307
  57.2 4.2 %collective-permute-done.21 = f16[248,128]{1,0:T(8,128)(2,1)S(1)} collective-permute-done((f16[248,128]{1,0:T(8,128)(2,1)S(1)}, f16[248,128]{1,0:T(8,128)(2,1)S(1)}, u32[]{:S(2)}, u32[]{:S(2)}) %collective-permute-start.21) | collective-permute-done | bytes 63520 | tf_op jit(solution)/shard_map/ppermute | solution.py:51
  61.7 2.1 %collective-permute-start.24 = (f16[248,128]{1,0:T(8,128)(2,1)S(1)}, f16[248,128]{1,0:T(8,128)(2,1)S(1)}, u32[]{:S(2)}, u32[]{:S(2)}) collective-permute-start(f16[248,128]{1,0:T(8,128)(2,1)S(1)} %add_convert_fusion), channel_id=1, source_target_pairs={{12,0},{13,1},{14,2},{15,3},{8,4},{9,5},{10,6},{11,7},{4,8},{5,9},... | collective-permute-start | bytes 190472 | tf_op jit(solution)/shard_map/ppermute | solution.py:40
  63.7 1.2 %collective-permute-start.23 = (f16[248,128]{1,0:T(8,128)(2,1)S(1)}, f16[248,128]{1,0:T(8,128)(2,1)S(1)}, u32[]{:S(2)}, u32[]{:S(2)}) collective-permute-start(f16[248,128]{1,0:T(8,128)(2,1)S(1)} %add_convert_fusion), channel_id=1, source_target_pairs={{4,0},{5,1},{6,2},{7,3},{0,4},{1,5},{2,6},{3,7},{12,8},{13,9},{14,... | collective-permute-start | bytes 190472 | tf_op jit(solution)/shard_map/ppermute | solution.py:40
  65.8 1.1 %collective-permute-done.24 = f16[248,128]{1,0:T(8,128)(2,1)S(1)} collective-permute-done((f16[248,128]{1,0:T(8,128)(2,1)S(1)}, f16[248,128]{1,0:T(8,128)(2,1)S(1)}, u32[]{:S(2)}, u32[]{:S(2)}) %collective-permute-start.24) | collective-permute-done | bytes 63520 | tf_op jit(solution)/shard_map/ppermute | solution.py:40
  66.8 1.2 %collective-permute-done.23 = f16[248,128]{1,0:T(8,128)(2,1)S(1)} collective-permute-done((f16[248,128]{1,0:T(8,128)(2,1)S(1)}, f16[248,128]{1,0:T(8,128)(2,1)S(1)}, u32[]{:S(2)}, u32[]{:S(2)}) %collective-permute-start.23) | collective-permute-done | bytes 63520 | tf_op jit(solution)/shard_map/ppermute | solution.py:40
  68.0 1.4 %shard_map.121 = (f32[480,128]{1,0:T(8,128)}, f32[1,480]{1,0:T(1,128)}) custom-call(s32[1,1]{1,0:T(1,128)} %bitcast.7.refs_1_.side, f32[248,128]{1,0:T(8,128)S(1)} %convert_add_fusion.1.mine, f32[248,128]{1,0:T(8,128)S(1)} %convert_add_fusion.other, f32[240,128]{1,0:T(8,128)S(1)} %get-tuple-element.70.table, f32[1,240]{1,0:T(1,128)S(1)} %get-tuple-element.71.line, ...), custom_call_target="tpu_custom_call" | custom-call | tf_op jit(solution)/shard_map/pallas_call | solution.py:307
  (82 shorter events, 18.6 us)
Async XLA Ops:
  0.6 9.4 %collective-permute-start = (f32[480,128]{1,0:T(8,128)}, f32[480,128]{1,0:T(8,128)S(1)}, u32[]{:S(2)}, u32[]{:S(2)}) collective-permute-start(f32[480,128]{1,0:T(8,128)} %refs_0_.3), channel_id=1, source_target_pairs={{2,0},{3,1},{0,2},{1,3},{6,4},{7,5},{4,6},{5,7},{10,8},{11,9},{8,1... | collective-permute-start | bytes 737288 | tf_op jit(solution)/shard_map/ppermute | solution.py:40
  3.6 7.5 %collective-permute-start.1 = (f32[480,128]{1,0:T(8,128)}, f32[480,128]{1,0:T(8,128)S(1)}, u32[]{:S(2)}, u32[]{:S(2)}) collective-permute-start(f32[480,128]{1,0:T(8,128)} %refs_0_.3), channel_id=1, source_target_pairs={{1,0},{0,1},{3,2},{2,3},{5,4},{4,5},{7,6},{6,7},{9,8},{8,9},{11,10... | collective-permute-start | bytes 737288 | tf_op jit(solution)/shard_map/ppermute | solution.py:40
  5.0 12.5 %all-to-all-start = ((bf16[32,8,128]{2,1,0:T(8,128)(2,1)}), bf16[32,8,128]{2,1,0:T(8,128)(2,1)S(1)}, u32[]{:S(2)}, u32[]{:S(2)}) async-start(bf16[32,8,128]{2,1,0:T(8,128)(2,1)} %broadcast_in_dim.67), calls=%async_computation | async-start | bytes 131072 | tf_op jit(solution)/shard_map/all_to_all | solution.py:404
  18.3 1.6 %collective-permute-start.3 = (bf16[992,128]{1,0:T(8,128)(2,1)S(1)}, bf16[992,128]{1,0:T(8,128)(2,1)S(1)}, u32[]{:S(2)}, u32[]{:S(2)}) collective-permute-start(bf16[992,128]{1,0:T(8,128)(2,1)S(1)} %get-tuple-element.45), channel_id=1, source_target_pairs={{1,0},{0,1},{3,2},{2,3},{5,4},{4,5},{7,6},{6,7},{9,8},{8,9},{11,10... | collective-permute-start | bytes 761864 | tf_op jit(solution)/shard_map/ppermute | solution.py:40
  19.9 5.7 %collective-permute-start.6 = (f16[248,128]{1,0:T(8,128)(2,1)S(1)}, f16[248,128]{1,0:T(8,128)(2,1)S(1)}, u32[]{:S(2)}, u32[]{:S(2)}) collective-permute-start(f16[248,128]{1,0:T(8,128)(2,1)S(1)} %get-tuple-element.90), channel_id=1, source_target_pairs={{6,0},{7,1},{4,2},{5,3},{2,4},{3,5},{0,6},{1,7},{14,8},{15,9},{12,... | collective-permute-start | bytes 190472 | tf_op jit(solution)/shard_map/ppermute | solution.py:40
  20.7 5.0 %collective-permute-start.5 = (f16[248,128]{1,0:T(8,128)(2,1)S(1)}, f16[248,128]{1,0:T(8,128)(2,1)S(1)}, u32[]{:S(2)}, u32[]{:S(2)}) collective-permute-start(f16[248,128]{1,0:T(8,128)(2,1)S(1)} %get-tuple-element.91), channel_id=1, source_target_pairs={{2,0},{3,1},{0,2},{1,3},{6,4},{7,5},{4,6},{5,7},{10,8},{11,9},{8,1... | collective-permute-start | bytes 190472 | tf_op jit(solution)/shard_map/ppermute | solution.py:40
  22.1 4.3 %collective-permute-start.4 = (f16[248,128]{1,0:T(8,128)(2,1)S(1)}, f16[248,128]{1,0:T(8,128)(2,1)S(1)}, u32[]{:S(2)}, u32[]{:S(2)}) collective-permute-start(f16[248,128]{1,0:T(8,128)(2,1)S(1)} %get-tuple-element.89), channel_id=1, source_target_pairs={{4,0},{5,1},{6,2},{7,3},{0,4},{1,5},{2,6},{3,7},{12,8},{13,9},{14,... | collective-permute-start | bytes 190472 | tf_op jit(solution)/shard_map/ppermute | solution.py:40
  26.4 5.9 %collective-permute-start.7 = (f16[248,128]{1,0:T(8,128)(2,1)S(1)}, f16[248,128]{1,0:T(8,128)(2,1)S(1)}, u32[]{:S(2)}, u32[]{:S(2)}) collective-permute-start(f16[248,128]{1,0:T(8,128)(2,1)S(1)} %fusion.13), channel_id=1, source_target_pairs={{16,0},{20,4},{24,8},{28,12},{0,16},{4,20},{8,24},{12,28},{17,1},{... | collective-permute-start | bytes 190472 | tf_op jit(solution)/shard_map/ppermute | solution.py:51
  32.3 4.3 %collective-permute-start.8 = (f16[248,128]{1,0:T(8,128)(2,1)S(1)}, f16[248,128]{1,0:T(8,128)(2,1)S(1)}, u32[]{:S(2)}, u32[]{:S(2)}) collective-permute-start(f16[248,128]{1,0:T(8,128)(2,1)S(1)} %add_convert_fusion.1), channel_id=1, source_target_pairs={{8,0},{9,1},{10,2},{11,3},{12,4},{13,5},{14,6},{15,7},{0,8},{1,9},... | collective-permute-start | bytes 190472 | tf_op jit(solution)/shard_map/ppermute | solution.py:40
  32.4 5.7 %collective-permute-start.10 = (f16[248,128]{1,0:T(8,128)(2,1)S(1)}, f16[248,128]{1,0:T(8,128)(2,1)S(1)}, u32[]{:S(2)}, u32[]{:S(2)}) collective-permute-start(f16[248,128]{1,0:T(8,128)(2,1)S(1)} %add_convert_fusion.1), channel_id=1, source_target_pairs={{12,0},{13,1},{14,2},{15,3},{8,4},{9,5},{10,6},{11,7},{4,8},{5,9},... | collective-permute-start | bytes 190472 | tf_op jit(solution)/shard_map/ppermute | solution.py:40
  35.3 4.2 %collective-permute-start.9 = (f16[248,128]{1,0:T(8,128)(2,1)S(1)}, f16[248,128]{1,0:T(8,128)(2,1)S(1)}, u32[]{:S(2)}, u32[]{:S(2)}) collective-permute-start(f16[248,128]{1,0:T(8,128)(2,1)S(1)} %add_convert_fusion.1), channel_id=1, source_target_pairs={{4,0},{5,1},{6,2},{7,3},{0,4},{1,5},{2,6},{3,7},{12,8},{13,9},{14,... | collective-permute-start | bytes 190472 | tf_op jit(solution)/shard_map/ppermute | solution.py:40
  37.1 4.5 %collective-permute-start.11 = (f16[240,128]{1,0:T(8,128)(2,1)S(1)}, f16[240,128]{1,0:T(8,128)(2,1)S(1)}, u32[]{:S(2)}, u32[]{:S(2)}) collective-permute-start(f16[240,128]{1,0:T(8,128)(2,1)S(1)} %get-tuple-element.83), channel_id=1, source_target_pairs={{2,0},{3,1},{0,2},{1,3},{6,4},{7,5},{4,6},{5,7},{10,8},{11,9},{8,1... | collective-permute-start | bytes 184328 | tf_op jit(solution)/shard_map/ppermute | solution.py:40
  37.8 6.5 %collective-permute-start.13 = (f16[240,128]{1,0:T(8,128)(2,1)S(1)}, f16[240,128]{1,0:T(8,128)(2,1)S(1)}, u32[]{:S(2)}, u32[]{:S(2)}) collective-permute-start(f16[240,128]{1,0:T(8,128)(2,1)S(1)} %get-tuple-element.83), channel_id=1, source_target_pairs={{1,0},{0,1},{3,2},{2,3},{5,4},{4,5},{7,6},{6,7},{9,8},{8,9},{11,10... | collective-permute-start | bytes 184328 | tf_op jit(solution)/shard_map/ppermute | solution.py:40
  40.0 4.3 %collective-permute-start.12 = (f16[240,128]{1,0:T(8,128)(2,1)S(1)}, f16[240,128]{1,0:T(8,128)(2,1)S(1)}, u32[]{:S(2)}, u32[]{:S(2)}) collective-permute-start(f16[240,128]{1,0:T(8,128)(2,1)S(1)} %get-tuple-element.81), channel_id=1, source_target_pairs={{2,0},{3,1},{0,2},{1,3},{6,4},{7,5},{4,6},{5,7},{10,8},{11,9},{8,1... | collective-permute-start | bytes 184328 | tf_op jit(solution)/shard_map/ppermute | solution.py:40
  40.5 3.9 %collective-permute-start.14 = (f16[240,128]{1,0:T(8,128)(2,1)S(1)}, f16[240,128]{1,0:T(8,128)(2,1)S(1)}, u32[]{:S(2)}, u32[]{:S(2)}) collective-permute-start(f16[240,128]{1,0:T(8,128)(2,1)S(1)} %get-tuple-element.81), channel_id=1, source_target_pairs={{1,0},{0,1},{3,2},{2,3},{5,4},{4,5},{7,6},{6,7},{9,8},{8,9},{11,10... | collective-permute-start | bytes 184328 | tf_op jit(solution)/shard_map/ppermute | solution.py:40
  41.6 2.7 %collective-permute-start.15 = (f16[240,128]{1,0:T(8,128)(2,1)S(1)}, f16[240,128]{1,0:T(8,128)(2,1)S(1)}, u32[]{:S(2)}, u32[]{:S(2)}) collective-permute-start(f16[240,128]{1,0:T(8,128)(2,1)S(1)} %collective-permute-done.11), channel_id=1, source_target_pairs={{1,0},{0,1},{3,2},{2,3},{5,4},{4,5},{7,6},{6,7},{9,8},{8,9},{11,10... | collective-permute-start | bytes 184328 | tf_op jit(solution)/shard_map/ppermute | solution.py:40
  46.7 1.7 %collective-permute-start.17 = (bf16[992,128]{1,0:T(8,128)(2,1)S(1)}, bf16[992,128]{1,0:T(8,128)(2,1)S(1)}, u32[]{:S(2)}, u32[]{:S(2)}) collective-permute-start(bf16[992,128]{1,0:T(8,128)(2,1)S(1)} %get-tuple-element.61), channel_id=1, source_target_pairs={{1,0},{0,1},{3,2},{2,3},{5,4},{4,5},{7,6},{6,7},{9,8},{8,9},{11,10... | collective-permute-start | bytes 761864 | tf_op jit(solution)/shard_map/ppermute | solution.py:40
  48.5 4.4 %collective-permute-start.18 = (f16[248,128]{1,0:T(8,128)(2,1)S(1)}, f16[248,128]{1,0:T(8,128)(2,1)S(1)}, u32[]{:S(2)}, u32[]{:S(2)}) collective-permute-start(f16[248,128]{1,0:T(8,128)(2,1)S(1)} %get-tuple-element.88), channel_id=1, source_target_pairs={{4,0},{5,1},{6,2},{7,3},{0,4},{1,5},{2,6},{3,7},{12,8},{13,9},{14,... | collective-permute-start | bytes 190472 | tf_op jit(solution)/shard_map/ppermute | solution.py:40
  49.2 5.6 %collective-permute-start.20 = (f16[248,128]{1,0:T(8,128)(2,1)S(1)}, f16[248,128]{1,0:T(8,128)(2,1)S(1)}, u32[]{:S(2)}, u32[]{:S(2)}) collective-permute-start(f16[248,128]{1,0:T(8,128)(2,1)S(1)} %get-tuple-element.87), channel_id=1, source_target_pairs={{6,0},{7,1},{4,2},{5,3},{2,4},{3,5},{0,6},{1,7},{14,8},{15,9},{12,... | collective-permute-start | bytes 190472 | tf_op jit(solution)/shard_map/ppermute | solution.py:40
  50.5 5.0 %collective-permute-start.19 = (f16[248,128]{1,0:T(8,128)(2,1)S(1)}, f16[248,128]{1,0:T(8,128)(2,1)S(1)}, u32[]{:S(2)}, u32[]{:S(2)}) collective-permute-start(f16[248,128]{1,0:T(8,128)(2,1)S(1)} %get-tuple-element.86), channel_id=1, source_target_pairs={{2,0},{3,1},{0,2},{1,3},{6,4},{7,5},{4,6},{5,7},{10,8},{11,9},{8,1... | collective-permute-start | bytes 190472 | tf_op jit(solution)/shard_map/ppermute | solution.py:40
  55.5 5.9 %collective-permute-start.21 = (f16[248,128]{1,0:T(8,128)(2,1)S(1)}, f16[248,128]{1,0:T(8,128)(2,1)S(1)}, u32[]{:S(2)}, u32[]{:S(2)}) collective-permute-start(f16[248,128]{1,0:T(8,128)(2,1)S(1)} %fusion.6), channel_id=1, source_target_pairs={{16,0},{20,4},{24,8},{28,12},{0,16},{4,20},{8,24},{12,28},{17,1},{... | collective-permute-start | bytes 190472 | tf_op jit(solution)/shard_map/ppermute | solution.py:51
  61.4 4.3 %collective-permute-start.22 = (f16[248,128]{1,0:T(8,128)(2,1)S(1)}, f16[248,128]{1,0:T(8,128)(2,1)S(1)}, u32[]{:S(2)}, u32[]{:S(2)}) collective-permute-start(f16[248,128]{1,0:T(8,128)(2,1)S(1)} %add_convert_fusion), channel_id=1, source_target_pairs={{8,0},{9,1},{10,2},{11,3},{12,4},{13,5},{14,6},{15,7},{0,8},{1,9},... | collective-permute-start | bytes 190472 | tf_op jit(solution)/shard_map/ppermute | solution.py:40
  61.7 5.1 %collective-permute-start.24 = (f16[248,128]{1,0:T(8,128)(2,1)S(1)}, f16[248,128]{1,0:T(8,128)(2,1)S(1)}, u32[]{:S(2)}, u32[]{:S(2)}) collective-permute-start(f16[248,128]{1,0:T(8,128)(2,1)S(1)} %add_convert_fusion), channel_id=1, source_target_pairs={{12,0},{13,1},{14,2},{15,3},{8,4},{9,5},{10,6},{11,7},{4,8},{5,9},... | collective-permute-start | bytes 190472 | tf_op jit(solution)/shard_map/ppermute | solution.py:40
  63.7 4.2 %collective-permute-start.23 = (f16[248,128]{1,0:T(8,128)(2,1)S(1)}, f16[248,128]{1,0:T(8,128)(2,1)S(1)}, u32[]{:S(2)}, u32[]{:S(2)}) collective-permute-start(f16[248,128]{1,0:T(8,128)(2,1)S(1)} %add_convert_fusion), channel_id=1, source_target_pairs={{4,0},{5,1},{6,2},{7,3},{0,4},{1,5},{2,6},{3,7},{12,8},{13,9},{14,... | collective-permute-start | bytes 190472 | tf_op jit(solution)/shard_map/ppermute | solution.py:40
  (8 other events, 31.7 us)

commit v8 on v7

--- a/solution.py
+++ b/solution.py
@@ -212,15 +212,7 @@
     dense(0, stride, line, rows, told, out)
 
 
-def widen(line):
-    return jnp.pad(line, ((0, 0), (0, -line.shape[1] % 128)))
-
-
-def shift(line, count):
-    return pltpu.roll(line, count % line.shape[1], 1)
-
-
-def late_kernel(step, given, queries, item, negatives, _, *refs):
+def late_kernel(step, given, scale, queries, item, negatives, _, *refs):
     query, query_norm = unit_of(queries[step].astype(f32))
     if given:
         moment, sums, refs = refs[0][...], negatives[...], refs[1:]
@@ -241,12 +233,12 @@
     if step == 0:
         fifo, side, table, accum, loss_out, grad_out, fifo_out, *halves = refs
         loss_out[...], grad_out[...], fifo_out[...] = loss, grad, fifo[...]
+        rows = table[...]
+        values = (rows, column(accum[...]), scale / unit_of(rows)[1])
         first, count = side[...] == 0, halves[0].shape[0]
-        low, high = table[:count, :], table[count:, :]
-        halves[0][...], halves[2][...] = jnp.where(first, low, high), jnp.where(first, high, low)
-        accum = widen(accum[...])
-        low, high = accum[:, :count], shift(accum, -count)[:, :count]
-        halves[1][...], halves[3][...] = jnp.where(first, low, high), jnp.where(first, high, low)
+        for near, far, value in zip(halves[:3], halves[3:], values):
+            low, high = value[:count], value[count:]
+            near[...], far[...] = jnp.where(first, low, high), jnp.where(first, high, low)
         return
     loss_before, grad_before, fifo, head, *tops, losses, grads, fifo_out = refs
     losses[0:1, :], losses[1:2, :] = loss_before[...], loss
@@ -268,38 +260,33 @@
     out[...] = jnp.where(told[...] >= 0, item, negatives[...].astype(f32)).astype(bf16)
 
 
-def adagrad(scale, grad, table, line):
-    _, norm = unit_of(table)
-    grad = grad * (scale / norm)
-    square = grad * grad
-    moved = column(line) + jnp.mean(square, 1, keepdims=True)
-    ones = jnp.full((8, square.shape[1]), 1.0, f32)
-    sums = lax.dot_general(
-        ones, square, (((1,), (1,)), ((), ())), precision=lax.Precision.HIGHEST,
-        preferred_element_type=f32,
-    )
-    return table - learn_rate * grad / jnp.sqrt(moved), line + sums[:1] / square.shape[1]
-
-
-def update_kernel(scale, total, table, line, table_out, line_out, unit):
-    rows, line_out[...] = adagrad(scale, total[: table.shape[0], :], table[...], line[...])
+def adagrad(grad, table, accum, inverse):
+    grad = grad * inverse
+    accum = accum + jnp.mean(grad * grad, 1, keepdims=True)
+    return table - learn_rate * grad / jnp.sqrt(accum), accum
+
+
+def update_kernel(scale, total, table, accum, inverse, table_out, accum_out, inverse_out, unit):
+    grad = total[: table.shape[0], :]
+    rows, accum_out[...] = adagrad(grad, table[...], accum[...], inverse[...])
     table_out[...] = rows
-    unit[...], _ = unit_of(rows)
-
-
-def finish_kernel(scale, side, mine, other, table, line, far_table, far_line, table_out, line_out):
-    count, first = table.shape[0], side[...] == 0
+    unit[...], norm = unit_of(rows)
+    inverse_out[...] = scale / norm
+
+
+def finish_kernel(side, mine, other, *refs):
+    near, far, (table_out, line_out) = refs[:3], refs[3:6], refs[6:]
+    count, first = near[0].shape[0], side[...] == 0
 
     def in_order(near, far):
         return jnp.concatenate([jnp.where(first, near, far), jnp.where(first, far, near)])
 
-    near, far = widen(line[...]), widen(far_line[...])
-    gap = jnp.zeros((1, -(-2 * count // 128) * 128 - near.shape[1]), f32)
-    near, far = jnp.concatenate([near, gap], 1), jnp.concatenate([far, gap], 1)
-    line = jnp.where(first, near, far) + shift(jnp.where(first, far, near), count)
-    grad = in_order(mine[:count, :], other[:count, :])
-    rows = in_order(table[...], far_table[...])
-    table_out[...], line_out[...] = adagrad(scale, grad, rows, line[:, : 2 * count])
+    state = [in_order(a[...], b[...]) for a, b in zip(near, far)]
+    rows, accum = adagrad(in_order(mine[:count, :], other[:count, :]), *state)
+    table_out[...] = rows
+    wide = jnp.pad(accum, ((0, -2 * count % 128), (0, 0)))
+    wide = jnp.broadcast_to(wide, (wide.shape[0], 128))
+    line_out[...] = jnp.transpose(wide)[:1, : 2 * count]
 
 
 def call(kernel, outs, *args):
@@ -459,7 +446,9 @@
 
         more = step + 1 < step_count
         args = [queries, unit, queue if small else negatives, early, *([] if small else [moment])]
-        half_shard = [((part_rows, width), f32), ((1, part_rows), f32)]
+        scalar = ((part_rows, 1), f32)
+        half_shard = [((part_rows, width), f32), scalar, scalar]
+        scale = score_scale / grad_scale
         if more:
             outs = [((1, query_count), f32), (matrix, bf16), (fifo.shape, bf16)]
             outs += half_shard + half_shard
@@ -467,20 +456,19 @@
         else:
             outs = [((step_count, query_count), f32), (queries.shape, bf16), (fifo.shape, bf16)]
             args += [loss, query_grad, fifo, fifo_head[None], *tops]
-        kernel = functools.partial(late_kernel, step, not small)
+        kernel = functools.partial(late_kernel, step, not small, scale)
         loss, query_grad, fifo, *rest, zero = call(kernel, outs + [(total.shape, f32)], *args)
         mine, other = reduce_far(total, zero)
-        scale = score_scale / grad_scale
         if more:
             kernel, outs = functools.partial(update_kernel, scale), half_shard + half_shard[:1]
-            *near, unit = call(kernel, outs, mine, *rest[:2])
-            *far, far_unit = call(kernel, outs, other, *rest[2:])
+            *near, unit = call(kernel, outs, mine, *rest[:3])
+            *far, far_unit = call(kernel, outs, other, *rest[3:])
             queue, zero = next_queue(queue, mine[part_rows:])
             parts = gather_whole(unit.astype(f16), far_unit.astype(f16))
         else:
             outs = [(table.shape, f32), (line.shape, f32)]
             args = [jnp.full((1, 1), side), mine, other, *near, *far]
-            table, line = call(functools.partial(finish_kernel, scale), outs, *args)
+            table, line = call(finish_kernel, outs, *args)
 
     return (loss, query_grad, table, line[0], fifo)
 

time: 69.6 us -> 69.3 us (level)
  no operation moved by 1% of the time
where the time goes in v8:
time: 69.3 us; the launch traced here: 69 us
  waiting for transfers between devices  27.5 us (40%)
  starting transfers between devices  26.1 us (38%)
  Pallas kernels  10.7 us (15%)
  local copies, waits for them, and re-layouts  1.73 us (2%)
  between operations  1.58 us (2%)
  other arithmetic  1.39 us (2%)
    ppermute x23, starting transfers between devices, flip(): lax.ppermute(piece, ('batch', 'table'), [(i ^ mask, i) for i in range(cou...  20.1 us
    ppermute x23, waiting for transfers between devices, flip(): lax.ppermute(piece, ('batch', 'table'), [(i ^ mask, i) for i in range(cou...  16 us
    pallas_call x12, Pallas kernels, call(): pl.pallas_call(kernel, out_shape=[jax.ShapeDtypeStruct(shape, dtype) for...  10.7 us
    ppermute x2, waiting for transfers between devices, turned(): found.append(lax.ppermute(piece, 'batch', pairs))  7.65 us
    all_to_all x1, starting transfers between devices, per_device(): lax.all_to_all(queue, ('batch', 'table'), 0, 0, tiled=True)  5.03 us
    all_to_all x1, waiting for transfers between devices, per_device(): lax.all_to_all(queue, ('batch', 'table'), 0, 0, tiled=True)  3.86 us
  transfers between devices with their start and end apart: 26, of which 18 were waited for; matrix products, arithmetic and copies ran while one was open for 3% of the time, Pallas kernels for 11%

profile of v8, /device:TPU:0, one launch (start us, length us, event | category | flops | bytes accessed | tf_op | source)
XLA Modules:
  0.0 69.0 jit_solution(2203975571486393247)
XLA Ops:
  0.6 3.0 %collective-permute-start = (f32[480,128]{1,0:T(8,128)}, f32[480,128]{1,0:T(8,128)S(1)}, u32[]{:S(2)}, u32[]{:S(2)}) collective-permute-start(f32[480,128]{1,0:T(8,128)} %refs_0_.3), channel_id=1, source_target_pairs={{2,0},{3,1},{0,2},{1,3},{6,4},{7,5},{4,6},{5,7},{10,8},{11,9},{8,1... | collective-permute-start | bytes 737288 | tf_op jit(solution)/shard_map/ppermute | solution.py:40
  5.0 5.0 %all-to-all-start = ((bf16[32,8,128]{2,1,0:T(8,128)(2,1)}), bf16[32,8,128]{2,1,0:T(8,128)(2,1)S(1)}, u32[]{:S(2)}, u32[]{:S(2)}) async-start(bf16[32,8,128]{2,1,0:T(8,128)(2,1)} %broadcast_in_dim.67), calls=%async_computation | async-start | bytes 131072 | tf_op jit(solution)/shard_map/all_to_all | solution.py:391
  11.7 1.9 %shard_map.110 = (f32[512,128]{1,0:T(8,128)S(1)}, f32[512,128]{1,0:T(8,128)S(1)}, f32[512,1]{1,0:T(8,128)}, f32[8,128]{1,0:T(8,128)S(1)}) custom-call(bf16[2,512,128]{2,1,0:T(8,128)(2,1)S(1)} %copy-done, s32[1,512]{1,0:T(1,128)S(1)} %get-tuple-element.92.line.found_line, f32[512,1]{1,0:T(8,128)S(1)} %broadcast_in_dim.64.negatives, s32[1,1]{1,0:T(1,128)} %bitcast.3.refs_0_, ...), custom_call_target="tpu_custom_call" | custom-call | tf_op jit(solution)/shard_map/pallas_call | solution.py:294
  13.6 3.9 %all-to-all-done = bf16[32,8,128]{2,1,0:T(8,128)(2,1)S(1)} async-done(((bf16[32,8,128]{2,1,0:T(8,128)(2,1)}), bf16[32,8,128]{2,1,0:T(8,128)(2,1)S(1)}, u32[]{:S(2)}, u32[]{:S(2)}) %all-to-all-start) | async-done | bytes 65568 | tf_op jit(solution)/shard_map/all_to_all | solution.py:391
  18.9 1.0 %collective-permute-done.3 = bf16[992,128]{1,0:T(8,128)(2,1)S(1)} collective-permute-done((bf16[992,128]{1,0:T(8,128)(2,1)S(1)}, bf16[992,128]{1,0:T(8,128)(2,1)S(1)}, u32[]{:S(2)}, u32[]{:S(2)}) %collective-permute-start.3) | collective-permute-done | bytes 253984 | tf_op jit(solution)/shard_map/ppermute | solution.py:40
  20.7 1.3 %collective-permute-start.5 = (f16[248,128]{1,0:T(8,128)(2,1)S(1)}, f16[248,128]{1,0:T(8,128)(2,1)S(1)}, u32[]{:S(2)}, u32[]{:S(2)}) collective-permute-start(f16[248,128]{1,0:T(8,128)(2,1)S(1)} %get-tuple-element.99), channel_id=1, source_target_pairs={{2,0},{3,1},{0,2},{1,3},{6,4},{7,5},{4,6},{5,7},{10,8},{11,9},{8,1... | collective-permute-start | bytes 190472 | tf_op jit(solution)/shard_map/ppermute | solution.py:40
  22.1 1.4 %collective-permute-start.4 = (f16[248,128]{1,0:T(8,128)(2,1)S(1)}, f16[248,128]{1,0:T(8,128)(2,1)S(1)}, u32[]{:S(2)}, u32[]{:S(2)}) collective-permute-start(f16[248,128]{1,0:T(8,128)(2,1)S(1)} %get-tuple-element.97), channel_id=1, source_target_pairs={{4,0},{5,1},{6,2},{7,3},{0,4},{1,5},{2,6},{3,7},{12,8},{13,9},{14,... | collective-permute-start | bytes 190472 | tf_op jit(solution)/shard_map/ppermute | solution.py:40
  23.5 2.2 %collective-permute-done.6 = f16[248,128]{1,0:T(8,128)(2,1)S(1)} collective-permute-done((f16[248,128]{1,0:T(8,128)(2,1)S(1)}, f16[248,128]{1,0:T(8,128)(2,1)S(1)}, u32[]{:S(2)}, u32[]{:S(2)}) %collective-permute-start.6) | collective-permute-done | bytes 63520 | tf_op jit(solution)/shard_map/ppermute | solution.py:40
  28.8 3.5 %collective-permute-done.7 = f16[248,128]{1,0:T(8,128)(2,1)S(1)} collective-permute-done((f16[248,128]{1,0:T(8,128)(2,1)S(1)}, f16[248,128]{1,0:T(8,128)(2,1)S(1)}, u32[]{:S(2)}, u32[]{:S(2)}) %collective-permute-start.7) | collective-permute-done | bytes 63520 | tf_op jit(solution)/shard_map/ppermute | solution.py:51
  32.4 2.8 %collective-permute-start.10 = (f16[248,128]{1,0:T(8,128)(2,1)S(1)}, f16[248,128]{1,0:T(8,128)(2,1)S(1)}, u32[]{:S(2)}, u32[]{:S(2)}) collective-permute-start(f16[248,128]{1,0:T(8,128)(2,1)S(1)} %add_convert_fusion.1), channel_id=1, source_target_pairs={{12,0},{13,1},{14,2},{15,3},{8,4},{9,5},{10,6},{11,7},{4,8},{5,9},... | collective-permute-start | bytes 190472 | tf_op jit(solution)/shard_map/ppermute | solution.py:40
  38.1 1.4 %collective-permute-done.9 = f16[248,128]{1,0:T(8,128)(2,1)S(1)} collective-permute-done((f16[248,128]{1,0:T(8,128)(2,1)S(1)}, f16[248,128]{1,0:T(8,128)(2,1)S(1)}, u32[]{:S(2)}, u32[]{:S(2)}) %collective-permute-start.9) | collective-permute-done | bytes 63520 | tf_op jit(solution)/shard_map/ppermute | solution.py:40
  42.1 2.1 %collective-permute-done.12 = f16[240,128]{1,0:T(8,128)(2,1)S(1)} collective-permute-done((f16[240,128]{1,0:T(8,128)(2,1)S(1)}, f16[240,128]{1,0:T(8,128)(2,1)S(1)}, u32[]{:S(2)}, u32[]{:S(2)}) %collective-permute-start.12) | collective-permute-done | bytes 61472 | tf_op jit(solution)/shard_map/ppermute | solution.py:40
  44.3 1.1 %shard_map.117 = (f32[512,128]{1,0:T(8,128)S(1)}, f32[512,128]{1,0:T(8,128)S(1)}, f32[512,1]{1,0:T(8,128)S(1)}) custom-call(bf16[2,512,128]{2,1,0:T(8,128)(2,1)S(1)} %copy-done, s32[1,512]{1,0:T(1,128)S(1)} %multiply_add_fusion.1.line.found_line, bf16[256,128]{1,0:T(8,128)(2,1)S(1)} %get-tuple-element.52.negatives, ...), custom_call_target="tpu_custom_call" | custom-call | tf_op jit(solution)/shard_map/pallas_call | solution.py:294
  45.5 1.2 %shard_map.118 = (bf16[992,128]{1,0:T(8,128)(2,1)S(1)}, bf16[512,128]{1,0:T(8,128)(2,1)S(1)}, f32[512,128]{1,0:T(8,128)S(1)}, f32[8,128]{1,0:T(8,128)S(1)}) custom-call(f32[512,128]{1,0:T(8,128)S(1)} %get-tuple-element.62.found, s32[1,512]{1,0:T(1,128)S(1)} %multiply_add_fusion.1.line.found_line, s32[1,512]{1,0:T(1,128)S(1)} %get-tuple-element.100.line, ...), custom_call_target="tpu_custom_call" | custom-call | tf_op jit(solution)/shard_map/pallas_call | solution.py:294
  49.2 1.3 %collective-permute-start.20 = (f16[248,128]{1,0:T(8,128)(2,1)S(1)}, f16[248,128]{1,0:T(8,128)(2,1)S(1)}, u32[]{:S(2)}, u32[]{:S(2)}) collective-permute-start(f16[248,128]{1,0:T(8,128)(2,1)S(1)} %get-tuple-element.95), channel_id=1, source_target_pairs={{6,0},{7,1},{4,2},{5,3},{2,4},{3,5},{0,6},{1,7},{14,8},{15,9},{12,... | collective-permute-start | bytes 190472 | tf_op jit(solution)/shard_map/ppermute | solution.py:40
  50.4 1.6 %collective-permute-start.19 = (f16[248,128]{1,0:T(8,128)(2,1)S(1)}, f16[248,128]{1,0:T(8,128)(2,1)S(1)}, u32[]{:S(2)}, u32[]{:S(2)}) collective-permute-start(f16[248,128]{1,0:T(8,128)(2,1)S(1)} %get-tuple-element.94), channel_id=1, source_target_pairs={{2,0},{3,1},{0,2},{1,3},{6,4},{7,5},{4,6},{5,7},{10,8},{11,9},{8,1... | collective-permute-start | bytes 190472 | tf_op jit(solution)/shard_map/ppermute | solution.py:40
  52.8 1.9 %collective-permute-done.20 = f16[248,128]{1,0:T(8,128)(2,1)S(1)} collective-permute-done((f16[248,128]{1,0:T(8,128)(2,1)S(1)}, f16[248,128]{1,0:T(8,128)(2,1)S(1)}, u32[]{:S(2)}, u32[]{:S(2)}) %collective-permute-start.20) | collective-permute-done | bytes 63520 | tf_op jit(solution)/shard_map/ppermute | solution.py:40
  55.7 1.5 %shard_map.120 = (f32[2,512]{1,0:T(2,128)}, bf16[2,512,128]{2,1,0:T(8,128)(2,1)}, bf16[8,128]{1,0:T(8,128)(2,1)}, f32[248,128]{1,0:T(8,128)S(1)}) custom-call(bf16[2,512,128]{2,1,0:T(8,128)(2,1)S(1)} %copy-done, f32[512,128]{1,0:T(8,128)S(1)} %get-tuple-element.65.item, bf16[256,128]{1,0:T(8,128)(2,1)S(1)} %get-tuple-element.52.negatives, ...), custom_call_target="tpu_custom_call" | custom-call | tf_op jit(solution)/shard_map/pallas_call | solution.py:294
  57.2 4.2 %collective-permute-done.21 = f16[248,128]{1,0:T(8,128)(2,1)S(1)} collective-permute-done((f16[248,128]{1,0:T(8,128)(2,1)S(1)}, f16[248,128]{1,0:T(8,128)(2,1)S(1)}, u32[]{:S(2)}, u32[]{:S(2)}) %collective-permute-start.21) | collective-permute-done | bytes 63520 | tf_op jit(solution)/shard_map/ppermute | solution.py:51
  61.6 2.1 %collective-permute-start.24 = (f16[248,128]{1,0:T(8,128)(2,1)S(1)}, f16[248,128]{1,0:T(8,128)(2,1)S(1)}, u32[]{:S(2)}, u32[]{:S(2)}) collective-permute-start(f16[248,128]{1,0:T(8,128)(2,1)S(1)} %add_convert_fusion), channel_id=1, source_target_pairs={{12,0},{13,1},{14,2},{15,3},{8,4},{9,5},{10,6},{11,7},{4,8},{5,9},... | collective-permute-start | bytes 190472 | tf_op jit(solution)/shard_map/ppermute | solution.py:40
  63.7 1.2 %collective-permute-start.23 = (f16[248,128]{1,0:T(8,128)(2,1)S(1)}, f16[248,128]{1,0:T(8,128)(2,1)S(1)}, u32[]{:S(2)}, u32[]{:S(2)}) collective-permute-start(f16[248,128]{1,0:T(8,128)(2,1)S(1)} %add_convert_fusion), channel_id=1, source_target_pairs={{4,0},{5,1},{6,2},{7,3},{0,4},{1,5},{2,6},{3,7},{12,8},{13,9},{14,... | collective-permute-start | bytes 190472 | tf_op jit(solution)/shard_map/ppermute | solution.py:40
  65.7 1.1 %collective-permute-done.24 = f16[248,128]{1,0:T(8,128)(2,1)S(1)} collective-permute-done((f16[248,128]{1,0:T(8,128)(2,1)S(1)}, f16[248,128]{1,0:T(8,128)(2,1)S(1)}, u32[]{:S(2)}, u32[]{:S(2)}) %collective-permute-start.24) | collective-permute-done | bytes 63520 | tf_op jit(solution)/shard_map/ppermute | solution.py:40
  66.7 1.2 %collective-permute-done.23 = f16[248,128]{1,0:T(8,128)(2,1)S(1)} collective-permute-done((f16[248,128]{1,0:T(8,128)(2,1)S(1)}, f16[248,128]{1,0:T(8,128)(2,1)S(1)}, u32[]{:S(2)}, u32[]{:S(2)}) %collective-permute-start.23) | collective-permute-done | bytes 63520 | tf_op jit(solution)/shard_map/ppermute | solution.py:40
  67.9 1.1 %shard_map.121 = (f32[480,128]{1,0:T(8,128)}, f32[1,480]{1,0:T(1,128)}) custom-call(s32[1,1]{1,0:T(1,128)} %bitcast.7.refs_1_.side, f32[248,128]{1,0:T(8,128)S(1)} %convert_add_fusion.1.mine, f32[248,128]{1,0:T(8,128)S(1)} %convert_add_fusion.other, f32[240,128]{1,0:T(8,128)S(1)} %get-tuple-element.76.refs_0_, f32[240,1]{1,0:T(8,128)S(1)} %get-tuple-element.77.refs_1_, ...), custom_call_target="tpu_custom_call" | custom-call | tf_op jit(solution)/shard_map/pallas_call | solution.py:294
  (82 shorter events, 18.7 us)
Async XLA Ops:
  0.6 9.4 %collective-permute-start = (f32[480,128]{1,0:T(8,128)}, f32[480,128]{1,0:T(8,128)S(1)}, u32[]{:S(2)}, u32[]{:S(2)}) collective-permute-start(f32[480,128]{1,0:T(8,128)} %refs_0_.3), channel_id=1, source_target_pairs={{2,0},{3,1},{0,2},{1,3},{6,4},{7,5},{4,6},{5,7},{10,8},{11,9},{8,1... | collective-permute-start | bytes 737288 | tf_op jit(solution)/shard_map/ppermute | solution.py:40
  3.6 7.5 %collective-permute-start.1 = (f32[480,128]{1,0:T(8,128)}, f32[480,128]{1,0:T(8,128)S(1)}, u32[]{:S(2)}, u32[]{:S(2)}) collective-permute-start(f32[480,128]{1,0:T(8,128)} %refs_0_.3), channel_id=1, source_target_pairs={{1,0},{0,1},{3,2},{2,3},{5,4},{4,5},{7,6},{6,7},{9,8},{8,9},{11,10... | collective-permute-start | bytes 737288 | tf_op jit(solution)/shard_map/ppermute | solution.py:40
  5.0 12.5 %all-to-all-start = ((bf16[32,8,128]{2,1,0:T(8,128)(2,1)}), bf16[32,8,128]{2,1,0:T(8,128)(2,1)S(1)}, u32[]{:S(2)}, u32[]{:S(2)}) async-start(bf16[32,8,128]{2,1,0:T(8,128)(2,1)} %broadcast_in_dim.67), calls=%async_computation | async-start | bytes 131072 | tf_op jit(solution)/shard_map/all_to_all | solution.py:391
  18.3 1.6 %collective-permute-start.3 = (bf16[992,128]{1,0:T(8,128)(2,1)S(1)}, bf16[992,128]{1,0:T(8,128)(2,1)S(1)}, u32[]{:S(2)}, u32[]{:S(2)}) collective-permute-start(bf16[992,128]{1,0:T(8,128)(2,1)S(1)} %get-tuple-element.49), channel_id=1, source_target_pairs={{1,0},{0,1},{3,2},{2,3},{5,4},{4,5},{7,6},{6,7},{9,8},{8,9},{11,10... | collective-permute-start | bytes 761864 | tf_op jit(solution)/shard_map/ppermute | solution.py:40
  19.9 5.7 %collective-permute-start.6 = (f16[248,128]{1,0:T(8,128)(2,1)S(1)}, f16[248,128]{1,0:T(8,128)(2,1)S(1)}, u32[]{:S(2)}, u32[]{:S(2)}) collective-permute-start(f16[248,128]{1,0:T(8,128)(2,1)S(1)} %get-tuple-element.98), channel_id=1, source_target_pairs={{6,0},{7,1},{4,2},{5,3},{2,4},{3,5},{0,6},{1,7},{14,8},{15,9},{12,... | collective-permute-start | bytes 190472 | tf_op jit(solution)/shard_map/ppermute | solution.py:40
  20.7 5.0 %collective-permute-start.5 = (f16[248,128]{1,0:T(8,128)(2,1)S(1)}, f16[248,128]{1,0:T(8,128)(2,1)S(1)}, u32[]{:S(2)}, u32[]{:S(2)}) collective-permute-start(f16[248,128]{1,0:T(8,128)(2,1)S(1)} %get-tuple-element.99), channel_id=1, source_target_pairs={{2,0},{3,1},{0,2},{1,3},{6,4},{7,5},{4,6},{5,7},{10,8},{11,9},{8,1... | collective-permute-start | bytes 190472 | tf_op jit(solution)/shard_map/ppermute | solution.py:40
  22.1 4.3 %collective-permute-start.4 = (f16[248,128]{1,0:T(8,128)(2,1)S(1)}, f16[248,128]{1,0:T(8,128)(2,1)S(1)}, u32[]{:S(2)}, u32[]{:S(2)}) collective-permute-start(f16[248,128]{1,0:T(8,128)(2,1)S(1)} %get-tuple-element.97), channel_id=1, source_target_pairs={{4,0},{5,1},{6,2},{7,3},{0,4},{1,5},{2,6},{3,7},{12,8},{13,9},{14,... | collective-permute-start | bytes 190472 | tf_op jit(solution)/shard_map/ppermute | solution.py:40
  26.4 5.9 %collective-permute-start.7 = (f16[248,128]{1,0:T(8,128)(2,1)S(1)}, f16[248,128]{1,0:T(8,128)(2,1)S(1)}, u32[]{:S(2)}, u32[]{:S(2)}) collective-permute-start(f16[248,128]{1,0:T(8,128)(2,1)S(1)} %fusion.13), channel_id=1, source_target_pairs={{16,0},{20,4},{24,8},{28,12},{0,16},{4,20},{8,24},{12,28},{17,1},{... | collective-permute-start | bytes 190472 | tf_op jit(solution)/shard_map/ppermute | solution.py:51
  32.3 4.3 %collective-permute-start.8 = (f16[248,128]{1,0:T(8,128)(2,1)S(1)}, f16[248,128]{1,0:T(8,128)(2,1)S(1)}, u32[]{:S(2)}, u32[]{:S(2)}) collective-permute-start(f16[248,128]{1,0:T(8,128)(2,1)S(1)} %add_convert_fusion.1), channel_id=1, source_target_pairs={{8,0},{9,1},{10,2},{11,3},{12,4},{13,5},{14,6},{15,7},{0,8},{1,9},... | collective-permute-start | bytes 190472 | tf_op jit(solution)/shard_map/ppermute | solution.py:40
  32.4 5.7 %collective-permute-start.10 = (f16[248,128]{1,0:T(8,128)(2,1)S(1)}, f16[248,128]{1,0:T(8,128)(2,1)S(1)}, u32[]{:S(2)}, u32[]{:S(2)}) collective-permute-start(f16[248,128]{1,0:T(8,128)(2,1)S(1)} %add_convert_fusion.1), channel_id=1, source_target_pairs={{12,0},{13,1},{14,2},{15,3},{8,4},{9,5},{10,6},{11,7},{4,8},{5,9},... | collective-permute-start | bytes 190472 | tf_op jit(solution)/shard_map/ppermute | solution.py:40
  35.2 4.2 %collective-permute-start.9 = (f16[248,128]{1,0:T(8,128)(2,1)S(1)}, f16[248,128]{1,0:T(8,128)(2,1)S(1)}, u32[]{:S(2)}, u32[]{:S(2)}) collective-permute-start(f16[248,128]{1,0:T(8,128)(2,1)S(1)} %add_convert_fusion.1), channel_id=1, source_target_pairs={{4,0},{5,1},{6,2},{7,3},{0,4},{1,5},{2,6},{3,7},{12,8},{13,9},{14,... | collective-permute-start | bytes 190472 | tf_op jit(solution)/shard_map/ppermute | solution.py:40
  37.1 4.5 %collective-permute-start.11 = (f16[240,128]{1,0:T(8,128)(2,1)S(1)}, f16[240,128]{1,0:T(8,128)(2,1)S(1)}, u32[]{:S(2)}, u32[]{:S(2)}) collective-permute-start(f16[240,128]{1,0:T(8,128)(2,1)S(1)} %get-tuple-element.91), channel_id=1, source_target_pairs={{2,0},{3,1},{0,2},{1,3},{6,4},{7,5},{4,6},{5,7},{10,8},{11,9},{8,1... | collective-permute-start | bytes 184328 | tf_op jit(solution)/shard_map/ppermute | solution.py:40
  37.8 6.5 %collective-permute-start.13 = (f16[240,128]{1,0:T(8,128)(2,1)S(1)}, f16[240,128]{1,0:T(8,128)(2,1)S(1)}, u32[]{:S(2)}, u32[]{:S(2)}) collective-permute-start(f16[240,128]{1,0:T(8,128)(2,1)S(1)} %get-tuple-element.91), channel_id=1, source_target_pairs={{1,0},{0,1},{3,2},{2,3},{5,4},{4,5},{7,6},{6,7},{9,8},{8,9},{11,10... | collective-permute-start | bytes 184328 | tf_op jit(solution)/shard_map/ppermute | solution.py:40
  39.9 4.3 %collective-permute-start.12 = (f16[240,128]{1,0:T(8,128)(2,1)S(1)}, f16[240,128]{1,0:T(8,128)(2,1)S(1)}, u32[]{:S(2)}, u32[]{:S(2)}) collective-permute-start(f16[240,128]{1,0:T(8,128)(2,1)S(1)} %get-tuple-element.89), channel_id=1, source_target_pairs={{2,0},{3,1},{0,2},{1,3},{6,4},{7,5},{4,6},{5,7},{10,8},{11,9},{8,1... | collective-permute-start | bytes 184328 | tf_op jit(solution)/shard_map/ppermute | solution.py:40
  40.4 3.9 %collective-permute-start.14 = (f16[240,128]{1,0:T(8,128)(2,1)S(1)}, f16[240,128]{1,0:T(8,128)(2,1)S(1)}, u32[]{:S(2)}, u32[]{:S(2)}) collective-permute-start(f16[240,128]{1,0:T(8,128)(2,1)S(1)} %get-tuple-element.89), channel_id=1, source_target_pairs={{1,0},{0,1},{3,2},{2,3},{5,4},{4,5},{7,6},{6,7},{9,8},{8,9},{11,10... | collective-permute-start | bytes 184328 | tf_op jit(solution)/shard_map/ppermute | solution.py:40
  41.6 2.7 %collective-permute-start.15 = (f16[240,128]{1,0:T(8,128)(2,1)S(1)}, f16[240,128]{1,0:T(8,128)(2,1)S(1)}, u32[]{:S(2)}, u32[]{:S(2)}) collective-permute-start(f16[240,128]{1,0:T(8,128)(2,1)S(1)} %collective-permute-done.11), channel_id=1, source_target_pairs={{1,0},{0,1},{3,2},{2,3},{5,4},{4,5},{7,6},{6,7},{9,8},{8,9},{11,10... | collective-permute-start | bytes 184328 | tf_op jit(solution)/shard_map/ppermute | solution.py:40
  46.6 1.7 %collective-permute-start.17 = (bf16[992,128]{1,0:T(8,128)(2,1)S(1)}, bf16[992,128]{1,0:T(8,128)(2,1)S(1)}, u32[]{:S(2)}, u32[]{:S(2)}) collective-permute-start(bf16[992,128]{1,0:T(8,128)(2,1)S(1)} %get-tuple-element.67), channel_id=1, source_target_pairs={{1,0},{0,1},{3,2},{2,3},{5,4},{4,5},{7,6},{6,7},{9,8},{8,9},{11,10... | collective-permute-start | bytes 761864 | tf_op jit(solution)/shard_map/ppermute | solution.py:40
  48.4 4.4 %collective-permute-start.18 = (f16[248,128]{1,0:T(8,128)(2,1)S(1)}, f16[248,128]{1,0:T(8,128)(2,1)S(1)}, u32[]{:S(2)}, u32[]{:S(2)}) collective-permute-start(f16[248,128]{1,0:T(8,128)(2,1)S(1)} %get-tuple-element.96), channel_id=1, source_target_pairs={{4,0},{5,1},{6,2},{7,3},{0,4},{1,5},{2,6},{3,7},{12,8},{13,9},{14,... | collective-permute-start | bytes 190472 | tf_op jit(solution)/shard_map/ppermute | solution.py:40
  49.2 5.6 %collective-permute-start.20 = (f16[248,128]{1,0:T(8,128)(2,1)S(1)}, f16[248,128]{1,0:T(8,128)(2,1)S(1)}, u32[]{:S(2)}, u32[]{:S(2)}) collective-permute-start(f16[248,128]{1,0:T(8,128)(2,1)S(1)} %get-tuple-element.95), channel_id=1, source_target_pairs={{6,0},{7,1},{4,2},{5,3},{2,4},{3,5},{0,6},{1,7},{14,8},{15,9},{12,... | collective-permute-start | bytes 190472 | tf_op jit(solution)/shard_map/ppermute | solution.py:40
  50.4 5.0 %collective-permute-start.19 = (f16[248,128]{1,0:T(8,128)(2,1)S(1)}, f16[248,128]{1,0:T(8,128)(2,1)S(1)}, u32[]{:S(2)}, u32[]{:S(2)}) collective-permute-start(f16[248,128]{1,0:T(8,128)(2,1)S(1)} %get-tuple-element.94), channel_id=1, source_target_pairs={{2,0},{3,1},{0,2},{1,3},{6,4},{7,5},{4,6},{5,7},{10,8},{11,9},{8,1... | collective-permute-start | bytes 190472 | tf_op jit(solution)/shard_map/ppermute | solution.py:40
  55.4 5.9 %collective-permute-start.21 = (f16[248,128]{1,0:T(8,128)(2,1)S(1)}, f16[248,128]{1,0:T(8,128)(2,1)S(1)}, u32[]{:S(2)}, u32[]{:S(2)}) collective-permute-start(f16[248,128]{1,0:T(8,128)(2,1)S(1)} %fusion.6), channel_id=1, source_target_pairs={{16,0},{20,4},{24,8},{28,12},{0,16},{4,20},{8,24},{12,28},{17,1},{... | collective-permute-start | bytes 190472 | tf_op jit(solution)/shard_map/ppermute | solution.py:51
  61.4 4.3 %collective-permute-start.22 = (f16[248,128]{1,0:T(8,128)(2,1)S(1)}, f16[248,128]{1,0:T(8,128)(2,1)S(1)}, u32[]{:S(2)}, u32[]{:S(2)}) collective-permute-start(f16[248,128]{1,0:T(8,128)(2,1)S(1)} %add_convert_fusion), channel_id=1, source_target_pairs={{8,0},{9,1},{10,2},{11,3},{12,4},{13,5},{14,6},{15,7},{0,8},{1,9},... | collective-permute-start | bytes 190472 | tf_op jit(solution)/shard_map/ppermute | solution.py:40
  61.6 5.1 %collective-permute-start.24 = (f16[248,128]{1,0:T(8,128)(2,1)S(1)}, f16[248,128]{1,0:T(8,128)(2,1)S(1)}, u32[]{:S(2)}, u32[]{:S(2)}) collective-permute-start(f16[248,128]{1,0:T(8,128)(2,1)S(1)} %add_convert_fusion), channel_id=1, source_target_pairs={{12,0},{13,1},{14,2},{15,3},{8,4},{9,5},{10,6},{11,7},{4,8},{5,9},... | collective-permute-start | bytes 190472 | tf_op jit(solution)/shard_map/ppermute | solution.py:40
  63.7 4.2 %collective-permute-start.23 = (f16[248,128]{1,0:T(8,128)(2,1)S(1)}, f16[248,128]{1,0:T(8,128)(2,1)S(1)}, u32[]{:S(2)}, u32[]{:S(2)}) collective-permute-start(f16[248,128]{1,0:T(8,128)(2,1)S(1)} %add_convert_fusion), channel_id=1, source_target_pairs={{4,0},{5,1},{6,2},{7,3},{0,4},{1,5},{2,6},{3,7},{12,8},{13,9},{14,... | collective-permute-start | bytes 190472 | tf_op jit(solution)/shard_map/ppermute | solution.py:40
  (8 other events, 31.7 us)

commit v9 on v8

--- a/solution.py
+++ b/solution.py
@@ -167,7 +167,12 @@
 
 
 def first_kernel(step, count, scalars, queries, line, negatives, *refs):
-    ids, blocks, (unit, found, sums, *told) = refs[:scalars], refs[scalars : scalars + count], refs[scalars + count :]
+    ids, blocks, refs = refs[:scalars], refs[scalars : scalars + count], refs[scalars + count :]
+    if step == 0:
+        places, unit, found, sums, *told = refs
+        told = (places, *told)
+    else:
+        unit, found, sums = refs
     unit[...], _ = unit_of(queries[step].astype(f32))
     item = split_dot(column(line[...]), blocks)
     found[...] = unit_of(item)[0] if step == 0 else item
@@ -175,8 +180,22 @@
         sums[...] = jnp.sum(weights_of(unit[...], negatives[...]), 1, keepdims=True)
     else:
         sums[...] = negatives[...]
-    if told:
-        told[0][...] = told_block(*ids, *told[0].shape)
+    if step == 0:
+        places, away, half, notes, top, *told = told
+        query, item = unit[...], found[...]
+        cosine = jnp.sum(query * item, 1, keepdims=True)
+        away[...] = (query - item * cosine).astype(bf16)
+        half[...] = query.astype(bf16)
+        spread = jnp.broadcast_to(score_scale * cosine, item.shape)
+        weight = jnp.exp(jnp.transpose(spread)[:1])
+        line = places[...].astype(f32)
+        notes[:8, :] = jnp.concatenate([weight, line, jnp.zeros((6, line.shape[1]), f32)])
+        top[...] = item[: top.shape[0]]
+        if told:
+            block = told_block(*ids, *told[0].shape)
+            told[0][...] = block
+            gap = jnp.zeros((block.shape[0], line.shape[1] - block.shape[1]), f32)
+            notes[8:, :] = jnp.concatenate([block, gap], 1)
 
 
 def main_kernel(first, count, stride, found, found_line, line, queries, negatives, *refs):
@@ -198,14 +217,36 @@
     dense(sent.shape[0], stride, line, rows, told, sent)
 
 
-def dense(first, stride, line, rows, told, out):
-    half, count = out.shape[0], told.shape[0]
-    chosen = one_hot(line[...], first, half, False)
-    found = jnp.dot(chosen, rows[...], preferred_element_type=f32)
+def dense_rows(first, half, stride, line, rows, told, lack=1.0):
+    count = told.shape[0]
+    numbers = lax.broadcasted_iota(jnp.int32, (half, rows.shape[0]), 0)
+    chosen = jnp.where(numbers == line - first, lack, 0.0).astype(bf16)
+    found = jnp.dot(chosen, rows, preferred_element_type=f32)
     pieces = []
     for start in range(0, half, stride):
-        pieces += [found[start : start + stride - count], told[...]]
-    out[...] = jnp.concatenate(pieces).astype(out.dtype)
+        pieces += [found[start : start + stride - count], told]
+    return jnp.concatenate(pieces)
+
+
+def dense(first, stride, line, rows, told, out):
+    found = dense_rows(first, out.shape[0], stride, line[...], rows[...], told[...])
+    out[...] = found.astype(out.dtype)
+
+
+def start_kernel(stride, far, away, half, notes, told, negatives, *refs):
+    out = refs[-1]
+    if negatives.dtype == bf16:
+        scores = lax.dot_general(
+            negatives[...], half[...], (((1,), (1,)), ((), ())), preferred_element_type=f32
+        )
+        sums = jnp.sum(jnp.exp(score_scale * scores), 0, keepdims=True)
+    else:
+        sums = negatives[...]
+    weight, line = notes[0:1, :], notes[1:2, :].astype(jnp.int32)
+    lack = weight / (weight + sums) - 1.0
+    count = out.shape[0]
+    rows = dense_rows(count if far else 0, count, stride, line, away[...], told[...], lack)
+    out[...] = rows + refs[0][...] if far else rows
 
 
 def kept_kernel(stride, line, rows, told, out):
@@ -340,9 +381,11 @@
             pieces = pieces + [flip(piece, mask) for piece in pieces]
         return pieces
 
-    def reduce_near(kept, came):
+    def reduce_near(kept, came=None):
         spans = [slice(i * stride, (i + 1) * stride) for i in range(4)]
-        pieces = [kept[span] + came[span].astype(f32) for span in spans]
+        pieces = [kept[span] for span in spans]
+        if came is not None:
+            pieces = [piece + came[span].astype(f32) for piece, span in zip(pieces, spans)]
         near = [
             flip(piece.astype(f16), mask)
             for piece, mask in zip(pieces[1:], (owners, masks[0], owners + masks[0]))
@@ -411,38 +454,68 @@
         split = len(parts) if step == 0 else -1
         ids = [device, jnp.transpose(item_owner, (0, 2, 1)), item_row, fifo_head[None]]
         ids = ids if small and step == 0 else []
-        query_unit, found, sums, *own = call(
+        outs, extra = [(matrix, f32), (matrix, f32), (scalars, f32)], []
+        if step == 0:
+            extra = [places[None, :]]
+            outs += [(matrix, bf16), (matrix, bf16), ((8 + queue_rows * bool(ids), query_count), f32), ((8, width), f32)]
+            outs += [((queue_rows, width), f32)] if ids else []
+        query_unit, found, sums, *rest = call(
             functools.partial(first_kernel, step, len(parts[:split]), len(ids)),
-            [(matrix, f32), (matrix, f32), (scalars, f32)] + [((queue_rows, width), f32)] * bool(ids),
+            outs,
             queries,
             found_at[None, :],
             negatives,
             *ids,
             *parts[:split],
+            *extra,
         )
         if step == 0:
-            told = own[0] if own else own_told()
-        sent, rows, unit, top = call(
-            functools.partial(main_kernel, last_place, len(parts[split:]), stride),
-            [((half_rows, width), bf16), (matrix, bf16), (matrix, f32), ((8, width), f32)],
-            found,
-            found_at[None, :],
-            places[None, :],
-            query_unit,
-            queue if small and step == 0 else sums,
-            *parts[split:],
-            told,
-        )
+            away, half, notes, top, *own = rest
+            told, unit = own[0] if ids else own_told(), found
+            mine = [away, half, notes, told]
+            beside = [flip(notes, masks[-1])]
+            beside.append(beside[0][8:, :width] if ids else flip(told, masks[-1]))
+            quarter = query_count // 2
+            for part in (half, away):
+                pieces = [part[i * quarter : (i + 1) * quarter] for i in range(2)]
+                beside.insert(0, jnp.concatenate([flip(piece, masks[-1]) for piece in pieces]))
+            if small:
+                lines = [queue, queue]
+            else:
+                lines = [negatives.reshape(1, query_count)]
+                lines.append(flip(lines[0], masks[-1]))
+            outs = [((half_rows, width), f32)]
+            (kept,) = call(functools.partial(start_kernel, stride, False), outs, *mine, lines[0])
+            kernel = functools.partial(start_kernel, stride, True)
+            (kept,) = call(kernel, outs, *beside, lines[1], kept)
+            kept = grad_scale * kept
+            for mask in masks[-2:0:-1]:
+                middle = kept.shape[0] // 2
+                kept, sent = kept[:middle], kept[middle:].astype(f16)
+                kept = kept + flip(sent, mask).astype(f32)
+            total, early = reduce_near(kept)
+        else:
+            sent, rows, unit, top = call(
+                functools.partial(main_kernel, last_place, len(parts[split:]), stride),
+                [((half_rows, width), bf16), (matrix, bf16), (matrix, f32), ((8, width), f32)],
+                found,
+                found_at[None, :],
+                places[None, :],
+                query_unit,
+                sums,
+                *parts[split:],
+                told,
+            )
+            kernel = functools.partial(kept_kernel, stride)
+            (kept,) = call(kernel, [((half_rows, width), f32)], places[None, :], rows, told)
+            sent = (grad_scale * sent).astype(bf16)
+            kept = grad_scale * kept
+            for mask in masks[:1:-1]:
+                kept = kept + flip(sent, mask).astype(f32)
+                middle = kept.shape[0] // 2
+                kept, sent = kept[:middle], kept[middle:].astype(f16)
+            total, early = reduce_near(kept, flip(sent, masks[1]))
         tops.append(top)
-        kernel = functools.partial(kept_kernel, stride)
-        (kept,) = call(kernel, [((half_rows, width), f32)], places[None, :], rows, told)
-        sent = (grad_scale * sent).astype(bf16)
-        kept = grad_scale * kept
-        for mask in masks[:1:-1]:
-            kept = kept + flip(sent, mask).astype(f32)
-            middle = kept.shape[0] // 2
-            kept, sent = kept[:middle], kept[middle:].astype(f16)
-        total, early = reduce_near(kept, flip(sent, masks[1]))
 
         more = step + 1 < step_count
         args = [queries, unit, queue if small else negatives, early, *([] if small else [moment])]

time: 69.3 us -> 68.3 us (0.986)
  waiting for transfers between devices: 27.5 us -> 23.8 us
  starting transfers between devices: 26.1 us -> 28.5 us
    ppermute x2, starting transfers between devices: 1 us -> 2.89 us  [turned(): found.append(lax.ppermute(piece, 'batch', pairs))]
    ppermute x2, waiting for transfers between devices: 7.65 us -> 5.76 us  [turned(): found.append(lax.ppermute(piece, 'batch', pairs))]
    all_to_all x1, waiting for transfers between devices: 3.86 us -> 2.32 us  [per_device(): lax.all_to_all(queue, ('batch', 'table'), 0, 0, tiled=True)]
    ppermute x23 -> x27, starting transfers between devices: 20.1 us -> 20.6 us  [flip(): lax.ppermute(piece, ('batch', 'table'), [(i ^ mask, i) for i in range(cou...]
    ppermute x23 -> x27, waiting for transfers between devices: 16 us -> 15.7 us  [flip(): lax.ppermute(piece, ('batch', 'table'), [(i ^ mask, i) for i in range(cou...]
  transfers between devices with their start and end apart: 26 -> 30, of which waited for: 18 -> 18; matrix products, arithmetic and copies ran while one was open for 3% -> 3% of each run, Pallas kernels for 11% -> 12%
where the time goes in v9:
time: 68.3 us; the launch traced here: 68.1 us
  starting transfers between devices  28.5 us (42%)
  waiting for transfers between devices  23.8 us (35%)
  Pallas kernels  10.9 us (16%)
  local copies, waits for them, and re-layouts  1.79 us (3%)
  between operations  1.69 us (2%)
  other arithmetic  1.39 us (2%)
    ppermute x27, starting transfers between devices, flip(): lax.ppermute(piece, ('batch', 'table'), [(i ^ mask, i) for i in range(cou...  20.6 us
    ppermute x27, waiting for transfers between devices, flip(): lax.ppermute(piece, ('batch', 'table'), [(i ^ mask, i) for i in range(cou...  15.7 us
    pallas_call x12, Pallas kernels, call(): pl.pallas_call(kernel, out_shape=[jax.ShapeDtypeStruct(shape, dtype) for...  10.9 us
    ppermute x2, waiting for transfers between devices, turned(): found.append(lax.ppermute(piece, 'batch', pairs))  5.76 us
    all_to_all x1, starting transfers between devices, per_device(): lax.all_to_all(queue, ('batch', 'table'), 0, 0, tiled=True)  5.03 us
    ppermute x2, starting transfers between devices, turned(): found.append(lax.ppermute(piece, 'batch', pairs))  2.89 us
    all_to_all x1, waiting for transfers between devices, per_device(): lax.all_to_all(queue, ('batch', 'table'), 0, 0, tiled=True)  2.32 us
  transfers between devices with their start and end apart: 30, of which 18 were waited for; matrix products, arithmetic and copies ran while one was open for 3% of the time, Pallas kernels for 12%

profile of v9, /device:TPU:0, one launch (start us, length us, event | category | flops | bytes accessed | tf_op | source)
XLA Modules:
  0.0 68.1 jit_solution(7029120349864999162)
XLA Ops:
  0.6 3.0 %collective-permute-start = (f32[480,128]{1,0:T(8,128)}, f32[480,128]{1,0:T(8,128)S(1)}, u32[]{:S(2)}, u32[]{:S(2)}) collective-permute-start(f32[480,128]{1,0:T(8,128)} %refs_0_.3), channel_id=1, source_target_pairs={{2,0},{3,1},{0,2},{1,3},{6,4},{7,5},{4,6},{5,7},{10,8},{11,9},{8,1... | collective-permute-start | bytes 737288 | tf_op jit(solution)/shard_map/ppermute | solution.py:40
  5.0 5.0 %all-to-all-start = ((bf16[32,8,128]{2,1,0:T(8,128)(2,1)}), bf16[32,8,128]{2,1,0:T(8,128)(2,1)S(1)}, u32[]{:S(2)}, u32[]{:S(2)}) async-start(bf16[32,8,128]{2,1,0:T(8,128)(2,1)} %broadcast_in_dim.65), calls=%async_computation | async-start | bytes 131072 | tf_op jit(solution)/shard_map/all_to_all | solution.py:434
  11.7 2.0 %shard_map.110 = (f32[512,128]{1,0:T(8,128)}, f32[512,128]{1,0:T(8,128)S(1)}, f32[512,1]{1,0:T(8,128)}, bf16[512,128]{1,0:T(8,128)(2,1)S(1)}, bf16[512,128]{1,0:...) custom-call(bf16[2,512,128]{2,1,0:T(8,128)(2,1)S(1)} %copy-done, ...), custom_call_target="tpu_custom_call" | custom-call | tf_op jit(solution)/shard_map/pallas_call | solution.py:335
  15.1 2.3 %all-to-all-done = bf16[32,8,128]{2,1,0:T(8,128)(2,1)S(1)} async-done(((bf16[32,8,128]{2,1,0:T(8,128)(2,1)}), bf16[32,8,128]{2,1,0:T(8,128)(2,1)S(1)}, u32[]{:S(2)}, u32[]{:S(2)}) %all-to-all-start) | async-done | bytes 65568 | tf_op jit(solution)/shard_map/all_to_all | solution.py:434
  19.7 1.3 %collective-permute-start.9 = (f16[248,128]{1,0:T(8,128)(2,1)S(1)}, f16[248,128]{1,0:T(8,128)(2,1)S(1)}, u32[]{:S(2)}, u32[]{:S(2)}) collective-permute-start(f16[248,128]{1,0:T(8,128)(2,1)S(1)} %get-tuple-element.97), channel_id=1, source_target_pairs={{2,0},{3,1},{0,2},{1,3},{6,4},{7,5},{4,6},{5,7},{10,8},{11,9},{8,1... | collective-permute-start | bytes 190472 | tf_op jit(solution)/shard_map/ppermute | solution.py:40
  21.1 1.4 %collective-permute-start.8 = (f16[248,128]{1,0:T(8,128)(2,1)S(1)}, f16[248,128]{1,0:T(8,128)(2,1)S(1)}, u32[]{:S(2)}, u32[]{:S(2)}) collective-permute-start(f16[248,128]{1,0:T(8,128)(2,1)S(1)} %get-tuple-element.95), channel_id=1, source_target_pairs={{4,0},{5,1},{6,2},{7,3},{0,4},{1,5},{2,6},{3,7},{12,8},{13,9},{14,... | collective-permute-start | bytes 190472 | tf_op jit(solution)/shard_map/ppermute | solution.py:40
  22.5 2.2 %collective-permute-done.10 = f16[248,128]{1,0:T(8,128)(2,1)S(1)} collective-permute-done((f16[248,128]{1,0:T(8,128)(2,1)S(1)}, f16[248,128]{1,0:T(8,128)(2,1)S(1)}, u32[]{:S(2)}, u32[]{:S(2)}) %collective-permute-start.10) | collective-permute-done | bytes 63520 | tf_op jit(solution)/shard_map/ppermute | solution.py:40
  25.4 1.5 %collective-permute-start.11 = (f16[248,128]{1,0:T(8,128)(2,1)S(1)}, f16[248,128]{1,0:T(8,128)(2,1)S(1)}, u32[]{:S(2)}, u32[]{:S(2)}) collective-permute-start(f16[248,128]{1,0:T(8,128)(2,1)S(1)} %fusion.9), channel_id=1, source_target_pairs={{16,0},{20,4},{24,8},{28,12},{0,16},{4,20},{8,24},{12,28},{17,1},{... | collective-permute-start | bytes 190472 | tf_op jit(solution)/shard_map/ppermute | solution.py:51
  28.6 2.7 %collective-permute-done.11 = f16[248,128]{1,0:T(8,128)(2,1)S(1)} collective-permute-done((f16[248,128]{1,0:T(8,128)(2,1)S(1)}, f16[248,128]{1,0:T(8,128)(2,1)S(1)}, u32[]{:S(2)}, u32[]{:S(2)}) %collective-permute-start.11) | collective-permute-done | bytes 63520 | tf_op jit(solution)/shard_map/ppermute | solution.py:51
  31.4 2.8 %collective-permute-start.14 = (f16[248,128]{1,0:T(8,128)(2,1)S(1)}, f16[248,128]{1,0:T(8,128)(2,1)S(1)}, u32[]{:S(2)}, u32[]{:S(2)}) collective-permute-start(f16[248,128]{1,0:T(8,128)(2,1)S(1)} %add_convert_fusion.1), channel_id=1, source_target_pairs={{12,0},{13,1},{14,2},{15,3},{8,4},{9,5},{10,6},{11,7},{4,8},{5,9},... | collective-permute-start | bytes 190472 | tf_op jit(solution)/shard_map/ppermute | solution.py:40
  37.2 1.4 %collective-permute-done.13 = f16[248,128]{1,0:T(8,128)(2,1)S(1)} collective-permute-done((f16[248,128]{1,0:T(8,128)(2,1)S(1)}, f16[248,128]{1,0:T(8,128)(2,1)S(1)}, u32[]{:S(2)}, u32[]{:S(2)}) %collective-permute-start.13) | collective-permute-done | bytes 63520 | tf_op jit(solution)/shard_map/ppermute | solution.py:40
  41.2 2.1 %collective-permute-done.16 = f16[240,128]{1,0:T(8,128)(2,1)S(1)} collective-permute-done((f16[240,128]{1,0:T(8,128)(2,1)S(1)}, f16[240,128]{1,0:T(8,128)(2,1)S(1)}, u32[]{:S(2)}, u32[]{:S(2)}) %collective-permute-start.16) | collective-permute-done | bytes 61472 | tf_op jit(solution)/shard_map/ppermute | solution.py:40
  43.3 1.1 %shard_map.117 = (f32[512,128]{1,0:T(8,128)S(1)}, f32[512,128]{1,0:T(8,128)S(1)}, f32[512,1]{1,0:T(8,128)S(1)}) custom-call(bf16[2,512,128]{2,1,0:T(8,128)(2,1)S(1)} %copy-done, s32[1,512]{1,0:T(1,128)S(1)} %multiply_add_fusion.1.line.found_line, bf16[256,128]{1,0:T(8,128)(2,1)S(1)} %get-tuple-element.50.negatives, ...), custom_call_target="tpu_custom_call" | custom-call | tf_op jit(solution)/shard_map/pallas_call | solution.py:335
  44.5 1.2 %shard_map.118 = (bf16[992,128]{1,0:T(8,128)(2,1)S(1)}, bf16[512,128]{1,0:T(8,128)(2,1)S(1)}, f32[512,128]{1,0:T(8,128)S(1)}, f32[8,128]{1,0:T(8,128)S(1)}) custom-call(f32[512,128]{1,0:T(8,128)S(1)} %get-tuple-element.60.found, s32[1,512]{1,0:T(1,128)S(1)} %multiply_add_fusion.1.line.found_line, s32[1,512]{1,0:T(1,128)S(1)} %get-tuple-element.102.line, ...), custom_call_target="tpu_custom_call" | custom-call | tf_op jit(solution)/shard_map/pallas_call | solution.py:335
  48.2 1.3 %collective-permute-start.24 = (f16[248,128]{1,0:T(8,128)(2,1)S(1)}, f16[248,128]{1,0:T(8,128)(2,1)S(1)}, u32[]{:S(2)}, u32[]{:S(2)}) collective-permute-start(f16[248,128]{1,0:T(8,128)(2,1)S(1)} %get-tuple-element.93), channel_id=1, source_target_pairs={{6,0},{7,1},{4,2},{5,3},{2,4},{3,5},{0,6},{1,7},{14,8},{15,9},{12,... | collective-permute-start | bytes 190472 | tf_op jit(solution)/shard_map/ppermute | solution.py:40
  49.4 1.6 %collective-permute-start.23 = (f16[248,128]{1,0:T(8,128)(2,1)S(1)}, f16[248,128]{1,0:T(8,128)(2,1)S(1)}, u32[]{:S(2)}, u32[]{:S(2)}) collective-permute-start(f16[248,128]{1,0:T(8,128)(2,1)S(1)} %get-tuple-element.92), channel_id=1, source_target_pairs={{2,0},{3,1},{0,2},{1,3},{6,4},{7,5},{4,6},{5,7},{10,8},{11,9},{8,1... | collective-permute-start | bytes 190472 | tf_op jit(solution)/shard_map/ppermute | solution.py:40
  51.0 1.5 %collective-permute-done.22 = f16[248,128]{1,0:T(8,128)(2,1)S(1)} collective-permute-done((f16[248,128]{1,0:T(8,128)(2,1)S(1)}, f16[248,128]{1,0:T(8,128)(2,1)S(1)}, u32[]{:S(2)}, u32[]{:S(2)}) %collective-permute-start.22) | collective-permute-done | bytes 63520 | tf_op jit(solution)/shard_map/ppermute | solution.py:40
  52.5 1.2 %collective-permute-done.24 = f16[248,128]{1,0:T(8,128)(2,1)S(1)} collective-permute-done((f16[248,128]{1,0:T(8,128)(2,1)S(1)}, f16[248,128]{1,0:T(8,128)(2,1)S(1)}, u32[]{:S(2)}, u32[]{:S(2)}) %collective-permute-start.24) | collective-permute-done | bytes 63520 | tf_op jit(solution)/shard_map/ppermute | solution.py:40
  54.5 1.4 %collective-permute-start.25 = (f16[248,128]{1,0:T(8,128)(2,1)S(1)}, f16[248,128]{1,0:T(8,128)(2,1)S(1)}, u32[]{:S(2)}, u32[]{:S(2)}) collective-permute-start(f16[248,128]{1,0:T(8,128)(2,1)S(1)} %fusion.6), channel_id=1, source_target_pairs={{16,0},{20,4},{24,8},{28,12},{0,16},{4,20},{8,24},{12,28},{17,1},{... | collective-permute-start | bytes 190472 | tf_op jit(solution)/shard_map/ppermute | solution.py:51
  55.8 1.5 %shard_map.120 = (f32[2,512]{1,0:T(2,128)}, bf16[2,512,128]{2,1,0:T(8,128)(2,1)}, bf16[8,128]{1,0:T(8,128)(2,1)}, f32[248,128]{1,0:T(8,128)S(1)}) custom-call(bf16[2,512,128]{2,1,0:T(8,128)(2,1)S(1)} %copy-done, f32[512,128]{1,0:T(8,128)S(1)} %get-tuple-element.63.item, bf16[256,128]{1,0:T(8,128)(2,1)S(1)} %get-tuple-element.50.negatives, ...), custom_call_target="tpu_custom_call" | custom-call | tf_op jit(solution)/shard_map/pallas_call | solution.py:335
  57.3 3.1 %collective-permute-done.25 = f16[248,128]{1,0:T(8,128)(2,1)S(1)} collective-permute-done((f16[248,128]{1,0:T(8,128)(2,1)S(1)}, f16[248,128]{1,0:T(8,128)(2,1)S(1)}, u32[]{:S(2)}, u32[]{:S(2)}) %collective-permute-start.25) | collective-permute-done | bytes 63520 | tf_op jit(solution)/shard_map/ppermute | solution.py:51
  60.6 2.1 %collective-permute-start.28 = (f16[248,128]{1,0:T(8,128)(2,1)S(1)}, f16[248,128]{1,0:T(8,128)(2,1)S(1)}, u32[]{:S(2)}, u32[]{:S(2)}) collective-permute-start(f16[248,128]{1,0:T(8,128)(2,1)S(1)} %add_convert_fusion), channel_id=1, source_target_pairs={{12,0},{13,1},{14,2},{15,3},{8,4},{9,5},{10,6},{11,7},{4,8},{5,9},... | collective-permute-start | bytes 190472 | tf_op jit(solution)/shard_map/ppermute | solution.py:40
  62.7 1.2 %collective-permute-start.27 = (f16[248,128]{1,0:T(8,128)(2,1)S(1)}, f16[248,128]{1,0:T(8,128)(2,1)S(1)}, u32[]{:S(2)}, u32[]{:S(2)}) collective-permute-start(f16[248,128]{1,0:T(8,128)(2,1)S(1)} %add_convert_fusion), channel_id=1, source_target_pairs={{4,0},{5,1},{6,2},{7,3},{0,4},{1,5},{2,6},{3,7},{12,8},{13,9},{14,... | collective-permute-start | bytes 190472 | tf_op jit(solution)/shard_map/ppermute | solution.py:40
  65.8 1.2 %collective-permute-done.27 = f16[248,128]{1,0:T(8,128)(2,1)S(1)} collective-permute-done((f16[248,128]{1,0:T(8,128)(2,1)S(1)}, f16[248,128]{1,0:T(8,128)(2,1)S(1)}, u32[]{:S(2)}, u32[]{:S(2)}) %collective-permute-start.27) | collective-permute-done | bytes 63520 | tf_op jit(solution)/shard_map/ppermute | solution.py:40
  (96 shorter events, 20.3 us)
Async XLA Ops:
  0.6 9.4 %collective-permute-start = (f32[480,128]{1,0:T(8,128)}, f32[480,128]{1,0:T(8,128)S(1)}, u32[]{:S(2)}, u32[]{:S(2)}) collective-permute-start(f32[480,128]{1,0:T(8,128)} %refs_0_.3), channel_id=1, source_target_pairs={{2,0},{3,1},{0,2},{1,3},{6,4},{7,5},{4,6},{5,7},{10,8},{11,9},{8,1... | collective-permute-start | bytes 737288 | tf_op jit(solution)/shard_map/ppermute | solution.py:40
  3.6 7.5 %collective-permute-start.1 = (f32[480,128]{1,0:T(8,128)}, f32[480,128]{1,0:T(8,128)S(1)}, u32[]{:S(2)}, u32[]{:S(2)}) collective-permute-start(f32[480,128]{1,0:T(8,128)} %refs_0_.3), channel_id=1, source_target_pairs={{1,0},{0,1},{3,2},{2,3},{5,4},{4,5},{7,6},{6,7},{9,8},{8,9},{11,10... | collective-permute-start | bytes 737288 | tf_op jit(solution)/shard_map/ppermute | solution.py:40
  5.0 12.5 %all-to-all-start = ((bf16[32,8,128]{2,1,0:T(8,128)(2,1)}), bf16[32,8,128]{2,1,0:T(8,128)(2,1)S(1)}, u32[]{:S(2)}, u32[]{:S(2)}) async-start(bf16[32,8,128]{2,1,0:T(8,128)(2,1)} %broadcast_in_dim.65), calls=%async_computation | async-start | bytes 131072 | tf_op jit(solution)/shard_map/all_to_all | solution.py:434
  13.7 4.4 %collective-permute-start.4 = (bf16[256,128]{1,0:T(8,128)(2,1)S(1)}, bf16[256,128]{1,0:T(8,128)(2,1)S(1)}, u32[]{:S(2)}, u32[]{:S(2)}) collective-permute-start(bf16[256,128]{1,0:T(8,128)(2,1)S(1)} %get-tuple-element.101), channel_id=1, source_target_pairs={{1,0},{0,1},{3,2},{2,3},{5,4},{4,5},{7,6},{6,7},{9,8},{8,9},{11,10... | collective-permute-start | bytes 196616 | tf_op jit(solution)/shard_map/ppermute | solution.py:40
  14.0 4.1 %collective-permute-start.3 = (bf16[256,128]{1,0:T(8,128)(2,1)S(1)}, bf16[256,128]{1,0:T(8,128)(2,1)S(1)}, u32[]{:S(2)}, u32[]{:S(2)}) collective-permute-start(bf16[256,128]{1,0:T(8,128)(2,1)S(1)} %get-tuple-element.100), channel_id=1, source_target_pairs={{1,0},{0,1},{3,2},{2,3},{5,4},{4,5},{7,6},{6,7},{9,8},{8,9},{11,10... | collective-permute-start | bytes 196616 | tf_op jit(solution)/shard_map/ppermute | solution.py:40
  14.3 3.8 %collective-permute-start.7 = (f32[16,512]{1,0:T(8,128)S(1)}, f32[16,512]{1,0:T(8,128)S(1)}, u32[]{:S(2)}, u32[]{:S(2)}) collective-permute-start(f32[16,512]{1,0:T(8,128)S(1)} %get-tuple-element.46.notes), channel_id=1, source_target_pairs={{1,0},{0,1},{3,2},{2,3},{5,4},{4,5},{7,6},{6,7},{9,8},{8,9},{11,10... | collective-permute-start | bytes 98312 | tf_op jit(solution)/shard_map/ppermute | solution.py:40
  19.0 5.7 %collective-permute-start.10 = (f16[248,128]{1,0:T(8,128)(2,1)S(1)}, f16[248,128]{1,0:T(8,128)(2,1)S(1)}, u32[]{:S(2)}, u32[]{:S(2)}) collective-permute-start(f16[248,128]{1,0:T(8,128)(2,1)S(1)} %get-tuple-element.96), channel_id=1, source_target_pairs={{6,0},{7,1},{4,2},{5,3},{2,4},{3,5},{0,6},{1,7},{14,8},{15,9},{12,... | collective-permute-start | bytes 190472 | tf_op jit(solution)/shard_map/ppermute | solution.py:40
  19.7 4.9 %collective-permute-start.9 = (f16[248,128]{1,0:T(8,128)(2,1)S(1)}, f16[248,128]{1,0:T(8,128)(2,1)S(1)}, u32[]{:S(2)}, u32[]{:S(2)}) collective-permute-start(f16[248,128]{1,0:T(8,128)(2,1)S(1)} %get-tuple-element.97), channel_id=1, source_target_pairs={{2,0},{3,1},{0,2},{1,3},{6,4},{7,5},{4,6},{5,7},{10,8},{11,9},{8,1... | collective-permute-start | bytes 190472 | tf_op jit(solution)/shard_map/ppermute | solution.py:40
  21.1 4.3 %collective-permute-start.8 = (f16[248,128]{1,0:T(8,128)(2,1)S(1)}, f16[248,128]{1,0:T(8,128)(2,1)S(1)}, u32[]{:S(2)}, u32[]{:S(2)}) collective-permute-start(f16[248,128]{1,0:T(8,128)(2,1)S(1)} %get-tuple-element.95), channel_id=1, source_target_pairs={{4,0},{5,1},{6,2},{7,3},{0,4},{1,5},{2,6},{3,7},{12,8},{13,9},{14,... | collective-permute-start | bytes 190472 | tf_op jit(solution)/shard_map/ppermute | solution.py:40
  25.4 5.9 %collective-permute-start.11 = (f16[248,128]{1,0:T(8,128)(2,1)S(1)}, f16[248,128]{1,0:T(8,128)(2,1)S(1)}, u32[]{:S(2)}, u32[]{:S(2)}) collective-permute-start(f16[248,128]{1,0:T(8,128)(2,1)S(1)} %fusion.9), channel_id=1, source_target_pairs={{16,0},{20,4},{24,8},{28,12},{0,16},{4,20},{8,24},{12,28},{17,1},{... | collective-permute-start | bytes 190472 | tf_op jit(solution)/shard_map/ppermute | solution.py:51
  31.3 4.3 %collective-permute-start.12 = (f16[248,128]{1,0:T(8,128)(2,1)S(1)}, f16[248,128]{1,0:T(8,128)(2,1)S(1)}, u32[]{:S(2)}, u32[]{:S(2)}) collective-permute-start(f16[248,128]{1,0:T(8,128)(2,1)S(1)} %add_convert_fusion.1), channel_id=1, source_target_pairs={{8,0},{9,1},{10,2},{11,3},{12,4},{13,5},{14,6},{15,7},{0,8},{1,9},... | collective-permute-start | bytes 190472 | tf_op jit(solution)/shard_map/ppermute | solution.py:40
  31.4 5.7 %collective-permute-start.14 = (f16[248,128]{1,0:T(8,128)(2,1)S(1)}, f16[248,128]{1,0:T(8,128)(2,1)S(1)}, u32[]{:S(2)}, u32[]{:S(2)}) collective-permute-start(f16[248,128]{1,0:T(8,128)(2,1)S(1)} %add_convert_fusion.1), channel_id=1, source_target_pairs={{12,0},{13,1},{14,2},{15,3},{8,4},{9,5},{10,6},{11,7},{4,8},{5,9},... | collective-permute-start | bytes 190472 | tf_op jit(solution)/shard_map/ppermute | solution.py:40
  34.3 4.2 %collective-permute-start.13 = (f16[248,128]{1,0:T(8,128)(2,1)S(1)}, f16[248,128]{1,0:T(8,128)(2,1)S(1)}, u32[]{:S(2)}, u32[]{:S(2)}) collective-permute-start(f16[248,128]{1,0:T(8,128)(2,1)S(1)} %add_convert_fusion.1), channel_id=1, source_target_pairs={{4,0},{5,1},{6,2},{7,3},{0,4},{1,5},{2,6},{3,7},{12,8},{13,9},{14,... | collective-permute-start | bytes 190472 | tf_op jit(solution)/shard_map/ppermute | solution.py:40
  36.1 4.6 %collective-permute-start.15 = (f16[240,128]{1,0:T(8,128)(2,1)S(1)}, f16[240,128]{1,0:T(8,128)(2,1)S(1)}, u32[]{:S(2)}, u32[]{:S(2)}) collective-permute-start(f16[240,128]{1,0:T(8,128)(2,1)S(1)} %get-tuple-element.89), channel_id=1, source_target_pairs={{2,0},{3,1},{0,2},{1,3},{6,4},{7,5},{4,6},{5,7},{10,8},{11,9},{8,1... | collective-permute-start | bytes 184328 | tf_op jit(solution)/shard_map/ppermute | solution.py:40
  36.1 7.1 %collective-permute-start.17 = (f16[240,128]{1,0:T(8,128)(2,1)S(1)}, f16[240,128]{1,0:T(8,128)(2,1)S(1)}, u32[]{:S(2)}, u32[]{:S(2)}) collective-permute-start(f16[240,128]{1,0:T(8,128)(2,1)S(1)} %get-tuple-element.89), channel_id=1, source_target_pairs={{1,0},{0,1},{3,2},{2,3},{5,4},{4,5},{7,6},{6,7},{9,8},{8,9},{11,10... | collective-permute-start | bytes 184328 | tf_op jit(solution)/shard_map/ppermute | solution.py:40
  38.9 4.3 %collective-permute-start.16 = (f16[240,128]{1,0:T(8,128)(2,1)S(1)}, f16[240,128]{1,0:T(8,128)(2,1)S(1)}, u32[]{:S(2)}, u32[]{:S(2)}) collective-permute-start(f16[240,128]{1,0:T(8,128)(2,1)S(1)} %get-tuple-element.87), channel_id=1, source_target_pairs={{2,0},{3,1},{0,2},{1,3},{6,4},{7,5},{4,6},{5,7},{10,8},{11,9},{8,1... | collective-permute-start | bytes 184328 | tf_op jit(solution)/shard_map/ppermute | solution.py:40
  39.4 3.9 %collective-permute-start.18 = (f16[240,128]{1,0:T(8,128)(2,1)S(1)}, f16[240,128]{1,0:T(8,128)(2,1)S(1)}, u32[]{:S(2)}, u32[]{:S(2)}) collective-permute-start(f16[240,128]{1,0:T(8,128)(2,1)S(1)} %get-tuple-element.87), channel_id=1, source_target_pairs={{1,0},{0,1},{3,2},{2,3},{5,4},{4,5},{7,6},{6,7},{9,8},{8,9},{11,10... | collective-permute-start | bytes 184328 | tf_op jit(solution)/shard_map/ppermute | solution.py:40
  47.5 5.1 %collective-permute-start.22 = (f16[248,128]{1,0:T(8,128)(2,1)S(1)}, f16[248,128]{1,0:T(8,128)(2,1)S(1)}, u32[]{:S(2)}, u32[]{:S(2)}) collective-permute-start(f16[248,128]{1,0:T(8,128)(2,1)S(1)} %get-tuple-element.94), channel_id=1, source_target_pairs={{4,0},{5,1},{6,2},{7,3},{0,4},{1,5},{2,6},{3,7},{12,8},{13,9},{14,... | collective-permute-start | bytes 190472 | tf_op jit(solution)/shard_map/ppermute | solution.py:40
  48.2 5.6 %collective-permute-start.24 = (f16[248,128]{1,0:T(8,128)(2,1)S(1)}, f16[248,128]{1,0:T(8,128)(2,1)S(1)}, u32[]{:S(2)}, u32[]{:S(2)}) collective-permute-start(f16[248,128]{1,0:T(8,128)(2,1)S(1)} %get-tuple-element.93), channel_id=1, source_target_pairs={{6,0},{7,1},{4,2},{5,3},{2,4},{3,5},{0,6},{1,7},{14,8},{15,9},{12,... | collective-permute-start | bytes 190472 | tf_op jit(solution)/shard_map/ppermute | solution.py:40
  49.4 5.0 %collective-permute-start.23 = (f16[248,128]{1,0:T(8,128)(2,1)S(1)}, f16[248,128]{1,0:T(8,128)(2,1)S(1)}, u32[]{:S(2)}, u32[]{:S(2)}) collective-permute-start(f16[248,128]{1,0:T(8,128)(2,1)S(1)} %get-tuple-element.92), channel_id=1, source_target_pairs={{2,0},{3,1},{0,2},{1,3},{6,4},{7,5},{4,6},{5,7},{10,8},{11,9},{8,1... | collective-permute-start | bytes 190472 | tf_op jit(solution)/shard_map/ppermute | solution.py:40
  54.5 5.9 %collective-permute-start.25 = (f16[248,128]{1,0:T(8,128)(2,1)S(1)}, f16[248,128]{1,0:T(8,128)(2,1)S(1)}, u32[]{:S(2)}, u32[]{:S(2)}) collective-permute-start(f16[248,128]{1,0:T(8,128)(2,1)S(1)} %fusion.6), channel_id=1, source_target_pairs={{16,0},{20,4},{24,8},{28,12},{0,16},{4,20},{8,24},{12,28},{17,1},{... | collective-permute-start | bytes 190472 | tf_op jit(solution)/shard_map/ppermute | solution.py:51
  60.4 4.3 %collective-permute-start.26 = (f16[248,128]{1,0:T(8,128)(2,1)S(1)}, f16[248,128]{1,0:T(8,128)(2,1)S(1)}, u32[]{:S(2)}, u32[]{:S(2)}) collective-permute-start(f16[248,128]{1,0:T(8,128)(2,1)S(1)} %add_convert_fusion), channel_id=1, source_target_pairs={{8,0},{9,1},{10,2},{11,3},{12,4},{13,5},{14,6},{15,7},{0,8},{1,9},... | collective-permute-start | bytes 190472 | tf_op jit(solution)/shard_map/ppermute | solution.py:40
  60.6 5.1 %collective-permute-start.28 = (f16[248,128]{1,0:T(8,128)(2,1)S(1)}, f16[248,128]{1,0:T(8,128)(2,1)S(1)}, u32[]{:S(2)}, u32[]{:S(2)}) collective-permute-start(f16[248,128]{1,0:T(8,128)(2,1)S(1)} %add_convert_fusion), channel_id=1, source_target_pairs={{12,0},{13,1},{14,2},{15,3},{8,4},{9,5},{10,6},{11,7},{4,8},{5,9},... | collective-permute-start | bytes 190472 | tf_op jit(solution)/shard_map/ppermute | solution.py:40
  62.7 4.2 %collective-permute-start.27 = (f16[248,128]{1,0:T(8,128)(2,1)S(1)}, f16[248,128]{1,0:T(8,128)(2,1)S(1)}, u32[]{:S(2)}, u32[]{:S(2)}) collective-permute-start(f16[248,128]{1,0:T(8,128)(2,1)S(1)} %add_convert_fusion), channel_id=1, source_target_pairs={{4,0},{5,1},{6,2},{7,3},{0,4},{1,5},{2,6},{3,7},{12,8},{13,9},{14,... | collective-permute-start | bytes 190472 | tf_op jit(solution)/shard_map/ppermute | solution.py:40
  (12 other events, 43.0 us)

commit v10 on v9

--- a/solution.py
+++ b/solution.py
@@ -307,25 +307,24 @@
     return table - learn_rate * grad / jnp.sqrt(accum), accum
 
 
-def update_kernel(scale, total, table, accum, inverse, table_out, accum_out, inverse_out, unit):
+def update_kernel(scale, total, table, accum, inverse, table_out, accum_out, *more):
     grad = total[: table.shape[0], :]
     rows, accum_out[...] = adagrad(grad, table[...], accum[...], inverse[...])
     table_out[...] = rows
-    unit[...], norm = unit_of(rows)
-    inverse_out[...] = scale / norm
-
-
-def finish_kernel(side, mine, other, *refs):
-    near, far, (table_out, line_out) = refs[:3], refs[3:6], refs[6:]
-    count, first = near[0].shape[0], side[...] == 0
-
-    def in_order(near, far):
-        return jnp.concatenate([jnp.where(first, near, far), jnp.where(first, far, near)])
-
-    state = [in_order(a[...], b[...]) for a, b in zip(near, far)]
-    rows, accum = adagrad(in_order(mine[:count, :], other[:count, :]), *state)
-    table_out[...] = rows
-    wide = jnp.pad(accum, ((0, -2 * count % 128), (0, 0)))
+    if more:
+        inverse_out, unit = more
+        unit[...], norm = unit_of(rows)
+        inverse_out[...] = scale / norm
+
+
+def finish_kernel(side, other, near_table, near_accum, table, accum, inverse, table_out, line_out):
+    count, first = table.shape[0], side[...] == 0
+    rows, far = adagrad(other[:count, :], table[...], accum[...], inverse[...])
+    near_rows, near = near_table[...], near_accum[...]
+    table_out[:count, :] = jnp.where(first, near_rows, rows)
+    table_out[count:, :] = jnp.where(first, rows, near_rows)
+    tall = jnp.concatenate([jnp.where(first, near, far), jnp.where(first, far, near)])
+    wide = jnp.pad(tall, ((0, -2 * count % 128), (0, 0)))
     wide = jnp.broadcast_to(wide, (wide.shape[0], 128))
     line_out[...] = jnp.transpose(wide)[:1, : 2 * count]
 
@@ -540,7 +539,9 @@
             parts = gather_whole(unit.astype(f16), far_unit.astype(f16))
         else:
             outs = [(table.shape, f32), (line.shape, f32)]
-            args = [jnp.full((1, 1), side), mine, other, *near, *far]
+            kernel = functools.partial(update_kernel, scale)
+            near = call(kernel, half_shard[:2], mine, *near)
+            args = [jnp.full((1, 1), side), other, *near, *far]
             table, line = call(finish_kernel, outs, *args)
 
     return (loss, query_grad, table, line[0], fifo)

time: 68.3 us -> 68.3 us (level)
    pallas_call x12 -> x13, Pallas kernels: 10.9 us -> 11.1 us  [call(): pl.pallas_call(kernel, out_shape=[jax.ShapeDtypeStruct(shape, dtype) for...]
where the time goes in v10:
time: 68.3 us; the launch traced here: 68 us
  starting transfers between devices  28.5 us (42%)
  waiting for transfers between devices  23.5 us (34%)
  Pallas kernels  11.1 us (16%)
  local copies, waits for them, and re-layouts  1.79 us (3%)
  between operations  1.69 us (2%)
  other arithmetic  1.39 us (2%)
    ppermute x27, starting transfers between devices, flip(): lax.ppermute(piece, ('batch', 'table'), [(i ^ mask, i) for i in range(cou...  20.6 us
    ppermute x27, waiting for transfers between devices, flip(): lax.ppermute(piece, ('batch', 'table'), [(i ^ mask, i) for i in range(cou...  15.4 us
    pallas_call x13, Pallas kernels, call(): pl.pallas_call(kernel, out_shape=[jax.ShapeDtypeStruct(shape, dtype) for...  11.1 us
    ppermute x2, waiting for transfers between devices, turned(): found.append(lax.ppermute(piece, 'batch', pairs))  5.78 us
    all_to_all x1, starting transfers between devices, per_device(): lax.all_to_all(queue, ('batch', 'table'), 0, 0, tiled=True)  5.03 us
    ppermute x2, starting transfers between devices, turned(): found.append(lax.ppermute(piece, 'batch', pairs))  2.87 us
    all_to_all x1, waiting for transfers between devices, per_device(): lax.all_to_all(queue, ('batch', 'table'), 0, 0, tiled=True)  2.32 us
  transfers between devices with their start and end apart: 30, of which 18 were waited for; matrix products, arithmetic and copies ran while one was open for 3% of the time, Pallas kernels for 12%

profile of v10, /device:TPU:0, one launch (start us, length us, event | category | flops | bytes accessed | tf_op | source)
XLA Modules:
  0.0 68.0 jit_solution(1444390184243351854)
XLA Ops:
  0.6 3.0 %collective-permute-start = (f32[480,128]{1,0:T(8,128)}, f32[480,128]{1,0:T(8,128)S(1)}, u32[]{:S(2)}, u32[]{:S(2)}) collective-permute-start(f32[480,128]{1,0:T(8,128)} %refs_0_.3), channel_id=1, source_target_pairs={{2,0},{3,1},{0,2},{1,3},{6,4},{7,5},{4,6},{5,7},{10,8},{11,9},{8,1... | collective-permute-start | bytes 737288 | tf_op jit(solution)/shard_map/ppermute | solution.py:40
  5.0 5.0 %all-to-all-start = ((bf16[32,8,128]{2,1,0:T(8,128)(2,1)}), bf16[32,8,128]{2,1,0:T(8,128)(2,1)S(1)}, u32[]{:S(2)}, u32[]{:S(2)}) async-start(bf16[32,8,128]{2,1,0:T(8,128)(2,1)} %broadcast_in_dim.65), calls=%async_computation | async-start | bytes 131072 | tf_op jit(solution)/shard_map/all_to_all | solution.py:433
  11.7 2.0 %shard_map.110 = (f32[512,128]{1,0:T(8,128)}, f32[512,128]{1,0:T(8,128)S(1)}, f32[512,1]{1,0:T(8,128)}, bf16[512,128]{1,0:T(8,128)(2,1)S(1)}, bf16[512,128]{1,0:...) custom-call(bf16[2,512,128]{2,1,0:T(8,128)(2,1)S(1)} %copy-done, ...), custom_call_target="tpu_custom_call" | custom-call | tf_op jit(solution)/shard_map/pallas_call | solution.py:334
  15.1 2.3 %all-to-all-done = bf16[32,8,128]{2,1,0:T(8,128)(2,1)S(1)} async-done(((bf16[32,8,128]{2,1,0:T(8,128)(2,1)}), bf16[32,8,128]{2,1,0:T(8,128)(2,1)S(1)}, u32[]{:S(2)}, u32[]{:S(2)}) %all-to-all-start) | async-done | bytes 65568 | tf_op jit(solution)/shard_map/all_to_all | solution.py:433
  19.7 1.3 %collective-permute-start.9 = (f16[248,128]{1,0:T(8,128)(2,1)S(1)}, f16[248,128]{1,0:T(8,128)(2,1)S(1)}, u32[]{:S(2)}, u32[]{:S(2)}) collective-permute-start(f16[248,128]{1,0:T(8,128)(2,1)S(1)} %get-tuple-element.101), channel_id=1, source_target_pairs={{2,0},{3,1},{0,2},{1,3},{6,4},{7,5},{4,6},{5,7},{10,8},{11,9},{8,1... | collective-permute-start | bytes 190472 | tf_op jit(solution)/shard_map/ppermute | solution.py:40
  21.1 1.4 %collective-permute-start.8 = (f16[248,128]{1,0:T(8,128)(2,1)S(1)}, f16[248,128]{1,0:T(8,128)(2,1)S(1)}, u32[]{:S(2)}, u32[]{:S(2)}) collective-permute-start(f16[248,128]{1,0:T(8,128)(2,1)S(1)} %get-tuple-element.99), channel_id=1, source_target_pairs={{4,0},{5,1},{6,2},{7,3},{0,4},{1,5},{2,6},{3,7},{12,8},{13,9},{14,... | collective-permute-start | bytes 190472 | tf_op jit(solution)/shard_map/ppermute | solution.py:40
  22.5 2.2 %collective-permute-done.10 = f16[248,128]{1,0:T(8,128)(2,1)S(1)} collective-permute-done((f16[248,128]{1,0:T(8,128)(2,1)S(1)}, f16[248,128]{1,0:T(8,128)(2,1)S(1)}, u32[]{:S(2)}, u32[]{:S(2)}) %collective-permute-start.10) | collective-permute-done | bytes 63520 | tf_op jit(solution)/shard_map/ppermute | solution.py:40
  25.4 1.5 %collective-permute-start.11 = (f16[248,128]{1,0:T(8,128)(2,1)S(1)}, f16[248,128]{1,0:T(8,128)(2,1)S(1)}, u32[]{:S(2)}, u32[]{:S(2)}) collective-permute-start(f16[248,128]{1,0:T(8,128)(2,1)S(1)} %fusion.9), channel_id=1, source_target_pairs={{16,0},{20,4},{24,8},{28,12},{0,16},{4,20},{8,24},{12,28},{17,1},{... | collective-permute-start | bytes 190472 | tf_op jit(solution)/shard_map/ppermute | solution.py:51
  28.6 2.7 %collective-permute-done.11 = f16[248,128]{1,0:T(8,128)(2,1)S(1)} collective-permute-done((f16[248,128]{1,0:T(8,128)(2,1)S(1)}, f16[248,128]{1,0:T(8,128)(2,1)S(1)}, u32[]{:S(2)}, u32[]{:S(2)}) %collective-permute-start.11) | collective-permute-done | bytes 63520 | tf_op jit(solution)/shard_map/ppermute | solution.py:51
  31.4 2.8 %collective-permute-start.14 = (f16[248,128]{1,0:T(8,128)(2,1)S(1)}, f16[248,128]{1,0:T(8,128)(2,1)S(1)}, u32[]{:S(2)}, u32[]{:S(2)}) collective-permute-start(f16[248,128]{1,0:T(8,128)(2,1)S(1)} %add_convert_fusion.1), channel_id=1, source_target_pairs={{12,0},{13,1},{14,2},{15,3},{8,4},{9,5},{10,6},{11,7},{4,8},{5,9},... | collective-permute-start | bytes 190472 | tf_op jit(solution)/shard_map/ppermute | solution.py:40
  37.2 1.4 %collective-permute-done.13 = f16[248,128]{1,0:T(8,128)(2,1)S(1)} collective-permute-done((f16[248,128]{1,0:T(8,128)(2,1)S(1)}, f16[248,128]{1,0:T(8,128)(2,1)S(1)}, u32[]{:S(2)}, u32[]{:S(2)}) %collective-permute-start.13) | collective-permute-done | bytes 63520 | tf_op jit(solution)/shard_map/ppermute | solution.py:40
  41.2 2.1 %collective-permute-done.16 = f16[240,128]{1,0:T(8,128)(2,1)S(1)} collective-permute-done((f16[240,128]{1,0:T(8,128)(2,1)S(1)}, f16[240,128]{1,0:T(8,128)(2,1)S(1)}, u32[]{:S(2)}, u32[]{:S(2)}) %collective-permute-start.16) | collective-permute-done | bytes 61472 | tf_op jit(solution)/shard_map/ppermute | solution.py:40
  43.3 1.1 %shard_map.117 = (f32[512,128]{1,0:T(8,128)S(1)}, f32[512,128]{1,0:T(8,128)S(1)}, f32[512,1]{1,0:T(8,128)S(1)}) custom-call(bf16[2,512,128]{2,1,0:T(8,128)(2,1)S(1)} %copy-done, s32[1,512]{1,0:T(1,128)S(1)} %multiply_add_fusion.1.line.found_line, bf16[256,128]{1,0:T(8,128)(2,1)S(1)} %get-tuple-element.52.negatives, ...), custom_call_target="tpu_custom_call" | custom-call | tf_op jit(solution)/shard_map/pallas_call | solution.py:334
  44.5 1.2 %shard_map.118 = (bf16[992,128]{1,0:T(8,128)(2,1)S(1)}, bf16[512,128]{1,0:T(8,128)(2,1)S(1)}, f32[512,128]{1,0:T(8,128)S(1)}, f32[8,128]{1,0:T(8,128)S(1)}) custom-call(f32[512,128]{1,0:T(8,128)S(1)} %get-tuple-element.62.found, s32[1,512]{1,0:T(1,128)S(1)} %multiply_add_fusion.1.line.found_line, s32[1,512]{1,0:T(1,128)S(1)} %get-tuple-element.106.line, ...), custom_call_target="tpu_custom_call" | custom-call | tf_op jit(solution)/shard_map/pallas_call | solution.py:334
  48.2 1.3 %collective-permute-start.24 = (f16[248,128]{1,0:T(8,128)(2,1)S(1)}, f16[248,128]{1,0:T(8,128)(2,1)S(1)}, u32[]{:S(2)}, u32[]{:S(2)}) collective-permute-start(f16[248,128]{1,0:T(8,128)(2,1)S(1)} %get-tuple-element.97), channel_id=1, source_target_pairs={{6,0},{7,1},{4,2},{5,3},{2,4},{3,5},{0,6},{1,7},{14,8},{15,9},{12,... | collective-permute-start | bytes 190472 | tf_op jit(solution)/shard_map/ppermute | solution.py:40
  49.4 1.6 %collective-permute-start.23 = (f16[248,128]{1,0:T(8,128)(2,1)S(1)}, f16[248,128]{1,0:T(8,128)(2,1)S(1)}, u32[]{:S(2)}, u32[]{:S(2)}) collective-permute-start(f16[248,128]{1,0:T(8,128)(2,1)S(1)} %get-tuple-element.96), channel_id=1, source_target_pairs={{2,0},{3,1},{0,2},{1,3},{6,4},{7,5},{4,6},{5,7},{10,8},{11,9},{8,1... | collective-permute-start | bytes 190472 | tf_op jit(solution)/shard_map/ppermute | solution.py:40
  51.0 1.5 %collective-permute-done.22 = f16[248,128]{1,0:T(8,128)(2,1)S(1)} collective-permute-done((f16[248,128]{1,0:T(8,128)(2,1)S(1)}, f16[248,128]{1,0:T(8,128)(2,1)S(1)}, u32[]{:S(2)}, u32[]{:S(2)}) %collective-permute-start.22) | collective-permute-done | bytes 63520 | tf_op jit(solution)/shard_map/ppermute | solution.py:40
  52.5 1.2 %collective-permute-done.24 = f16[248,128]{1,0:T(8,128)(2,1)S(1)} collective-permute-done((f16[248,128]{1,0:T(8,128)(2,1)S(1)}, f16[248,128]{1,0:T(8,128)(2,1)S(1)}, u32[]{:S(2)}, u32[]{:S(2)}) %collective-permute-start.24) | collective-permute-done | bytes 63520 | tf_op jit(solution)/shard_map/ppermute | solution.py:40
  54.5 1.4 %collective-permute-start.25 = (f16[248,128]{1,0:T(8,128)(2,1)S(1)}, f16[248,128]{1,0:T(8,128)(2,1)S(1)}, u32[]{:S(2)}, u32[]{:S(2)}) collective-permute-start(f16[248,128]{1,0:T(8,128)(2,1)S(1)} %fusion.6), channel_id=1, source_target_pairs={{16,0},{20,4},{24,8},{28,12},{0,16},{4,20},{8,24},{12,28},{17,1},{... | collective-permute-start | bytes 190472 | tf_op jit(solution)/shard_map/ppermute | solution.py:51
  55.8 1.5 %shard_map.120 = (f32[2,512]{1,0:T(2,128)}, bf16[2,512,128]{2,1,0:T(8,128)(2,1)}, bf16[8,128]{1,0:T(8,128)(2,1)}, f32[248,128]{1,0:T(8,128)S(1)}) custom-call(bf16[2,512,128]{2,1,0:T(8,128)(2,1)S(1)} %copy-done, f32[512,128]{1,0:T(8,128)S(1)} %get-tuple-element.65.item, bf16[256,128]{1,0:T(8,128)(2,1)S(1)} %get-tuple-element.52.negatives, ...), custom_call_target="tpu_custom_call" | custom-call | tf_op jit(solution)/shard_map/pallas_call | solution.py:334
  57.3 3.1 %collective-permute-done.25 = f16[248,128]{1,0:T(8,128)(2,1)S(1)} collective-permute-done((f16[248,128]{1,0:T(8,128)(2,1)S(1)}, f16[248,128]{1,0:T(8,128)(2,1)S(1)}, u32[]{:S(2)}, u32[]{:S(2)}) %collective-permute-start.25) | collective-permute-done | bytes 63520 | tf_op jit(solution)/shard_map/ppermute | solution.py:51
  60.6 2.1 %collective-permute-start.27 = (f16[248,128]{1,0:T(8,128)(2,1)S(1)}, f16[248,128]{1,0:T(8,128)(2,1)S(1)}, u32[]{:S(2)}, u32[]{:S(2)}) collective-permute-start(f16[248,128]{1,0:T(8,128)(2,1)S(1)} %add_convert_fusion), channel_id=1, source_target_pairs={{12,0},{13,1},{14,2},{15,3},{8,4},{9,5},{10,6},{11,7},{4,8},{5,9},... | collective-permute-start | bytes 190472 | tf_op jit(solution)/shard_map/ppermute | solution.py:40
  62.7 1.2 %collective-permute-start.26 = (f16[248,128]{1,0:T(8,128)(2,1)S(1)}, f16[248,128]{1,0:T(8,128)(2,1)S(1)}, u32[]{:S(2)}, u32[]{:S(2)}) collective-permute-start(f16[248,128]{1,0:T(8,128)(2,1)S(1)} %add_convert_fusion), channel_id=1, source_target_pairs={{4,0},{5,1},{6,2},{7,3},{0,4},{1,5},{2,6},{3,7},{12,8},{13,9},{14,... | collective-permute-start | bytes 190472 | tf_op jit(solution)/shard_map/ppermute | solution.py:40
  65.8 1.2 %collective-permute-done.26 = f16[248,128]{1,0:T(8,128)(2,1)S(1)} collective-permute-done((f16[248,128]{1,0:T(8,128)(2,1)S(1)}, f16[248,128]{1,0:T(8,128)(2,1)S(1)}, u32[]{:S(2)}, u32[]{:S(2)}) %collective-permute-start.26) | collective-permute-done | bytes 63520 | tf_op jit(solution)/shard_map/ppermute | solution.py:40
  (97 shorter events, 20.3 us)
Async XLA Ops:
  0.6 9.4 %collective-permute-start = (f32[480,128]{1,0:T(8,128)}, f32[480,128]{1,0:T(8,128)S(1)}, u32[]{:S(2)}, u32[]{:S(2)}) collective-permute-start(f32[480,128]{1,0:T(8,128)} %refs_0_.3), channel_id=1, source_target_pairs={{2,0},{3,1},{0,2},{1,3},{6,4},{7,5},{4,6},{5,7},{10,8},{11,9},{8,1... | collective-permute-start | bytes 737288 | tf_op jit(solution)/shard_map/ppermute | solution.py:40
  3.6 7.5 %collective-permute-start.1 = (f32[480,128]{1,0:T(8,128)}, f32[480,128]{1,0:T(8,128)S(1)}, u32[]{:S(2)}, u32[]{:S(2)}) collective-permute-start(f32[480,128]{1,0:T(8,128)} %refs_0_.3), channel_id=1, source_target_pairs={{1,0},{0,1},{3,2},{2,3},{5,4},{4,5},{7,6},{6,7},{9,8},{8,9},{11,10... | collective-permute-start | bytes 737288 | tf_op jit(solution)/shard_map/ppermute | solution.py:40
  5.0 12.5 %all-to-all-start = ((bf16[32,8,128]{2,1,0:T(8,128)(2,1)}), bf16[32,8,128]{2,1,0:T(8,128)(2,1)S(1)}, u32[]{:S(2)}, u32[]{:S(2)}) async-start(bf16[32,8,128]{2,1,0:T(8,128)(2,1)} %broadcast_in_dim.65), calls=%async_computation | async-start | bytes 131072 | tf_op jit(solution)/shard_map/all_to_all | solution.py:433
  13.7 4.4 %collective-permute-start.4 = (bf16[256,128]{1,0:T(8,128)(2,1)S(1)}, bf16[256,128]{1,0:T(8,128)(2,1)S(1)}, u32[]{:S(2)}, u32[]{:S(2)}) collective-permute-start(bf16[256,128]{1,0:T(8,128)(2,1)S(1)} %get-tuple-element.105), channel_id=1, source_target_pairs={{1,0},{0,1},{3,2},{2,3},{5,4},{4,5},{7,6},{6,7},{9,8},{8,9},{11,10... | collective-permute-start | bytes 196616 | tf_op jit(solution)/shard_map/ppermute | solution.py:40
  14.0 4.1 %collective-permute-start.3 = (bf16[256,128]{1,0:T(8,128)(2,1)S(1)}, bf16[256,128]{1,0:T(8,128)(2,1)S(1)}, u32[]{:S(2)}, u32[]{:S(2)}) collective-permute-start(bf16[256,128]{1,0:T(8,128)(2,1)S(1)} %get-tuple-element.104), channel_id=1, source_target_pairs={{1,0},{0,1},{3,2},{2,3},{5,4},{4,5},{7,6},{6,7},{9,8},{8,9},{11,10... | collective-permute-start | bytes 196616 | tf_op jit(solution)/shard_map/ppermute | solution.py:40
  14.3 3.8 %collective-permute-start.7 = (f32[16,512]{1,0:T(8,128)S(1)}, f32[16,512]{1,0:T(8,128)S(1)}, u32[]{:S(2)}, u32[]{:S(2)}) collective-permute-start(f32[16,512]{1,0:T(8,128)S(1)} %get-tuple-element.48.notes), channel_id=1, source_target_pairs={{1,0},{0,1},{3,2},{2,3},{5,4},{4,5},{7,6},{6,7},{9,8},{8,9},{11,10... | collective-permute-start | bytes 98312 | tf_op jit(solution)/shard_map/ppermute | solution.py:40
  19.0 5.7 %collective-permute-start.10 = (f16[248,128]{1,0:T(8,128)(2,1)S(1)}, f16[248,128]{1,0:T(8,128)(2,1)S(1)}, u32[]{:S(2)}, u32[]{:S(2)}) collective-permute-start(f16[248,128]{1,0:T(8,128)(2,1)S(1)} %get-tuple-element.100), channel_id=1, source_target_pairs={{6,0},{7,1},{4,2},{5,3},{2,4},{3,5},{0,6},{1,7},{14,8},{15,9},{12,... | collective-permute-start | bytes 190472 | tf_op jit(solution)/shard_map/ppermute | solution.py:40
  19.7 4.9 %collective-permute-start.9 = (f16[248,128]{1,0:T(8,128)(2,1)S(1)}, f16[248,128]{1,0:T(8,128)(2,1)S(1)}, u32[]{:S(2)}, u32[]{:S(2)}) collective-permute-start(f16[248,128]{1,0:T(8,128)(2,1)S(1)} %get-tuple-element.101), channel_id=1, source_target_pairs={{2,0},{3,1},{0,2},{1,3},{6,4},{7,5},{4,6},{5,7},{10,8},{11,9},{8,1... | collective-permute-start | bytes 190472 | tf_op jit(solution)/shard_map/ppermute | solution.py:40
  21.1 4.3 %collective-permute-start.8 = (f16[248,128]{1,0:T(8,128)(2,1)S(1)}, f16[248,128]{1,0:T(8,128)(2,1)S(1)}, u32[]{:S(2)}, u32[]{:S(2)}) collective-permute-start(f16[248,128]{1,0:T(8,128)(2,1)S(1)} %get-tuple-element.99), channel_id=1, source_target_pairs={{4,0},{5,1},{6,2},{7,3},{0,4},{1,5},{2,6},{3,7},{12,8},{13,9},{14,... | collective-permute-start | bytes 190472 | tf_op jit(solution)/shard_map/ppermute | solution.py:40
  25.4 5.9 %collective-permute-start.11 = (f16[248,128]{1,0:T(8,128)(2,1)S(1)}, f16[248,128]{1,0:T(8,128)(2,1)S(1)}, u32[]{:S(2)}, u32[]{:S(2)}) collective-permute-start(f16[248,128]{1,0:T(8,128)(2,1)S(1)} %fusion.9), channel_id=1, source_target_pairs={{16,0},{20,4},{24,8},{28,12},{0,16},{4,20},{8,24},{12,28},{17,1},{... | collective-permute-start | bytes 190472 | tf_op jit(solution)/shard_map/ppermute | solution.py:51
  31.3 4.3 %collective-permute-start.12 = (f16[248,128]{1,0:T(8,128)(2,1)S(1)}, f16[248,128]{1,0:T(8,128)(2,1)S(1)}, u32[]{:S(2)}, u32[]{:S(2)}) collective-permute-start(f16[248,128]{1,0:T(8,128)(2,1)S(1)} %add_convert_fusion.1), channel_id=1, source_target_pairs={{8,0},{9,1},{10,2},{11,3},{12,4},{13,5},{14,6},{15,7},{0,8},{1,9},... | collective-permute-start | bytes 190472 | tf_op jit(solution)/shard_map/ppermute | solution.py:40
  31.4 5.7 %collective-permute-start.14 = (f16[248,128]{1,0:T(8,128)(2,1)S(1)}, f16[248,128]{1,0:T(8,128)(2,1)S(1)}, u32[]{:S(2)}, u32[]{:S(2)}) collective-permute-start(f16[248,128]{1,0:T(8,128)(2,1)S(1)} %add_convert_fusion.1), channel_id=1, source_target_pairs={{12,0},{13,1},{14,2},{15,3},{8,4},{9,5},{10,6},{11,7},{4,8},{5,9},... | collective-permute-start | bytes 190472 | tf_op jit(solution)/shard_map/ppermute | solution.py:40
  34.3 4.2 %collective-permute-start.13 = (f16[248,128]{1,0:T(8,128)(2,1)S(1)}, f16[248,128]{1,0:T(8,128)(2,1)S(1)}, u32[]{:S(2)}, u32[]{:S(2)}) collective-permute-start(f16[248,128]{1,0:T(8,128)(2,1)S(1)} %add_convert_fusion.1), channel_id=1, source_target_pairs={{4,0},{5,1},{6,2},{7,3},{0,4},{1,5},{2,6},{3,7},{12,8},{13,9},{14,... | collective-permute-start | bytes 190472 | tf_op jit(solution)/shard_map/ppermute | solution.py:40
  36.1 4.6 %collective-permute-start.15 = (f16[240,128]{1,0:T(8,128)(2,1)S(1)}, f16[240,128]{1,0:T(8,128)(2,1)S(1)}, u32[]{:S(2)}, u32[]{:S(2)}) collective-permute-start(f16[240,128]{1,0:T(8,128)(2,1)S(1)} %get-tuple-element.93), channel_id=1, source_target_pairs={{2,0},{3,1},{0,2},{1,3},{6,4},{7,5},{4,6},{5,7},{10,8},{11,9},{8,1... | collective-permute-start | bytes 184328 | tf_op jit(solution)/shard_map/ppermute | solution.py:40
  36.1 7.1 %collective-permute-start.17 = (f16[240,128]{1,0:T(8,128)(2,1)S(1)}, f16[240,128]{1,0:T(8,128)(2,1)S(1)}, u32[]{:S(2)}, u32[]{:S(2)}) collective-permute-start(f16[240,128]{1,0:T(8,128)(2,1)S(1)} %get-tuple-element.93), channel_id=1, source_target_pairs={{1,0},{0,1},{3,2},{2,3},{5,4},{4,5},{7,6},{6,7},{9,8},{8,9},{11,10... | collective-permute-start | bytes 184328 | tf_op jit(solution)/shard_map/ppermute | solution.py:40
  38.9 4.3 %collective-permute-start.16 = (f16[240,128]{1,0:T(8,128)(2,1)S(1)}, f16[240,128]{1,0:T(8,128)(2,1)S(1)}, u32[]{:S(2)}, u32[]{:S(2)}) collective-permute-start(f16[240,128]{1,0:T(8,128)(2,1)S(1)} %get-tuple-element.91), channel_id=1, source_target_pairs={{2,0},{3,1},{0,2},{1,3},{6,4},{7,5},{4,6},{5,7},{10,8},{11,9},{8,1... | collective-permute-start | bytes 184328 | tf_op jit(solution)/shard_map/ppermute | solution.py:40
  39.4 3.9 %collective-permute-start.18 = (f16[240,128]{1,0:T(8,128)(2,1)S(1)}, f16[240,128]{1,0:T(8,128)(2,1)S(1)}, u32[]{:S(2)}, u32[]{:S(2)}) collective-permute-start(f16[240,128]{1,0:T(8,128)(2,1)S(1)} %get-tuple-element.91), channel_id=1, source_target_pairs={{1,0},{0,1},{3,2},{2,3},{5,4},{4,5},{7,6},{6,7},{9,8},{8,9},{11,10... | collective-permute-start | bytes 184328 | tf_op jit(solution)/shard_map/ppermute | solution.py:40
  47.5 5.1 %collective-permute-start.22 = (f16[248,128]{1,0:T(8,128)(2,1)S(1)}, f16[248,128]{1,0:T(8,128)(2,1)S(1)}, u32[]{:S(2)}, u32[]{:S(2)}) collective-permute-start(f16[248,128]{1,0:T(8,128)(2,1)S(1)} %get-tuple-element.98), channel_id=1, source_target_pairs={{4,0},{5,1},{6,2},{7,3},{0,4},{1,5},{2,6},{3,7},{12,8},{13,9},{14,... | collective-permute-start | bytes 190472 | tf_op jit(solution)/shard_map/ppermute | solution.py:40
  48.2 5.6 %collective-permute-start.24 = (f16[248,128]{1,0:T(8,128)(2,1)S(1)}, f16[248,128]{1,0:T(8,128)(2,1)S(1)}, u32[]{:S(2)}, u32[]{:S(2)}) collective-permute-start(f16[248,128]{1,0:T(8,128)(2,1)S(1)} %get-tuple-element.97), channel_id=1, source_target_pairs={{6,0},{7,1},{4,2},{5,3},{2,4},{3,5},{0,6},{1,7},{14,8},{15,9},{12,... | collective-permute-start | bytes 190472 | tf_op jit(solution)/shard_map/ppermute | solution.py:40
  49.4 5.0 %collective-permute-start.23 = (f16[248,128]{1,0:T(8,128)(2,1)S(1)}, f16[248,128]{1,0:T(8,128)(2,1)S(1)}, u32[]{:S(2)}, u32[]{:S(2)}) collective-permute-start(f16[248,128]{1,0:T(8,128)(2,1)S(1)} %get-tuple-element.96), channel_id=1, source_target_pairs={{2,0},{3,1},{0,2},{1,3},{6,4},{7,5},{4,6},{5,7},{10,8},{11,9},{8,1... | collective-permute-start | bytes 190472 | tf_op jit(solution)/shard_map/ppermute | solution.py:40
  54.5 5.9 %collective-permute-start.25 = (f16[248,128]{1,0:T(8,128)(2,1)S(1)}, f16[248,128]{1,0:T(8,128)(2,1)S(1)}, u32[]{:S(2)}, u32[]{:S(2)}) collective-permute-start(f16[248,128]{1,0:T(8,128)(2,1)S(1)} %fusion.6), channel_id=1, source_target_pairs={{16,0},{20,4},{24,8},{28,12},{0,16},{4,20},{8,24},{12,28},{17,1},{... | collective-permute-start | bytes 190472 | tf_op jit(solution)/shard_map/ppermute | solution.py:51
  60.4 4.3 %collective-permute-start.28 = (f16[248,128]{1,0:T(8,128)(2,1)S(1)}, f16[248,128]{1,0:T(8,128)(2,1)S(1)}, u32[]{:S(2)}, u32[]{:S(2)}) collective-permute-start(f16[248,128]{1,0:T(8,128)(2,1)S(1)} %add_convert_fusion), channel_id=1, source_target_pairs={{8,0},{9,1},{10,2},{11,3},{12,4},{13,5},{14,6},{15,7},{0,8},{1,9},... | collective-permute-start | bytes 190472 | tf_op jit(solution)/shard_map/ppermute | solution.py:40
  60.6 5.1 %collective-permute-start.27 = (f16[248,128]{1,0:T(8,128)(2,1)S(1)}, f16[248,128]{1,0:T(8,128)(2,1)S(1)}, u32[]{:S(2)}, u32[]{:S(2)}) collective-permute-start(f16[248,128]{1,0:T(8,128)(2,1)S(1)} %add_convert_fusion), channel_id=1, source_target_pairs={{12,0},{13,1},{14,2},{15,3},{8,4},{9,5},{10,6},{11,7},{4,8},{5,9},... | collective-permute-start | bytes 190472 | tf_op jit(solution)/shard_map/ppermute | solution.py:40
  62.7 4.2 %collective-permute-start.26 = (f16[248,128]{1,0:T(8,128)(2,1)S(1)}, f16[248,128]{1,0:T(8,128)(2,1)S(1)}, u32[]{:S(2)}, u32[]{:S(2)}) collective-permute-start(f16[248,128]{1,0:T(8,128)(2,1)S(1)} %add_convert_fusion), channel_id=1, source_target_pairs={{4,0},{5,1},{6,2},{7,3},{0,4},{1,5},{2,6},{3,7},{12,8},{13,9},{14,... | collective-permute-start | bytes 190472 | tf_op jit(solution)/shard_map/ppermute | solution.py:40
  (12 other events, 43.0 us)
